TPU v7x, 256 devices: a whole 4x4x8 slice. The times are simulated.
256 devices in a mesh: wide: 16 (over x, y_lo, core), narrow: 16 (over z, y_hi).
Axes of the slice: x: 4, y: 4 (y_hi: 2, y_lo: 2; y = y_hi * 2 + y_lo), z: 8, core: 2. Of those that a mesh axis runs over, the one named last changes fastest.
Arguments:
- hamiltonian_tiles: float32 [24576, 24576], P('wide', 'narrow'), may hold values from -0.02734375 to 0.02734375
- row_columns: int32 [16, 16], P('wide'), may hold values from 0 to 15, as said below
- start_vectors: float32 [24576, 128], P(('wide', 'narrow')), may hold values from -60 to 60
Outputs:
- new_vectors: float32 [24576, 128], P(('wide', 'narrow'))
Inputs may be any that keep to these rules, and one draw needn't show every extreme that they name: For block row r = w + j // 16, row_columns[w, j] = (r + d) mod 16, with d = 0 where j % 16 = 0 and, for the other tiles of that block row, distinct d between 1 and 15; a block's mirror may also be stored.
All inputs are finite; a program needn't handle non-finite values.
Results may differ from a plain program's by a relative error of at most 0.0003.
Values sent between devices are 32-bit elements; how exact they have to be, the bound alone decides.
No kernel may reach another device: no remote copies, remote signals or barrier semaphores. Data moves between devices by JAX's collectives and lax.ppermute only.
A program may use at most 64 MiB of HBM per device.

v0:
```python
import jax
import jax.numpy as jnp
from jax import lax
from jax.experimental import pallas as pl
from jax.experimental.pallas import tpu as pltpu
from jax.sharding import PartitionSpec as P

NS_STEPS = 5
WIDE, NARROW = "wide", "narrow"
HIGHEST = lax.Precision.HIGHEST


def exchange(parts, axis):
    return lax.all_to_all(parts, axis, 0, 0, tiled=True)


def to_everyone(value, axis):
    return exchange(jnp.broadcast_to(value[None], (lax.axis_size(axis), *value.shape)), axis)


def move_blocks(blocks, columns, scatter):
    count = blocks.shape[0]

    def kernel(columns_ref, blocks_ref, moved_ref, done):
        copies = []
        for i in range(count):
            column = columns_ref[i]
            source, target = (i, column) if scatter else (column, i)
            copies.append(
                pltpu.make_async_copy(blocks_ref.at[source], moved_ref.at[target], done.at[i])
            )
        for copy in copies:
            copy.start()
        for copy in copies:
            copy.wait()

    return pl.pallas_call(
        kernel,
        out_shape=jax.ShapeDtypeStruct(blocks.shape, blocks.dtype),
        in_specs=[pl.BlockSpec(memory_space=pltpu.SMEM), pl.BlockSpec(memory_space=pl.ANY)],
        out_specs=pl.BlockSpec(memory_space=pl.ANY),
        scratch_shapes=[pltpu.SemaphoreType.DMA((count,))],
        compiler_params=pltpu.CompilerParams(vmem_limit_bytes=1 << 20),
        cost_estimate=pl.CostEstimate(flops=0, bytes_accessed=8 * blocks.size, transcendentals=0),
    )(columns, blocks)


def high_low(value):
    high = value.astype(jnp.bfloat16)
    return high, (value - high.astype(jnp.float32)).astype(jnp.bfloat16)


def product_of(left, right):
    return jnp.dot(left, right, preferred_element_type=jnp.float32)


def kernel_cost(tile, width):
    return pl.CostEstimate(flops=3 * tile.size * width, bytes_accessed=2 * tile.size, transcendentals=0)


def direct_half(tile, column_block, half, places):
    groups, _, rows, order = tile.shape
    width = column_block.shape[1]
    steps = 2
    each = groups // steps

    def kernel(where_ref, tile_ref, column_ref, out_ref, both):
        step = pl.program_id(0)

        @pl.when(step == 0)
        def _():
            high, low = high_low(column_ref[...])
            both[:, :width] = high
            both[:, width:] = low

        high, low = high_low(tile_ref[...].reshape(each * rows, order))
        wide = product_of(high, both[...])
        total = wide[:, :width] + wide[:, width:] + product_of(low, both[:, :width])
        for k in range(each):
            out_ref[where_ref[1 + step * each + k]] = total[k * rows : (k + 1) * rows]

    return pl.pallas_call(
        kernel,
        out_shape=jax.ShapeDtypeStruct((groups, rows, width), jnp.float32),
        grid_spec=pltpu.PrefetchScalarGridSpec(
            num_scalar_prefetch=1,
            grid=(steps,),
            in_specs=[
                pl.BlockSpec((each, 1, rows, order), lambda g, where: (g, where[0], 0, 0)),
                pl.BlockSpec((order, width), lambda g, where: (0, 0)),
            ],
            out_specs=pl.BlockSpec((groups, rows, width), lambda g, where: (0, 0, 0)),
            scratch_shapes=[pltpu.VMEM((order, 2 * width), jnp.bfloat16)],
        ),
        compiler_params=pltpu.CompilerParams(vmem_limit_bytes=60 << 20),
        cost_estimate=kernel_cost(tile, width),
    )(jnp.concatenate([half[None], places]), tile, column_block)


def transposed_half(tile, row_half, half, places, partial=None):
    groups, _, rows, order = tile.shape
    width = row_half.shape[2]
    depth = groups * rows
    steps = 3
    chunk = order // steps

    def kernel(where_ref, tile_ref, row_ref, *rest):
        partial_ref, (out_ref, gathered, both) = (rest[0], rest[1:]) if partial is not None else (None, rest)

        @pl.when(pl.program_id(0) == 0)
        def _():
            for k in range(groups):
                gathered[k * rows : (k + 1) * rows] = row_ref[where_ref[1 + k]]
            high, low = high_low(gathered[...].T)
            both[:width] = high
            both[width:] = low

        high, low = high_low(tile_ref[...].reshape(depth, chunk))
        wide = product_of(both[...], high)
        total = wide[:width] + wide[width:] + product_of(both[:width], low)
        if partial_ref is None:
            out_ref[...] = total
        else:
            out_ref[...] = (total + partial_ref[...]).T

    flat = pl.BlockSpec((width, chunk), lambda g, where: (0, g))
    return pl.pallas_call(
        kernel,
        out_shape=jax.ShapeDtypeStruct((width, order) if partial is None else (order, width), jnp.float32),
        grid_spec=pltpu.PrefetchScalarGridSpec(
            num_scalar_prefetch=1,
            grid=(steps,),
            in_specs=[
                pl.BlockSpec((groups, 1, rows, chunk), lambda g, where: (0, where[0], 0, g)),
                pl.BlockSpec((groups, rows, width), lambda g, where: (0, 0, 0)),
            ]
            + ([] if partial is None else [flat]),
            out_specs=flat if partial is None else pl.BlockSpec((chunk, width), lambda g, where: (g, 0)),
            scratch_shapes=[
                pltpu.VMEM((depth, width), jnp.float32),
                pltpu.VMEM((2 * width, depth), jnp.bfloat16),
            ],
        ),
        compiler_params=pltpu.CompilerParams(vmem_limit_bytes=60 << 20),
        cost_estimate=kernel_cost(tile, width),
    )(jnp.concatenate([half[None], places]), tile, row_half, *([] if partial is None else [partial]))


def swap(value, axis, bit):
    size = lax.axis_size(axis)
    return lax.ppermute(value, axis, [(i, i ^ bit) for i in range(size)])


def bits_of(size):
    bit = size // 2
    while bit:
        yield bit
        bit //= 2


def relative_places(mine, groups):
    offset = jnp.arange(groups, dtype=jnp.int32) ^ mine
    count = groups.bit_length() - 1
    return sum(((offset >> k) & 1) << (count - 1 - k) for k in range(count))


def doubled(held, axis, bits):
    for bit in bits:
        held = jnp.concatenate([held, swap(held, axis, bit)], axis=0)
    return held


def halved(mine, got, axis):
    for bit in reversed(list(bits_of(lax.axis_size(axis)))):
        if bit > 1:
            half = mine.shape[0] // 2
            sent = mine[half:] + got[half:]
            mine, got = mine[:half] + got[:half], swap(sent, axis, bit)
    return mine[0] + got[0]


def summed(value, axis):
    for bit in bits_of(lax.axis_size(axis)):
        value = value + swap(value, axis, bit)
    return value


def apply_hamiltonian(tile, columns, vectors):
    rows, width = vectors.shape
    count = lax.axis_size(NARROW)
    order = tile.shape[0]
    groups = count // 2
    me = lax.axis_index(NARROW).astype(jnp.int32)
    near, far = me & 1, (me & 1) ^ 1
    places = relative_places(me >> 1, groups)
    tile = tile.reshape(groups, 2, rows, order)
    with jax.named_scope("gather_wide"):
        slices = to_everyone(vectors, WIDE)
    bits = list(bits_of(groups))
    with jax.named_scope("gather_row"):
        near_rows = doubled(vectors[None], NARROW, [2 * bit for bit in bits[:2]])
        slices, near_rows = lax.optimization_barrier((slices, near_rows))
        near_rows = doubled(near_rows, NARROW, [2 * bit for bit in bits[2:]])
        far_rows = swap(near_rows, NARROW, 1)
    with jax.named_scope("gather_column"):
        picked = move_blocks(slices, columns, scatter=False)
        column_block = exchange(picked, NARROW).reshape(order, width)
    with jax.named_scope("transposed"):
        partial = transposed_half(tile, near_rows, near, places)
        transposed = transposed_half(tile, far_rows, far, places, partial)
    with jax.named_scope("back_transposed"):
        arrived = exchange(transposed.reshape(count, rows, width), NARROW)
        placed = move_blocks(arrived, columns, scatter=True)
    with jax.named_scope("direct"):
        sent = direct_half(tile, column_block, far, places)
        got = swap(sent, NARROW, 1)
        kept = direct_half(tile, column_block, near, places)
    with jax.named_scope("back_direct"):
        direct_sum = halved(kept, got, NARROW)
    with jax.named_scope("back_wide"):
        transposed_sum = exchange(placed, WIDE).sum(axis=0)
    return direct_sum + transposed_sum, (near_rows, far_rows)


def inverse_root(gram, total_rows):
    identity = jnp.eye(gram.shape[0], dtype=jnp.float32)
    scale = jnp.sqrt(jnp.sum(gram * gram) + 1e-06)
    current = gram / scale
    inverse = identity
    for repeat in range(NS_STEPS):
        middle = 1.5 * identity - 0.5 * jnp.dot(inverse, current, precision=HIGHEST)
        current = jnp.dot(current, middle, precision=HIGHEST)
        inverse = jnp.dot(middle, inverse, precision=HIGHEST)
    return inverse * jnp.sqrt(total_rows / scale)


def gram_of(value):
    return lax.dot_general(value, value, (((0,), (0,)), ((), ())), precision=HIGHEST)


def on_device(tile, row_columns, start_vectors):
    total_rows = float(lax.axis_size(WIDE) * lax.axis_size(NARROW) * start_vectors.shape[0])
    columns = row_columns[0]
    first, _ = apply_hamiltonian(tile, columns, start_vectors)
    second, first_halves = apply_hamiltonian(tile, columns, first)
    with jax.named_scope("gram_first"):
        grams = [gram_of(half.reshape(-1, half.shape[2])) for half in first_halves]
        gram_first = summed(grams[0] + grams[1], WIDE)
    with jax.named_scope("gram_second"):
        gram_second = summed(summed(gram_of(second), WIDE), NARROW)
    with jax.named_scope("inverse_first"):
        root_first = inverse_root(gram_first, total_rows)
    with jax.named_scope("inverse_second"):
        gram = jnp.dot(
            root_first.T, jnp.dot(gram_second, root_first, precision=HIGHEST), precision=HIGHEST
        )
        root_second = inverse_root(gram, total_rows)
    with jax.named_scope("finish"):
        return jnp.dot(
            jnp.dot(second, root_first, precision=HIGHEST), root_second, precision=HIGHEST
        )


def solution(mesh):
    return jax.shard_map(
        on_device,
        mesh=mesh,
        in_specs=(P(WIDE, NARROW), P(WIDE, None), P((WIDE, NARROW), None)),
        out_specs=P((WIDE, NARROW), None),
        check_vma=False,
    )
```

profile of v0, /device:TPU:8, one launch (start us, length us, event | category | flops | bytes accessed | tf_op | source)
XLA Modules:
  0.0 319.1 jit_solution(4815459611764895954)
XLA Ops:
  1.8 5.8 %all-to-all-start = ((f32[16,96,128]{2,1,0:T(8,128)}), f32[16,96,128]{2,1,0:T(8,128)S(1)}, u32[]{:S(2)}, u32[]{:S(2)}) async-start(f32[16,96,128]{2,1,0:T(8,128)} %broadcast_in_dim.13), calls=%async_computation | async-start | bytes 1572864 | tf_op jit(solution)/shard_map/gather_wide/all_to_all | solution.py:14
  7.6 7.2 %collective-permute-start = (f32[1,96,128]{2,1,0:T(8,128)}, f32[1,96,128]{2,1,0:T(8,128)S(1)}, u32[]{:S(2)}, u32[]{:S(2)}) collective-permute-start(f32[1,96,128]{2,1,0:T(8,128)} %bitcast.106), channel_id=1, source_target_pairs={{0,8},{1,9},{2,10},{3,11},{4,12},{5,13},{6,14},{7,15},{8,0},{9,1},... | collective-permute-start | bytes 147464 | tf_op jit(solution)/shard_map/gather_row/ppermute | solution.py:151
  17.9 2.9 collective-permute-start.1
  20.8 4.0 %collective-permute-done.1 = f32[2,96,128]{2,1,0:T(8,128)S(1)} collective-permute-done((f32[2,96,128]{2,1,0:T(8,128)S(1)}, f32[2,96,128]{2,1,0:T(8,128)S(1)}, u32[]{:S(2)}, u32[]{:S(2)}) %collective-permute-start.1) | collective-permute-done | bytes 98336 | tf_op jit(solution)/shard_map/gather_row/ppermute | solution.py:151
  27.9 8.2 %all-to-all-start.1 = ((f32[16,96,128]{2,1,0:T(8,128)}), f32[16,96,128]{2,1,0:T(8,128)S(1)}, u32[]{:S(2)}, u32[]{:S(2)}) async-start(f32[16,96,128]{2,1,0:T(8,128)} %gather_column.2), calls=%async_computation.1 | async-start | bytes 1572864 | tf_op jit(solution)/shard_map/gather_column/all_to_all | solution.py:14
  38.0 20.0 %collective-permute-done.6 = f32[4,96,128]{2,1,0:T(8,128)S(1)} collective-permute-done((f32[4,96,128]{2,1,0:T(8,128)S(1)}, f32[4,96,128]{2,1,0:T(8,128)S(1)}, u32[]{:S(2)}, u32[]{:S(2)}) %collective-permute-start.6) | collective-permute-done | bytes 196640 | tf_op jit(solution)/shard_map/gather_row/ppermute | solution.py:151
  58.1 3.1 collective-permute-start.7
  61.7 5.7 %transposed.4.rest_0_ = f32[128,1536]{1,0:T(8,128)} custom-call(s32[9]{0:T(128)} %get-tuple-element.23.where_ref, f32[8,2,96,1536]{3,2,1,0:T(8,128)} %bitcast.91, f32[8,96,128]{2,1,0:T(8,128)} %copy-done.6), custom_call_target="tpu_custom_call" | custom-call | flops 905969664 | bytes 4718592 | tf_op jit(solution)/shard_map/transposed/pallas_call | solution.py:127
  70.5 5.9 %transposed.5 = f32[1536,128]{1,0:T(8,128)} custom-call(s32[9]{0:T(128)} %get-tuple-element.24.where_ref, f32[8,2,96,1536]{3,2,1,0:T(8,128)} %bitcast.92, f32[8,96,128]{2,1,0:T(8,128)} %copy-done.7, f32[128,1536]{1,0:T(8,128)} %transposed.4.rest_0_), custom_call_target="tpu_custom_call" | custom-call | flops 905969664 | bytes 4718592 | tf_op jit(solution)/shard_map/transposed/pallas_call | solution.py:127
  76.4 8.1 %all-to-all-start.2 = ((f32[16,96,128]{2,1,0:T(8,128)}), f32[16,96,128]{2,1,0:T(8,128)S(1)}, u32[]{:S(2)}, u32[]{:S(2)}) async-start(f32[16,96,128]{2,1,0:T(8,128)} %bitcast.104), calls=%async_computation.2 | async-start | bytes 1572864 | tf_op jit(solution)/shard_map/back_transposed/all_to_all | solution.py:14
  84.5 5.1 %direct.5 = f32[8,96,128]{2,1,0:T(8,128)} custom-call(s32[9]{0:T(128)} %get-tuple-element.24.where_ref, f32[8,2,96,1536]{3,2,1,0:T(8,128)} %bitcast.93, f32[1536,128]{1,0:T(8,128)} %bitcast.101), custom_call_target="tpu_custom_call" | custom-call | flops 905969664 | bytes 4718592 | tf_op jit(solution)/shard_map/direct/pallas_call | solution.py:82
  89.6 3.4 %collective-permute-start.2 = (f32[8,96,128]{2,1,0:T(8,128)}, f32[8,96,128]{2,1,0:T(8,128)S(1)}, u32[]{:S(2)}, u32[]{:S(2)}) collective-permute-start(f32[8,96,128]{2,1,0:T(8,128)} %direct.5), channel_id=1, source_target_pairs={{0,1},{1,0},{2,3},{3,2},{4,5},{5,4},{6,7},{7,6},{8,9},{9,8},{10,11... | collective-permute-start | bytes 1179656 | tf_op jit(solution)/shard_map/direct/ppermute | solution.py:151
  93.1 5.0 %direct.4 = f32[8,96,128]{2,1,0:T(8,128)} custom-call(s32[9]{0:T(128)} %get-tuple-element.23.where_ref, f32[8,2,96,1536]{3,2,1,0:T(8,128)} %bitcast.94, f32[1536,128]{1,0:T(8,128)} %bitcast.102), custom_call_target="tpu_custom_call" | custom-call | flops 905969664 | bytes 4718592 | tf_op jit(solution)/shard_map/direct/pallas_call | solution.py:82
  98.1 9.0 %collective-permute-done.2 = f32[8,96,128]{2,1,0:T(8,128)S(1)} collective-permute-done((f32[8,96,128]{2,1,0:T(8,128)}, f32[8,96,128]{2,1,0:T(8,128)S(1)}, u32[]{:S(2)}, u32[]{:S(2)}) %collective-permute-start.2) | collective-permute-done | bytes 393248 | tf_op jit(solution)/shard_map/direct/ppermute | solution.py:151
  111.3 5.7 %all-to-all-start.3 = ((f32[16,96,128]{2,1,0:T(8,128)}), f32[16,96,128]{2,1,0:T(8,128)S(1)}, u32[]{:S(2)}, u32[]{:S(2)}) async-start(f32[16,96,128]{2,1,0:T(8,128)} %back_transposed.2), calls=%async_computation.3 | async-start | bytes 1572864 | tf_op jit(solution)/shard_map/back_wide/all_to_all | solution.py:14
  119.3 5.7 %collective-permute-done.4 = f32[2,96,128]{2,1,0:T(8,128)S(1)} collective-permute-done((f32[2,96,128]{2,1,0:T(8,128)S(1)}, f32[2,96,128]{2,1,0:T(8,128)S(1)}, u32[]{:S(2)}, u32[]{:S(2)}) %collective-permute-start.4) | collective-permute-done | bytes 98336 | tf_op jit(solution)/shard_map/back_direct/ppermute | solution.py:151
  125.0 4.4 %collective-permute-start.5 = (f32[1,96,128]{2,1,0:T(8,128)S(1)}, f32[1,96,128]{2,1,0:T(8,128)S(1)}, u32[]{:S(2)}, u32[]{:S(2)}) collective-permute-start(f32[1,96,128]{2,1,0:T(8,128)S(1)} %slice_add_fusion.10), channel_id=1, source_target_pairs={{0,8},{1,9},{2,10},{3,11},{4,12},{5,13},{6,14},{7,15},{8,0},{9,1},... | collective-permute-start | bytes 147464 | tf_op jit(solution)/shard_map/back_direct/ppermute | solution.py:151
  129.5 3.6 %collective-permute-done.5 = f32[1,96,128]{2,1,0:T(8,128)S(1)} collective-permute-done((f32[1,96,128]{2,1,0:T(8,128)S(1)}, f32[1,96,128]{2,1,0:T(8,128)S(1)}, u32[]{:S(2)}, u32[]{:S(2)}) %collective-permute-start.5) | collective-permute-done | bytes 49184 | tf_op jit(solution)/shard_map/back_direct/ppermute | solution.py:151
  134.1 5.7 %all-to-all-start.4 = ((f32[16,96,128]{2,1,0:T(8,128)}), f32[16,96,128]{2,1,0:T(8,128)S(1)}, u32[]{:S(2)}, u32[]{:S(2)}) async-start(f32[16,96,128]{2,1,0:T(8,128)} %broadcast_in_dim.17), calls=%async_computation.4 | async-start | bytes 1572864 | tf_op jit(solution)/shard_map/gather_wide/all_to_all | solution.py:14
  139.8 4.3 %collective-permute-start.8 = (f32[1,96,128]{2,1,0:T(8,128)S(1)}, f32[1,96,128]{2,1,0:T(8,128)S(1)}, u32[]{:S(2)}, u32[]{:S(2)}) collective-permute-start(f32[1,96,128]{2,1,0:T(8,128)S(1)} %fusion.17), channel_id=1, source_target_pairs={{0,8},{1,9},{2,10},{3,11},{4,12},{5,13},{6,14},{7,15},{8,0},{9,1},... | collective-permute-start | bytes 147464 | tf_op jit(solution)/shard_map/gather_row/ppermute | solution.py:151
  144.1 4.7 %collective-permute-done.8 = f32[1,96,128]{2,1,0:T(8,128)S(1)} collective-permute-done((f32[1,96,128]{2,1,0:T(8,128)S(1)}, f32[1,96,128]{2,1,0:T(8,128)S(1)}, u32[]{:S(2)}, u32[]{:S(2)}) %collective-permute-start.8) | collective-permute-done | bytes 49184 | tf_op jit(solution)/shard_map/gather_row/ppermute | solution.py:151
  149.0 5.5 %collective-permute-done.9 = f32[2,96,128]{2,1,0:T(8,128)S(1)} collective-permute-done((f32[2,96,128]{2,1,0:T(8,128)S(1)}, f32[2,96,128]{2,1,0:T(8,128)S(1)}, u32[]{:S(2)}, u32[]{:S(2)}) %collective-permute-start.9) | collective-permute-done | bytes 98336 | tf_op jit(solution)/shard_map/gather_row/ppermute | solution.py:151
  156.2 8.1 %all-to-all-start.5 = ((f32[16,96,128]{2,1,0:T(8,128)}), f32[16,96,128]{2,1,0:T(8,128)S(1)}, u32[]{:S(2)}, u32[]{:S(2)}) async-start(f32[16,96,128]{2,1,0:T(8,128)} %gather_column.3), calls=%async_computation.5 | async-start | bytes 1572864 | tf_op jit(solution)/shard_map/gather_column/all_to_all | solution.py:14
  164.4 3.7 %collective-permute-start.15 = (f32[8,96,128]{2,1,0:T(8,128)S(1)}, f32[8,96,128]{2,1,0:T(8,128)S(1)}, u32[]{:S(2)}, u32[]{:S(2)}) collective-permute-start(f32[8,96,128]{2,1,0:T(8,128)S(1)} %constant_dynamic-update-slice_fusion.2.row_ref), channel_id=1, source_target_pairs={{0,1},{1,0},{2,3},{3,2},{4,5},{5,4},{6,7},{7,6},{8,9},{9,8},{10,11... | collective-permute-start | bytes 1179656 | tf_op jit(solution)/shard_map/gather_row/ppermute | solution.py:151
  168.1 12.3 %collective-permute-done.15.row_ref = f32[8,96,128]{2,1,0:T(8,128)S(1)} collective-permute-done((f32[8,96,128]{2,1,0:T(8,128)S(1)}, f32[8,96,128]{2,1,0:T(8,128)S(1)}, u32[]{:S(2)}, u32[]{:S(2)}) %collective-permute-start.15) | collective-permute-done | bytes 393248 | tf_op jit(solution)/shard_map/gather_row/ppermute | solution.py:151
  182.0 3.1 collective-permute-start.16
  185.0 2.8 collective-permute-done.16
  193.3 5.7 %transposed.6.rest_0_ = f32[128,1536]{1,0:T(8,128)} custom-call(s32[9]{0:T(128)} %get-tuple-element.23.where_ref, f32[8,2,96,1536]{3,2,1,0:T(8,128)} %bitcast.95, f32[8,96,128]{2,1,0:T(8,128)} %copy-done.4), custom_call_target="tpu_custom_call" | custom-call | flops 905969664 | bytes 4718592 | tf_op jit(solution)/shard_map/transposed/pallas_call | solution.py:127
  199.2 5.9 %transposed.7 = f32[1536,128]{1,0:T(8,128)} custom-call(s32[9]{0:T(128)} %get-tuple-element.24.where_ref, f32[8,2,96,1536]{3,2,1,0:T(8,128)} %bitcast.96, f32[8,96,128]{2,1,0:T(8,128)} %copy-done.5, f32[128,1536]{1,0:T(8,128)} %transposed.6.rest_0_), custom_call_target="tpu_custom_call" | custom-call | flops 905969664 | bytes 4718592 | tf_op jit(solution)/shard_map/transposed/pallas_call | solution.py:127
  206.4 12.1 %all-to-all-start.6 = ((f32[16,96,128]{2,1,0:T(8,128)}), f32[16,96,128]{2,1,0:T(8,128)S(1)}, u32[]{:S(2)}, u32[]{:S(2)}) async-start(f32[16,96,128]{2,1,0:T(8,128)} %bitcast.103), calls=%async_computation.6 | async-start | bytes 1572864 | tf_op jit(solution)/shard_map/back_transposed/all_to_all | solution.py:14
  219.0 5.0 %direct.7 = f32[8,96,128]{2,1,0:T(8,128)} custom-call(s32[9]{0:T(128)} %get-tuple-element.24.where_ref, f32[8,2,96,1536]{3,2,1,0:T(8,128)} %bitcast.97, f32[1536,128]{1,0:T(8,128)} %bitcast.99), custom_call_target="tpu_custom_call" | custom-call | flops 905969664 | bytes 4718592 | tf_op jit(solution)/shard_map/direct/pallas_call | solution.py:82
  224.0 3.4 %collective-permute-start.10 = (f32[8,96,128]{2,1,0:T(8,128)}, f32[8,96,128]{2,1,0:T(8,128)S(1)}, u32[]{:S(2)}, u32[]{:S(2)}) collective-permute-start(f32[8,96,128]{2,1,0:T(8,128)} %direct.7), channel_id=1, source_target_pairs={{0,1},{1,0},{2,3},{3,2},{4,5},{5,4},{6,7},{7,6},{8,9},{9,8},{10,11... | collective-permute-start | bytes 1179656 | tf_op jit(solution)/shard_map/direct/ppermute | solution.py:151
  227.8 5.0 %direct.6 = f32[8,96,128]{2,1,0:T(8,128)} custom-call(s32[9]{0:T(128)} %get-tuple-element.23.where_ref, f32[8,2,96,1536]{3,2,1,0:T(8,128)} %bitcast.98, f32[1536,128]{1,0:T(8,128)} %bitcast.100), custom_call_target="tpu_custom_call" | custom-call | flops 905969664 | bytes 4718592 | tf_op jit(solution)/shard_map/direct/pallas_call | solution.py:82
  232.8 11.3 %collective-permute-done.10 = f32[8,96,128]{2,1,0:T(8,128)S(1)} collective-permute-done((f32[8,96,128]{2,1,0:T(8,128)}, f32[8,96,128]{2,1,0:T(8,128)S(1)}, u32[]{:S(2)}, u32[]{:S(2)}) %collective-permute-start.10) | collective-permute-done | bytes 393248 | tf_op jit(solution)/shard_map/direct/ppermute | solution.py:151
  248.4 6.7 %all-to-all-start.7 = ((f32[16,96,128]{2,1,0:T(8,128)}), f32[16,96,128]{2,1,0:T(8,128)S(1)}, u32[]{:S(2)}, u32[]{:S(2)}) async-start(f32[16,96,128]{2,1,0:T(8,128)} %back_transposed.3), calls=%async_computation.7 | async-start | bytes 1572864 | tf_op jit(solution)/shard_map/back_wide/all_to_all | solution.py:14
  255.1 3.0 collective-permute-start.12
  258.3 5.0 %collective-permute-done.12 = f32[2,96,128]{2,1,0:T(8,128)S(1)} collective-permute-done((f32[2,96,128]{2,1,0:T(8,128)S(1)}, f32[2,96,128]{2,1,0:T(8,128)S(1)}, u32[]{:S(2)}, u32[]{:S(2)}) %collective-permute-start.12) | collective-permute-done | bytes 98336 | tf_op jit(solution)/shard_map/back_direct/ppermute | solution.py:151
  263.3 4.9 %collective-permute-start.13 = (f32[1,96,128]{2,1,0:T(8,128)S(1)}, f32[1,96,128]{2,1,0:T(8,128)S(1)}, u32[]{:S(2)}, u32[]{:S(2)}) collective-permute-start(f32[1,96,128]{2,1,0:T(8,128)S(1)} %slice_add_fusion.8), channel_id=1, source_target_pairs={{0,8},{1,9},{2,10},{3,11},{4,12},{5,13},{6,14},{7,15},{8,0},{9,1},... | collective-permute-start | bytes 147464 | tf_op jit(solution)/shard_map/back_direct/ppermute | solution.py:151
  268.5 3.0 collective-permute-done.13
  271.8 3.1 collective-permute-start.20
  275.1 2.6 collective-permute-done.20
  279.7 2.6 collective-permute-done.21
  283.2 3.4 %collective-permute-done.22 = f32[128,128]{1,0:T(8,128)S(1)} collective-permute-done((f32[128,128]{1,0:T(8,128)S(1)}, f32[128,128]{1,0:T(8,128)S(1)}, u32[]{:S(2)}, u32[]{:S(2)}) %collective-permute-start.22) | collective-permute-done | bytes 65568 | tf_op jit(solution)/shard_map/gram_second/ppermute | solution.py:151
  288.0 4.8 %collective-permute-start.24 = (f32[128,128]{1,0:T(8,128)S(1)}, f32[128,128]{1,0:T(8,128)S(1)}, u32[]{:S(2)}, u32[]{:S(2)}) collective-permute-start(f32[128,128]{1,0:T(8,128)S(1)} %add.144), channel_id=1, source_target_pairs={{0,8},{1,9},{2,10},{3,11},{4,12},{5,13},{6,14},{7,15},{8,0},{9,1},... | collective-permute-start | bytes 196616 | tf_op jit(solution)/shard_map/gram_second/ppermute | solution.py:151
  293.0 4.7 %collective-permute-done.24 = f32[128,128]{1,0:T(8,128)S(1)} collective-permute-done((f32[128,128]{1,0:T(8,128)S(1)}, f32[128,128]{1,0:T(8,128)S(1)}, u32[]{:S(2)}, u32[]{:S(2)}) %collective-permute-start.24) | collective-permute-done | bytes 65568 | tf_op jit(solution)/shard_map/gram_second/ppermute | solution.py:151
  298.1 5.1 %collective-permute-done.25 = f32[128,128]{1,0:T(8,128)S(1)} collective-permute-done((f32[128,128]{1,0:T(8,128)S(1)}, f32[128,128]{1,0:T(8,128)S(1)}, u32[]{:S(2)}, u32[]{:S(2)}) %collective-permute-start.25) | collective-permute-done | bytes 65568 | tf_op jit(solution)/shard_map/gram_second/ppermute | solution.py:151
  303.5 4.0 %collective-permute-done.26 = f32[128,128]{1,0:T(8,128)S(1)} collective-permute-done((f32[128,128]{1,0:T(8,128)S(1)}, f32[128,128]{1,0:T(8,128)S(1)}, u32[]{:S(2)}, u32[]{:S(2)}) %collective-permute-start.26) | collective-permute-done | bytes 65568 | tf_op jit(solution)/shard_map/gram_second/ppermute | solution.py:151
  309.4 4.0 %collective-permute-done.27 = f32[128,128]{1,0:T(8,128)S(1)} collective-permute-done((f32[128,128]{1,0:T(8,128)S(1)}, f32[128,128]{1,0:T(8,128)S(1)}, u32[]{:S(2)}, u32[]{:S(2)}) %collective-permute-start.27) | collective-permute-done | bytes 65568 | tf_op jit(solution)/shard_map/gram_second/ppermute | solution.py:151
  (119 shorter events, 48.5 us)
Async XLA Ops:
  1.8 23.9 %all-to-all-start = ((f32[16,96,128]{2,1,0:T(8,128)}), f32[16,96,128]{2,1,0:T(8,128)S(1)}, u32[]{:S(2)}, u32[]{:S(2)}) async-start(f32[16,96,128]{2,1,0:T(8,128)} %broadcast_in_dim.13), calls=%async_computation | async-start | bytes 1572864 | tf_op jit(solution)/shard_map/gather_wide/all_to_all | solution.py:14
  7.6 9.6 %collective-permute-start = (f32[1,96,128]{2,1,0:T(8,128)}, f32[1,96,128]{2,1,0:T(8,128)S(1)}, u32[]{:S(2)}, u32[]{:S(2)}) collective-permute-start(f32[1,96,128]{2,1,0:T(8,128)} %bitcast.106), channel_id=1, source_target_pairs={{0,8},{1,9},{2,10},{3,11},{4,12},{5,13},{6,14},{7,15},{8,0},{9,1},... | collective-permute-start | bytes 147464 | tf_op jit(solution)/shard_map/gather_row/ppermute | solution.py:151
  17.9 6.9 %collective-permute-start.1 = (f32[2,96,128]{2,1,0:T(8,128)S(1)}, f32[2,96,128]{2,1,0:T(8,128)S(1)}, u32[]{:S(2)}, u32[]{:S(2)}) collective-permute-start(f32[2,96,128]{2,1,0:T(8,128)S(1)} %pad_maximum_fusion.2), channel_id=1, source_target_pairs={{0,4},{1,5},{2,6},{3,7},{4,0},{5,1},{6,2},{7,3},{8,12},{9,13},{10,... | collective-permute-start | bytes 294920 | tf_op jit(solution)/shard_map/gather_row/ppermute | solution.py:151
  25.7 0.7 copy-start
  27.9 48.5 %all-to-all-start.1 = ((f32[16,96,128]{2,1,0:T(8,128)}), f32[16,96,128]{2,1,0:T(8,128)S(1)}, u32[]{:S(2)}, u32[]{:S(2)}) async-start(f32[16,96,128]{2,1,0:T(8,128)} %gather_column.2), calls=%async_computation.1 | async-start | bytes 1572864 | tf_op jit(solution)/shard_map/gather_column/all_to_all | solution.py:14
  36.1 21.9 %collective-permute-start.6 = (f32[4,96,128]{2,1,0:T(8,128)S(1)}, f32[4,96,128]{2,1,0:T(8,128)S(1)}, u32[]{:S(2)}, u32[]{:S(2)}) collective-permute-start(f32[4,96,128]{2,1,0:T(8,128)S(1)} %pad_maximum_fusion), channel_id=1, source_target_pairs={{0,2},{1,3},{2,0},{3,1},{4,6},{5,7},{6,4},{7,5},{8,10},{9,11},{10,... | collective-permute-start | bytes 589832 | tf_op jit(solution)/shard_map/gather_row/ppermute | solution.py:151
  58.0 3.7 %copy-start.6 = (f32[8,96,128]{2,1,0:T(8,128)}, f32[8,96,128]{2,1,0:T(8,128)S(1)}, u32[]{:S(2)}) copy-start(f32[8,96,128]{2,1,0:T(8,128)S(1)} %constant_dynamic-update-slice_fusion.row_ref) | copy-start | bytes 1179652
  58.1 11.7 %collective-permute-start.7 = (f32[8,96,128]{2,1,0:T(8,128)S(1)}, f32[8,96,128]{2,1,0:T(8,128)S(1)}, u32[]{:S(2)}, u32[]{:S(2)}) collective-permute-start(f32[8,96,128]{2,1,0:T(8,128)S(1)} %constant_dynamic-update-slice_fusion.row_ref), channel_id=1, source_target_pairs={{0,1},{1,0},{2,3},{3,2},{4,5},{5,4},{6,7},{7,6},{8,9},{9,8},{10,11... | collective-permute-start | bytes 1179656 | tf_op jit(solution)/shard_map/gather_row/ppermute | solution.py:151
  69.7 0.7 copy-start.7
  76.4 8.1 %copy-start.3 = (f32[16,96,128]{2,1,0:T(8,128)}, f32[16,96,128]{2,1,0:T(8,128)S(1)}, u32[]{:S(2)}) copy-start(f32[16,96,128]{2,1,0:T(8,128)S(1)} %all-to-all-done.1) | copy-start | bytes 2359300
  76.4 33.3 %all-to-all-start.2 = ((f32[16,96,128]{2,1,0:T(8,128)}), f32[16,96,128]{2,1,0:T(8,128)S(1)}, u32[]{:S(2)}, u32[]{:S(2)}) async-start(f32[16,96,128]{2,1,0:T(8,128)} %bitcast.104), calls=%async_computation.2 | async-start | bytes 1572864 | tf_op jit(solution)/shard_map/back_transposed/all_to_all | solution.py:14
  84.5 25.2 %copy-start.1 = (s32[1,16]{1,0:T(1,128)S(1)}, s32[1,16]{1,0:T(1,128)}, u32[]{:S(2)}) copy-start(s32[1,16]{1,0:T(1,128)} %param.4) | copy-start | bytes 196
  89.6 17.4 %collective-permute-start.2 = (f32[8,96,128]{2,1,0:T(8,128)}, f32[8,96,128]{2,1,0:T(8,128)S(1)}, u32[]{:S(2)}, u32[]{:S(2)}) collective-permute-start(f32[8,96,128]{2,1,0:T(8,128)} %direct.5), channel_id=1, source_target_pairs={{0,1},{1,0},{2,3},{3,2},{4,5},{5,4},{6,7},{7,6},{8,9},{9,8},{10,11... | collective-permute-start | bytes 1179656 | tf_op jit(solution)/shard_map/direct/ppermute | solution.py:151
  108.1 8.9 %collective-permute-start.3 = (f32[4,96,128]{2,1,0:T(8,128)S(1)}, f32[4,96,128]{2,1,0:T(8,128)S(1)}, u32[]{:S(2)}, u32[]{:S(2)}) collective-permute-start(f32[4,96,128]{2,1,0:T(8,128)S(1)} %get-tuple-element.18), channel_id=1, source_target_pairs={{0,2},{1,3},{2,0},{3,1},{4,6},{5,7},{6,4},{7,5},{8,10},{9,11},{10,... | collective-permute-start | bytes 589832 | tf_op jit(solution)/shard_map/back_direct/ppermute | solution.py:151
  111.3 18.1 %all-to-all-start.3 = ((f32[16,96,128]{2,1,0:T(8,128)}), f32[16,96,128]{2,1,0:T(8,128)S(1)}, u32[]{:S(2)}, u32[]{:S(2)}) async-start(f32[16,96,128]{2,1,0:T(8,128)} %back_transposed.2), calls=%async_computation.3 | async-start | bytes 1572864 | tf_op jit(solution)/shard_map/back_wide/all_to_all | solution.py:14
  117.1 7.9 %collective-permute-start.4 = (f32[2,96,128]{2,1,0:T(8,128)S(1)}, f32[2,96,128]{2,1,0:T(8,128)S(1)}, u32[]{:S(2)}, u32[]{:S(2)}) collective-permute-start(f32[2,96,128]{2,1,0:T(8,128)S(1)} %get-tuple-element.22), channel_id=1, source_target_pairs={{0,4},{1,5},{2,6},{3,7},{4,0},{5,1},{6,2},{7,3},{8,12},{9,13},{10,... | collective-permute-start | bytes 294920 | tf_op jit(solution)/shard_map/back_direct/ppermute | solution.py:151
  125.0 8.1 %collective-permute-start.5 = (f32[1,96,128]{2,1,0:T(8,128)S(1)}, f32[1,96,128]{2,1,0:T(8,128)S(1)}, u32[]{:S(2)}, u32[]{:S(2)}) collective-permute-start(f32[1,96,128]{2,1,0:T(8,128)S(1)} %slice_add_fusion.10), channel_id=1, source_target_pairs={{0,8},{1,9},{2,10},{3,11},{4,12},{5,13},{6,14},{7,15},{8,0},{9,1},... | collective-permute-start | bytes 147464 | tf_op jit(solution)/shard_map/back_direct/ppermute | solution.py:151
  134.1 20.4 %all-to-all-start.4 = ((f32[16,96,128]{2,1,0:T(8,128)}), f32[16,96,128]{2,1,0:T(8,128)S(1)}, u32[]{:S(2)}, u32[]{:S(2)}) async-start(f32[16,96,128]{2,1,0:T(8,128)} %broadcast_in_dim.17), calls=%async_computation.4 | async-start | bytes 1572864 | tf_op jit(solution)/shard_map/gather_wide/all_to_all | solution.py:14
  139.8 9.1 %collective-permute-start.8 = (f32[1,96,128]{2,1,0:T(8,128)S(1)}, f32[1,96,128]{2,1,0:T(8,128)S(1)}, u32[]{:S(2)}, u32[]{:S(2)}) collective-permute-start(f32[1,96,128]{2,1,0:T(8,128)S(1)} %fusion.17), channel_id=1, source_target_pairs={{0,8},{1,9},{2,10},{3,11},{4,12},{5,13},{6,14},{7,15},{8,0},{9,1},... | collective-permute-start | bytes 147464 | tf_op jit(solution)/shard_map/gather_row/ppermute | solution.py:151
  148.9 5.6 %collective-permute-start.9 = (f32[2,96,128]{2,1,0:T(8,128)S(1)}, f32[2,96,128]{2,1,0:T(8,128)S(1)}, u32[]{:S(2)}, u32[]{:S(2)}) collective-permute-start(f32[2,96,128]{2,1,0:T(8,128)S(1)} %pad_maximum_fusion.3), channel_id=1, source_target_pairs={{0,4},{1,5},{2,6},{3,7},{4,0},{5,1},{6,2},{7,3},{8,12},{9,13},{10,... | collective-permute-start | bytes 294920 | tf_op jit(solution)/shard_map/gather_row/ppermute | solution.py:151
  154.5 9.9 %collective-permute-start.14 = (f32[4,96,128]{2,1,0:T(8,128)S(1)}, f32[4,96,128]{2,1,0:T(8,128)S(1)}, u32[]{:S(2)}, u32[]{:S(2)}) collective-permute-start(f32[4,96,128]{2,1,0:T(8,128)S(1)} %pad_maximum_fusion.1), channel_id=1, source_target_pairs={{0,2},{1,3},{2,0},{3,1},{4,6},{5,7},{6,4},{7,5},{8,10},{9,11},{10,... | collective-permute-start | bytes 589832 | tf_op jit(solution)/shard_map/gather_row/ppermute | solution.py:151
  156.2 50.2 %all-to-all-start.5 = ((f32[16,96,128]{2,1,0:T(8,128)}), f32[16,96,128]{2,1,0:T(8,128)S(1)}, u32[]{:S(2)}, u32[]{:S(2)}) async-start(f32[16,96,128]{2,1,0:T(8,128)} %gather_column.3), calls=%async_computation.5 | async-start | bytes 1572864 | tf_op jit(solution)/shard_map/gather_column/all_to_all | solution.py:14
  164.4 29.0 %copy-start.4 = (f32[8,96,128]{2,1,0:T(8,128)}, f32[8,96,128]{2,1,0:T(8,128)S(1)}, u32[]{:S(2)}) copy-start(f32[8,96,128]{2,1,0:T(8,128)S(1)} %constant_dynamic-update-slice_fusion.2.row_ref) | copy-start | bytes 1179652
  164.4 15.9 %collective-permute-start.15 = (f32[8,96,128]{2,1,0:T(8,128)S(1)}, f32[8,96,128]{2,1,0:T(8,128)S(1)}, u32[]{:S(2)}, u32[]{:S(2)}) collective-permute-start(f32[8,96,128]{2,1,0:T(8,128)S(1)} %constant_dynamic-update-slice_fusion.2.row_ref), channel_id=1, source_target_pairs={{0,1},{1,0},{2,3},{3,2},{4,5},{5,4},{6,7},{7,6},{8,9},{9,8},{10,11... | collective-permute-start | bytes 1179656 | tf_op jit(solution)/shard_map/gather_row/ppermute | solution.py:151
  180.3 18.8 %copy-start.5 = (f32[8,96,128]{2,1,0:T(8,128)}, f32[8,96,128]{2,1,0:T(8,128)S(1)}, u32[]{:S(2)}) copy-start(f32[8,96,128]{2,1,0:T(8,128)S(1)} %collective-permute-done.15.row_ref) | copy-start | bytes 1179652
  182.0 5.9 %collective-permute-start.16 = (f32[128,128]{1,0:T(8,128)S(1)}, f32[128,128]{1,0:T(8,128)S(1)}, u32[]{:S(2)}, u32[]{:S(2)}) collective-permute-start(f32[128,128]{1,0:T(8,128)S(1)} %fusion.10), channel_id=1, source_target_pairs={{0,128},{16,144},{32,160},{48,176},{64,192},{80,208},{96,224},{112... | collective-permute-start | bytes 196616 | tf_op jit(solution)/shard_map/gram_first/ppermute | solution.py:151
  187.8 4.4 %collective-permute-start.17 = (f32[128,128]{1,0:T(8,128)S(1)}, f32[128,128]{1,0:T(8,128)S(1)}, u32[]{:S(2)}, u32[]{:S(2)}) collective-permute-start(f32[128,128]{1,0:T(8,128)S(1)} %add.134), channel_id=1, source_target_pairs={{0,64},{16,80},{32,96},{48,112},{64,0},{80,16},{96,32},{112,48},{1... | collective-permute-start | bytes 196616 | tf_op jit(solution)/shard_map/gram_first/ppermute | solution.py:151
  192.2 6.8 %collective-permute-start.18 = (f32[128,128]{1,0:T(8,128)S(1)}, f32[128,128]{1,0:T(8,128)S(1)}, u32[]{:S(2)}, u32[]{:S(2)}) collective-permute-start(f32[128,128]{1,0:T(8,128)S(1)} %add.135), channel_id=1, source_target_pairs={{0,32},{16,48},{32,0},{48,16},{64,96},{80,112},{96,64},{112,80},{1... | collective-permute-start | bytes 196616 | tf_op jit(solution)/shard_map/gram_first/ppermute | solution.py:151
  199.1 6.0 %collective-permute-start.19 = (f32[128,128]{1,0:T(8,128)S(1)}, f32[128,128]{1,0:T(8,128)S(1)}, u32[]{:S(2)}, u32[]{:S(2)}) collective-permute-start(f32[128,128]{1,0:T(8,128)S(1)} %add.136), channel_id=1, source_target_pairs={{0,16},{16,0},{32,48},{48,32},{64,80},{80,64},{96,112},{112,96},{1... | collective-permute-start | bytes 196616 | tf_op jit(solution)/shard_map/gram_first/ppermute | solution.py:151
  206.4 12.6 %copy-start.2 = (f32[16,96,128]{2,1,0:T(8,128)}, f32[16,96,128]{2,1,0:T(8,128)S(1)}, u32[]{:S(2)}) copy-start(f32[16,96,128]{2,1,0:T(8,128)S(1)} %all-to-all-done.5) | copy-start | bytes 2359300
  206.4 40.4 %all-to-all-start.6 = ((f32[16,96,128]{2,1,0:T(8,128)}), f32[16,96,128]{2,1,0:T(8,128)S(1)}, u32[]{:S(2)}, u32[]{:S(2)}) async-start(f32[16,96,128]{2,1,0:T(8,128)} %bitcast.103), calls=%async_computation.6 | async-start | bytes 1572864 | tf_op jit(solution)/shard_map/back_transposed/all_to_all | solution.py:14
  224.0 20.2 %collective-permute-start.10 = (f32[8,96,128]{2,1,0:T(8,128)}, f32[8,96,128]{2,1,0:T(8,128)S(1)}, u32[]{:S(2)}, u32[]{:S(2)}) collective-permute-start(f32[8,96,128]{2,1,0:T(8,128)} %direct.7), channel_id=1, source_target_pairs={{0,1},{1,0},{2,3},{3,2},{4,5},{5,4},{6,7},{7,6},{8,9},{9,8},{10,11... | collective-permute-start | bytes 1179656 | tf_op jit(solution)/shard_map/direct/ppermute | solution.py:151
  245.2 9.8 %collective-permute-start.11 = (f32[4,96,128]{2,1,0:T(8,128)S(1)}, f32[4,96,128]{2,1,0:T(8,128)S(1)}, u32[]{:S(2)}, u32[]{:S(2)}) collective-permute-start(f32[4,96,128]{2,1,0:T(8,128)S(1)} %get-tuple-element.16), channel_id=1, source_target_pairs={{0,2},{1,3},{2,0},{3,1},{4,6},{5,7},{6,4},{7,5},{8,10},{9,11},{10,... | collective-permute-start | bytes 589832 | tf_op jit(solution)/shard_map/back_direct/ppermute | solution.py:151
  248.4 20.0 %all-to-all-start.7 = ((f32[16,96,128]{2,1,0:T(8,128)}), f32[16,96,128]{2,1,0:T(8,128)S(1)}, u32[]{:S(2)}, u32[]{:S(2)}) async-start(f32[16,96,128]{2,1,0:T(8,128)} %back_transposed.3), calls=%async_computation.7 | async-start | bytes 1572864 | tf_op jit(solution)/shard_map/back_wide/all_to_all | solution.py:14
  255.1 8.2 %collective-permute-start.12 = (f32[2,96,128]{2,1,0:T(8,128)S(1)}, f32[2,96,128]{2,1,0:T(8,128)S(1)}, u32[]{:S(2)}, u32[]{:S(2)}) collective-permute-start(f32[2,96,128]{2,1,0:T(8,128)S(1)} %get-tuple-element.20), channel_id=1, source_target_pairs={{0,4},{1,5},{2,6},{3,7},{4,0},{5,1},{6,2},{7,3},{8,12},{9,13},{10,... | collective-permute-start | bytes 294920 | tf_op jit(solution)/shard_map/back_direct/ppermute | solution.py:151
  263.3 8.2 %collective-permute-start.13 = (f32[1,96,128]{2,1,0:T(8,128)S(1)}, f32[1,96,128]{2,1,0:T(8,128)S(1)}, u32[]{:S(2)}, u32[]{:S(2)}) collective-permute-start(f32[1,96,128]{2,1,0:T(8,128)S(1)} %slice_add_fusion.8), channel_id=1, source_target_pairs={{0,8},{1,9},{2,10},{3,11},{4,12},{5,13},{6,14},{7,15},{8,0},{9,1},... | collective-permute-start | bytes 147464 | tf_op jit(solution)/shard_map/back_direct/ppermute | solution.py:151
  271.8 5.9 %collective-permute-start.20 = (f32[128,128]{1,0:T(8,128)S(1)}, f32[128,128]{1,0:T(8,128)S(1)}, u32[]{:S(2)}, u32[]{:S(2)}) collective-permute-start(f32[128,128]{1,0:T(8,128)S(1)} %fusion.18), channel_id=1, source_target_pairs={{0,128},{16,144},{32,160},{48,176},{64,192},{80,208},{96,224},{112... | collective-permute-start | bytes 196616 | tf_op jit(solution)/shard_map/gram_second/ppermute | solution.py:151
  277.7 4.6 %collective-permute-start.21 = (f32[128,128]{1,0:T(8,128)S(1)}, f32[128,128]{1,0:T(8,128)S(1)}, u32[]{:S(2)}, u32[]{:S(2)}) collective-permute-start(f32[128,128]{1,0:T(8,128)S(1)} %add.141), channel_id=1, source_target_pairs={{0,64},{16,80},{32,96},{48,112},{64,0},{80,16},{96,32},{112,48},{1... | collective-permute-start | bytes 196616 | tf_op jit(solution)/shard_map/gram_second/ppermute | solution.py:151
  282.3 4.4 %collective-permute-start.22 = (f32[128,128]{1,0:T(8,128)S(1)}, f32[128,128]{1,0:T(8,128)S(1)}, u32[]{:S(2)}, u32[]{:S(2)}) collective-permute-start(f32[128,128]{1,0:T(8,128)S(1)} %add.142), channel_id=1, source_target_pairs={{0,32},{16,48},{32,0},{48,16},{64,96},{80,112},{96,64},{112,80},{1... | collective-permute-start | bytes 196616 | tf_op jit(solution)/shard_map/gram_second/ppermute | solution.py:151
  286.6 1.3 collective-permute-start.23
  288.0 9.7 %collective-permute-start.24 = (f32[128,128]{1,0:T(8,128)S(1)}, f32[128,128]{1,0:T(8,128)S(1)}, u32[]{:S(2)}, u32[]{:S(2)}) collective-permute-start(f32[128,128]{1,0:T(8,128)S(1)} %add.144), channel_id=1, source_target_pairs={{0,8},{1,9},{2,10},{3,11},{4,12},{5,13},{6,14},{7,15},{8,0},{9,1},... | collective-permute-start | bytes 196616 | tf_op jit(solution)/shard_map/gram_second/ppermute | solution.py:151
  297.7 5.5 %collective-permute-start.25 = (f32[128,128]{1,0:T(8,128)S(1)}, f32[128,128]{1,0:T(8,128)S(1)}, u32[]{:S(2)}, u32[]{:S(2)}) collective-permute-start(f32[128,128]{1,0:T(8,128)S(1)} %add.145), channel_id=1, source_target_pairs={{0,4},{1,5},{2,6},{3,7},{4,0},{5,1},{6,2},{7,3},{8,12},{9,13},{10,... | collective-permute-start | bytes 196616 | tf_op jit(solution)/shard_map/gram_second/ppermute | solution.py:151
  303.2 4.4 %collective-permute-start.26 = (f32[128,128]{1,0:T(8,128)S(1)}, f32[128,128]{1,0:T(8,128)S(1)}, u32[]{:S(2)}, u32[]{:S(2)}) collective-permute-start(f32[128,128]{1,0:T(8,128)S(1)} %add.146), channel_id=1, source_target_pairs={{0,2},{1,3},{2,0},{3,1},{4,6},{5,7},{6,4},{7,5},{8,10},{9,11},{10,... | collective-permute-start | bytes 196616 | tf_op jit(solution)/shard_map/gram_second/ppermute | solution.py:151
  307.6 5.9 %collective-permute-start.27 = (f32[128,128]{1,0:T(8,128)S(1)}, f32[128,128]{1,0:T(8,128)S(1)}, u32[]{:S(2)}, u32[]{:S(2)}) collective-permute-start(f32[128,128]{1,0:T(8,128)S(1)} %add.147), channel_id=1, source_target_pairs={{0,1},{1,0},{2,3},{3,2},{4,5},{5,4},{6,7},{7,6},{8,9},{9,8},{10,11... | collective-permute-start | bytes 196616 | tf_op jit(solution)/shard_map/gram_second/ppermute | solution.py:151
where the time goes:
time: 321 us; the launch traced here: 319 us
  starting transfers between devices  126 us (39%)
  waiting for transfers between devices  122 us (38%)
  Pallas kernels  49.8 us (16%)
  matrix products  9.63 us (3%)
  other arithmetic  5.23 us (2%)
  local copies, waits for them, and re-layouts  4.24 us (1%)
    ppermute x28, waiting for transfers between devices, swap(): return lax.ppermute(value, axis, [(i, i ^ bit) for i in range(size)])  122 us
    ppermute x28, starting transfers between devices, swap(): return lax.ppermute(value, axis, [(i, i ^ bit) for i in range(size)])  66 us
    all_to_all x8, starting transfers between devices, exchange(): return lax.all_to_all(parts, axis, 0, 0, tiled=True)  60.4 us
    pallas_call x4, Pallas kernels, transposed_half(): pl.pallas_call(kernel, out_shape=jax.ShapeDtypeStruct((width, order) if p...  23.2 us
    pallas_call x4, Pallas kernels, direct_half(): pl.pallas_call(kernel, out_shape=jax.ShapeDtypeStruct((groups, rows, widt...  20.2 us
  transfers between devices with their start and end apart: 36, of which 23 were waited for; matrix products, arithmetic and copies ran while one was open for 3% of the time, Pallas kernels for 15%

commit v1 on v0

--- a/solution.py
+++ b/solution.py
@@ -18,17 +18,30 @@
     return exchange(jnp.broadcast_to(value[None], (lax.axis_size(axis), *value.shape)), axis)
 
 
-def move_blocks(blocks, columns, scatter):
-    count = blocks.shape[0]
-
-    def kernel(columns_ref, blocks_ref, moved_ref, done):
+def move_blocks(blocks, columns, scatter, extra=None):
+    count, rows, width = blocks.shape
+    arrays = [blocks] if extra is None else [blocks, extra]
+    more = 0 if extra is None else extra.shape[0] // count
+
+    def kernel(columns_ref, blocks_ref, *rest):
+        moved_ref, done = rest[-2:]
         copies = []
         for i in range(count):
             column = columns_ref[i]
             source, target = (i, column) if scatter else (column, i)
             copies.append(
-                pltpu.make_async_copy(blocks_ref.at[source], moved_ref.at[target], done.at[i])
+                pltpu.make_async_copy(
+                    blocks_ref.at[source], moved_ref.at[target, pl.ds(0, rows)], done.at[i]
+                )
             )
+            if more:
+                copies.append(
+                    pltpu.make_async_copy(
+                        rest[0].at[pl.ds(i * more, more)],
+                        moved_ref.at[i, pl.ds(rows, more)],
+                        done.at[count + i],
+                    )
+                )
         for copy in copies:
             copy.start()
         for copy in copies:
@@ -36,13 +49,14 @@
 
     return pl.pallas_call(
         kernel,
-        out_shape=jax.ShapeDtypeStruct(blocks.shape, blocks.dtype),
-        in_specs=[pl.BlockSpec(memory_space=pltpu.SMEM), pl.BlockSpec(memory_space=pl.ANY)],
+        out_shape=jax.ShapeDtypeStruct((count, rows + more, width), blocks.dtype),
+        in_specs=[pl.BlockSpec(memory_space=pltpu.SMEM)]
+        + [pl.BlockSpec(memory_space=pl.ANY)] * len(arrays),
         out_specs=pl.BlockSpec(memory_space=pl.ANY),
-        scratch_shapes=[pltpu.SemaphoreType.DMA((count,))],
+        scratch_shapes=[pltpu.SemaphoreType.DMA((len(arrays) * count,))],
         compiler_params=pltpu.CompilerParams(vmem_limit_bytes=1 << 20),
         cost_estimate=pl.CostEstimate(flops=0, bytes_accessed=8 * blocks.size, transcendentals=0),
-    )(columns, blocks)
+    )(columns, *arrays)
 
 
 def high_low(value):
@@ -179,13 +193,7 @@
     return mine[0] + got[0]
 
 
-def summed(value, axis):
-    for bit in bits_of(lax.axis_size(axis)):
-        value = value + swap(value, axis, bit)
-    return value
-
-
-def apply_hamiltonian(tile, columns, vectors):
+def apply_hamiltonian(tile, columns, vectors, want_gram):
     rows, width = vectors.shape
     count = lax.axis_size(NARROW)
     order = tile.shape[0]
@@ -198,9 +206,8 @@
         slices = to_everyone(vectors, WIDE)
     bits = list(bits_of(groups))
     with jax.named_scope("gather_row"):
-        near_rows = doubled(vectors[None], NARROW, [2 * bit for bit in bits[:2]])
+        near_rows = doubled(vectors[None], NARROW, [2 * bit for bit in bits])
         slices, near_rows = lax.optimization_barrier((slices, near_rows))
-        near_rows = doubled(near_rows, NARROW, [2 * bit for bit in bits[2:]])
         far_rows = swap(near_rows, NARROW, 1)
     with jax.named_scope("gather_column"):
         picked = move_blocks(slices, columns, scatter=False)
@@ -210,28 +217,50 @@
         transposed = transposed_half(tile, far_rows, far, places, partial)
     with jax.named_scope("back_transposed"):
         arrived = exchange(transposed.reshape(count, rows, width), NARROW)
-        placed = move_blocks(arrived, columns, scatter=True)
     with jax.named_scope("direct"):
         sent = direct_half(tile, column_block, far, places)
         got = swap(sent, NARROW, 1)
         kept = direct_half(tile, column_block, near, places)
+    gram = None
+    if want_gram:
+        with jax.named_scope("gram_block_row"):
+            near_rows, far_rows, kept = lax.optimization_barrier((near_rows, far_rows, kept))
+            gram = gram_of(near_rows.reshape(-1, width)) + gram_of(far_rows.reshape(-1, width))
     with jax.named_scope("back_direct"):
         direct_sum = halved(kept, got, NARROW)
     with jax.named_scope("back_wide"):
-        transposed_sum = exchange(placed, WIDE).sum(axis=0)
-    return direct_sum + transposed_sum, (near_rows, far_rows)
+        placed = move_blocks(arrived, columns, scatter=True, extra=gram)
+        sums = exchange(placed, WIDE).sum(axis=0)
+    return direct_sum + sums[:rows], sums[rows:]
+
+
+def exact(left, right):
+    return jnp.dot(left, right, precision=HIGHEST, preferred_element_type=jnp.float32)
 
 
 def inverse_root(gram, total_rows):
-    identity = jnp.eye(gram.shape[0], dtype=jnp.float32)
-    scale = jnp.sqrt(jnp.sum(gram * gram) + 1e-06)
+    width = gram.shape[0]
+    row = lax.broadcasted_iota(jnp.int32, (width, width), 0)
+    identity = (row == lax.broadcasted_iota(jnp.int32, (width, width), 1)).astype(jnp.float32)
+    scale = jnp.sqrt(jnp.sum(gram * gram, keepdims=True) + 1e-06)
     current = gram / scale
     inverse = identity
     for repeat in range(NS_STEPS):
-        middle = 1.5 * identity - 0.5 * jnp.dot(inverse, current, precision=HIGHEST)
-        current = jnp.dot(current, middle, precision=HIGHEST)
-        inverse = jnp.dot(middle, inverse, precision=HIGHEST)
+        middle = 1.5 * identity - 0.5 * exact(inverse, current)
+        current = exact(current, middle)
+        inverse = exact(middle, inverse)
     return inverse * jnp.sqrt(total_rows / scale)
+
+
+def in_kernel(function, shape, *arrays):
+    def kernel(*refs):
+        refs[-1][...] = function(*(ref[...] for ref in refs[:-1]))
+
+    return pl.pallas_call(
+        kernel,
+        out_shape=jax.ShapeDtypeStruct(shape, jnp.float32),
+        cost_estimate=pl.CostEstimate(flops=1 << 30, bytes_accessed=1 << 20, transcendentals=0),
+    )(*arrays)
 
 
 def gram_of(value):
@@ -241,24 +270,29 @@
 def on_device(tile, row_columns, start_vectors):
     total_rows = float(lax.axis_size(WIDE) * lax.axis_size(NARROW) * start_vectors.shape[0])
     columns = row_columns[0]
-    first, _ = apply_hamiltonian(tile, columns, start_vectors)
-    second, first_halves = apply_hamiltonian(tile, columns, first)
-    with jax.named_scope("gram_first"):
-        grams = [gram_of(half.reshape(-1, half.shape[2])) for half in first_halves]
-        gram_first = summed(grams[0] + grams[1], WIDE)
-    with jax.named_scope("gram_second"):
-        gram_second = summed(summed(gram_of(second), WIDE), NARROW)
+    first, _ = apply_hamiltonian(tile, columns, start_vectors, want_gram=False)
+    second, gram_rows = apply_hamiltonian(tile, columns, first, want_gram=True)
+    width = second.shape[1]
+    wide = lax.axis_size(WIDE)
+    with jax.named_scope("gram_sum_wide"):
+        parts = gram_of(second).reshape(wide, width // wide, width)
+        given = jnp.broadcast_to(gram_rows[None], parts.shape)
+        got = exchange(jnp.concatenate([parts, given], axis=1), WIDE)
+        gram_second = got[:, : width // wide].sum(axis=0)
+        gram_first = got[:, width // wide :].reshape(width, width)
+    with jax.named_scope("gram_sum_narrow"):
+        gram_second = to_everyone(gram_second, NARROW).sum(axis=0)
     with jax.named_scope("inverse_first"):
-        root_first = inverse_root(gram_first, total_rows)
-    with jax.named_scope("inverse_second"):
-        gram = jnp.dot(
-            root_first.T, jnp.dot(gram_second, root_first, precision=HIGHEST), precision=HIGHEST
-        )
-        root_second = inverse_root(gram, total_rows)
+        root_first = in_kernel(lambda gram: inverse_root(gram, total_rows), (width, width), gram_first)
+    with jax.named_scope("gram_whole"):
+        gram_second = to_everyone(gram_second, WIDE).reshape(width, width)
+
+    def finish(gram, root, value):
+        gram = exact(root.T, exact(gram, root))
+        return exact(exact(value, root), inverse_root(gram, total_rows))
+
     with jax.named_scope("finish"):
-        return jnp.dot(
-            jnp.dot(second, root_first, precision=HIGHEST), root_second, precision=HIGHEST
-        )
+        return in_kernel(finish, second.shape, gram_second, root_first, second)
 
 
 def solution(mesh):

time: 321 us -> 291 us (0.907)
  waiting for transfers between devices: 122 us -> 79.1 us
  blocking collectives: 0 us -> 27.9 us
  starting transfers between devices: 126 us -> 107 us
  Pallas kernels: 49.8 us -> 58.3 us
  matrix products: 9.63 us -> 1.92 us
    ppermute x28 -> x16, waiting for transfers between devices: 122 us -> 74.3 us  [swap(): return lax.ppermute(value, axis, [(i, i ^ bit) for i in range(size)])]
    all_to_all x0 -> x2, blocking collectives: none -> 27.9 us  [exchange(): return lax.all_to_all(parts, axis, 0, 0, tiled=True)]
    ppermute x28 -> x16, starting transfers between devices: 66 us -> 42.2 us  [swap(): return lax.ppermute(value, axis, [(i, i ^ bit) for i in range(size)])]
    pallas_call x4 -> x6, Pallas kernels: 6.37 us -> 14.9 us  [the longest x2 8.35 us: in_kernel(): pl.pallas_call(kernel, out_shape=jax.ShapeDtypeStruct(shape, jnp.float32)...]
    dot_general x32 -> x0, matrix products: 7.72 us -> none  [the longest x10 2.02 us: inverse_root(): middle = 1.5 * identity - 0.5 * jnp.dot(inverse, current, precision=HIGHEST)]
    all_to_all x8 -> x9, waiting for transfers between devices: 0.02 us -> 4.86 us  [exchange(): return lax.all_to_all(parts, axis, 0, 0, tiled=True)]
    all_to_all x8 -> x9, starting transfers between devices: 60.4 us -> 65 us  [exchange(): return lax.all_to_all(parts, axis, 0, 0, tiled=True)]
  transfers between devices with their start and end apart: 36 -> 25, of which waited for: 23 -> 19; matrix products, arithmetic and copies ran while one was open for 3% -> 2% of each run, Pallas kernels for 15% -> 18%
where the time goes in v1:
time: 291 us; the launch traced here: 287 us
  starting transfers between devices  107 us (37%)
  waiting for transfers between devices  79.1 us (27%)
  Pallas kernels  58.3 us (20%)
  blocking collectives  27.9 us (10%)
  local copies, waits for them, and re-layouts  6.26 us (2%)
  other arithmetic  6.21 us (2%)
    ppermute x16, waiting for transfers between devices, swap(): return lax.ppermute(value, axis, [(i, i ^ bit) for i in range(size)])  74.3 us
    all_to_all x9, starting transfers between devices, exchange(): return lax.all_to_all(parts, axis, 0, 0, tiled=True)  65 us
    ppermute x16, starting transfers between devices, swap(): return lax.ppermute(value, axis, [(i, i ^ bit) for i in range(size)])  42.2 us
    all_to_all x2, blocking collectives, exchange(): return lax.all_to_all(parts, axis, 0, 0, tiled=True)  27.9 us
    pallas_call x4, Pallas kernels, transposed_half(): pl.pallas_call(kernel, out_shape=jax.ShapeDtypeStruct((width, order) if p...  23.2 us
    pallas_call x4, Pallas kernels, direct_half(): pl.pallas_call(kernel, out_shape=jax.ShapeDtypeStruct((groups, rows, widt...  20.3 us
    pallas_call x2, Pallas kernels, in_kernel(): pl.pallas_call(kernel, out_shape=jax.ShapeDtypeStruct(shape, jnp.float32)...  8.35 us
    pallas_call x4, Pallas kernels, move_blocks(): pl.pallas_call(kernel, out_shape=jax.ShapeDtypeStruct((count, rows + more...  6.53 us
  transfers between devices with their start and end apart: 25, of which 19 were waited for; matrix products, arithmetic and copies ran while one was open for 2% of the time, Pallas kernels for 18%

profile of v1, /device:TPU:8, one launch (start us, length us, event | category | flops | bytes accessed | tf_op | source)
XLA Modules:
  0.0 287.3 jit_solution(3911923388443836418)
XLA Ops:
  0.0 1.8 broadcast_in_dim.19
  1.8 5.8 %all-to-all-start = ((f32[16,96,128]{2,1,0:T(8,128)}), f32[16,96,128]{2,1,0:T(8,128)S(1)}, u32[]{:S(2)}, u32[]{:S(2)}) async-start(f32[16,96,128]{2,1,0:T(8,128)} %broadcast_in_dim.19), calls=%async_computation | async-start | bytes 1572864 | tf_op jit(solution)/shard_map/gather_wide/all_to_all | solution.py:14
  7.5 7.2 %collective-permute-start = (f32[1,96,128]{2,1,0:T(8,128)}, f32[1,96,128]{2,1,0:T(8,128)S(1)}, u32[]{:S(2)}, u32[]{:S(2)}) collective-permute-start(f32[1,96,128]{2,1,0:T(8,128)} %bitcast.52), channel_id=1, source_target_pairs={{0,8},{1,9},{2,10},{3,11},{4,12},{5,13},{6,14},{7,15},{8,0},{9,1},... | collective-permute-start | bytes 147464 | tf_op jit(solution)/shard_map/gather_row/ppermute | solution.py:165
  14.7 2.4 collective-permute-done
  17.9 2.9 collective-permute-start.1
  20.8 4.0 %collective-permute-done.1 = f32[2,96,128]{2,1,0:T(8,128)S(1)} collective-permute-done((f32[2,96,128]{2,1,0:T(8,128)S(1)}, f32[2,96,128]{2,1,0:T(8,128)S(1)}, u32[]{:S(2)}, u32[]{:S(2)}) %collective-permute-start.1) | collective-permute-done | bytes 98336 | tf_op jit(solution)/shard_map/gather_row/ppermute | solution.py:165
  25.9 5.5 %collective-permute-done.2 = f32[4,96,128]{2,1,0:T(8,128)S(1)} collective-permute-done((f32[4,96,128]{2,1,0:T(8,128)S(1)}, f32[4,96,128]{2,1,0:T(8,128)S(1)}, u32[]{:S(2)}, u32[]{:S(2)}) %collective-permute-start.2) | collective-permute-done | bytes 196640 | tf_op jit(solution)/shard_map/gather_row/ppermute | solution.py:165
  34.5 8.2 %all-to-all-start.1 = ((f32[16,96,128]{2,1,0:T(8,128)}), f32[16,96,128]{2,1,0:T(8,128)S(1)}, u32[]{:S(2)}, u32[]{:S(2)}) async-start(f32[16,96,128]{2,1,0:T(8,128)} %gather_column.2), calls=%async_computation.1 | async-start | bytes 1572864 | tf_op jit(solution)/shard_map/gather_column/all_to_all | solution.py:14
  42.7 3.4 %collective-permute-start.7 = (f32[8,96,128]{2,1,0:T(8,128)S(1)}, f32[8,96,128]{2,1,0:T(8,128)S(1)}, u32[]{:S(2)}, u32[]{:S(2)}) collective-permute-start(f32[8,96,128]{2,1,0:T(8,128)S(1)} %pad_maximum_fusion.row_ref), channel_id=1, source_target_pairs={{0,1},{1,0},{2,3},{3,2},{4,5},{5,4},{6,7},{7,6},{8,9},{9,8},{10,11... | collective-permute-start | bytes 1179656 | tf_op jit(solution)/shard_map/gather_row/ppermute | solution.py:165
  46.8 5.7 %transposed.4.rest_0_ = f32[128,1536]{1,0:T(8,128)} custom-call(s32[9]{0:T(128)} %get-tuple-element.29.where_ref, f32[8,2,96,1536]{3,2,1,0:T(8,128)} %bitcast.37, f32[8,96,128]{2,1,0:T(8,128)} %copy-done.8), custom_call_target="tpu_custom_call" | custom-call | flops 905969664 | bytes 4718592 | tf_op jit(solution)/shard_map/transposed/pallas_call | solution.py:141
  52.5 3.7 %collective-permute-done.7.row_ref = f32[8,96,128]{2,1,0:T(8,128)S(1)} collective-permute-done((f32[8,96,128]{2,1,0:T(8,128)S(1)}, f32[8,96,128]{2,1,0:T(8,128)S(1)}, u32[]{:S(2)}, u32[]{:S(2)}) %collective-permute-start.7) | collective-permute-done | bytes 393248 | tf_op jit(solution)/shard_map/gather_row/ppermute | solution.py:165
  57.0 5.9 %transposed.5 = f32[1536,128]{1,0:T(8,128)} custom-call(s32[9]{0:T(128)} %get-tuple-element.30.where_ref, f32[8,2,96,1536]{3,2,1,0:T(8,128)} %bitcast.38, f32[8,96,128]{2,1,0:T(8,128)} %copy-done.10, f32[128,1536]{1,0:T(8,128)} %transposed.4.rest_0_), custom_call_target="tpu_custom_call" | custom-call | flops 905969664 | bytes 4718592 | tf_op jit(solution)/shard_map/transposed/pallas_call | solution.py:141
  64.1 12.1 %all-to-all-start.2 = ((f32[16,96,128]{2,1,0:T(8,128)}), f32[16,96,128]{2,1,0:T(8,128)S(1)}, u32[]{:S(2)}, u32[]{:S(2)}) async-start(f32[16,96,128]{2,1,0:T(8,128)} %bitcast.50), calls=%async_computation.2 | async-start | bytes 1572864 | tf_op jit(solution)/shard_map/back_transposed/all_to_all | solution.py:14
  76.2 5.1 %direct.5 = f32[8,96,128]{2,1,0:T(8,128)} custom-call(s32[9]{0:T(128)} %get-tuple-element.30.where_ref, f32[8,2,96,1536]{3,2,1,0:T(8,128)} %bitcast.39, f32[1536,128]{1,0:T(8,128)} %bitcast.45), custom_call_target="tpu_custom_call" | custom-call | flops 905969664 | bytes 4718592 | tf_op jit(solution)/shard_map/direct/pallas_call | solution.py:96
  81.3 3.4 %collective-permute-start.3 = (f32[8,96,128]{2,1,0:T(8,128)}, f32[8,96,128]{2,1,0:T(8,128)S(1)}, u32[]{:S(2)}, u32[]{:S(2)}) collective-permute-start(f32[8,96,128]{2,1,0:T(8,128)} %direct.5), channel_id=1, source_target_pairs={{0,1},{1,0},{2,3},{3,2},{4,5},{5,4},{6,7},{7,6},{8,9},{9,8},{10,11... | collective-permute-start | bytes 1179656 | tf_op jit(solution)/shard_map/direct/ppermute | solution.py:165
  84.8 5.0 %direct.4 = f32[8,96,128]{2,1,0:T(8,128)} custom-call(s32[9]{0:T(128)} %get-tuple-element.29.where_ref, f32[8,2,96,1536]{3,2,1,0:T(8,128)} %bitcast.40, f32[1536,128]{1,0:T(8,128)} %bitcast.46), custom_call_target="tpu_custom_call" | custom-call | flops 905969664 | bytes 4718592 | tf_op jit(solution)/shard_map/direct/pallas_call | solution.py:96
  89.8 6.9 %collective-permute-done.3 = f32[8,96,128]{2,1,0:T(8,128)S(1)} collective-permute-done((f32[8,96,128]{2,1,0:T(8,128)}, f32[8,96,128]{2,1,0:T(8,128)S(1)}, u32[]{:S(2)}, u32[]{:S(2)}) %collective-permute-start.3) | collective-permute-done | bytes 393248 | tf_op jit(solution)/shard_map/direct/ppermute | solution.py:165
  101.0 5.7 %all-to-all-start.3 = ((f32[16,96,128]{2,1,0:T(8,128)}), f32[16,96,128]{2,1,0:T(8,128)S(1)}, u32[]{:S(2)}, u32[]{:S(2)}) async-start(f32[16,96,128]{2,1,0:T(8,128)} %back_wide.2), calls=%async_computation.3 | async-start | bytes 1572864 | tf_op jit(solution)/shard_map/back_wide/all_to_all | solution.py:14
  106.7 1.9 collective-permute-start.5
  108.7 6.0 %collective-permute-done.5 = f32[2,96,128]{2,1,0:T(8,128)S(1)} collective-permute-done((f32[2,96,128]{2,1,0:T(8,128)S(1)}, f32[2,96,128]{2,1,0:T(8,128)S(1)}, u32[]{:S(2)}, u32[]{:S(2)}) %collective-permute-start.5) | collective-permute-done | bytes 98336 | tf_op jit(solution)/shard_map/back_direct/ppermute | solution.py:165
  114.7 3.8 %collective-permute-start.6 = (f32[1,96,128]{2,1,0:T(8,128)S(1)}, f32[1,96,128]{2,1,0:T(8,128)S(1)}, u32[]{:S(2)}, u32[]{:S(2)}) collective-permute-start(f32[1,96,128]{2,1,0:T(8,128)S(1)} %slice_add_fusion.11), channel_id=1, source_target_pairs={{0,8},{1,9},{2,10},{3,11},{4,12},{5,13},{6,14},{7,15},{8,0},{9,1},... | collective-permute-start | bytes 147464 | tf_op jit(solution)/shard_map/back_direct/ppermute | solution.py:165
  118.9 4.4 %collective-permute-done.6 = f32[1,96,128]{2,1,0:T(8,128)S(1)} collective-permute-done((f32[1,96,128]{2,1,0:T(8,128)S(1)}, f32[1,96,128]{2,1,0:T(8,128)S(1)}, u32[]{:S(2)}, u32[]{:S(2)}) %collective-permute-start.6) | collective-permute-done | bytes 49184 | tf_op jit(solution)/shard_map/back_direct/ppermute | solution.py:165
  124.3 5.7 %all-to-all-start.4 = ((f32[16,96,128]{2,1,0:T(8,128)}), f32[16,96,128]{2,1,0:T(8,128)S(1)}, u32[]{:S(2)}, u32[]{:S(2)}) async-start(f32[16,96,128]{2,1,0:T(8,128)} %broadcast_in_dim.23), calls=%async_computation.4 | async-start | bytes 1572864 | tf_op jit(solution)/shard_map/gather_wide/all_to_all | solution.py:14
  130.0 3.2 %collective-permute-start.8 = (f32[1,96,128]{2,1,0:T(8,128)S(1)}, f32[1,96,128]{2,1,0:T(8,128)S(1)}, u32[]{:S(2)}, u32[]{:S(2)}) collective-permute-start(f32[1,96,128]{2,1,0:T(8,128)S(1)} %fusion.4), channel_id=1, source_target_pairs={{0,8},{1,9},{2,10},{3,11},{4,12},{5,13},{6,14},{7,15},{8,0},{9,1},... | collective-permute-start | bytes 147464 | tf_op jit(solution)/shard_map/gather_row/ppermute | solution.py:165
  133.2 5.4 %collective-permute-done.8 = f32[1,96,128]{2,1,0:T(8,128)S(1)} collective-permute-done((f32[1,96,128]{2,1,0:T(8,128)S(1)}, f32[1,96,128]{2,1,0:T(8,128)S(1)}, u32[]{:S(2)}, u32[]{:S(2)}) %collective-permute-start.8) | collective-permute-done | bytes 49184 | tf_op jit(solution)/shard_map/gather_row/ppermute | solution.py:165
  138.7 6.5 %collective-permute-done.9 = f32[2,96,128]{2,1,0:T(8,128)S(1)} collective-permute-done((f32[2,96,128]{2,1,0:T(8,128)S(1)}, f32[2,96,128]{2,1,0:T(8,128)S(1)}, u32[]{:S(2)}, u32[]{:S(2)}) %collective-permute-start.9) | collective-permute-done | bytes 98336 | tf_op jit(solution)/shard_map/gather_row/ppermute | solution.py:165
  145.3 6.8 %collective-permute-done.10 = f32[4,96,128]{2,1,0:T(8,128)S(1)} collective-permute-done((f32[4,96,128]{2,1,0:T(8,128)S(1)}, f32[4,96,128]{2,1,0:T(8,128)S(1)}, u32[]{:S(2)}, u32[]{:S(2)}) %collective-permute-start.10) | collective-permute-done | bytes 196640 | tf_op jit(solution)/shard_map/gather_row/ppermute | solution.py:165
  153.7 4.8 %all-to-all-start.5 = ((f32[16,96,128]{2,1,0:T(8,128)}), f32[16,96,128]{2,1,0:T(8,128)S(1)}, u32[]{:S(2)}, u32[]{:S(2)}) async-start(f32[16,96,128]{2,1,0:T(8,128)} %gather_column.3), calls=%async_computation.5 | async-start | bytes 1572864 | tf_op jit(solution)/shard_map/gather_column/all_to_all | solution.py:14
  158.5 3.4 %collective-permute-start.11 = (f32[8,96,128]{2,1,0:T(8,128)S(1)}, f32[8,96,128]{2,1,0:T(8,128)S(1)}, u32[]{:S(2)}, u32[]{:S(2)}) collective-permute-start(f32[8,96,128]{2,1,0:T(8,128)S(1)} %pad_maximum_fusion.1.row_ref), channel_id=1, source_target_pairs={{0,1},{1,0},{2,3},{3,2},{4,5},{5,4},{6,7},{7,6},{8,9},{9,8},{10,11... | collective-permute-start | bytes 1179656 | tf_op jit(solution)/shard_map/gather_row/ppermute | solution.py:165
  162.0 5.7 %transposed.6.rest_0_ = f32[128,1536]{1,0:T(8,128)} custom-call(s32[9]{0:T(128)} %get-tuple-element.29.where_ref, f32[8,2,96,1536]{3,2,1,0:T(8,128)} %bitcast.41, f32[8,96,128]{2,1,0:T(8,128)} %copy-done.4), custom_call_target="tpu_custom_call" | custom-call | flops 905969664 | bytes 4718592 | tf_op jit(solution)/shard_map/transposed/pallas_call | solution.py:141
  167.6 6.1 %collective-permute-done.11.row_ref = f32[8,96,128]{2,1,0:T(8,128)S(1)} collective-permute-done((f32[8,96,128]{2,1,0:T(8,128)S(1)}, f32[8,96,128]{2,1,0:T(8,128)S(1)}, u32[]{:S(2)}, u32[]{:S(2)}) %collective-permute-start.11) | collective-permute-done | bytes 393248 | tf_op jit(solution)/shard_map/gather_row/ppermute | solution.py:165
  174.4 5.9 %transposed.7 = f32[1536,128]{1,0:T(8,128)} custom-call(s32[9]{0:T(128)} %get-tuple-element.30.where_ref, f32[8,2,96,1536]{3,2,1,0:T(8,128)} %bitcast.42, f32[8,96,128]{2,1,0:T(8,128)} %copy-done.6, f32[128,1536]{1,0:T(8,128)} %transposed.6.rest_0_), custom_call_target="tpu_custom_call" | custom-call | flops 905969664 | bytes 4718592 | tf_op jit(solution)/shard_map/transposed/pallas_call | solution.py:141
  181.7 11.8 %all-to-all-start.6 = ((f32[16,96,128]{2,1,0:T(8,128)}), f32[16,96,128]{2,1,0:T(8,128)S(1)}, u32[]{:S(2)}, u32[]{:S(2)}) async-start(f32[16,96,128]{2,1,0:T(8,128)} %bitcast.49), calls=%async_computation.6 | async-start | bytes 1572864 | tf_op jit(solution)/shard_map/back_transposed/all_to_all | solution.py:14
  193.5 5.1 %direct.7 = f32[8,96,128]{2,1,0:T(8,128)} custom-call(s32[9]{0:T(128)} %get-tuple-element.30.where_ref, f32[8,2,96,1536]{3,2,1,0:T(8,128)} %bitcast.43, f32[1536,128]{1,0:T(8,128)} %bitcast.47), custom_call_target="tpu_custom_call" | custom-call | flops 905969664 | bytes 4718592 | tf_op jit(solution)/shard_map/direct/pallas_call | solution.py:96
  198.7 3.4 %collective-permute-start.12 = (f32[8,96,128]{2,1,0:T(8,128)}, f32[8,96,128]{2,1,0:T(8,128)S(1)}, u32[]{:S(2)}, u32[]{:S(2)}) collective-permute-start(f32[8,96,128]{2,1,0:T(8,128)} %direct.7), channel_id=1, source_target_pairs={{0,1},{1,0},{2,3},{3,2},{4,5},{5,4},{6,7},{7,6},{8,9},{9,8},{10,11... | collective-permute-start | bytes 1179656 | tf_op jit(solution)/shard_map/direct/ppermute | solution.py:165
  202.1 5.0 %direct.6 = f32[8,96,128]{2,1,0:T(8,128)} custom-call(s32[9]{0:T(128)} %get-tuple-element.29.where_ref, f32[8,2,96,1536]{3,2,1,0:T(8,128)} %bitcast.44, f32[1536,128]{1,0:T(8,128)} %bitcast.48), custom_call_target="tpu_custom_call" | custom-call | flops 905969664 | bytes 4718592 | tf_op jit(solution)/shard_map/direct/pallas_call | solution.py:96
  207.9 7.5 %collective-permute-done.12 = f32[8,96,128]{2,1,0:T(8,128)S(1)} collective-permute-done((f32[8,96,128]{2,1,0:T(8,128)}, f32[8,96,128]{2,1,0:T(8,128)S(1)}, u32[]{:S(2)}, u32[]{:S(2)}) %collective-permute-start.12) | collective-permute-done | bytes 393248 | tf_op jit(solution)/shard_map/direct/ppermute | solution.py:165
  218.9 1.8 back_wide.3
  220.7 5.7 %all-to-all-start.7 = ((f32[16,104,128]{2,1,0:T(8,128)}), f32[16,104,128]{2,1,0:T(8,128)S(1)}, u32[]{:S(2)}, u32[]{:S(2)}) async-start(f32[16,104,128]{2,1,0:T(8,128)} %back_wide.3), calls=%async_computation.7 | async-start | bytes 1703936 | tf_op jit(solution)/shard_map/back_wide/all_to_all | solution.py:14
  226.4 1.9 collective-permute-start.14
  228.4 6.0 %collective-permute-done.14 = f32[2,96,128]{2,1,0:T(8,128)S(1)} collective-permute-done((f32[2,96,128]{2,1,0:T(8,128)S(1)}, f32[2,96,128]{2,1,0:T(8,128)S(1)}, u32[]{:S(2)}, u32[]{:S(2)}) %collective-permute-start.14) | collective-permute-done | bytes 98336 | tf_op jit(solution)/shard_map/back_direct/ppermute | solution.py:165
  234.4 4.0 %collective-permute-start.15 = (f32[1,96,128]{2,1,0:T(8,128)S(1)}, f32[1,96,128]{2,1,0:T(8,128)S(1)}, u32[]{:S(2)}, u32[]{:S(2)}) collective-permute-start(f32[1,96,128]{2,1,0:T(8,128)S(1)} %slice_add_fusion.9), channel_id=1, source_target_pairs={{0,8},{1,9},{2,10},{3,11},{4,12},{5,13},{6,14},{7,15},{8,0},{9,1},... | collective-permute-start | bytes 147464 | tf_op jit(solution)/shard_map/back_direct/ppermute | solution.py:165
  239.3 3.1 %collective-permute-done.15 = f32[1,96,128]{2,1,0:T(8,128)S(1)} collective-permute-done((f32[1,96,128]{2,1,0:T(8,128)S(1)}, f32[1,96,128]{2,1,0:T(8,128)S(1)}, u32[]{:S(2)}, u32[]{:S(2)}) %collective-permute-start.15) | collective-permute-done | bytes 49184 | tf_op jit(solution)/shard_map/back_direct/ppermute | solution.py:165
  242.8 10.7 %all_to_all.55 = f32[16,16,128]{2,1,0:T(8,128)S(1)} all-to-all(f32[16,16,128]{2,1,0:T(8,128)S(1)} %pad_maximum_fusion.4), channel_id=1, replica_groups=mesh['wide'=16,'narrow'=16] {'wide'}, dimensions={0} | all-to-all | bytes 262144 | tf_op jit(solution)/shard_map/gram_sum_wide/all_to_all | solution.py:14
  254.2 17.2 %all_to_all.56 = f32[16,8,128]{2,1,0:T(8,128)S(1)} all-to-all(f32[16,8,128]{2,1,0:T(8,128)S(1)} %broadcast_in_dim.25), channel_id=1, replica_groups=mesh['wide'=16,'narrow'=16] {'narrow'}, dimensions={0} | all-to-all | bytes 131072 | tf_op jit(solution)/shard_map/gram_sum_narrow/all_to_all | solution.py:14
  272.1 5.2 %all-to-all-start.10 = ((f32[16,8,128]{2,1,0:T(8,128)}), f32[16,8,128]{2,1,0:T(8,128)S(1)}, u32[]{:S(2)}, u32[]{:S(2)}) async-start(f32[16,8,128]{2,1,0:T(8,128)} %broadcast_in_dim.26), calls=%async_computation.10 | async-start | bytes 131072 | tf_op jit(solution)/shard_map/gram_whole/all_to_all | solution.py:14
  277.3 3.8 %inverse_first.1.refs_1_ = f32[128,128]{1,0:T(8,128)} custom-call(f32[128,128]{1,0:T(8,128)} %get-tuple-element.27.refs_0_), custom_call_target="tpu_custom_call" | custom-call | flops 1073741824 | bytes 1048576 | tf_op jit(solution)/shard_map/inverse_first/pallas_call | solution.py:259
  282.8 4.5 %finish.1 = f32[96,128]{1,0:T(8,128)} custom-call(f32[128,128]{1,0:T(8,128)} %bitcast.56, f32[128,128]{1,0:T(8,128)} %inverse_first.1.refs_1_, f32[96,128]{1,0:T(8,128)} %copy-done.9), custom_call_target="tpu_custom_call" | custom-call | flops 1073741824 | bytes 1048576 | tf_op jit(solution)/shard_map/finish/pallas_call | solution.py:259
  (72 shorter events, 25.8 us)
Async XLA Ops:
  1.8 30.5 %all-to-all-start = ((f32[16,96,128]{2,1,0:T(8,128)}), f32[16,96,128]{2,1,0:T(8,128)S(1)}, u32[]{:S(2)}, u32[]{:S(2)}) async-start(f32[16,96,128]{2,1,0:T(8,128)} %broadcast_in_dim.19), calls=%async_computation | async-start | bytes 1572864 | tf_op jit(solution)/shard_map/gather_wide/all_to_all | solution.py:14
  7.5 9.6 %collective-permute-start = (f32[1,96,128]{2,1,0:T(8,128)}, f32[1,96,128]{2,1,0:T(8,128)S(1)}, u32[]{:S(2)}, u32[]{:S(2)}) collective-permute-start(f32[1,96,128]{2,1,0:T(8,128)} %bitcast.52), channel_id=1, source_target_pairs={{0,8},{1,9},{2,10},{3,11},{4,12},{5,13},{6,14},{7,15},{8,0},{9,1},... | collective-permute-start | bytes 147464 | tf_op jit(solution)/shard_map/gather_row/ppermute | solution.py:165
  17.9 6.9 %collective-permute-start.1 = (f32[2,96,128]{2,1,0:T(8,128)S(1)}, f32[2,96,128]{2,1,0:T(8,128)S(1)}, u32[]{:S(2)}, u32[]{:S(2)}) collective-permute-start(f32[2,96,128]{2,1,0:T(8,128)S(1)} %pad_maximum_fusion.5), channel_id=1, source_target_pairs={{0,4},{1,5},{2,6},{3,7},{4,0},{5,1},{6,2},{7,3},{8,12},{9,13},{10,... | collective-permute-start | bytes 294920 | tf_op jit(solution)/shard_map/gather_row/ppermute | solution.py:165
  25.6 5.8 %collective-permute-start.2 = (f32[4,96,128]{2,1,0:T(8,128)S(1)}, f32[4,96,128]{2,1,0:T(8,128)S(1)}, u32[]{:S(2)}, u32[]{:S(2)}) collective-permute-start(f32[4,96,128]{2,1,0:T(8,128)S(1)} %pad_maximum_fusion.2), channel_id=1, source_target_pairs={{0,2},{1,3},{2,0},{3,1},{4,6},{5,7},{6,4},{7,5},{8,10},{9,11},{10,... | collective-permute-start | bytes 589832 | tf_op jit(solution)/shard_map/gather_row/ppermute | solution.py:165
  32.2 14.6 %copy-start.8 = (f32[8,96,128]{2,1,0:T(8,128)}, f32[8,96,128]{2,1,0:T(8,128)S(1)}, u32[]{:S(2)}) copy-start(f32[8,96,128]{2,1,0:T(8,128)S(1)} %pad_maximum_fusion.row_ref) | copy-start | bytes 1179652
  32.3 0.7 copy-start
  34.5 29.5 %all-to-all-start.1 = ((f32[16,96,128]{2,1,0:T(8,128)}), f32[16,96,128]{2,1,0:T(8,128)S(1)}, u32[]{:S(2)}, u32[]{:S(2)}) async-start(f32[16,96,128]{2,1,0:T(8,128)} %gather_column.2), calls=%async_computation.1 | async-start | bytes 1572864 | tf_op jit(solution)/shard_map/gather_column/all_to_all | solution.py:14
  42.7 13.5 %collective-permute-start.7 = (f32[8,96,128]{2,1,0:T(8,128)S(1)}, f32[8,96,128]{2,1,0:T(8,128)S(1)}, u32[]{:S(2)}, u32[]{:S(2)}) collective-permute-start(f32[8,96,128]{2,1,0:T(8,128)S(1)} %pad_maximum_fusion.row_ref), channel_id=1, source_target_pairs={{0,1},{1,0},{2,3},{3,2},{4,5},{5,4},{6,7},{7,6},{8,9},{9,8},{10,11... | collective-permute-start | bytes 1179656 | tf_op jit(solution)/shard_map/gather_row/ppermute | solution.py:165
  56.2 0.8 copy-start.10
  64.1 12.1 %copy-start.2 = (f32[16,96,128]{2,1,0:T(8,128)}, f32[16,96,128]{2,1,0:T(8,128)S(1)}, u32[]{:S(2)}) copy-start(f32[16,96,128]{2,1,0:T(8,128)S(1)} %all-to-all-done.1) | copy-start | bytes 2359300
  64.1 35.3 %all-to-all-start.2 = ((f32[16,96,128]{2,1,0:T(8,128)}), f32[16,96,128]{2,1,0:T(8,128)S(1)}, u32[]{:S(2)}, u32[]{:S(2)}) async-start(f32[16,96,128]{2,1,0:T(8,128)} %bitcast.50), calls=%async_computation.2 | async-start | bytes 1572864 | tf_op jit(solution)/shard_map/back_transposed/all_to_all | solution.py:14
  76.2 23.2 %copy-start.1 = (s32[1,16]{1,0:T(1,128)S(1)}, s32[1,16]{1,0:T(1,128)}, u32[]{:S(2)}) copy-start(s32[1,16]{1,0:T(1,128)} %param.4) | copy-start | bytes 196
  81.3 15.4 %collective-permute-start.3 = (f32[8,96,128]{2,1,0:T(8,128)}, f32[8,96,128]{2,1,0:T(8,128)S(1)}, u32[]{:S(2)}, u32[]{:S(2)}) collective-permute-start(f32[8,96,128]{2,1,0:T(8,128)} %direct.5), channel_id=1, source_target_pairs={{0,1},{1,0},{2,3},{3,2},{4,5},{5,4},{6,7},{7,6},{8,9},{9,8},{10,11... | collective-permute-start | bytes 1179656 | tf_op jit(solution)/shard_map/direct/ppermute | solution.py:165
  97.8 8.9 %collective-permute-start.4 = (f32[4,96,128]{2,1,0:T(8,128)S(1)}, f32[4,96,128]{2,1,0:T(8,128)S(1)}, u32[]{:S(2)}, u32[]{:S(2)}) collective-permute-start(f32[4,96,128]{2,1,0:T(8,128)S(1)} %get-tuple-element.22), channel_id=1, source_target_pairs={{0,2},{1,3},{2,0},{3,1},{4,6},{5,7},{6,4},{7,5},{8,10},{9,11},{10,... | collective-permute-start | bytes 589832 | tf_op jit(solution)/shard_map/back_direct/ppermute | solution.py:165
  101.0 17.9 %all-to-all-start.3 = ((f32[16,96,128]{2,1,0:T(8,128)}), f32[16,96,128]{2,1,0:T(8,128)S(1)}, u32[]{:S(2)}, u32[]{:S(2)}) async-start(f32[16,96,128]{2,1,0:T(8,128)} %back_wide.2), calls=%async_computation.3 | async-start | bytes 1572864 | tf_op jit(solution)/shard_map/back_wide/all_to_all | solution.py:14
  106.7 7.9 %collective-permute-start.5 = (f32[2,96,128]{2,1,0:T(8,128)S(1)}, f32[2,96,128]{2,1,0:T(8,128)S(1)}, u32[]{:S(2)}, u32[]{:S(2)}) collective-permute-start(f32[2,96,128]{2,1,0:T(8,128)S(1)} %get-tuple-element.26), channel_id=1, source_target_pairs={{0,4},{1,5},{2,6},{3,7},{4,0},{5,1},{6,2},{7,3},{8,12},{9,13},{10,... | collective-permute-start | bytes 294920 | tf_op jit(solution)/shard_map/back_direct/ppermute | solution.py:165
  114.7 8.6 %collective-permute-start.6 = (f32[1,96,128]{2,1,0:T(8,128)S(1)}, f32[1,96,128]{2,1,0:T(8,128)S(1)}, u32[]{:S(2)}, u32[]{:S(2)}) collective-permute-start(f32[1,96,128]{2,1,0:T(8,128)S(1)} %slice_add_fusion.11), channel_id=1, source_target_pairs={{0,8},{1,9},{2,10},{3,11},{4,12},{5,13},{6,14},{7,15},{8,0},{9,1},... | collective-permute-start | bytes 147464 | tf_op jit(solution)/shard_map/back_direct/ppermute | solution.py:165
  124.3 27.8 %all-to-all-start.4 = ((f32[16,96,128]{2,1,0:T(8,128)}), f32[16,96,128]{2,1,0:T(8,128)S(1)}, u32[]{:S(2)}, u32[]{:S(2)}) async-start(f32[16,96,128]{2,1,0:T(8,128)} %broadcast_in_dim.23), calls=%async_computation.4 | async-start | bytes 1572864 | tf_op jit(solution)/shard_map/gather_wide/all_to_all | solution.py:14
  130.0 8.6 %collective-permute-start.8 = (f32[1,96,128]{2,1,0:T(8,128)S(1)}, f32[1,96,128]{2,1,0:T(8,128)S(1)}, u32[]{:S(2)}, u32[]{:S(2)}) collective-permute-start(f32[1,96,128]{2,1,0:T(8,128)S(1)} %fusion.4), channel_id=1, source_target_pairs={{0,8},{1,9},{2,10},{3,11},{4,12},{5,13},{6,14},{7,15},{8,0},{9,1},... | collective-permute-start | bytes 147464 | tf_op jit(solution)/shard_map/gather_row/ppermute | solution.py:165
  138.6 6.6 %collective-permute-start.9 = (f32[2,96,128]{2,1,0:T(8,128)S(1)}, f32[2,96,128]{2,1,0:T(8,128)S(1)}, u32[]{:S(2)}, u32[]{:S(2)}) collective-permute-start(f32[2,96,128]{2,1,0:T(8,128)S(1)} %pad_maximum_fusion.6), channel_id=1, source_target_pairs={{0,4},{1,5},{2,6},{3,7},{4,0},{5,1},{6,2},{7,3},{8,12},{9,13},{10,... | collective-permute-start | bytes 294920 | tf_op jit(solution)/shard_map/gather_row/ppermute | solution.py:165
  145.2 6.9 %collective-permute-start.10 = (f32[4,96,128]{2,1,0:T(8,128)S(1)}, f32[4,96,128]{2,1,0:T(8,128)S(1)}, u32[]{:S(2)}, u32[]{:S(2)}) collective-permute-start(f32[4,96,128]{2,1,0:T(8,128)S(1)} %pad_maximum_fusion.3), channel_id=1, source_target_pairs={{0,2},{1,3},{2,0},{3,1},{4,6},{5,7},{6,4},{7,5},{8,10},{9,11},{10,... | collective-permute-start | bytes 589832 | tf_op jit(solution)/shard_map/gather_row/ppermute | solution.py:165
  152.1 9.9 %copy-start.4 = (f32[8,96,128]{2,1,0:T(8,128)}, f32[8,96,128]{2,1,0:T(8,128)S(1)}, u32[]{:S(2)}) copy-start(f32[8,96,128]{2,1,0:T(8,128)S(1)} %pad_maximum_fusion.1.row_ref) | copy-start | bytes 1179652
  153.7 28.0 %all-to-all-start.5 = ((f32[16,96,128]{2,1,0:T(8,128)}), f32[16,96,128]{2,1,0:T(8,128)S(1)}, u32[]{:S(2)}, u32[]{:S(2)}) async-start(f32[16,96,128]{2,1,0:T(8,128)} %gather_column.3), calls=%async_computation.5 | async-start | bytes 1572864 | tf_op jit(solution)/shard_map/gather_column/all_to_all | solution.py:14
  158.5 15.2 %collective-permute-start.11 = (f32[8,96,128]{2,1,0:T(8,128)S(1)}, f32[8,96,128]{2,1,0:T(8,128)S(1)}, u32[]{:S(2)}, u32[]{:S(2)}) collective-permute-start(f32[8,96,128]{2,1,0:T(8,128)S(1)} %pad_maximum_fusion.1.row_ref), channel_id=1, source_target_pairs={{0,1},{1,0},{2,3},{3,2},{4,5},{5,4},{6,7},{7,6},{8,9},{9,8},{10,11... | collective-permute-start | bytes 1179656 | tf_op jit(solution)/shard_map/gather_row/ppermute | solution.py:165
  173.7 0.8 copy-start.6
  181.7 11.8 %copy-start.3 = (f32[16,96,128]{2,1,0:T(8,128)}, f32[16,96,128]{2,1,0:T(8,128)S(1)}, u32[]{:S(2)}) copy-start(f32[16,96,128]{2,1,0:T(8,128)S(1)} %all-to-all-done.5) | copy-start | bytes 2359300
  181.7 37.2 %all-to-all-start.6 = ((f32[16,96,128]{2,1,0:T(8,128)}), f32[16,96,128]{2,1,0:T(8,128)S(1)}, u32[]{:S(2)}, u32[]{:S(2)}) async-start(f32[16,96,128]{2,1,0:T(8,128)} %bitcast.49), calls=%async_computation.6 | async-start | bytes 1572864 | tf_op jit(solution)/shard_map/back_transposed/all_to_all | solution.py:14
  193.5 13.6 %copy-start.7 = (f32[8,96,128]{2,1,0:T(8,128)S(1)}, f32[8,96,128]{2,1,0:T(8,128)}, u32[]{:S(2)}) copy-start(f32[8,96,128]{2,1,0:T(8,128)} %copy-done.6) | copy-start | bytes 1179652
  193.5 24.6 %copy-start.5 = (f32[8,96,128]{2,1,0:T(8,128)S(1)}, f32[8,96,128]{2,1,0:T(8,128)}, u32[]{:S(2)}) copy-start(f32[8,96,128]{2,1,0:T(8,128)} %copy-done.4) | copy-start | bytes 1179652
  198.7 16.8 %collective-permute-start.12 = (f32[8,96,128]{2,1,0:T(8,128)}, f32[8,96,128]{2,1,0:T(8,128)S(1)}, u32[]{:S(2)}, u32[]{:S(2)}) collective-permute-start(f32[8,96,128]{2,1,0:T(8,128)} %direct.7), channel_id=1, source_target_pairs={{0,1},{1,0},{2,3},{3,2},{4,5},{5,4},{6,7},{7,6},{8,9},{9,8},{10,11... | collective-permute-start | bytes 1179656 | tf_op jit(solution)/shard_map/direct/ppermute | solution.py:165
  216.5 9.9 %collective-permute-start.13 = (f32[4,96,128]{2,1,0:T(8,128)S(1)}, f32[4,96,128]{2,1,0:T(8,128)S(1)}, u32[]{:S(2)}, u32[]{:S(2)}) collective-permute-start(f32[4,96,128]{2,1,0:T(8,128)S(1)} %get-tuple-element.20), channel_id=1, source_target_pairs={{0,2},{1,3},{2,0},{3,1},{4,6},{5,7},{6,4},{7,5},{8,10},{9,11},{10,... | collective-permute-start | bytes 589832 | tf_op jit(solution)/shard_map/back_direct/ppermute | solution.py:165
  220.7 18.6 %all-to-all-start.7 = ((f32[16,104,128]{2,1,0:T(8,128)}), f32[16,104,128]{2,1,0:T(8,128)S(1)}, u32[]{:S(2)}, u32[]{:S(2)}) async-start(f32[16,104,128]{2,1,0:T(8,128)} %back_wide.3), calls=%async_computation.7 | async-start | bytes 1703936 | tf_op jit(solution)/shard_map/back_wide/all_to_all | solution.py:14
  226.4 7.9 %collective-permute-start.14 = (f32[2,96,128]{2,1,0:T(8,128)S(1)}, f32[2,96,128]{2,1,0:T(8,128)S(1)}, u32[]{:S(2)}, u32[]{:S(2)}) collective-permute-start(f32[2,96,128]{2,1,0:T(8,128)S(1)} %get-tuple-element.24), channel_id=1, source_target_pairs={{0,4},{1,5},{2,6},{3,7},{4,0},{5,1},{6,2},{7,3},{8,12},{9,13},{10,... | collective-permute-start | bytes 294920 | tf_op jit(solution)/shard_map/back_direct/ppermute | solution.py:165
  234.4 8.1 %collective-permute-start.15 = (f32[1,96,128]{2,1,0:T(8,128)S(1)}, f32[1,96,128]{2,1,0:T(8,128)S(1)}, u32[]{:S(2)}, u32[]{:S(2)}) collective-permute-start(f32[1,96,128]{2,1,0:T(8,128)S(1)} %slice_add_fusion.9), channel_id=1, source_target_pairs={{0,8},{1,9},{2,10},{3,11},{4,12},{5,13},{6,14},{7,15},{8,0},{9,1},... | collective-permute-start | bytes 147464 | tf_op jit(solution)/shard_map/back_direct/ppermute | solution.py:165
  242.5 39.7 %copy-start.9 = (f32[96,128]{1,0:T(8,128)}, f32[96,128]{1,0:T(8,128)S(1)}, u32[]{:S(2)}) copy-start(f32[96,128]{1,0:T(8,128)S(1)} %slice_add_fusion.8.refs_2_) | copy-start | bytes 147460
  272.1 10.1 %all-to-all-start.10 = ((f32[16,8,128]{2,1,0:T(8,128)}), f32[16,8,128]{2,1,0:T(8,128)S(1)}, u32[]{:S(2)}, u32[]{:S(2)}) async-start(f32[16,8,128]{2,1,0:T(8,128)} %broadcast_in_dim.26), calls=%async_computation.10 | async-start | bytes 131072 | tf_op jit(solution)/shard_map/gram_whole/all_to_all | solution.py:14
  282.2 0.6 copy-start.11

commit v2 on v1

--- a/solution.py
+++ b/solution.py
@@ -78,7 +78,7 @@
     steps = 2
     each = groups // steps
 
-    def kernel(where_ref, tile_ref, column_ref, out_ref, both):
+    def kernel(where_ref, tile_ref, column_ref, first_ref, second_ref, both):
         step = pl.program_id(0)
 
         @pl.when(step == 0)
@@ -91,11 +91,21 @@
         wide = product_of(high, both[...])
         total = wide[:, :width] + wide[:, width:] + product_of(low, both[:, :width])
         for k in range(each):
-            out_ref[where_ref[1 + step * each + k]] = total[k * rows : (k + 1) * rows]
-
+            place = where_ref[1 + step * each + k]
+            part = total[k * rows : (k + 1) * rows]
+
+            @pl.when(place < each)
+            def _():
+                first_ref[place] = part
+
+            @pl.when(place >= each)
+            def _():
+                second_ref[place - each] = part
+
+    out = jax.ShapeDtypeStruct((each, rows, width), jnp.float32)
     return pl.pallas_call(
         kernel,
-        out_shape=jax.ShapeDtypeStruct((groups, rows, width), jnp.float32),
+        out_shape=(out, out),
         grid_spec=pltpu.PrefetchScalarGridSpec(
             num_scalar_prefetch=1,
             grid=(steps,),
@@ -103,7 +113,7 @@
                 pl.BlockSpec((each, 1, rows, order), lambda g, where: (g, where[0], 0, 0)),
                 pl.BlockSpec((order, width), lambda g, where: (0, 0)),
             ],
-            out_specs=pl.BlockSpec((groups, rows, width), lambda g, where: (0, 0, 0)),
+            out_specs=[pl.BlockSpec((each, rows, width), lambda g, where: (0, 0, 0))] * 2,
             scratch_shapes=[pltpu.VMEM((order, 2 * width), jnp.bfloat16)],
         ),
         compiler_params=pltpu.CompilerParams(vmem_limit_bytes=60 << 20),
@@ -111,20 +121,23 @@
     )(jnp.concatenate([half[None], places]), tile, column_block)
 
 
-def transposed_half(tile, row_half, half, places, partial=None):
+def transposed_half(tile, quarters, half, spots, partial=None):
     groups, _, rows, order = tile.shape
-    width = row_half.shape[2]
+    width = quarters[0].shape[2]
     depth = groups * rows
+    each = groups // 2
     steps = 3
     chunk = order // steps
 
-    def kernel(where_ref, tile_ref, row_ref, *rest):
+    def kernel(where_ref, tile_ref, first_ref, second_ref, *rest):
         partial_ref, (out_ref, gathered, both) = (rest[0], rest[1:]) if partial is not None else (None, rest)
 
         @pl.when(pl.program_id(0) == 0)
         def _():
             for k in range(groups):
-                gathered[k * rows : (k + 1) * rows] = row_ref[where_ref[1 + k]]
+                spot = pl.multiple_of(where_ref[1 + k] * rows, rows)
+                part = first_ref[k] if k < each else second_ref[k - each]
+                gathered[pl.ds(spot, rows)] = part
             high, low = high_low(gathered[...].T)
             both[:width] = high
             both[width:] = low
@@ -146,8 +159,8 @@
             grid=(steps,),
             in_specs=[
                 pl.BlockSpec((groups, 1, rows, chunk), lambda g, where: (0, where[0], 0, g)),
-                pl.BlockSpec((groups, rows, width), lambda g, where: (0, 0, 0)),
             ]
+            + [pl.BlockSpec((each, rows, width), lambda g, where: (0, 0, 0))] * 2
             + ([] if partial is None else [flat]),
             out_specs=flat if partial is None else pl.BlockSpec((chunk, width), lambda g, where: (g, 0)),
             scratch_shapes=[
@@ -157,40 +170,21 @@
         ),
         compiler_params=pltpu.CompilerParams(vmem_limit_bytes=60 << 20),
         cost_estimate=kernel_cost(tile, width),
-    )(jnp.concatenate([half[None], places]), tile, row_half, *([] if partial is None else [partial]))
-
-
-def swap(value, axis, bit):
-    size = lax.axis_size(axis)
-    return lax.ppermute(value, axis, [(i, i ^ bit) for i in range(size)])
-
-
-def bits_of(size):
-    bit = size // 2
-    while bit:
-        yield bit
-        bit //= 2
-
-
-def relative_places(mine, groups):
-    offset = jnp.arange(groups, dtype=jnp.int32) ^ mine
-    count = groups.bit_length() - 1
-    return sum(((offset >> k) & 1) << (count - 1 - k) for k in range(count))
-
-
-def doubled(held, axis, bits):
-    for bit in bits:
-        held = jnp.concatenate([held, swap(held, axis, bit)], axis=0)
-    return held
-
-
-def halved(mine, got, axis):
-    for bit in reversed(list(bits_of(lax.axis_size(axis)))):
-        if bit > 1:
-            half = mine.shape[0] // 2
-            sent = mine[half:] + got[half:]
-            mine, got = mine[:half] + got[:half], swap(sent, axis, bit)
-    return mine[0] + got[0]
+    )(jnp.concatenate([half[None], spots]), tile, *quarters, *([] if partial is None else [partial]))
+
+
+def swap(value, mask):
+    size = lax.axis_size(NARROW)
+    return lax.ppermute(value, NARROW, [(i, i ^ mask) for i in range(size)])
+
+
+ENTRIES = (0, 8, 4, 12)
+QUARTERS = (0, 2, 1, 3)
+REVERSED = (0, 4, 2, 6, 1, 5, 3, 7)
+
+
+def reversed_bits(value):
+    return ((value & 1) << 2) | (value & 2) | (value >> 2)
 
 
 def apply_hamiltonian(tile, columns, vectors, want_gram):
@@ -200,34 +194,40 @@
     groups = count // 2
     me = lax.axis_index(NARROW).astype(jnp.int32)
     near, far = me & 1, (me & 1) ^ 1
-    places = relative_places(me >> 1, groups)
+    table = jnp.array(REVERSED, jnp.int32)
+    spots, places = table ^ (me >> 1), table ^ reversed_bits(me >> 1)
     tile = tile.reshape(groups, 2, rows, order)
     with jax.named_scope("gather_wide"):
         slices = to_everyone(vectors, WIDE)
-    bits = list(bits_of(groups))
     with jax.named_scope("gather_row"):
-        near_rows = doubled(vectors[None], NARROW, [2 * bit for bit in bits])
-        slices, near_rows = lax.optimization_barrier((slices, near_rows))
-        far_rows = swap(near_rows, NARROW, 1)
+        quarter = jnp.stack([vectors] + [swap(vectors, mask) for mask in ENTRIES[1:]])
+        quarters = [quarter] + [swap(quarter, mask) for mask in QUARTERS[1:]]
+        slices, quarters = lax.optimization_barrier((slices, quarters))
     with jax.named_scope("gather_column"):
         picked = move_blocks(slices, columns, scatter=False)
         column_block = exchange(picked, NARROW).reshape(order, width)
     with jax.named_scope("transposed"):
-        partial = transposed_half(tile, near_rows, near, places)
-        transposed = transposed_half(tile, far_rows, far, places, partial)
+        partial = transposed_half(tile, quarters[:2], near, spots)
+        transposed = transposed_half(tile, quarters[2:], far, spots, partial)
+        transposed, column_block = lax.optimization_barrier((transposed, column_block))
     with jax.named_scope("back_transposed"):
         arrived = exchange(transposed.reshape(count, rows, width), NARROW)
     with jax.named_scope("direct"):
-        sent = direct_half(tile, column_block, far, places)
-        got = swap(sent, NARROW, 1)
-        kept = direct_half(tile, column_block, near, places)
+        sums = list(direct_half(tile, column_block, far, places))
+        got = [swap(value, mask) for value, mask in zip(sums, QUARTERS[2:])]
+        kept, sent = direct_half(tile, column_block, near, places)
+        arrived, got, kept, sent = lax.optimization_barrier((arrived, got, kept, sent))
+        got.append(swap(sent, QUARTERS[1]))
     gram = None
     if want_gram:
         with jax.named_scope("gram_block_row"):
-            near_rows, far_rows, kept = lax.optimization_barrier((near_rows, far_rows, kept))
-            gram = gram_of(near_rows.reshape(-1, width)) + gram_of(far_rows.reshape(-1, width))
+            quarters, _ = lax.optimization_barrier((quarters, sums))
+            gram = sum(gram_of(quarter.reshape(-1, width)) for quarter in quarters)
     with jax.named_scope("back_direct"):
-        direct_sum = halved(kept, got, NARROW)
+        kept = kept + got[0] + got[1] + got[2]
+        direct_sum = kept[0]
+        for m, mask in enumerate(ENTRIES[1:]):
+            direct_sum = direct_sum + swap(kept[m + 1], mask)
     with jax.named_scope("back_wide"):
         placed = move_blocks(arrived, columns, scatter=True, extra=gram)
         sums = exchange(placed, WIDE).sum(axis=0)

time: 291 us -> 290 us (level)
  waiting for transfers between devices: 79.1 us -> 90.7 us
  starting transfers between devices: 107 us -> 96.6 us
    all_to_all x9, waiting for transfers between devices: 4.86 us -> 23.2 us  [exchange(): return lax.all_to_all(parts, axis, 0, 0, tiled=True)]
    all_to_all x9, starting transfers between devices: 65 us -> 48.1 us  [exchange(): return lax.all_to_all(parts, axis, 0, 0, tiled=True)]
    ppermute x16 -> x24, waiting for transfers between devices: 74.3 us -> 67.4 us  [swap(): return lax.ppermute(value, NARROW, [(i, i ^ mask) for i in range(size)])]
    ppermute x16 -> x24, starting transfers between devices: 42.2 us -> 48.6 us  [swap(): return lax.ppermute(value, NARROW, [(i, i ^ mask) for i in range(size)])]
  transfers between devices with their start and end apart: 25 -> 33, of which waited for: 19 -> 23; matrix products, arithmetic and copies ran while one was open for 2% -> 2% of each run, Pallas kernels for 18% -> 17%
where the time goes in v2:
time: 290 us; the launch traced here: 286 us
  starting transfers between devices  96.6 us (33%)
  waiting for transfers between devices  90.7 us (31%)
  Pallas kernels  58.8 us (20%)
  blocking collectives  27.1 us (9%)
  other arithmetic  5.49 us (2%)
  local copies, waits for them, and re-layouts  4.77 us (2%)
    ppermute x24, waiting for transfers between devices, swap(): return lax.ppermute(value, NARROW, [(i, i ^ mask) for i in range(size)])  67.4 us
    ppermute x24, starting transfers between devices, swap(): return lax.ppermute(value, NARROW, [(i, i ^ mask) for i in range(size)])  48.6 us
    all_to_all x9, starting transfers between devices, exchange(): return lax.all_to_all(parts, axis, 0, 0, tiled=True)  48.1 us
    all_to_all x2, blocking collectives, exchange(): return lax.all_to_all(parts, axis, 0, 0, tiled=True)  27.1 us
    pallas_call x4, Pallas kernels, transposed_half(): pl.pallas_call(kernel, out_shape=jax.ShapeDtypeStruct((width, order) if p...  23.2 us
    all_to_all x9, waiting for transfers between devices, exchange(): return lax.all_to_all(parts, axis, 0, 0, tiled=True)  23.2 us
    pallas_call x4, Pallas kernels, direct_half(): pl.pallas_call(kernel, out_shape=(out, out), grid_spec=pltpu.PrefetchScal...  20.7 us
    pallas_call x2, Pallas kernels, in_kernel(): pl.pallas_call(kernel, out_shape=jax.ShapeDtypeStruct(shape, jnp.float32)...  8.35 us
  transfers between devices with their start and end apart: 33, of which 23 were waited for; matrix products, arithmetic and copies ran while one was open for 2% of the time, Pallas kernels for 17%

profile of v2, /device:TPU:8, one launch (start us, length us, event | category | flops | bytes accessed | tf_op | source)
XLA Modules:
  0.0 286.1 jit_solution(13727327573796358756)
XLA Ops:
  1.7 5.8 %all-to-all-start = ((f32[16,96,128]{2,1,0:T(8,128)}), f32[16,96,128]{2,1,0:T(8,128)S(1)}, u32[]{:S(2)}, u32[]{:S(2)}) async-start(f32[16,96,128]{2,1,0:T(8,128)} %broadcast_in_dim.19), calls=%async_computation | async-start | bytes 1572864 | tf_op jit(solution)/shard_map/gather_wide/all_to_all | solution.py:14
  7.5 7.2 %collective-permute-start = (f32[96,128]{1,0:T(8,128)}, f32[96,128]{1,0:T(8,128)S(1)}, u32[]{:S(2)}, u32[]{:S(2)}) collective-permute-start(f32[96,128]{1,0:T(8,128)} %param.7), channel_id=1, source_target_pairs={{0,8},{1,9},{2,10},{3,11},{4,12},{5,13},{6,14},{7,15},{8,0},{9,1},... | collective-permute-start | bytes 147464 | tf_op jit(solution)/shard_map/gather_row/ppermute | solution.py:178
  17.5 3.6 %collective-permute-done.2 = f32[96,128]{1,0:T(8,128)S(1)} collective-permute-done((f32[96,128]{1,0:T(8,128)}, f32[96,128]{1,0:T(8,128)S(1)}, u32[]{:S(2)}, u32[]{:S(2)}) %collective-permute-start.2) | collective-permute-done | bytes 49184 | tf_op jit(solution)/shard_map/gather_row/ppermute | solution.py:178
  22.0 3.4 %collective-permute-start.5 = (f32[4,96,128]{2,1,0:T(8,128)S(1)}, f32[4,96,128]{2,1,0:T(8,128)S(1)}, u32[]{:S(2)}, u32[]{:S(2)}) collective-permute-start(f32[4,96,128]{2,1,0:T(8,128)S(1)} %pad_maximum_fusion.first_ref), channel_id=1, source_target_pairs={{0,3},{1,2},{2,1},{3,0},{4,7},{5,6},{6,5},{7,4},{8,11},{9,10},{10,... | collective-permute-start | bytes 589832 | tf_op jit(solution)/shard_map/gather_row/ppermute | solution.py:178
  27.0 5.0 %collective-permute-done.5.second_ref = f32[4,96,128]{2,1,0:T(8,128)S(1)} collective-permute-done((f32[4,96,128]{2,1,0:T(8,128)S(1)}, f32[4,96,128]{2,1,0:T(8,128)S(1)}, u32[]{:S(2)}, u32[]{:S(2)}) %collective-permute-start.5) | collective-permute-done | bytes 196640 | tf_op jit(solution)/shard_map/gather_row/ppermute | solution.py:178
  32.1 2.6 collective-permute-done.4.first_ref
  36.9 6.9 %all-to-all-start.1 = ((f32[16,96,128]{2,1,0:T(8,128)}), f32[16,96,128]{2,1,0:T(8,128)S(1)}, u32[]{:S(2)}, u32[]{:S(2)}) async-start(f32[16,96,128]{2,1,0:T(8,128)} %gather_column.2), calls=%async_computation.1 | async-start | bytes 1572864 | tf_op jit(solution)/shard_map/gather_column/all_to_all | solution.py:14
  45.1 5.7 %transposed.4.rest_0_ = f32[128,1536]{1,0:T(8,128)} custom-call(s32[9]{0:T(128)} %get-tuple-element.89.where_ref, f32[8,2,96,1536]{3,2,1,0:T(8,128)} %bitcast.81, f32[4,96,128]{2,1,0:T(8,128)} %copy-done.12, f32[4,96,128]{2,1,0:T(8,128)} %copy-done.16), custom_call_target="tpu_custom_call" | custom-call | flops 905969664 | bytes 4718592 | tf_op jit(solution)/shard_map/transposed/pallas_call | solution.py:154
  50.8 5.9 %transposed.5 = f32[1536,128]{1,0:T(8,128)} custom-call(s32[9]{0:T(128)} %get-tuple-element.90.where_ref, f32[8,2,96,1536]{3,2,1,0:T(8,128)} %bitcast.82, f32[4,96,128]{2,1,0:T(8,128)} %copy-done.15, f32[4,96,128]{2,1,0:T(8,128)} %copy-done.14, f32[128,1536]{1,0:T(8,128)} %transposed.4.rest_0_), custom_call_target="tpu_custom_call" | custom-call | flops 905969664 | bytes 4718592 | tf_op jit(solution)/shard_map/transposed/pallas_call | solution.py:154
  56.8 10.6 %all-to-all-done.1 = f32[16,96,128]{2,1,0:T(8,128)S(1)} async-done(((f32[16,96,128]{2,1,0:T(8,128)}), f32[16,96,128]{2,1,0:T(8,128)S(1)}, u32[]{:S(2)}, u32[]{:S(2)}) %all-to-all-start.1) | async-done | bytes 786464 | tf_op jit(solution)/shard_map/gather_column/all_to_all | solution.py:14
  67.3 3.6 %all-to-all-start.2 = ((f32[16,96,128]{2,1,0:T(8,128)}), f32[16,96,128]{2,1,0:T(8,128)S(1)}, u32[]{:S(2)}, u32[]{:S(2)}) async-start(f32[16,96,128]{2,1,0:T(8,128)} %bitcast.94), calls=%async_computation.2 | async-start | bytes 1572864 | tf_op jit(solution)/shard_map/back_transposed/all_to_all | solution.py:14
  71.5 5.3 %direct.4 = (f32[4,96,128]{2,1,0:T(8,128)}, f32[4,96,128]{2,1,0:T(8,128)}) custom-call(s32[9]{0:T(128)} %get-tuple-element.86.where_ref, f32[8,2,96,1536]{3,2,1,0:T(8,128)} %bitcast.83, f32[1536,128]{1,0:T(8,128)} %bitcast.89), custom_call_target="tpu_custom_call" | custom-call | flops 905969664 | bytes 4718592 | tf_op jit(solution)/shard_map/direct/pallas_call | solution.py:106
  76.8 3.3 %collective-permute-start.6 = (f32[4,96,128]{2,1,0:T(8,128)}, f32[4,96,128]{2,1,0:T(8,128)S(1)}, u32[]{:S(2)}, u32[]{:S(2)}) collective-permute-start(f32[4,96,128]{2,1,0:T(8,128)} %get-tuple-element.48), channel_id=1, source_target_pairs={{0,1},{1,0},{2,3},{3,2},{4,5},{5,4},{6,7},{7,6},{8,9},{9,8},{10,11... | collective-permute-start | bytes 589832 | tf_op jit(solution)/shard_map/direct/ppermute | solution.py:178
  81.6 5.1 %direct.5 = (f32[4,96,128]{2,1,0:T(8,128)}, f32[4,96,128]{2,1,0:T(8,128)}) custom-call(s32[9]{0:T(128)} %get-tuple-element.85.where_ref, f32[8,2,96,1536]{3,2,1,0:T(8,128)} %bitcast.84, f32[1536,128]{1,0:T(8,128)} %bitcast.90), custom_call_target="tpu_custom_call" | custom-call | flops 905969664 | bytes 4718592 | tf_op jit(solution)/shard_map/direct/pallas_call | solution.py:106
  86.7 8.3 %collective-permute-done.6 = f32[4,96,128]{2,1,0:T(8,128)S(1)} collective-permute-done((f32[4,96,128]{2,1,0:T(8,128)}, f32[4,96,128]{2,1,0:T(8,128)S(1)}, u32[]{:S(2)}, u32[]{:S(2)}) %collective-permute-start.6) | collective-permute-done | bytes 196640 | tf_op jit(solution)/shard_map/direct/ppermute | solution.py:178
  95.0 2.3 collective-permute-done.7
  99.0 5.7 %all-to-all-start.3 = ((f32[16,96,128]{2,1,0:T(8,128)}), f32[16,96,128]{2,1,0:T(8,128)S(1)}, u32[]{:S(2)}, u32[]{:S(2)}) async-start(f32[16,96,128]{2,1,0:T(8,128)} %back_wide.2), calls=%async_computation.3 | async-start | bytes 1572864 | tf_op jit(solution)/shard_map/back_wide/all_to_all | solution.py:14
  105.0 6.9 %collective-permute-done.8 = f32[4,96,128]{2,1,0:T(8,128)S(1)} collective-permute-done((f32[4,96,128]{2,1,0:T(8,128)}, f32[4,96,128]{2,1,0:T(8,128)S(1)}, u32[]{:S(2)}, u32[]{:S(2)}) %collective-permute-start.8) | collective-permute-done | bytes 196640 | tf_op jit(solution)/shard_map/direct/ppermute | solution.py:178
  112.9 4.2 %collective-permute-start.9 = (f32[96,128]{1,0:T(8,128)S(1)}, f32[96,128]{1,0:T(8,128)S(1)}, u32[]{:S(2)}, u32[]{:S(2)}) collective-permute-start(f32[96,128]{1,0:T(8,128)S(1)} %get-tuple-element.80), channel_id=1, source_target_pairs={{0,8},{1,9},{2,10},{3,11},{4,12},{5,13},{6,14},{7,15},{8,0},{9,1},... | collective-permute-start | bytes 147464 | tf_op jit(solution)/shard_map/back_direct/ppermute | solution.py:178
  121.1 2.3 collective-permute-done.11
  124.6 5.7 %all-to-all-start.4 = ((f32[16,96,128]{2,1,0:T(8,128)}), f32[16,96,128]{2,1,0:T(8,128)S(1)}, u32[]{:S(2)}, u32[]{:S(2)}) async-start(f32[16,96,128]{2,1,0:T(8,128)} %broadcast_in_dim.22), calls=%async_computation.4 | async-start | bytes 1572864 | tf_op jit(solution)/shard_map/gather_wide/all_to_all | solution.py:14
  130.3 2.7 collective-permute-start.14
  133.0 1.8 collective-permute-start.13
  134.9 2.0 collective-permute-start.12
  138.0 4.9 %collective-permute-done.12 = f32[96,128]{1,0:T(8,128)S(1)} collective-permute-done((f32[96,128]{1,0:T(8,128)S(1)}, f32[96,128]{1,0:T(8,128)S(1)}, u32[]{:S(2)}, u32[]{:S(2)}) %collective-permute-start.12) | collective-permute-done | bytes 49184 | tf_op jit(solution)/shard_map/gather_row/ppermute | solution.py:178
  142.9 1.9 collective-permute-start.17
  148.0 4.8 %collective-permute-done.17.second_ref = f32[4,96,128]{2,1,0:T(8,128)S(1)} collective-permute-done((f32[4,96,128]{2,1,0:T(8,128)S(1)}, f32[4,96,128]{2,1,0:T(8,128)S(1)}, u32[]{:S(2)}, u32[]{:S(2)}) %collective-permute-start.17) | collective-permute-done | bytes 196640 | tf_op jit(solution)/shard_map/gather_row/ppermute | solution.py:178
  152.8 2.1 collective-permute-done.16.first_ref
  156.5 5.8 %all-to-all-start.5 = ((f32[16,96,128]{2,1,0:T(8,128)}), f32[16,96,128]{2,1,0:T(8,128)S(1)}, u32[]{:S(2)}, u32[]{:S(2)}) async-start(f32[16,96,128]{2,1,0:T(8,128)} %gather_column.3), calls=%async_computation.5 | async-start | bytes 1572864 | tf_op jit(solution)/shard_map/gather_column/all_to_all | solution.py:14
  162.3 5.7 %transposed.6.rest_0_ = f32[128,1536]{1,0:T(8,128)} custom-call(s32[9]{0:T(128)} %get-tuple-element.89.where_ref, f32[8,2,96,1536]{3,2,1,0:T(8,128)} %bitcast.85, f32[4,96,128]{2,1,0:T(8,128)} %copy-done.4, f32[4,96,128]{2,1,0:T(8,128)} %copy-done.10), custom_call_target="tpu_custom_call" | custom-call | flops 905969664 | bytes 4718592 | tf_op jit(solution)/shard_map/transposed/pallas_call | solution.py:154
  168.0 5.9 %transposed.7 = f32[1536,128]{1,0:T(8,128)} custom-call(s32[9]{0:T(128)} %get-tuple-element.90.where_ref, f32[8,2,96,1536]{3,2,1,0:T(8,128)} %bitcast.86, f32[4,96,128]{2,1,0:T(8,128)} %copy-done.8, f32[4,96,128]{2,1,0:T(8,128)} %copy-done.6, f32[128,1536]{1,0:T(8,128)} %transposed.6.rest_0_), custom_call_target="tpu_custom_call" | custom-call | flops 905969664 | bytes 4718592 | tf_op jit(solution)/shard_map/transposed/pallas_call | solution.py:154
  173.9 11.6 %all-to-all-done.5 = f32[16,96,128]{2,1,0:T(8,128)S(1)} async-done(((f32[16,96,128]{2,1,0:T(8,128)}), f32[16,96,128]{2,1,0:T(8,128)S(1)}, u32[]{:S(2)}, u32[]{:S(2)}) %all-to-all-start.5) | async-done | bytes 786464 | tf_op jit(solution)/shard_map/gather_column/all_to_all | solution.py:14
  185.5 3.6 %all-to-all-start.6 = ((f32[16,96,128]{2,1,0:T(8,128)}), f32[16,96,128]{2,1,0:T(8,128)S(1)}, u32[]{:S(2)}, u32[]{:S(2)}) async-start(f32[16,96,128]{2,1,0:T(8,128)} %bitcast.93), calls=%async_computation.6 | async-start | bytes 1572864 | tf_op jit(solution)/shard_map/back_transposed/all_to_all | solution.py:14
  189.1 5.3 %direct.6 = (f32[4,96,128]{2,1,0:T(8,128)}, f32[4,96,128]{2,1,0:T(8,128)}) custom-call(s32[9]{0:T(128)} %get-tuple-element.86.where_ref, f32[8,2,96,1536]{3,2,1,0:T(8,128)} %bitcast.87, f32[1536,128]{1,0:T(8,128)} %bitcast.91), custom_call_target="tpu_custom_call" | custom-call | flops 905969664 | bytes 4718592 | tf_op jit(solution)/shard_map/direct/pallas_call | solution.py:106
  194.4 3.3 %collective-permute-start.18 = (f32[4,96,128]{2,1,0:T(8,128)}, f32[4,96,128]{2,1,0:T(8,128)S(1)}, u32[]{:S(2)}, u32[]{:S(2)}) collective-permute-start(f32[4,96,128]{2,1,0:T(8,128)} %get-tuple-element.64), channel_id=1, source_target_pairs={{0,1},{1,0},{2,3},{3,2},{4,5},{5,4},{6,7},{7,6},{8,9},{9,8},{10,11... | collective-permute-start | bytes 589832 | tf_op jit(solution)/shard_map/direct/ppermute | solution.py:178
  199.2 5.1 %direct.7 = (f32[4,96,128]{2,1,0:T(8,128)}, f32[4,96,128]{2,1,0:T(8,128)}) custom-call(s32[9]{0:T(128)} %get-tuple-element.85.where_ref, f32[8,2,96,1536]{3,2,1,0:T(8,128)} %bitcast.88, f32[1536,128]{1,0:T(8,128)} %bitcast.92), custom_call_target="tpu_custom_call" | custom-call | flops 905969664 | bytes 4718592 | tf_op jit(solution)/shard_map/direct/pallas_call | solution.py:106
  206.3 6.4 %collective-permute-done.18 = f32[4,96,128]{2,1,0:T(8,128)S(1)} collective-permute-done((f32[4,96,128]{2,1,0:T(8,128)}, f32[4,96,128]{2,1,0:T(8,128)S(1)}, u32[]{:S(2)}, u32[]{:S(2)}) %collective-permute-start.18) | collective-permute-done | bytes 196640 | tf_op jit(solution)/shard_map/direct/ppermute | solution.py:178
  212.7 2.9 %collective-permute-done.19 = f32[4,96,128]{2,1,0:T(8,128)S(1)} collective-permute-done((f32[4,96,128]{2,1,0:T(8,128)}, f32[4,96,128]{2,1,0:T(8,128)S(1)}, u32[]{:S(2)}, u32[]{:S(2)}) %collective-permute-start.19) | collective-permute-done | bytes 196640 | tf_op jit(solution)/shard_map/direct/ppermute | solution.py:178
  215.5 1.8 back_wide.3
  217.3 5.7 %all-to-all-start.7 = ((f32[16,104,128]{2,1,0:T(8,128)}), f32[16,104,128]{2,1,0:T(8,128)S(1)}, u32[]{:S(2)}, u32[]{:S(2)}) async-start(f32[16,104,128]{2,1,0:T(8,128)} %back_wide.3), calls=%async_computation.7 | async-start | bytes 1703936 | tf_op jit(solution)/shard_map/back_wide/all_to_all | solution.py:14
  223.3 6.9 %collective-permute-done.20 = f32[4,96,128]{2,1,0:T(8,128)S(1)} collective-permute-done((f32[4,96,128]{2,1,0:T(8,128)}, f32[4,96,128]{2,1,0:T(8,128)S(1)}, u32[]{:S(2)}, u32[]{:S(2)}) %collective-permute-start.20) | collective-permute-done | bytes 196640 | tf_op jit(solution)/shard_map/direct/ppermute | solution.py:178
  231.2 3.7 %collective-permute-start.21 = (f32[96,128]{1,0:T(8,128)S(1)}, f32[96,128]{1,0:T(8,128)S(1)}, u32[]{:S(2)}, u32[]{:S(2)}) collective-permute-start(f32[96,128]{1,0:T(8,128)S(1)} %get-tuple-element.77), channel_id=1, source_target_pairs={{0,8},{1,9},{2,10},{3,11},{4,12},{5,13},{6,14},{7,15},{8,0},{9,1},... | collective-permute-start | bytes 147464 | tf_op jit(solution)/shard_map/back_direct/ppermute | solution.py:178
  234.9 2.1 collective-permute-start.23
  242.3 10.7 %all_to_all.55 = f32[16,16,128]{2,1,0:T(8,128)S(1)} all-to-all(f32[16,16,128]{2,1,0:T(8,128)S(1)} %pad_maximum_fusion.2), channel_id=1, replica_groups=mesh['wide'=16,'narrow'=16] {'wide'}, dimensions={0} | all-to-all | bytes 262144 | tf_op jit(solution)/shard_map/gram_sum_wide/all_to_all | solution.py:14
  253.7 16.4 %all_to_all.56 = f32[16,8,128]{2,1,0:T(8,128)S(1)} all-to-all(f32[16,8,128]{2,1,0:T(8,128)S(1)} %broadcast_in_dim.25), channel_id=1, replica_groups=mesh['wide'=16,'narrow'=16] {'narrow'}, dimensions={0} | all-to-all | bytes 131072 | tf_op jit(solution)/shard_map/gram_sum_narrow/all_to_all | solution.py:14
  270.8 5.2 %all-to-all-start.10 = ((f32[16,8,128]{2,1,0:T(8,128)}), f32[16,8,128]{2,1,0:T(8,128)S(1)}, u32[]{:S(2)}, u32[]{:S(2)}) async-start(f32[16,8,128]{2,1,0:T(8,128)} %broadcast_in_dim.26), calls=%async_computation.10 | async-start | bytes 131072 | tf_op jit(solution)/shard_map/gram_whole/all_to_all | solution.py:14
  276.0 3.8 %inverse_first.1.refs_1_ = f32[128,128]{1,0:T(8,128)} custom-call(f32[128,128]{1,0:T(8,128)} %get-tuple-element.83.refs_0_), custom_call_target="tpu_custom_call" | custom-call | flops 1073741824 | bytes 1048576 | tf_op jit(solution)/shard_map/inverse_first/pallas_call | solution.py:259
  281.5 4.5 %finish.1 = f32[96,128]{1,0:T(8,128)} custom-call(f32[128,128]{1,0:T(8,128)} %bitcast.97, f32[128,128]{1,0:T(8,128)} %inverse_first.1.refs_1_, f32[96,128]{1,0:T(8,128)} %copy-done.13), custom_call_target="tpu_custom_call" | custom-call | flops 1073741824 | bytes 1048576 | tf_op jit(solution)/shard_map/finish/pallas_call | solution.py:259
  (97 shorter events, 39.9 us)
Async XLA Ops:
  1.7 32.9 %all-to-all-start = ((f32[16,96,128]{2,1,0:T(8,128)}), f32[16,96,128]{2,1,0:T(8,128)S(1)}, u32[]{:S(2)}, u32[]{:S(2)}) async-start(f32[16,96,128]{2,1,0:T(8,128)} %broadcast_in_dim.19), calls=%async_computation | async-start | bytes 1572864 | tf_op jit(solution)/shard_map/gather_wide/all_to_all | solution.py:14
  7.5 10.0 %collective-permute-start = (f32[96,128]{1,0:T(8,128)}, f32[96,128]{1,0:T(8,128)S(1)}, u32[]{:S(2)}, u32[]{:S(2)}) collective-permute-start(f32[96,128]{1,0:T(8,128)} %param.7), channel_id=1, source_target_pairs={{0,8},{1,9},{2,10},{3,11},{4,12},{5,13},{6,14},{7,15},{8,0},{9,1},... | collective-permute-start | bytes 147464 | tf_op jit(solution)/shard_map/gather_row/ppermute | solution.py:178
  14.7 6.4 %collective-permute-start.2 = (f32[96,128]{1,0:T(8,128)}, f32[96,128]{1,0:T(8,128)S(1)}, u32[]{:S(2)}, u32[]{:S(2)}) collective-permute-start(f32[96,128]{1,0:T(8,128)} %param.7), channel_id=1, source_target_pairs={{0,12},{1,13},{2,14},{3,15},{4,8},{5,9},{6,10},{7,11},{8,4},{9,5},... | collective-permute-start | bytes 147464 | tf_op jit(solution)/shard_map/gather_row/ppermute | solution.py:178
  14.7 6.4 %collective-permute-start.1 = (f32[96,128]{1,0:T(8,128)}, f32[96,128]{1,0:T(8,128)S(1)}, u32[]{:S(2)}, u32[]{:S(2)}) collective-permute-start(f32[96,128]{1,0:T(8,128)} %param.7), channel_id=1, source_target_pairs={{0,4},{1,5},{2,6},{3,7},{4,0},{5,1},{6,2},{7,3},{8,12},{9,13},{10,... | collective-permute-start | bytes 147464 | tf_op jit(solution)/shard_map/gather_row/ppermute | solution.py:178
  21.9 23.2 %copy-start.12 = (f32[4,96,128]{2,1,0:T(8,128)}, f32[4,96,128]{2,1,0:T(8,128)S(1)}, u32[]{:S(2)}) copy-start(f32[4,96,128]{2,1,0:T(8,128)S(1)} %pad_maximum_fusion.first_ref) | copy-start | bytes 589828
  22.0 10.1 %collective-permute-start.5 = (f32[4,96,128]{2,1,0:T(8,128)S(1)}, f32[4,96,128]{2,1,0:T(8,128)S(1)}, u32[]{:S(2)}, u32[]{:S(2)}) collective-permute-start(f32[4,96,128]{2,1,0:T(8,128)S(1)} %pad_maximum_fusion.first_ref), channel_id=1, source_target_pairs={{0,3},{1,2},{2,1},{3,0},{4,7},{5,6},{6,5},{7,4},{8,11},{9,10},{10,... | collective-permute-start | bytes 589832 | tf_op jit(solution)/shard_map/gather_row/ppermute | solution.py:178
  25.3 9.3 %collective-permute-start.4 = (f32[4,96,128]{2,1,0:T(8,128)S(1)}, f32[4,96,128]{2,1,0:T(8,128)S(1)}, u32[]{:S(2)}, u32[]{:S(2)}) collective-permute-start(f32[4,96,128]{2,1,0:T(8,128)S(1)} %pad_maximum_fusion.first_ref), channel_id=1, source_target_pairs={{0,1},{1,0},{2,3},{3,2},{4,5},{5,4},{6,7},{7,6},{8,9},{9,8},{10,11... | collective-permute-start | bytes 589832 | tf_op jit(solution)/shard_map/gather_row/ppermute | solution.py:178
  26.6 8.1 %collective-permute-start.3 = (f32[4,96,128]{2,1,0:T(8,128)S(1)}, f32[4,96,128]{2,1,0:T(8,128)S(1)}, u32[]{:S(2)}, u32[]{:S(2)}) collective-permute-start(f32[4,96,128]{2,1,0:T(8,128)S(1)} %pad_maximum_fusion.first_ref), channel_id=1, source_target_pairs={{0,2},{1,3},{2,0},{3,1},{4,6},{5,7},{6,4},{7,5},{8,10},{9,11},{10,... | collective-permute-start | bytes 589832 | tf_op jit(solution)/shard_map/gather_row/ppermute | solution.py:178
  32.1 18.7 %copy-start.14 = (f32[4,96,128]{2,1,0:T(8,128)}, f32[4,96,128]{2,1,0:T(8,128)S(1)}, u32[]{:S(2)}) copy-start(f32[4,96,128]{2,1,0:T(8,128)S(1)} %collective-permute-done.5.second_ref) | copy-start | bytes 589828
  34.6 16.2 %copy-start.15 = (f32[4,96,128]{2,1,0:T(8,128)}, f32[4,96,128]{2,1,0:T(8,128)S(1)}, u32[]{:S(2)}) copy-start(f32[4,96,128]{2,1,0:T(8,128)S(1)} %collective-permute-done.4.first_ref) | copy-start | bytes 589828
  34.6 10.5 %copy-start.16 = (f32[4,96,128]{2,1,0:T(8,128)}, f32[4,96,128]{2,1,0:T(8,128)S(1)}, u32[]{:S(2)}) copy-start(f32[4,96,128]{2,1,0:T(8,128)S(1)} %collective-permute-done.3.second_ref) | copy-start | bytes 589828
  36.9 30.4 %all-to-all-start.1 = ((f32[16,96,128]{2,1,0:T(8,128)}), f32[16,96,128]{2,1,0:T(8,128)S(1)}, u32[]{:S(2)}, u32[]{:S(2)}) async-start(f32[16,96,128]{2,1,0:T(8,128)} %gather_column.2), calls=%async_computation.1 | async-start | bytes 1572864 | tf_op jit(solution)/shard_map/gather_column/all_to_all | solution.py:14
  67.3 4.2 %copy-start.2 = (f32[16,96,128]{2,1,0:T(8,128)}, f32[16,96,128]{2,1,0:T(8,128)S(1)}, u32[]{:S(2)}) copy-start(f32[16,96,128]{2,1,0:T(8,128)S(1)} %all-to-all-done.1) | copy-start | bytes 2359300
  67.3 30.0 %all-to-all-start.2 = ((f32[16,96,128]{2,1,0:T(8,128)}), f32[16,96,128]{2,1,0:T(8,128)S(1)}, u32[]{:S(2)}, u32[]{:S(2)}) async-start(f32[16,96,128]{2,1,0:T(8,128)} %bitcast.94), calls=%async_computation.2 | async-start | bytes 1572864 | tf_op jit(solution)/shard_map/back_transposed/all_to_all | solution.py:14
  71.5 25.8 %copy-start.1 = (s32[1,16]{1,0:T(1,128)S(1)}, s32[1,16]{1,0:T(1,128)}, u32[]{:S(2)}) copy-start(s32[1,16]{1,0:T(1,128)} %param.6) | copy-start | bytes 196
  76.8 18.2 %collective-permute-start.6 = (f32[4,96,128]{2,1,0:T(8,128)}, f32[4,96,128]{2,1,0:T(8,128)S(1)}, u32[]{:S(2)}, u32[]{:S(2)}) collective-permute-start(f32[4,96,128]{2,1,0:T(8,128)} %get-tuple-element.48), channel_id=1, source_target_pairs={{0,1},{1,0},{2,3},{3,2},{4,5},{5,4},{6,7},{7,6},{8,9},{9,8},{10,11... | collective-permute-start | bytes 589832 | tf_op jit(solution)/shard_map/direct/ppermute | solution.py:178
  80.1 17.2 %collective-permute-start.7 = (f32[4,96,128]{2,1,0:T(8,128)}, f32[4,96,128]{2,1,0:T(8,128)S(1)}, u32[]{:S(2)}, u32[]{:S(2)}) collective-permute-start(f32[4,96,128]{2,1,0:T(8,128)} %get-tuple-element.49), channel_id=1, source_target_pairs={{0,3},{1,2},{2,1},{3,0},{4,7},{5,6},{6,5},{7,4},{8,11},{9,10},{10,... | collective-permute-start | bytes 589832 | tf_op jit(solution)/shard_map/direct/ppermute | solution.py:178
  99.0 20.5 %all-to-all-start.3 = ((f32[16,96,128]{2,1,0:T(8,128)}), f32[16,96,128]{2,1,0:T(8,128)S(1)}, u32[]{:S(2)}, u32[]{:S(2)}) async-start(f32[16,96,128]{2,1,0:T(8,128)} %back_wide.2), calls=%async_computation.3 | async-start | bytes 1572864 | tf_op jit(solution)/shard_map/back_wide/all_to_all | solution.py:14
  104.7 7.2 %collective-permute-start.8 = (f32[4,96,128]{2,1,0:T(8,128)}, f32[4,96,128]{2,1,0:T(8,128)S(1)}, u32[]{:S(2)}, u32[]{:S(2)}) collective-permute-start(f32[4,96,128]{2,1,0:T(8,128)} %get-tuple-element.55), channel_id=1, source_target_pairs={{0,2},{1,3},{2,0},{3,1},{4,6},{5,7},{6,4},{7,5},{8,10},{9,11},{10,... | collective-permute-start | bytes 589832 | tf_op jit(solution)/shard_map/direct/ppermute | solution.py:178
  112.9 8.3 %collective-permute-start.9 = (f32[96,128]{1,0:T(8,128)S(1)}, f32[96,128]{1,0:T(8,128)S(1)}, u32[]{:S(2)}, u32[]{:S(2)}) collective-permute-start(f32[96,128]{1,0:T(8,128)S(1)} %get-tuple-element.80), channel_id=1, source_target_pairs={{0,8},{1,9},{2,10},{3,11},{4,12},{5,13},{6,14},{7,15},{8,0},{9,1},... | collective-permute-start | bytes 147464 | tf_op jit(solution)/shard_map/back_direct/ppermute | solution.py:178
  117.1 6.4 %collective-permute-start.11 = (f32[96,128]{1,0:T(8,128)S(1)}, f32[96,128]{1,0:T(8,128)S(1)}, u32[]{:S(2)}, u32[]{:S(2)}) collective-permute-start(f32[96,128]{1,0:T(8,128)S(1)} %get-tuple-element.81), channel_id=1, source_target_pairs={{0,12},{1,13},{2,14},{3,15},{4,8},{5,9},{6,10},{7,11},{8,4},{9,5},... | collective-permute-start | bytes 147464 | tf_op jit(solution)/shard_map/back_direct/ppermute | solution.py:178
  118.6 5.0 %collective-permute-start.10 = (f32[96,128]{1,0:T(8,128)S(1)}, f32[96,128]{1,0:T(8,128)S(1)}, u32[]{:S(2)}, u32[]{:S(2)}) collective-permute-start(f32[96,128]{1,0:T(8,128)S(1)} %get-tuple-element.82), channel_id=1, source_target_pairs={{0,4},{1,5},{2,6},{3,7},{4,0},{5,1},{6,2},{7,3},{8,12},{9,13},{10,... | collective-permute-start | bytes 147464 | tf_op jit(solution)/shard_map/back_direct/ppermute | solution.py:178
  124.6 30.3 %all-to-all-start.4 = ((f32[16,96,128]{2,1,0:T(8,128)}), f32[16,96,128]{2,1,0:T(8,128)S(1)}, u32[]{:S(2)}, u32[]{:S(2)}) async-start(f32[16,96,128]{2,1,0:T(8,128)} %broadcast_in_dim.22), calls=%async_computation.4 | async-start | bytes 1572864 | tf_op jit(solution)/shard_map/gather_wide/all_to_all | solution.py:14
  130.3 6.5 %collective-permute-start.14 = (f32[96,128]{1,0:T(8,128)S(1)}, f32[96,128]{1,0:T(8,128)S(1)}, u32[]{:S(2)}, u32[]{:S(2)}) collective-permute-start(f32[96,128]{1,0:T(8,128)S(1)} %fusion.9), channel_id=1, source_target_pairs={{0,12},{1,13},{2,14},{3,15},{4,8},{5,9},{6,10},{7,11},{8,4},{9,5},... | collective-permute-start | bytes 147464 | tf_op jit(solution)/shard_map/gather_row/ppermute | solution.py:178
  133.0 5.0 %collective-permute-start.13 = (f32[96,128]{1,0:T(8,128)S(1)}, f32[96,128]{1,0:T(8,128)S(1)}, u32[]{:S(2)}, u32[]{:S(2)}) collective-permute-start(f32[96,128]{1,0:T(8,128)S(1)} %fusion.9), channel_id=1, source_target_pairs={{0,4},{1,5},{2,6},{3,7},{4,0},{5,1},{6,2},{7,3},{8,12},{9,13},{10,... | collective-permute-start | bytes 147464 | tf_op jit(solution)/shard_map/gather_row/ppermute | solution.py:178
  134.9 8.0 %collective-permute-start.12 = (f32[96,128]{1,0:T(8,128)S(1)}, f32[96,128]{1,0:T(8,128)S(1)}, u32[]{:S(2)}, u32[]{:S(2)}) collective-permute-start(f32[96,128]{1,0:T(8,128)S(1)} %fusion.9), channel_id=1, source_target_pairs={{0,8},{1,9},{2,10},{3,11},{4,12},{5,13},{6,14},{7,15},{8,0},{9,1},... | collective-permute-start | bytes 147464 | tf_op jit(solution)/shard_map/gather_row/ppermute | solution.py:178
  142.9 19.4 %copy-start.4 = (f32[4,96,128]{2,1,0:T(8,128)}, f32[4,96,128]{2,1,0:T(8,128)S(1)}, u32[]{:S(2)}) copy-start(f32[4,96,128]{2,1,0:T(8,128)S(1)} %pad_maximum_fusion.1.first_ref) | copy-start | bytes 589828
  142.9 9.9 %collective-permute-start.17 = (f32[4,96,128]{2,1,0:T(8,128)S(1)}, f32[4,96,128]{2,1,0:T(8,128)S(1)}, u32[]{:S(2)}, u32[]{:S(2)}) collective-permute-start(f32[4,96,128]{2,1,0:T(8,128)S(1)} %pad_maximum_fusion.1.first_ref), channel_id=1, source_target_pairs={{0,3},{1,2},{2,1},{3,0},{4,7},{5,6},{6,5},{7,4},{8,11},{9,10},{10,... | collective-permute-start | bytes 589832 | tf_op jit(solution)/shard_map/gather_row/ppermute | solution.py:178
  144.8 10.1 %collective-permute-start.16 = (f32[4,96,128]{2,1,0:T(8,128)S(1)}, f32[4,96,128]{2,1,0:T(8,128)S(1)}, u32[]{:S(2)}, u32[]{:S(2)}) collective-permute-start(f32[4,96,128]{2,1,0:T(8,128)S(1)} %pad_maximum_fusion.1.first_ref), channel_id=1, source_target_pairs={{0,1},{1,0},{2,3},{3,2},{4,5},{5,4},{6,7},{7,6},{8,9},{9,8},{10,11... | collective-permute-start | bytes 589832 | tf_op jit(solution)/shard_map/gather_row/ppermute | solution.py:178
  146.4 8.5 %collective-permute-start.15 = (f32[4,96,128]{2,1,0:T(8,128)S(1)}, f32[4,96,128]{2,1,0:T(8,128)S(1)}, u32[]{:S(2)}, u32[]{:S(2)}) collective-permute-start(f32[4,96,128]{2,1,0:T(8,128)S(1)} %pad_maximum_fusion.1.first_ref), channel_id=1, source_target_pairs={{0,2},{1,3},{2,0},{3,1},{4,6},{5,7},{6,4},{7,5},{8,10},{9,11},{10,... | collective-permute-start | bytes 589832 | tf_op jit(solution)/shard_map/gather_row/ppermute | solution.py:178
  152.8 15.1 %copy-start.6 = (f32[4,96,128]{2,1,0:T(8,128)}, f32[4,96,128]{2,1,0:T(8,128)S(1)}, u32[]{:S(2)}) copy-start(f32[4,96,128]{2,1,0:T(8,128)S(1)} %collective-permute-done.17.second_ref) | copy-start | bytes 589828
  154.9 13.1 %copy-start.8 = (f32[4,96,128]{2,1,0:T(8,128)}, f32[4,96,128]{2,1,0:T(8,128)S(1)}, u32[]{:S(2)}) copy-start(f32[4,96,128]{2,1,0:T(8,128)S(1)} %collective-permute-done.16.first_ref) | copy-start | bytes 589828
  154.9 7.4 %copy-start.10 = (f32[4,96,128]{2,1,0:T(8,128)}, f32[4,96,128]{2,1,0:T(8,128)S(1)}, u32[]{:S(2)}) copy-start(f32[4,96,128]{2,1,0:T(8,128)S(1)} %collective-permute-done.15.second_ref) | copy-start | bytes 589828
  156.5 29.0 %all-to-all-start.5 = ((f32[16,96,128]{2,1,0:T(8,128)}), f32[16,96,128]{2,1,0:T(8,128)S(1)}, u32[]{:S(2)}, u32[]{:S(2)}) async-start(f32[16,96,128]{2,1,0:T(8,128)} %gather_column.3), calls=%async_computation.5 | async-start | bytes 1572864 | tf_op jit(solution)/shard_map/gather_column/all_to_all | solution.py:14
  185.5 30.1 %all-to-all-start.6 = ((f32[16,96,128]{2,1,0:T(8,128)}), f32[16,96,128]{2,1,0:T(8,128)S(1)}, u32[]{:S(2)}, u32[]{:S(2)}) async-start(f32[16,96,128]{2,1,0:T(8,128)} %bitcast.93), calls=%async_computation.6 | async-start | bytes 1572864 | tf_op jit(solution)/shard_map/back_transposed/all_to_all | solution.py:14
  189.1 15.2 %copy-start.11 = (f32[4,96,128]{2,1,0:T(8,128)S(1)}, f32[4,96,128]{2,1,0:T(8,128)}, u32[]{:S(2)}) copy-start(f32[4,96,128]{2,1,0:T(8,128)} %copy-done.10) | copy-start | bytes 589828
  189.1 15.7 %copy-start.9 = (f32[4,96,128]{2,1,0:T(8,128)S(1)}, f32[4,96,128]{2,1,0:T(8,128)}, u32[]{:S(2)}) copy-start(f32[4,96,128]{2,1,0:T(8,128)} %copy-done.8) | copy-start | bytes 589828
  189.1 16.2 %copy-start.7 = (f32[4,96,128]{2,1,0:T(8,128)S(1)}, f32[4,96,128]{2,1,0:T(8,128)}, u32[]{:S(2)}) copy-start(f32[4,96,128]{2,1,0:T(8,128)} %copy-done.6) | copy-start | bytes 589828
  189.1 16.7 %copy-start.5 = (f32[4,96,128]{2,1,0:T(8,128)S(1)}, f32[4,96,128]{2,1,0:T(8,128)}, u32[]{:S(2)}) copy-start(f32[4,96,128]{2,1,0:T(8,128)} %copy-done.4) | copy-start | bytes 589828
  194.4 18.3 %collective-permute-start.18 = (f32[4,96,128]{2,1,0:T(8,128)}, f32[4,96,128]{2,1,0:T(8,128)S(1)}, u32[]{:S(2)}, u32[]{:S(2)}) collective-permute-start(f32[4,96,128]{2,1,0:T(8,128)} %get-tuple-element.64), channel_id=1, source_target_pairs={{0,1},{1,0},{2,3},{3,2},{4,5},{5,4},{6,7},{7,6},{8,9},{9,8},{10,11... | collective-permute-start | bytes 589832 | tf_op jit(solution)/shard_map/direct/ppermute | solution.py:178
  197.7 17.8 %collective-permute-start.19 = (f32[4,96,128]{2,1,0:T(8,128)}, f32[4,96,128]{2,1,0:T(8,128)S(1)}, u32[]{:S(2)}, u32[]{:S(2)}) collective-permute-start(f32[4,96,128]{2,1,0:T(8,128)} %get-tuple-element.65), channel_id=1, source_target_pairs={{0,3},{1,2},{2,1},{3,0},{4,7},{5,6},{6,5},{7,4},{8,11},{9,10},{10,... | collective-permute-start | bytes 589832 | tf_op jit(solution)/shard_map/direct/ppermute | solution.py:178
  217.3 20.5 %all-to-all-start.7 = ((f32[16,104,128]{2,1,0:T(8,128)}), f32[16,104,128]{2,1,0:T(8,128)S(1)}, u32[]{:S(2)}, u32[]{:S(2)}) async-start(f32[16,104,128]{2,1,0:T(8,128)} %back_wide.3), calls=%async_computation.7 | async-start | bytes 1703936 | tf_op jit(solution)/shard_map/back_wide/all_to_all | solution.py:14
  223.1 7.2 %collective-permute-start.20 = (f32[4,96,128]{2,1,0:T(8,128)}, f32[4,96,128]{2,1,0:T(8,128)S(1)}, u32[]{:S(2)}, u32[]{:S(2)}) collective-permute-start(f32[4,96,128]{2,1,0:T(8,128)} %get-tuple-element.71), channel_id=1, source_target_pairs={{0,2},{1,3},{2,0},{3,1},{4,6},{5,7},{6,4},{7,5},{8,10},{9,11},{10,... | collective-permute-start | bytes 589832 | tf_op jit(solution)/shard_map/direct/ppermute | solution.py:178
  231.2 8.3 %collective-permute-start.21 = (f32[96,128]{1,0:T(8,128)S(1)}, f32[96,128]{1,0:T(8,128)S(1)}, u32[]{:S(2)}, u32[]{:S(2)}) collective-permute-start(f32[96,128]{1,0:T(8,128)S(1)} %get-tuple-element.77), channel_id=1, source_target_pairs={{0,8},{1,9},{2,10},{3,11},{4,12},{5,13},{6,14},{7,15},{8,0},{9,1},... | collective-permute-start | bytes 147464 | tf_op jit(solution)/shard_map/back_direct/ppermute | solution.py:178
  234.9 6.3 %collective-permute-start.23 = (f32[96,128]{1,0:T(8,128)S(1)}, f32[96,128]{1,0:T(8,128)S(1)}, u32[]{:S(2)}, u32[]{:S(2)}) collective-permute-start(f32[96,128]{1,0:T(8,128)S(1)} %get-tuple-element.78), channel_id=1, source_target_pairs={{0,12},{1,13},{2,14},{3,15},{4,8},{5,9},{6,10},{7,11},{8,4},{9,5},... | collective-permute-start | bytes 147464 | tf_op jit(solution)/shard_map/back_direct/ppermute | solution.py:178
  237.0 5.0 %collective-permute-start.22 = (f32[96,128]{1,0:T(8,128)S(1)}, f32[96,128]{1,0:T(8,128)S(1)}, u32[]{:S(2)}, u32[]{:S(2)}) collective-permute-start(f32[96,128]{1,0:T(8,128)S(1)} %get-tuple-element.79), channel_id=1, source_target_pairs={{0,4},{1,5},{2,6},{3,7},{4,0},{5,1},{6,2},{7,3},{8,12},{9,13},{10,... | collective-permute-start | bytes 147464 | tf_op jit(solution)/shard_map/back_direct/ppermute | solution.py:178
  242.0 38.9 %copy-start.13 = (f32[96,128]{1,0:T(8,128)}, f32[96,128]{1,0:T(8,128)S(1)}, u32[]{:S(2)}) copy-start(f32[96,128]{1,0:T(8,128)S(1)} %slice_add_fusion.refs_2_) | copy-start | bytes 147460
  270.8 10.1 %all-to-all-start.10 = ((f32[16,8,128]{2,1,0:T(8,128)}), f32[16,8,128]{2,1,0:T(8,128)S(1)}, u32[]{:S(2)}, u32[]{:S(2)}) async-start(f32[16,8,128]{2,1,0:T(8,128)} %broadcast_in_dim.26), calls=%async_computation.10 | async-start | bytes 131072 | tf_op jit(solution)/shard_map/gram_whole/all_to_all | solution.py:14
  (3 other events, 5.0 us)

commit v3 on v1

--- a/solution.py
+++ b/solution.py
@@ -72,13 +72,31 @@
     return pl.CostEstimate(flops=3 * tile.size * width, bytes_accessed=2 * tile.size, transcendentals=0)
 
 
+def split_tile(tile):
+    block = pl.BlockSpec((1, *tile.shape[1:]), lambda g: (g, 0, 0, 0))
+
+    def kernel(tile_ref, high_ref, low_ref):
+        high_ref[...], low_ref[...] = high_low(tile_ref[...])
+
+    out = jax.ShapeDtypeStruct(tile.shape, jnp.bfloat16)
+    return pl.pallas_call(
+        kernel,
+        out_shape=(out, out),
+        grid=(tile.shape[0],),
+        in_specs=[block],
+        out_specs=[block, block],
+        compiler_params=pltpu.CompilerParams(vmem_limit_bytes=60 << 20),
+        cost_estimate=pl.CostEstimate(flops=tile.size, bytes_accessed=8 * tile.size, transcendentals=0),
+    )(tile)
+
+
 def direct_half(tile, column_block, half, places):
-    groups, _, rows, order = tile.shape
+    groups, _, rows, order = tile[0].shape
     width = column_block.shape[1]
     steps = 2
     each = groups // steps
 
-    def kernel(where_ref, tile_ref, column_ref, out_ref, both):
+    def kernel(where_ref, high_ref, low_ref, column_ref, out_ref, both):
         step = pl.program_id(0)
 
         @pl.when(step == 0)
@@ -87,7 +105,7 @@
             both[:, :width] = high
             both[:, width:] = low
 
-        high, low = high_low(tile_ref[...].reshape(each * rows, order))
+        high, low = (ref[...].reshape(each * rows, order) for ref in (high_ref, low_ref))
         wide = product_of(high, both[...])
         total = wide[:, :width] + wide[:, width:] + product_of(low, both[:, :width])
         for k in range(each):
@@ -99,26 +117,26 @@
         grid_spec=pltpu.PrefetchScalarGridSpec(
             num_scalar_prefetch=1,
             grid=(steps,),
-            in_specs=[
-                pl.BlockSpec((each, 1, rows, order), lambda g, where: (g, where[0], 0, 0)),
+            in_specs=[pl.BlockSpec((each, 1, rows, order), lambda g, where: (g, where[0], 0, 0))] * 2
+            + [
                 pl.BlockSpec((order, width), lambda g, where: (0, 0)),
             ],
             out_specs=pl.BlockSpec((groups, rows, width), lambda g, where: (0, 0, 0)),
             scratch_shapes=[pltpu.VMEM((order, 2 * width), jnp.bfloat16)],
         ),
         compiler_params=pltpu.CompilerParams(vmem_limit_bytes=60 << 20),
-        cost_estimate=kernel_cost(tile, width),
-    )(jnp.concatenate([half[None], places]), tile, column_block)
+        cost_estimate=kernel_cost(tile[0], width),
+    )(jnp.concatenate([half[None], places]), *tile, column_block)
 
 
 def transposed_half(tile, row_half, half, places, partial=None):
-    groups, _, rows, order = tile.shape
+    groups, _, rows, order = tile[0].shape
     width = row_half.shape[2]
     depth = groups * rows
     steps = 3
     chunk = order // steps
 
-    def kernel(where_ref, tile_ref, row_ref, *rest):
+    def kernel(where_ref, high_ref, low_ref, row_ref, *rest):
         partial_ref, (out_ref, gathered, both) = (rest[0], rest[1:]) if partial is not None else (None, rest)
 
         @pl.when(pl.program_id(0) == 0)
@@ -129,7 +147,7 @@
             both[:width] = high
             both[width:] = low
 
-        high, low = high_low(tile_ref[...].reshape(depth, chunk))
+        high, low = (ref[...].reshape(depth, chunk) for ref in (high_ref, low_ref))
         wide = product_of(both[...], high)
         total = wide[:width] + wide[width:] + product_of(both[:width], low)
         if partial_ref is None:
@@ -144,8 +162,8 @@
         grid_spec=pltpu.PrefetchScalarGridSpec(
             num_scalar_prefetch=1,
             grid=(steps,),
-            in_specs=[
-                pl.BlockSpec((groups, 1, rows, chunk), lambda g, where: (0, where[0], 0, g)),
+            in_specs=[pl.BlockSpec((groups, 1, rows, chunk), lambda g, where: (0, where[0], 0, g))] * 2
+            + [
                 pl.BlockSpec((groups, rows, width), lambda g, where: (0, 0, 0)),
             ]
             + ([] if partial is None else [flat]),
@@ -156,20 +174,13 @@
             ],
         ),
         compiler_params=pltpu.CompilerParams(vmem_limit_bytes=60 << 20),
-        cost_estimate=kernel_cost(tile, width),
-    )(jnp.concatenate([half[None], places]), tile, row_half, *([] if partial is None else [partial]))
-
-
-def swap(value, axis, bit):
-    size = lax.axis_size(axis)
-    return lax.ppermute(value, axis, [(i, i ^ bit) for i in range(size)])
-
-
-def bits_of(size):
-    bit = size // 2
-    while bit:
-        yield bit
-        bit //= 2
+        cost_estimate=kernel_cost(tile[0], width),
+    )(jnp.concatenate([half[None], places]), *tile, row_half, *([] if partial is None else [partial]))
+
+
+def swap(value, mask):
+    size = lax.axis_size(NARROW)
+    return lax.ppermute(value, NARROW, [(i, i ^ mask) for i in range(size)])
 
 
 def relative_places(mine, groups):
@@ -178,60 +189,71 @@
     return sum(((offset >> k) & 1) << (count - 1 - k) for k in range(count))
 
 
-def doubled(held, axis, bits):
-    for bit in bits:
-        held = jnp.concatenate([held, swap(held, axis, bit)], axis=0)
-    return held
-
-
-def halved(mine, got, axis):
-    for bit in reversed(list(bits_of(lax.axis_size(axis)))):
-        if bit > 1:
-            half = mine.shape[0] // 2
-            sent = mine[half:] + got[half:]
-            mine, got = mine[:half] + got[:half], swap(sent, axis, bit)
-    return mine[0] + got[0]
+ENTRIES = (8, 4, 12)
+
+
+def gathered_half(value):
+    quarter = jnp.stack([value] + [swap(value, mask) for mask in ENTRIES])
+    return jnp.concatenate([quarter, swap(quarter, 2)], axis=0)
+
+
+def kept_half(kept, got):
+    half = kept.shape[0] // 2
+    sent = kept[half:] + got[half:]
+    return kept[:half] + got[:half] + swap(sent, 2)
+
+
+def summed_part(kept):
+    total = kept[0]
+    for k, mask in enumerate(ENTRIES):
+        total = total + swap(kept[k + 1], mask)
+    return total
 
 
 def apply_hamiltonian(tile, columns, vectors, want_gram):
     rows, width = vectors.shape
     count = lax.axis_size(NARROW)
-    order = tile.shape[0]
+    order = count * rows
     groups = count // 2
     me = lax.axis_index(NARROW).astype(jnp.int32)
     near, far = me & 1, (me & 1) ^ 1
     places = relative_places(me >> 1, groups)
-    tile = tile.reshape(groups, 2, rows, order)
     with jax.named_scope("gather_wide"):
         slices = to_everyone(vectors, WIDE)
-    bits = list(bits_of(groups))
     with jax.named_scope("gather_row"):
-        near_rows = doubled(vectors[None], NARROW, [2 * bit for bit in bits])
+        near_rows = gathered_half(vectors)
         slices, near_rows = lax.optimization_barrier((slices, near_rows))
-        far_rows = swap(near_rows, NARROW, 1)
+        far_rows = swap(near_rows, 1)
     with jax.named_scope("gather_column"):
         picked = move_blocks(slices, columns, scatter=False)
         column_block = exchange(picked, NARROW).reshape(order, width)
+    if not isinstance(tile, (list, tuple)):
+        with jax.named_scope("split_tile"):
+            tile, near_rows = lax.optimization_barrier((tile, near_rows))
+            tile = split_tile(tile.reshape(groups, 2, rows, order))
     with jax.named_scope("transposed"):
         partial = transposed_half(tile, near_rows, near, places)
         transposed = transposed_half(tile, far_rows, far, places, partial)
+        transposed, column_block = lax.optimization_barrier((transposed, column_block))
     with jax.named_scope("back_transposed"):
         arrived = exchange(transposed.reshape(count, rows, width), NARROW)
     with jax.named_scope("direct"):
         sent = direct_half(tile, column_block, far, places)
-        got = swap(sent, NARROW, 1)
+        got = swap(sent, 1)
         kept = direct_half(tile, column_block, near, places)
+        kept = kept_half(kept, got)
+        arrived, kept = lax.optimization_barrier((arrived, kept))
     gram = None
     if want_gram:
         with jax.named_scope("gram_block_row"):
-            near_rows, far_rows, kept = lax.optimization_barrier((near_rows, far_rows, kept))
+            near_rows, far_rows, _ = lax.optimization_barrier((near_rows, far_rows, sent))
             gram = gram_of(near_rows.reshape(-1, width)) + gram_of(far_rows.reshape(-1, width))
     with jax.named_scope("back_direct"):
-        direct_sum = halved(kept, got, NARROW)
+        direct_sum = summed_part(kept)
     with jax.named_scope("back_wide"):
         placed = move_blocks(arrived, columns, scatter=True, extra=gram)
         sums = exchange(placed, WIDE).sum(axis=0)
-    return direct_sum + sums[:rows], sums[rows:]
+    return direct_sum + sums[:rows], sums[rows:], tile
 
 
 def exact(left, right):
@@ -270,8 +292,8 @@
 def on_device(tile, row_columns, start_vectors):
     total_rows = float(lax.axis_size(WIDE) * lax.axis_size(NARROW) * start_vectors.shape[0])
     columns = row_columns[0]
-    first, _ = apply_hamiltonian(tile, columns, start_vectors, want_gram=False)
-    second, gram_rows = apply_hamiltonian(tile, columns, first, want_gram=True)
+    first, _, tile = apply_hamiltonian(tile, columns, start_vectors, want_gram=False)
+    second, gram_rows, _ = apply_hamiltonian(tile, columns, first, want_gram=True)
     width = second.shape[1]
     wide = lax.axis_size(WIDE)
     with jax.named_scope("gram_sum_wide"):

time: 291 us -> 295 us (1.014)
  waiting for transfers between devices: 79.1 us -> 69.6 us
  Pallas kernels: 58.3 us -> 67.6 us
  starting transfers between devices: 107 us -> 110 us
    ppermute x16 -> x20, waiting for transfers between devices: 74.3 us -> 45.1 us  [swap(): return lax.ppermute(value, NARROW, [(i, i ^ mask) for i in range(size)])]
    all_to_all x9, waiting for transfers between devices: 4.86 us -> 24.6 us  [exchange(): return lax.all_to_all(parts, axis, 0, 0, tiled=True)]
    pallas_call x0 -> x1, Pallas kernels: none -> 9.61 us  [split_tile(): pl.pallas_call(kernel, out_shape=(out, out), grid=(tile.shape[0],), in_sp...]
    ppermute x16 -> x20, starting transfers between devices: 42.2 us -> 47.4 us  [swap(): return lax.ppermute(value, NARROW, [(i, i ^ mask) for i in range(size)])]
  transfers between devices with their start and end apart: 25 -> 29, of which waited for: 19 -> 14; matrix products, arithmetic and copies ran while one was open for 2% -> 4% of each run, Pallas kernels for 18% -> 19%
where the time goes in v3:
time: 295 us; the launch traced here: 291 us
  starting transfers between devices  110 us (37%)
  waiting for transfers between devices  69.6 us (24%)
  Pallas kernels  67.6 us (23%)
  blocking collectives  28.7 us (10%)
  local copies, waits for them, and re-layouts  7.18 us (2%)
  other arithmetic  6.13 us (2%)
    all_to_all x9, starting transfers between devices, exchange(): return lax.all_to_all(parts, axis, 0, 0, tiled=True)  62.4 us
    ppermute x20, starting transfers between devices, swap(): return lax.ppermute(value, NARROW, [(i, i ^ mask) for i in range(size)])  47.4 us
    ppermute x20, waiting for transfers between devices, swap(): return lax.ppermute(value, NARROW, [(i, i ^ mask) for i in range(size)])  45.1 us
    all_to_all x2, blocking collectives, exchange(): return lax.all_to_all(parts, axis, 0, 0, tiled=True)  28.7 us
    all_to_all x9, waiting for transfers between devices, exchange(): return lax.all_to_all(parts, axis, 0, 0, tiled=True)  24.6 us
    pallas_call x4, Pallas kernels, transposed_half(): pl.pallas_call(kernel, out_shape=jax.ShapeDtypeStruct((width, order) if p...  23 us
    pallas_call x4, Pallas kernels, direct_half(): pl.pallas_call(kernel, out_shape=jax.ShapeDtypeStruct((groups, rows, widt...  20 us
    pallas_call x1, Pallas kernels, split_tile(): pl.pallas_call(kernel, out_shape=(out, out), grid=(tile.shape[0],), in_sp...  9.61 us
  transfers between devices with their start and end apart: 29, of which 14 were waited for; matrix products, arithmetic and copies ran while one was open for 4% of the time, Pallas kernels for 19%

profile of v3, /device:TPU:8, one launch (start us, length us, event | category | flops | bytes accessed | tf_op | source)
XLA Modules:
  0.0 291.3 jit_solution(14887890902007441936)
XLA Ops:
  0.0 7.2 %collective-permute-start = (f32[96,128]{1,0:T(8,128)}, f32[96,128]{1,0:T(8,128)S(1)}, u32[]{:S(2)}, u32[]{:S(2)}) collective-permute-start(f32[96,128]{1,0:T(8,128)} %param.5), channel_id=1, source_target_pairs={{0,8},{1,9},{2,10},{3,11},{4,12},{5,13},{6,14},{7,15},{8,0},{9,1},... | collective-permute-start | bytes 147464 | tf_op jit(solution)/shard_map/gather_row/ppermute | solution.py:183
  8.7 1.8 broadcast_in_dim.19
  10.5 5.8 %all-to-all-start = ((f32[16,96,128]{2,1,0:T(8,128)}), f32[16,96,128]{2,1,0:T(8,128)S(1)}, u32[]{:S(2)}, u32[]{:S(2)}) async-start(f32[16,96,128]{2,1,0:T(8,128)} %broadcast_in_dim.19), calls=%async_computation | async-start | bytes 1572864 | tf_op jit(solution)/shard_map/gather_wide/all_to_all | solution.py:14
  19.0 5.9 %collective-permute-done.3 = f32[4,96,128]{2,1,0:T(8,128)S(1)} collective-permute-done((f32[4,96,128]{2,1,0:T(8,128)S(1)}, f32[4,96,128]{2,1,0:T(8,128)S(1)}, u32[]{:S(2)}, u32[]{:S(2)}) %collective-permute-start.3) | collective-permute-done | bytes 196640 | tf_op jit(solution)/shard_map/gather_row/ppermute | solution.py:183
  25.0 3.5 %all-to-all-done.blocks_ref = f32[16,96,128]{2,1,0:T(8,128)S(1)} async-done(((f32[16,96,128]{2,1,0:T(8,128)}), f32[16,96,128]{2,1,0:T(8,128)S(1)}, u32[]{:S(2)}, u32[]{:S(2)}) %all-to-all-start) | async-done | bytes 786464 | tf_op jit(solution)/shard_map/gather_wide/all_to_all | solution.py:14
  29.1 1.6 gather_column.2
  30.7 8.1 %all-to-all-start.1 = ((f32[16,96,128]{2,1,0:T(8,128)}), f32[16,96,128]{2,1,0:T(8,128)S(1)}, u32[]{:S(2)}, u32[]{:S(2)}) async-start(f32[16,96,128]{2,1,0:T(8,128)} %gather_column.2), calls=%async_computation.1 | async-start | bytes 1572864 | tf_op jit(solution)/shard_map/gather_column/all_to_all | solution.py:14
  38.8 3.4 %collective-permute-start.4 = (f32[8,96,128]{2,1,0:T(8,128)S(1)}, f32[8,96,128]{2,1,0:T(8,128)S(1)}, u32[]{:S(2)}, u32[]{:S(2)}) collective-permute-start(f32[8,96,128]{2,1,0:T(8,128)S(1)} %constant_dynamic-update-slice_fusion.row_ref), channel_id=1, source_target_pairs={{0,1},{1,0},{2,3},{3,2},{4,5},{5,4},{6,7},{7,6},{8,9},{9,8},{10,11... | collective-permute-start | bytes 1179656 | tf_op jit(solution)/shard_map/gather_row/ppermute | solution.py:183
  42.9 9.6 %split_tile.1 = (bf16[8,2,96,1536]{3,2,1,0:T(8,128)(2,1)}, bf16[8,2,96,1536]{3,2,1,0:T(8,128)(2,1)}) custom-call(f32[8,2,96,1536]{3,2,1,0:T(8,128)} %bitcast.74), custom_call_target="tpu_custom_call" | custom-call | flops 2359296 | bytes 18874368 | tf_op jit(solution)/shard_map/split_tile/pallas_call | solution.py:82
  52.5 5.6 %transposed.4.rest_0_ = f32[128,1536]{1,0:T(8,128)} custom-call(s32[9]{0:T(128)} %get-tuple-element.51.where_ref, bf16[8,2,96,1536]{3,2,1,0:T(8,128)(2,1)} %get-tuple-element.25.high_ref, bf16[8,2,96,1536]{3,2,1,0:T(8,128)(2,1)} %get-tuple-element.26.low_ref, f32[8,96,128]{2,1,0:T(8,128)} %copy-done.8), custom_call_target="tpu_custom_call" | custom-call | flops 905969664 | bytes 4718592 | tf_op jit(solution)/shard_map/transposed/pallas_call | solution.py:159
  58.9 5.9 %transposed.5 = f32[1536,128]{1,0:T(8,128)} custom-call(s32[9]{0:T(128)} %get-tuple-element.52.where_ref, bf16[8,2,96,1536]{3,2,1,0:T(8,128)(2,1)} %get-tuple-element.25.high_ref, bf16[8,2,96,1536]{3,2,1,0:T(8,128)(2,1)} %get-tuple-element.26.low_ref, f32[8,96,128]{2,1,0:T(8,128)} %copy-done.10, f32[128,1536]{1,0:T(8,128)} %transposed.4.rest_0_), custom_call_target="tpu_custom_call" | custom-call | flops 905969664 | bytes 4718592 | tf_op jit(solution)/shard_map/transposed/pallas_call | solution.py:159
  64.8 9.9 %all-to-all-start.2 = ((f32[16,96,128]{2,1,0:T(8,128)}), f32[16,96,128]{2,1,0:T(8,128)S(1)}, u32[]{:S(2)}, u32[]{:S(2)}) async-start(f32[16,96,128]{2,1,0:T(8,128)} %bitcast.80), calls=%async_computation.2 | async-start | bytes 1572864 | tf_op jit(solution)/shard_map/back_transposed/all_to_all | solution.py:14
  74.8 5.0 %direct.5 = f32[8,96,128]{2,1,0:T(8,128)} custom-call(s32[9]{0:T(128)} %get-tuple-element.52.where_ref, bf16[8,2,96,1536]{3,2,1,0:T(8,128)(2,1)} %get-tuple-element.25.high_ref, bf16[8,2,96,1536]{3,2,1,0:T(8,128)(2,1)} %get-tuple-element.26.low_ref, f32[1536,128]{1,0:T(8,128)} %bitcast.75), custom_call_target="tpu_custom_call" | custom-call | flops 905969664 | bytes 4718592 | tf_op jit(solution)/shard_map/direct/pallas_call | solution.py:114
  79.8 3.4 %collective-permute-start.5 = (f32[8,96,128]{2,1,0:T(8,128)}, f32[8,96,128]{2,1,0:T(8,128)S(1)}, u32[]{:S(2)}, u32[]{:S(2)}) collective-permute-start(f32[8,96,128]{2,1,0:T(8,128)} %direct.5), channel_id=1, source_target_pairs={{0,1},{1,0},{2,3},{3,2},{4,5},{5,4},{6,7},{7,6},{8,9},{9,8},{10,11... | collective-permute-start | bytes 1179656 | tf_op jit(solution)/shard_map/direct/ppermute | solution.py:183
  83.2 5.0 %direct.4 = f32[8,96,128]{2,1,0:T(8,128)} custom-call(s32[9]{0:T(128)} %get-tuple-element.51.where_ref, bf16[8,2,96,1536]{3,2,1,0:T(8,128)(2,1)} %get-tuple-element.25.high_ref, bf16[8,2,96,1536]{3,2,1,0:T(8,128)(2,1)} %get-tuple-element.26.low_ref, f32[1536,128]{1,0:T(8,128)} %bitcast.76), custom_call_target="tpu_custom_call" | custom-call | flops 905969664 | bytes 4718592 | tf_op jit(solution)/shard_map/direct/pallas_call | solution.py:114
  88.2 10.0 %collective-permute-done.5 = f32[8,96,128]{2,1,0:T(8,128)S(1)} collective-permute-done((f32[8,96,128]{2,1,0:T(8,128)}, f32[8,96,128]{2,1,0:T(8,128)S(1)}, u32[]{:S(2)}, u32[]{:S(2)}) %collective-permute-start.5) | collective-permute-done | bytes 393248 | tf_op jit(solution)/shard_map/direct/ppermute | solution.py:183
  100.8 4.2 %collective-permute-done.6 = f32[4,96,128]{2,1,0:T(8,128)S(1)} collective-permute-done((f32[4,96,128]{2,1,0:T(8,128)S(1)}, f32[4,96,128]{2,1,0:T(8,128)S(1)}, u32[]{:S(2)}, u32[]{:S(2)}) %collective-permute-start.6) | collective-permute-done | bytes 196640 | tf_op jit(solution)/shard_map/direct/ppermute | solution.py:183
  106.0 1.6 back_wide.2
  107.6 4.3 %all-to-all-start.3 = ((f32[16,96,128]{2,1,0:T(8,128)}), f32[16,96,128]{2,1,0:T(8,128)S(1)}, u32[]{:S(2)}, u32[]{:S(2)}) async-start(f32[16,96,128]{2,1,0:T(8,128)} %back_wide.2), calls=%async_computation.3 | async-start | bytes 1572864 | tf_op jit(solution)/shard_map/back_wide/all_to_all | solution.py:14
  111.9 5.5 %collective-permute-start.7 = (f32[96,128]{1,0:T(8,128)S(1)}, f32[96,128]{1,0:T(8,128)S(1)}, u32[]{:S(2)}, u32[]{:S(2)}) collective-permute-start(f32[96,128]{1,0:T(8,128)S(1)} %get-tuple-element.46), channel_id=1, source_target_pairs={{0,8},{1,9},{2,10},{3,11},{4,12},{5,13},{6,14},{7,15},{8,0},{9,1},... | collective-permute-start | bytes 147464 | tf_op jit(solution)/shard_map/back_direct/ppermute | solution.py:183
  118.5 5.6 %all-to-all-done.3 = f32[16,96,128]{2,1,0:T(8,128)S(1)} async-done(((f32[16,96,128]{2,1,0:T(8,128)}), f32[16,96,128]{2,1,0:T(8,128)S(1)}, u32[]{:S(2)}, u32[]{:S(2)}) %all-to-all-start.3) | async-done | bytes 786464 | tf_op jit(solution)/shard_map/back_wide/all_to_all | solution.py:14
  124.2 3.6 %collective-permute-start.12 = (f32[96,128]{1,0:T(8,128)S(1)}, f32[96,128]{1,0:T(8,128)S(1)}, u32[]{:S(2)}, u32[]{:S(2)}) collective-permute-start(f32[96,128]{1,0:T(8,128)S(1)} %get-tuple-element.42), channel_id=1, source_target_pairs={{0,12},{1,13},{2,14},{3,15},{4,8},{5,9},{6,10},{7,11},{8,4},{9,5},... | collective-permute-start | bytes 147464 | tf_op jit(solution)/shard_map/gather_row/ppermute | solution.py:183
  127.8 2.4 collective-permute-start.11
  131.7 5.7 %all-to-all-start.4 = ((f32[16,96,128]{2,1,0:T(8,128)}), f32[16,96,128]{2,1,0:T(8,128)S(1)}, u32[]{:S(2)}, u32[]{:S(2)}) async-start(f32[16,96,128]{2,1,0:T(8,128)} %broadcast_in_dim.22), calls=%async_computation.4 | async-start | bytes 1572864 | tf_op jit(solution)/shard_map/gather_wide/all_to_all | solution.py:14
  139.6 5.0 %collective-permute-done.13 = f32[4,96,128]{2,1,0:T(8,128)S(1)} collective-permute-done((f32[4,96,128]{2,1,0:T(8,128)S(1)}, f32[4,96,128]{2,1,0:T(8,128)S(1)}, u32[]{:S(2)}, u32[]{:S(2)}) %collective-permute-start.13) | collective-permute-done | bytes 196640 | tf_op jit(solution)/shard_map/gather_row/ppermute | solution.py:183
  144.6 5.0 %all-to-all-done.4.blocks_ref = f32[16,96,128]{2,1,0:T(8,128)S(1)} async-done(((f32[16,96,128]{2,1,0:T(8,128)}), f32[16,96,128]{2,1,0:T(8,128)S(1)}, u32[]{:S(2)}, u32[]{:S(2)}) %all-to-all-start.4) | async-done | bytes 786464 | tf_op jit(solution)/shard_map/gather_wide/all_to_all | solution.py:14
  149.6 1.6 gather_column.3
  151.2 8.2 %all-to-all-start.5 = ((f32[16,96,128]{2,1,0:T(8,128)}), f32[16,96,128]{2,1,0:T(8,128)S(1)}, u32[]{:S(2)}, u32[]{:S(2)}) async-start(f32[16,96,128]{2,1,0:T(8,128)} %gather_column.3), calls=%async_computation.5 | async-start | bytes 1572864 | tf_op jit(solution)/shard_map/gather_column/all_to_all | solution.py:14
  159.5 3.4 %collective-permute-start.14 = (f32[8,96,128]{2,1,0:T(8,128)S(1)}, f32[8,96,128]{2,1,0:T(8,128)S(1)}, u32[]{:S(2)}, u32[]{:S(2)}) collective-permute-start(f32[8,96,128]{2,1,0:T(8,128)S(1)} %constant_dynamic-update-slice_fusion.5.row_ref), channel_id=1, source_target_pairs={{0,1},{1,0},{2,3},{3,2},{4,5},{5,4},{6,7},{7,6},{8,9},{9,8},{10,11... | collective-permute-start | bytes 1179656 | tf_op jit(solution)/shard_map/gather_row/ppermute | solution.py:183
  162.9 5.6 %transposed.6.rest_0_ = f32[128,1536]{1,0:T(8,128)} custom-call(s32[9]{0:T(128)} %get-tuple-element.51.where_ref, bf16[8,2,96,1536]{3,2,1,0:T(8,128)(2,1)} %get-tuple-element.25.high_ref, bf16[8,2,96,1536]{3,2,1,0:T(8,128)(2,1)} %get-tuple-element.26.low_ref, f32[8,96,128]{2,1,0:T(8,128)} %copy-done.4), custom_call_target="tpu_custom_call" | custom-call | flops 905969664 | bytes 4718592 | tf_op jit(solution)/shard_map/transposed/pallas_call | solution.py:159
  168.5 6.4 %collective-permute-done.14.row_ref = f32[8,96,128]{2,1,0:T(8,128)S(1)} collective-permute-done((f32[8,96,128]{2,1,0:T(8,128)S(1)}, f32[8,96,128]{2,1,0:T(8,128)S(1)}, u32[]{:S(2)}, u32[]{:S(2)}) %collective-permute-start.14) | collective-permute-done | bytes 393248 | tf_op jit(solution)/shard_map/gather_row/ppermute | solution.py:183
  175.7 5.9 %transposed.7 = f32[1536,128]{1,0:T(8,128)} custom-call(s32[9]{0:T(128)} %get-tuple-element.52.where_ref, bf16[8,2,96,1536]{3,2,1,0:T(8,128)(2,1)} %get-tuple-element.25.high_ref, bf16[8,2,96,1536]{3,2,1,0:T(8,128)(2,1)} %get-tuple-element.26.low_ref, f32[8,96,128]{2,1,0:T(8,128)} %copy-done.6, f32[128,1536]{1,0:T(8,128)} %transposed.6.rest_0_), custom_call_target="tpu_custom_call" | custom-call | flops 905969664 | bytes 4718592 | tf_op jit(solution)/shard_map/transposed/pallas_call | solution.py:159
  181.6 3.1 %all-to-all-done.5 = f32[16,96,128]{2,1,0:T(8,128)S(1)} async-done(((f32[16,96,128]{2,1,0:T(8,128)}), f32[16,96,128]{2,1,0:T(8,128)S(1)}, u32[]{:S(2)}, u32[]{:S(2)}) %all-to-all-start.5) | async-done | bytes 786464 | tf_op jit(solution)/shard_map/gather_column/all_to_all | solution.py:14
  184.7 10.7 %all-to-all-start.6 = ((f32[16,96,128]{2,1,0:T(8,128)}), f32[16,96,128]{2,1,0:T(8,128)S(1)}, u32[]{:S(2)}, u32[]{:S(2)}) async-start(f32[16,96,128]{2,1,0:T(8,128)} %bitcast.79), calls=%async_computation.6 | async-start | bytes 1572864 | tf_op jit(solution)/shard_map/back_transposed/all_to_all | solution.py:14
  195.4 5.0 %direct.7 = f32[8,96,128]{2,1,0:T(8,128)} custom-call(s32[9]{0:T(128)} %get-tuple-element.52.where_ref, bf16[8,2,96,1536]{3,2,1,0:T(8,128)(2,1)} %get-tuple-element.25.high_ref, bf16[8,2,96,1536]{3,2,1,0:T(8,128)(2,1)} %get-tuple-element.26.low_ref, f32[1536,128]{1,0:T(8,128)} %bitcast.77), custom_call_target="tpu_custom_call" | custom-call | flops 905969664 | bytes 4718592 | tf_op jit(solution)/shard_map/direct/pallas_call | solution.py:114
  200.5 3.4 %collective-permute-start.15 = (f32[8,96,128]{2,1,0:T(8,128)}, f32[8,96,128]{2,1,0:T(8,128)S(1)}, u32[]{:S(2)}, u32[]{:S(2)}) collective-permute-start(f32[8,96,128]{2,1,0:T(8,128)} %direct.7), channel_id=1, source_target_pairs={{0,1},{1,0},{2,3},{3,2},{4,5},{5,4},{6,7},{7,6},{8,9},{9,8},{10,11... | collective-permute-start | bytes 1179656 | tf_op jit(solution)/shard_map/direct/ppermute | solution.py:183
  203.9 5.0 %direct.6 = f32[8,96,128]{2,1,0:T(8,128)} custom-call(s32[9]{0:T(128)} %get-tuple-element.51.where_ref, bf16[8,2,96,1536]{3,2,1,0:T(8,128)(2,1)} %get-tuple-element.25.high_ref, bf16[8,2,96,1536]{3,2,1,0:T(8,128)(2,1)} %get-tuple-element.26.low_ref, f32[1536,128]{1,0:T(8,128)} %bitcast.78), custom_call_target="tpu_custom_call" | custom-call | flops 905969664 | bytes 4718592 | tf_op jit(solution)/shard_map/direct/pallas_call | solution.py:114
  209.7 9.2 %collective-permute-done.15 = f32[8,96,128]{2,1,0:T(8,128)S(1)} collective-permute-done((f32[8,96,128]{2,1,0:T(8,128)}, f32[8,96,128]{2,1,0:T(8,128)S(1)}, u32[]{:S(2)}, u32[]{:S(2)}) %collective-permute-start.15) | collective-permute-done | bytes 393248 | tf_op jit(solution)/shard_map/direct/ppermute | solution.py:183
  222.2 3.4 %collective-permute-done.16 = f32[4,96,128]{2,1,0:T(8,128)S(1)} collective-permute-done((f32[4,96,128]{2,1,0:T(8,128)S(1)}, f32[4,96,128]{2,1,0:T(8,128)S(1)}, u32[]{:S(2)}, u32[]{:S(2)}) %collective-permute-start.16) | collective-permute-done | bytes 196640 | tf_op jit(solution)/shard_map/direct/ppermute | solution.py:183
  226.6 1.7 back_wide.3
  228.4 4.3 %all-to-all-start.7 = ((f32[16,104,128]{2,1,0:T(8,128)}), f32[16,104,128]{2,1,0:T(8,128)S(1)}, u32[]{:S(2)}, u32[]{:S(2)}) async-start(f32[16,104,128]{2,1,0:T(8,128)} %back_wide.3), calls=%async_computation.7 | async-start | bytes 1703936 | tf_op jit(solution)/shard_map/back_wide/all_to_all | solution.py:14
  232.7 5.5 %collective-permute-start.17 = (f32[96,128]{1,0:T(8,128)S(1)}, f32[96,128]{1,0:T(8,128)S(1)}, u32[]{:S(2)}, u32[]{:S(2)}) collective-permute-start(f32[96,128]{1,0:T(8,128)S(1)} %get-tuple-element.43), channel_id=1, source_target_pairs={{0,8},{1,9},{2,10},{3,11},{4,12},{5,13},{6,14},{7,15},{8,0},{9,1},... | collective-permute-start | bytes 147464 | tf_op jit(solution)/shard_map/back_direct/ppermute | solution.py:183
  239.3 6.3 %all-to-all-done.7 = f32[16,104,128]{2,1,0:T(8,128)S(1)} async-done(((f32[16,104,128]{2,1,0:T(8,128)}), f32[16,104,128]{2,1,0:T(8,128)S(1)}, u32[]{:S(2)}, u32[]{:S(2)}) %all-to-all-start.7) | async-done | bytes 852000 | tf_op jit(solution)/shard_map/back_wide/all_to_all | solution.py:14
  246.0 10.0 %all_to_all.55 = f32[16,16,128]{2,1,0:T(8,128)S(1)} all-to-all(f32[16,16,128]{2,1,0:T(8,128)S(1)} %pad_maximum_fusion.2), channel_id=1, replica_groups=mesh['wide'=16,'narrow'=16] {'wide'}, dimensions={0} | all-to-all | bytes 262144 | tf_op jit(solution)/shard_map/gram_sum_wide/all_to_all | solution.py:14
  256.7 18.6 %all_to_all.56 = f32[16,8,128]{2,1,0:T(8,128)S(1)} all-to-all(f32[16,8,128]{2,1,0:T(8,128)S(1)} %broadcast_in_dim.25), channel_id=1, replica_groups=mesh['wide'=16,'narrow'=16] {'narrow'}, dimensions={0} | all-to-all | bytes 131072 | tf_op jit(solution)/shard_map/gram_sum_narrow/all_to_all | solution.py:14
  276.0 5.2 %all-to-all-start.10 = ((f32[16,8,128]{2,1,0:T(8,128)}), f32[16,8,128]{2,1,0:T(8,128)S(1)}, u32[]{:S(2)}, u32[]{:S(2)}) async-start(f32[16,8,128]{2,1,0:T(8,128)} %broadcast_in_dim.26), calls=%async_computation.10 | async-start | bytes 131072 | tf_op jit(solution)/shard_map/gram_whole/all_to_all | solution.py:14
  281.2 3.8 %inverse_first.1.refs_1_ = f32[128,128]{1,0:T(8,128)} custom-call(f32[128,128]{1,0:T(8,128)} %get-tuple-element.49.refs_0_), custom_call_target="tpu_custom_call" | custom-call | flops 1073741824 | bytes 1048576 | tf_op jit(solution)/shard_map/inverse_first/pallas_call | solution.py:281
  286.7 4.5 %finish.1 = f32[96,128]{1,0:T(8,128)} custom-call(f32[128,128]{1,0:T(8,128)} %bitcast.89, f32[128,128]{1,0:T(8,128)} %inverse_first.1.refs_1_, f32[96,128]{1,0:T(8,128)} %copy-done.9), custom_call_target="tpu_custom_call" | custom-call | flops 1073741824 | bytes 1048576 | tf_op jit(solution)/shard_map/finish/pallas_call | solution.py:281
  (86 shorter events, 25.0 us)
Async XLA Ops:
  0.0 17.1 %collective-permute-start = (f32[96,128]{1,0:T(8,128)}, f32[96,128]{1,0:T(8,128)S(1)}, u32[]{:S(2)}, u32[]{:S(2)}) collective-permute-start(f32[96,128]{1,0:T(8,128)} %param.5), channel_id=1, source_target_pairs={{0,8},{1,9},{2,10},{3,11},{4,12},{5,13},{6,14},{7,15},{8,0},{9,1},... | collective-permute-start | bytes 147464 | tf_op jit(solution)/shard_map/gather_row/ppermute | solution.py:183
  7.2 9.9 %collective-permute-start.2 = (f32[96,128]{1,0:T(8,128)}, f32[96,128]{1,0:T(8,128)S(1)}, u32[]{:S(2)}, u32[]{:S(2)}) collective-permute-start(f32[96,128]{1,0:T(8,128)} %param.5), channel_id=1, source_target_pairs={{0,12},{1,13},{2,14},{3,15},{4,8},{5,9},{6,10},{7,11},{8,4},{9,5},... | collective-permute-start | bytes 147464 | tf_op jit(solution)/shard_map/gather_row/ppermute | solution.py:183
  7.2 9.9 %collective-permute-start.1 = (f32[96,128]{1,0:T(8,128)}, f32[96,128]{1,0:T(8,128)S(1)}, u32[]{:S(2)}, u32[]{:S(2)}) collective-permute-start(f32[96,128]{1,0:T(8,128)} %param.5), channel_id=1, source_target_pairs={{0,4},{1,5},{2,6},{3,7},{4,0},{5,1},{6,2},{7,3},{8,12},{9,13},{10,... | collective-permute-start | bytes 147464 | tf_op jit(solution)/shard_map/gather_row/ppermute | solution.py:183
  10.5 17.9 %all-to-all-start = ((f32[16,96,128]{2,1,0:T(8,128)}), f32[16,96,128]{2,1,0:T(8,128)S(1)}, u32[]{:S(2)}, u32[]{:S(2)}) async-start(f32[16,96,128]{2,1,0:T(8,128)} %broadcast_in_dim.19), calls=%async_computation | async-start | bytes 1572864 | tf_op jit(solution)/shard_map/gather_wide/all_to_all | solution.py:14
  17.9 7.0 %collective-permute-start.3 = (f32[4,96,128]{2,1,0:T(8,128)S(1)}, f32[4,96,128]{2,1,0:T(8,128)S(1)}, u32[]{:S(2)}, u32[]{:S(2)}) collective-permute-start(f32[4,96,128]{2,1,0:T(8,128)S(1)} %pad_maximum_fusion), channel_id=1, source_target_pairs={{0,2},{1,3},{2,0},{3,1},{4,6},{5,7},{6,4},{7,5},{8,10},{9,11},{10,... | collective-permute-start | bytes 589832 | tf_op jit(solution)/shard_map/gather_row/ppermute | solution.py:183
  25.0 27.6 %copy-start.8 = (f32[8,96,128]{2,1,0:T(8,128)}, f32[8,96,128]{2,1,0:T(8,128)S(1)}, u32[]{:S(2)}) copy-start(f32[8,96,128]{2,1,0:T(8,128)S(1)} %constant_dynamic-update-slice_fusion.row_ref) | copy-start | bytes 1179652
  28.4 0.7 copy-start
  30.7 34.2 %all-to-all-start.1 = ((f32[16,96,128]{2,1,0:T(8,128)}), f32[16,96,128]{2,1,0:T(8,128)S(1)}, u32[]{:S(2)}, u32[]{:S(2)}) async-start(f32[16,96,128]{2,1,0:T(8,128)} %gather_column.2), calls=%async_computation.1 | async-start | bytes 1572864 | tf_op jit(solution)/shard_map/gather_column/all_to_all | solution.py:14
  38.8 19.3 %collective-permute-start.4 = (f32[8,96,128]{2,1,0:T(8,128)S(1)}, f32[8,96,128]{2,1,0:T(8,128)S(1)}, u32[]{:S(2)}, u32[]{:S(2)}) collective-permute-start(f32[8,96,128]{2,1,0:T(8,128)S(1)} %constant_dynamic-update-slice_fusion.row_ref), channel_id=1, source_target_pairs={{0,1},{1,0},{2,3},{3,2},{4,5},{5,4},{6,7},{7,6},{8,9},{9,8},{10,11... | collective-permute-start | bytes 1179656 | tf_op jit(solution)/shard_map/gather_row/ppermute | solution.py:183
  58.1 0.8 copy-start.10
  64.8 10.0 %copy-start.2 = (f32[16,96,128]{2,1,0:T(8,128)}, f32[16,96,128]{2,1,0:T(8,128)S(1)}, u32[]{:S(2)}) copy-start(f32[16,96,128]{2,1,0:T(8,128)S(1)} %all-to-all-done.1) | copy-start | bytes 2359300
  64.8 41.1 %all-to-all-start.2 = ((f32[16,96,128]{2,1,0:T(8,128)}), f32[16,96,128]{2,1,0:T(8,128)S(1)}, u32[]{:S(2)}, u32[]{:S(2)}) async-start(f32[16,96,128]{2,1,0:T(8,128)} %bitcast.80), calls=%async_computation.2 | async-start | bytes 1572864 | tf_op jit(solution)/shard_map/back_transposed/all_to_all | solution.py:14
  79.8 26.2 %copy-start.1 = (s32[1,16]{1,0:T(1,128)S(1)}, s32[1,16]{1,0:T(1,128)}, u32[]{:S(2)}) copy-start(s32[1,16]{1,0:T(1,128)} %param.4) | copy-start | bytes 196
  79.8 18.5 %collective-permute-start.5 = (f32[8,96,128]{2,1,0:T(8,128)}, f32[8,96,128]{2,1,0:T(8,128)S(1)}, u32[]{:S(2)}, u32[]{:S(2)}) collective-permute-start(f32[8,96,128]{2,1,0:T(8,128)} %direct.5), channel_id=1, source_target_pairs={{0,1},{1,0},{2,3},{3,2},{4,5},{5,4},{6,7},{7,6},{8,9},{9,8},{10,11... | collective-permute-start | bytes 1179656 | tf_op jit(solution)/shard_map/direct/ppermute | solution.py:183
  99.2 5.8 %collective-permute-start.6 = (f32[4,96,128]{2,1,0:T(8,128)S(1)}, f32[4,96,128]{2,1,0:T(8,128)S(1)}, u32[]{:S(2)}, u32[]{:S(2)}) collective-permute-start(f32[4,96,128]{2,1,0:T(8,128)S(1)} %slice_add_fusion.2), channel_id=1, source_target_pairs={{0,2},{1,3},{2,0},{3,1},{4,6},{5,7},{6,4},{7,5},{8,10},{9,11},{10,... | collective-permute-start | bytes 589832 | tf_op jit(solution)/shard_map/direct/ppermute | solution.py:183
  107.6 16.5 %all-to-all-start.3 = ((f32[16,96,128]{2,1,0:T(8,128)}), f32[16,96,128]{2,1,0:T(8,128)S(1)}, u32[]{:S(2)}, u32[]{:S(2)}) async-start(f32[16,96,128]{2,1,0:T(8,128)} %back_wide.2), calls=%async_computation.3 | async-start | bytes 1572864 | tf_op jit(solution)/shard_map/back_wide/all_to_all | solution.py:14
  111.9 12.2 %collective-permute-start.7 = (f32[96,128]{1,0:T(8,128)S(1)}, f32[96,128]{1,0:T(8,128)S(1)}, u32[]{:S(2)}, u32[]{:S(2)}) collective-permute-start(f32[96,128]{1,0:T(8,128)S(1)} %get-tuple-element.46), channel_id=1, source_target_pairs={{0,8},{1,9},{2,10},{3,11},{4,12},{5,13},{6,14},{7,15},{8,0},{9,1},... | collective-permute-start | bytes 147464 | tf_op jit(solution)/shard_map/back_direct/ppermute | solution.py:183
  117.4 6.7 %collective-permute-start.9 = (f32[96,128]{1,0:T(8,128)S(1)}, f32[96,128]{1,0:T(8,128)S(1)}, u32[]{:S(2)}, u32[]{:S(2)}) collective-permute-start(f32[96,128]{1,0:T(8,128)S(1)} %get-tuple-element.47), channel_id=1, source_target_pairs={{0,12},{1,13},{2,14},{3,15},{4,8},{5,9},{6,10},{7,11},{8,4},{9,5},... | collective-permute-start | bytes 147464 | tf_op jit(solution)/shard_map/back_direct/ppermute | solution.py:183
  117.9 6.3 %collective-permute-start.8 = (f32[96,128]{1,0:T(8,128)S(1)}, f32[96,128]{1,0:T(8,128)S(1)}, u32[]{:S(2)}, u32[]{:S(2)}) collective-permute-start(f32[96,128]{1,0:T(8,128)S(1)} %get-tuple-element.48), channel_id=1, source_target_pairs={{0,4},{1,5},{2,6},{3,7},{4,0},{5,1},{6,2},{7,3},{8,12},{9,13},{10,... | collective-permute-start | bytes 147464 | tf_op jit(solution)/shard_map/back_direct/ppermute | solution.py:183
  124.2 13.3 %collective-permute-start.12 = (f32[96,128]{1,0:T(8,128)S(1)}, f32[96,128]{1,0:T(8,128)S(1)}, u32[]{:S(2)}, u32[]{:S(2)}) collective-permute-start(f32[96,128]{1,0:T(8,128)S(1)} %get-tuple-element.42), channel_id=1, source_target_pairs={{0,12},{1,13},{2,14},{3,15},{4,8},{5,9},{6,10},{7,11},{8,4},{9,5},... | collective-permute-start | bytes 147464 | tf_op jit(solution)/shard_map/gather_row/ppermute | solution.py:183
  127.8 9.6 %collective-permute-start.11 = (f32[96,128]{1,0:T(8,128)S(1)}, f32[96,128]{1,0:T(8,128)S(1)}, u32[]{:S(2)}, u32[]{:S(2)}) collective-permute-start(f32[96,128]{1,0:T(8,128)S(1)} %get-tuple-element.42), channel_id=1, source_target_pairs={{0,4},{1,5},{2,6},{3,7},{4,0},{5,1},{6,2},{7,3},{8,12},{9,13},{10,... | collective-permute-start | bytes 147464 | tf_op jit(solution)/shard_map/gather_row/ppermute | solution.py:183
  130.3 8.2 %collective-permute-start.10 = (f32[96,128]{1,0:T(8,128)S(1)}, f32[96,128]{1,0:T(8,128)S(1)}, u32[]{:S(2)}, u32[]{:S(2)}) collective-permute-start(f32[96,128]{1,0:T(8,128)S(1)} %get-tuple-element.42), channel_id=1, source_target_pairs={{0,8},{1,9},{2,10},{3,11},{4,12},{5,13},{6,14},{7,15},{8,0},{9,1},... | collective-permute-start | bytes 147464 | tf_op jit(solution)/shard_map/gather_row/ppermute | solution.py:183
  131.7 17.9 %all-to-all-start.4 = ((f32[16,96,128]{2,1,0:T(8,128)}), f32[16,96,128]{2,1,0:T(8,128)S(1)}, u32[]{:S(2)}, u32[]{:S(2)}) async-start(f32[16,96,128]{2,1,0:T(8,128)} %broadcast_in_dim.22), calls=%async_computation.4 | async-start | bytes 1572864 | tf_op jit(solution)/shard_map/gather_wide/all_to_all | solution.py:14
  138.4 6.1 %collective-permute-start.13 = (f32[4,96,128]{2,1,0:T(8,128)S(1)}, f32[4,96,128]{2,1,0:T(8,128)S(1)}, u32[]{:S(2)}, u32[]{:S(2)}) collective-permute-start(f32[4,96,128]{2,1,0:T(8,128)S(1)} %pad_maximum_fusion.1), channel_id=1, source_target_pairs={{0,2},{1,3},{2,0},{3,1},{4,6},{5,7},{6,4},{7,5},{8,10},{9,11},{10,... | collective-permute-start | bytes 589832 | tf_op jit(solution)/shard_map/gather_row/ppermute | solution.py:183
  144.6 18.3 %copy-start.4 = (f32[8,96,128]{2,1,0:T(8,128)}, f32[8,96,128]{2,1,0:T(8,128)S(1)}, u32[]{:S(2)}) copy-start(f32[8,96,128]{2,1,0:T(8,128)S(1)} %constant_dynamic-update-slice_fusion.5.row_ref) | copy-start | bytes 1179652
  151.2 33.5 %all-to-all-start.5 = ((f32[16,96,128]{2,1,0:T(8,128)}), f32[16,96,128]{2,1,0:T(8,128)S(1)}, u32[]{:S(2)}, u32[]{:S(2)}) async-start(f32[16,96,128]{2,1,0:T(8,128)} %gather_column.3), calls=%async_computation.5 | async-start | bytes 1572864 | tf_op jit(solution)/shard_map/gather_column/all_to_all | solution.py:14
  159.5 15.4 %collective-permute-start.14 = (f32[8,96,128]{2,1,0:T(8,128)S(1)}, f32[8,96,128]{2,1,0:T(8,128)S(1)}, u32[]{:S(2)}, u32[]{:S(2)}) collective-permute-start(f32[8,96,128]{2,1,0:T(8,128)S(1)} %constant_dynamic-update-slice_fusion.5.row_ref), channel_id=1, source_target_pairs={{0,1},{1,0},{2,3},{3,2},{4,5},{5,4},{6,7},{7,6},{8,9},{9,8},{10,11... | collective-permute-start | bytes 1179656 | tf_op jit(solution)/shard_map/gather_row/ppermute | solution.py:183
  174.9 0.8 copy-start.6
  184.7 10.7 %copy-start.3 = (f32[16,96,128]{2,1,0:T(8,128)}, f32[16,96,128]{2,1,0:T(8,128)S(1)}, u32[]{:S(2)}) copy-start(f32[16,96,128]{2,1,0:T(8,128)S(1)} %all-to-all-done.5) | copy-start | bytes 2359300
  184.7 41.9 %all-to-all-start.6 = ((f32[16,96,128]{2,1,0:T(8,128)}), f32[16,96,128]{2,1,0:T(8,128)S(1)}, u32[]{:S(2)}, u32[]{:S(2)}) async-start(f32[16,96,128]{2,1,0:T(8,128)} %bitcast.79), calls=%async_computation.6 | async-start | bytes 1572864 | tf_op jit(solution)/shard_map/back_transposed/all_to_all | solution.py:14
  200.5 8.4 %copy-start.7 = (f32[8,96,128]{2,1,0:T(8,128)S(1)}, f32[8,96,128]{2,1,0:T(8,128)}, u32[]{:S(2)}) copy-start(f32[8,96,128]{2,1,0:T(8,128)} %copy-done.6) | copy-start | bytes 1179652
  200.5 20.9 %copy-start.5 = (f32[8,96,128]{2,1,0:T(8,128)S(1)}, f32[8,96,128]{2,1,0:T(8,128)}, u32[]{:S(2)}) copy-start(f32[8,96,128]{2,1,0:T(8,128)} %copy-done.4) | copy-start | bytes 1179652
  200.5 18.5 %collective-permute-start.15 = (f32[8,96,128]{2,1,0:T(8,128)}, f32[8,96,128]{2,1,0:T(8,128)S(1)}, u32[]{:S(2)}, u32[]{:S(2)}) collective-permute-start(f32[8,96,128]{2,1,0:T(8,128)} %direct.7), channel_id=1, source_target_pairs={{0,1},{1,0},{2,3},{3,2},{4,5},{5,4},{6,7},{7,6},{8,9},{9,8},{10,11... | collective-permute-start | bytes 1179656 | tf_op jit(solution)/shard_map/direct/ppermute | solution.py:183
  219.9 5.8 %collective-permute-start.16 = (f32[4,96,128]{2,1,0:T(8,128)S(1)}, f32[4,96,128]{2,1,0:T(8,128)S(1)}, u32[]{:S(2)}, u32[]{:S(2)}) collective-permute-start(f32[4,96,128]{2,1,0:T(8,128)S(1)} %slice_add_fusion), channel_id=1, source_target_pairs={{0,2},{1,3},{2,0},{3,1},{4,6},{5,7},{6,4},{7,5},{8,10},{9,11},{10,... | collective-permute-start | bytes 589832 | tf_op jit(solution)/shard_map/direct/ppermute | solution.py:183
  228.4 17.2 %all-to-all-start.7 = ((f32[16,104,128]{2,1,0:T(8,128)}), f32[16,104,128]{2,1,0:T(8,128)S(1)}, u32[]{:S(2)}, u32[]{:S(2)}) async-start(f32[16,104,128]{2,1,0:T(8,128)} %back_wide.3), calls=%async_computation.7 | async-start | bytes 1703936 | tf_op jit(solution)/shard_map/back_wide/all_to_all | solution.py:14
  232.7 12.9 %collective-permute-start.17 = (f32[96,128]{1,0:T(8,128)S(1)}, f32[96,128]{1,0:T(8,128)S(1)}, u32[]{:S(2)}, u32[]{:S(2)}) collective-permute-start(f32[96,128]{1,0:T(8,128)S(1)} %get-tuple-element.43), channel_id=1, source_target_pairs={{0,8},{1,9},{2,10},{3,11},{4,12},{5,13},{6,14},{7,15},{8,0},{9,1},... | collective-permute-start | bytes 147464 | tf_op jit(solution)/shard_map/back_direct/ppermute | solution.py:183
  238.2 7.4 %collective-permute-start.19 = (f32[96,128]{1,0:T(8,128)S(1)}, f32[96,128]{1,0:T(8,128)S(1)}, u32[]{:S(2)}, u32[]{:S(2)}) collective-permute-start(f32[96,128]{1,0:T(8,128)S(1)} %get-tuple-element.44), channel_id=1, source_target_pairs={{0,12},{1,13},{2,14},{3,15},{4,8},{5,9},{6,10},{7,11},{8,4},{9,5},... | collective-permute-start | bytes 147464 | tf_op jit(solution)/shard_map/back_direct/ppermute | solution.py:183
  238.6 7.0 %collective-permute-start.18 = (f32[96,128]{1,0:T(8,128)S(1)}, f32[96,128]{1,0:T(8,128)S(1)}, u32[]{:S(2)}, u32[]{:S(2)}) collective-permute-start(f32[96,128]{1,0:T(8,128)S(1)} %get-tuple-element.45), channel_id=1, source_target_pairs={{0,4},{1,5},{2,6},{3,7},{4,0},{5,1},{6,2},{7,3},{8,12},{9,13},{10,... | collective-permute-start | bytes 147464 | tf_op jit(solution)/shard_map/back_direct/ppermute | solution.py:183
  245.7 40.5 %copy-start.9 = (f32[96,128]{1,0:T(8,128)}, f32[96,128]{1,0:T(8,128)S(1)}, u32[]{:S(2)}) copy-start(f32[96,128]{1,0:T(8,128)S(1)} %slice_add_fusion.4.refs_2_) | copy-start | bytes 147460
  276.0 10.2 %all-to-all-start.10 = ((f32[16,8,128]{2,1,0:T(8,128)}), f32[16,8,128]{2,1,0:T(8,128)S(1)}, u32[]{:S(2)}, u32[]{:S(2)}) async-start(f32[16,8,128]{2,1,0:T(8,128)} %broadcast_in_dim.26), calls=%async_computation.10 | async-start | bytes 131072 | tf_op jit(solution)/shard_map/gram_whole/all_to_all | solution.py:14
  286.1 0.6 copy-start.11

commit v4 on v2

--- a/solution.py
+++ b/solution.py
@@ -178,19 +178,25 @@
     return lax.ppermute(value, NARROW, [(i, i ^ mask) for i in range(size)])
 
 
-ENTRIES = (0, 8, 4, 12)
-QUARTERS = (0, 2, 1, 3)
+ENTRIES = (8, 4, 12)
 REVERSED = (0, 4, 2, 6, 1, 5, 3, 7)
 
 
 def reversed_bits(value):
     return ((value & 1) << 2) | (value & 2) | (value >> 2)
+
+
+def summed_part(kept):
+    total = kept[0]
+    for k, mask in enumerate(ENTRIES):
+        total = total + swap(kept[k + 1], mask)
+    return total
 
 
 def apply_hamiltonian(tile, columns, vectors, want_gram):
     rows, width = vectors.shape
     count = lax.axis_size(NARROW)
-    order = tile.shape[0]
+    order = count * rows
     groups = count // 2
     me = lax.axis_index(NARROW).astype(jnp.int32)
     near, far = me & 1, (me & 1) ^ 1
@@ -200,34 +206,32 @@
     with jax.named_scope("gather_wide"):
         slices = to_everyone(vectors, WIDE)
     with jax.named_scope("gather_row"):
-        quarter = jnp.stack([vectors] + [swap(vectors, mask) for mask in ENTRIES[1:]])
-        quarters = [quarter] + [swap(quarter, mask) for mask in QUARTERS[1:]]
-        slices, quarters = lax.optimization_barrier((slices, quarters))
+        quarter = jnp.stack([vectors] + [swap(vectors, mask) for mask in ENTRIES])
+        near_rows, far_rows = [quarter, swap(quarter, 2)], [swap(quarter, 1)]
+        slices, near_rows, far_rows = lax.optimization_barrier((slices, near_rows, far_rows))
+        far_rows.append(swap(near_rows[1], 1))
     with jax.named_scope("gather_column"):
         picked = move_blocks(slices, columns, scatter=False)
         column_block = exchange(picked, NARROW).reshape(order, width)
     with jax.named_scope("transposed"):
-        partial = transposed_half(tile, quarters[:2], near, spots)
-        transposed = transposed_half(tile, quarters[2:], far, spots, partial)
+        partial = transposed_half(tile, near_rows, near, spots)
+        transposed = transposed_half(tile, far_rows, far, spots, partial)
         transposed, column_block = lax.optimization_barrier((transposed, column_block))
     with jax.named_scope("back_transposed"):
         arrived = exchange(transposed.reshape(count, rows, width), NARROW)
     with jax.named_scope("direct"):
-        sums = list(direct_half(tile, column_block, far, places))
-        got = [swap(value, mask) for value, mask in zip(sums, QUARTERS[2:])]
-        kept, sent = direct_half(tile, column_block, near, places)
-        arrived, got, kept, sent = lax.optimization_barrier((arrived, got, kept, sent))
-        got.append(swap(sent, QUARTERS[1]))
+        far_first, far_second = direct_half(tile, column_block, far, places)
+        got_second, got_first = swap(far_second, 1), swap(far_first, 1)
+        near_first, near_second = direct_half(tile, column_block, near, places)
+        kept = near_first + got_first + swap(near_second + got_second, 2)
+        arrived, kept = lax.optimization_barrier((arrived, kept))
     gram = None
     if want_gram:
         with jax.named_scope("gram_block_row"):
-            quarters, _ = lax.optimization_barrier((quarters, sums))
-            gram = sum(gram_of(quarter.reshape(-1, width)) for quarter in quarters)
+            block, _ = lax.optimization_barrier((near_rows + far_rows, far_first))
+            gram = sum(gram_of(quarter.reshape(-1, width)) for quarter in block)
     with jax.named_scope("back_direct"):
-        kept = kept + got[0] + got[1] + got[2]
-        direct_sum = kept[0]
-        for m, mask in enumerate(ENTRIES[1:]):
-            direct_sum = direct_sum + swap(kept[m + 1], mask)
+        direct_sum = summed_part(kept)
     with jax.named_scope("back_wide"):
         placed = move_blocks(arrived, columns, scatter=True, extra=gram)
         sums = exchange(placed, WIDE).sum(axis=0)

time: 290 us -> 273 us (0.941)
  waiting for transfers between devices: 90.7 us -> 66.1 us
    ppermute x24, waiting for transfers between devices: 67.4 us -> 41.3 us  [swap(): return lax.ppermute(value, NARROW, [(i, i ^ mask) for i in range(size)])]
    ppermute x24, starting transfers between devices: 48.6 us -> 52.4 us  [swap(): return lax.ppermute(value, NARROW, [(i, i ^ mask) for i in range(size)])]
  transfers between devices with their start and end apart: 33 -> 33, of which waited for: 23 -> 17; matrix products, arithmetic and copies ran while one was open for 2% -> 4% of each run, Pallas kernels for 17% -> 18%
where the time goes in v4:
time: 273 us; the launch traced here: 269 us
  starting transfers between devices  99.2 us (36%)
  waiting for transfers between devices  66.1 us (24%)
  Pallas kernels  58.8 us (22%)
  blocking collectives  28.1 us (10%)
  other arithmetic  7.4 us (3%)
  local copies, waits for them, and re-layouts  6.12 us (2%)
  matrix products  3.26 us (1%)
    ppermute x24, starting transfers between devices, swap(): return lax.ppermute(value, NARROW, [(i, i ^ mask) for i in range(size)])  52.4 us
    all_to_all x9, starting transfers between devices, exchange(): return lax.all_to_all(parts, axis, 0, 0, tiled=True)  46.9 us
    ppermute x24, waiting for transfers between devices, swap(): return lax.ppermute(value, NARROW, [(i, i ^ mask) for i in range(size)])  41.3 us
    all_to_all x2, blocking collectives, exchange(): return lax.all_to_all(parts, axis, 0, 0, tiled=True)  28.1 us
    all_to_all x9, waiting for transfers between devices, exchange(): return lax.all_to_all(parts, axis, 0, 0, tiled=True)  24.8 us
    pallas_call x4, Pallas kernels, transposed_half(): pl.pallas_call(kernel, out_shape=jax.ShapeDtypeStruct((width, order) if p...  23.2 us
    pallas_call x4, Pallas kernels, direct_half(): pl.pallas_call(kernel, out_shape=(out, out), grid_spec=pltpu.PrefetchScal...  20.7 us
    pallas_call x2, Pallas kernels, in_kernel(): pl.pallas_call(kernel, out_shape=jax.ShapeDtypeStruct(shape, jnp.float32)...  8.37 us
  transfers between devices with their start and end apart: 33, of which 17 were waited for; matrix products, arithmetic and copies ran while one was open for 4% of the time, Pallas kernels for 18%

profile of v4, /device:TPU:8, one launch (start us, length us, event | category | flops | bytes accessed | tf_op | source)
XLA Modules:
  0.0 269.4 jit_solution(11456962991726572681)
XLA Ops:
  0.0 1.8 broadcast_in_dim.19
  1.8 5.8 %all-to-all-start = ((f32[16,96,128]{2,1,0:T(8,128)}), f32[16,96,128]{2,1,0:T(8,128)S(1)}, u32[]{:S(2)}, u32[]{:S(2)}) async-start(f32[16,96,128]{2,1,0:T(8,128)} %broadcast_in_dim.19), calls=%async_computation | async-start | bytes 1572864 | tf_op jit(solution)/shard_map/gather_wide/all_to_all | solution.py:14
  7.6 7.2 %collective-permute-start = (f32[96,128]{1,0:T(8,128)}, f32[96,128]{1,0:T(8,128)S(1)}, u32[]{:S(2)}, u32[]{:S(2)}) collective-permute-start(f32[96,128]{1,0:T(8,128)} %param.7), channel_id=1, source_target_pairs={{0,8},{1,9},{2,10},{3,11},{4,12},{5,13},{6,14},{7,15},{8,0},{9,1},... | collective-permute-start | bytes 147464 | tf_op jit(solution)/shard_map/gather_row/ppermute | solution.py:178
  17.5 3.6 %collective-permute-done.2 = f32[96,128]{1,0:T(8,128)S(1)} collective-permute-done((f32[96,128]{1,0:T(8,128)}, f32[96,128]{1,0:T(8,128)S(1)}, u32[]{:S(2)}, u32[]{:S(2)}) %collective-permute-start.2) | collective-permute-done | bytes 49184 | tf_op jit(solution)/shard_map/gather_row/ppermute | solution.py:178
  22.0 2.4 collective-permute-start.4
  25.9 3.6 %collective-permute-done.4.first_ref = f32[4,96,128]{2,1,0:T(8,128)S(1)} collective-permute-done((f32[4,96,128]{2,1,0:T(8,128)S(1)}, f32[4,96,128]{2,1,0:T(8,128)S(1)}, u32[]{:S(2)}, u32[]{:S(2)}) %collective-permute-start.4) | collective-permute-done | bytes 196640 | tf_op jit(solution)/shard_map/gather_row/ppermute | solution.py:178
  32.3 7.1 %all-to-all-start.1 = ((f32[16,96,128]{2,1,0:T(8,128)}), f32[16,96,128]{2,1,0:T(8,128)S(1)}, u32[]{:S(2)}, u32[]{:S(2)}) async-start(f32[16,96,128]{2,1,0:T(8,128)} %gather_column.2), calls=%async_computation.1 | async-start | bytes 1572864 | tf_op jit(solution)/shard_map/gather_column/all_to_all | solution.py:14
  40.1 3.4 %collective-permute-start.5 = (f32[4,96,128]{2,1,0:T(8,128)S(1)}, f32[4,96,128]{2,1,0:T(8,128)S(1)}, u32[]{:S(2)}, u32[]{:S(2)}) collective-permute-start(f32[4,96,128]{2,1,0:T(8,128)S(1)} %collective-permute-done.3.second_ref), channel_id=1, source_target_pairs={{0,1},{1,0},{2,3},{3,2},{4,5},{5,4},{6,7},{7,6},{8,9},{9,8},{10,11... | collective-permute-start | bytes 589832 | tf_op jit(solution)/shard_map/gather_row/ppermute | solution.py:178
  44.1 5.7 %transposed.4.rest_0_ = f32[128,1536]{1,0:T(8,128)} custom-call(s32[9]{0:T(128)} %get-tuple-element.73.where_ref, f32[8,2,96,1536]{3,2,1,0:T(8,128)} %bitcast.77, f32[4,96,128]{2,1,0:T(8,128)} %copy-done.10, f32[4,96,128]{2,1,0:T(8,128)} %copy-done.13), custom_call_target="tpu_custom_call" | custom-call | flops 905969664 | bytes 4718592 | tf_op jit(solution)/shard_map/transposed/pallas_call | solution.py:154
  50.5 5.9 %transposed.5 = f32[1536,128]{1,0:T(8,128)} custom-call(s32[9]{0:T(128)} %get-tuple-element.74.where_ref, f32[8,2,96,1536]{3,2,1,0:T(8,128)} %bitcast.78, f32[4,96,128]{2,1,0:T(8,128)} %copy-done.12, f32[4,96,128]{2,1,0:T(8,128)} %copy-done.14, f32[128,1536]{1,0:T(8,128)} %transposed.4.rest_0_), custom_call_target="tpu_custom_call" | custom-call | flops 905969664 | bytes 4718592 | tf_op jit(solution)/shard_map/transposed/pallas_call | solution.py:154
  56.4 5.1 %all-to-all-done.1 = f32[16,96,128]{2,1,0:T(8,128)S(1)} async-done(((f32[16,96,128]{2,1,0:T(8,128)}), f32[16,96,128]{2,1,0:T(8,128)S(1)}, u32[]{:S(2)}, u32[]{:S(2)}) %all-to-all-start.1) | async-done | bytes 786464 | tf_op jit(solution)/shard_map/gather_column/all_to_all | solution.py:14
  61.5 4.6 %all-to-all-start.2 = ((f32[16,96,128]{2,1,0:T(8,128)}), f32[16,96,128]{2,1,0:T(8,128)S(1)}, u32[]{:S(2)}, u32[]{:S(2)}) async-start(f32[16,96,128]{2,1,0:T(8,128)} %bitcast.90), calls=%async_computation.2 | async-start | bytes 1572864 | tf_op jit(solution)/shard_map/back_transposed/all_to_all | solution.py:14
  66.8 5.2 %direct.5 = (f32[4,96,128]{2,1,0:T(8,128)}, f32[4,96,128]{2,1,0:T(8,128)}) custom-call(s32[9]{0:T(128)} %get-tuple-element.69.where_ref, f32[8,2,96,1536]{3,2,1,0:T(8,128)} %bitcast.79, f32[1536,128]{1,0:T(8,128)} %bitcast.85), custom_call_target="tpu_custom_call" | custom-call | flops 905969664 | bytes 4718592 | tf_op jit(solution)/shard_map/direct/pallas_call | solution.py:106
  72.0 3.4 %collective-permute-start.7 = (f32[4,96,128]{2,1,0:T(8,128)}, f32[4,96,128]{2,1,0:T(8,128)S(1)}, u32[]{:S(2)}, u32[]{:S(2)}) collective-permute-start(f32[4,96,128]{2,1,0:T(8,128)} %get-tuple-element.42), channel_id=1, source_target_pairs={{0,1},{1,0},{2,3},{3,2},{4,5},{5,4},{6,7},{7,6},{8,9},{9,8},{10,11... | collective-permute-start | bytes 589832 | tf_op jit(solution)/shard_map/direct/ppermute | solution.py:178
  75.5 5.1 %direct.4 = (f32[4,96,128]{2,1,0:T(8,128)}, f32[4,96,128]{2,1,0:T(8,128)}) custom-call(s32[9]{0:T(128)} %get-tuple-element.70.where_ref, f32[8,2,96,1536]{3,2,1,0:T(8,128)} %bitcast.80, f32[1536,128]{1,0:T(8,128)} %bitcast.86), custom_call_target="tpu_custom_call" | custom-call | flops 905969664 | bytes 4718592 | tf_op jit(solution)/shard_map/direct/pallas_call | solution.py:106
  80.7 4.8 %collective-permute-done.7 = f32[4,96,128]{2,1,0:T(8,128)S(1)} collective-permute-done((f32[4,96,128]{2,1,0:T(8,128)}, f32[4,96,128]{2,1,0:T(8,128)S(1)}, u32[]{:S(2)}, u32[]{:S(2)}) %collective-permute-start.7) | collective-permute-done | bytes 196640 | tf_op jit(solution)/shard_map/direct/ppermute | solution.py:178
  86.4 2.0 collective-permute-start.8
  88.4 3.8 %collective-permute-done.8 = f32[4,96,128]{2,1,0:T(8,128)S(1)} collective-permute-done((f32[4,96,128]{2,1,0:T(8,128)S(1)}, f32[4,96,128]{2,1,0:T(8,128)S(1)}, u32[]{:S(2)}, u32[]{:S(2)}) %collective-permute-start.8) | collective-permute-done | bytes 196640 | tf_op jit(solution)/shard_map/direct/ppermute | solution.py:178
  94.8 5.7 %all-to-all-start.3 = ((f32[16,96,128]{2,1,0:T(8,128)}), f32[16,96,128]{2,1,0:T(8,128)S(1)}, u32[]{:S(2)}, u32[]{:S(2)}) async-start(f32[16,96,128]{2,1,0:T(8,128)} %back_wide.2), calls=%async_computation.3 | async-start | bytes 1572864 | tf_op jit(solution)/shard_map/back_wide/all_to_all | solution.py:14
  100.5 5.7 %collective-permute-start.9 = (f32[96,128]{1,0:T(8,128)S(1)}, f32[96,128]{1,0:T(8,128)S(1)}, u32[]{:S(2)}, u32[]{:S(2)}) collective-permute-start(f32[96,128]{1,0:T(8,128)S(1)} %get-tuple-element.64), channel_id=1, source_target_pairs={{0,8},{1,9},{2,10},{3,11},{4,12},{5,13},{6,14},{7,15},{8,0},{9,1},... | collective-permute-start | bytes 147464 | tf_op jit(solution)/shard_map/back_direct/ppermute | solution.py:178
  107.2 5.5 %all-to-all-done.3 = f32[16,96,128]{2,1,0:T(8,128)S(1)} async-done(((f32[16,96,128]{2,1,0:T(8,128)}), f32[16,96,128]{2,1,0:T(8,128)S(1)}, u32[]{:S(2)}, u32[]{:S(2)}) %all-to-all-start.3) | async-done | bytes 786464 | tf_op jit(solution)/shard_map/back_wide/all_to_all | solution.py:14
  113.7 5.6 %all-to-all-start.4 = ((f32[16,96,128]{2,1,0:T(8,128)}), f32[16,96,128]{2,1,0:T(8,128)S(1)}, u32[]{:S(2)}, u32[]{:S(2)}) async-start(f32[16,96,128]{2,1,0:T(8,128)} %broadcast_in_dim.22), calls=%async_computation.4 | async-start | bytes 1572864 | tf_op jit(solution)/shard_map/gather_wide/all_to_all | solution.py:14
  119.3 3.7 %collective-permute-start.14 = (f32[96,128]{1,0:T(8,128)S(1)}, f32[96,128]{1,0:T(8,128)S(1)}, u32[]{:S(2)}, u32[]{:S(2)}) collective-permute-start(f32[96,128]{1,0:T(8,128)S(1)} %fusion.7), channel_id=1, source_target_pairs={{0,12},{1,13},{2,14},{3,15},{4,8},{5,9},{6,10},{7,11},{8,4},{9,5},... | collective-permute-start | bytes 147464 | tf_op jit(solution)/shard_map/gather_row/ppermute | solution.py:178
  123.1 1.9 collective-permute-start.13
  125.9 2.4 collective-permute-done.13
  128.3 5.1 %collective-permute-done.12 = f32[96,128]{1,0:T(8,128)S(1)} collective-permute-done((f32[96,128]{1,0:T(8,128)S(1)}, f32[96,128]{1,0:T(8,128)S(1)}, u32[]{:S(2)}, u32[]{:S(2)}) %collective-permute-start.12) | collective-permute-done | bytes 49184 | tf_op jit(solution)/shard_map/gather_row/ppermute | solution.py:178
  133.4 2.1 collective-permute-start.16
  136.1 4.6 %collective-permute-done.16.first_ref = f32[4,96,128]{2,1,0:T(8,128)S(1)} collective-permute-done((f32[4,96,128]{2,1,0:T(8,128)S(1)}, f32[4,96,128]{2,1,0:T(8,128)S(1)}, u32[]{:S(2)}, u32[]{:S(2)}) %collective-permute-start.16) | collective-permute-done | bytes 196640 | tf_op jit(solution)/shard_map/gather_row/ppermute | solution.py:178
  142.8 3.6 %all-to-all-start.5 = ((f32[16,96,128]{2,1,0:T(8,128)}), f32[16,96,128]{2,1,0:T(8,128)S(1)}, u32[]{:S(2)}, u32[]{:S(2)}) async-start(f32[16,96,128]{2,1,0:T(8,128)} %gather_column.3), calls=%async_computation.5 | async-start | bytes 1572864 | tf_op jit(solution)/shard_map/gather_column/all_to_all | solution.py:14
  146.4 3.4 %collective-permute-start.17 = (f32[4,96,128]{2,1,0:T(8,128)}, f32[4,96,128]{2,1,0:T(8,128)S(1)}, u32[]{:S(2)}, u32[]{:S(2)}) collective-permute-start(f32[4,96,128]{2,1,0:T(8,128)} %collective-permute-done.15.second_ref), channel_id=1, source_target_pairs={{0,1},{1,0},{2,3},{3,2},{4,5},{5,4},{6,7},{7,6},{8,9},{9,8},{10,11... | collective-permute-start | bytes 589832 | tf_op jit(solution)/shard_map/gather_row/ppermute | solution.py:178
  149.8 5.7 %transposed.6.rest_0_ = f32[128,1536]{1,0:T(8,128)} custom-call(s32[9]{0:T(128)} %get-tuple-element.73.where_ref, f32[8,2,96,1536]{3,2,1,0:T(8,128)} %bitcast.81, f32[4,96,128]{2,1,0:T(8,128)} %copy-done.4, f32[4,96,128]{2,1,0:T(8,128)} %collective-permute-done.15.second_ref), custom_call_target="tpu_custom_call" | custom-call | flops 905969664 | bytes 4718592 | tf_op jit(solution)/shard_map/transposed/pallas_call | solution.py:154
  156.2 5.9 %transposed.7 = f32[1536,128]{1,0:T(8,128)} custom-call(s32[9]{0:T(128)} %get-tuple-element.74.where_ref, f32[8,2,96,1536]{3,2,1,0:T(8,128)} %bitcast.82, f32[4,96,128]{2,1,0:T(8,128)} %copy-done.6, f32[4,96,128]{2,1,0:T(8,128)} %copy-done.8, f32[128,1536]{1,0:T(8,128)} %transposed.6.rest_0_), custom_call_target="tpu_custom_call" | custom-call | flops 905969664 | bytes 4718592 | tf_op jit(solution)/shard_map/transposed/pallas_call | solution.py:154
  162.1 6.9 %all-to-all-done.5 = f32[16,96,128]{2,1,0:T(8,128)S(1)} async-done(((f32[16,96,128]{2,1,0:T(8,128)}), f32[16,96,128]{2,1,0:T(8,128)S(1)}, u32[]{:S(2)}, u32[]{:S(2)}) %all-to-all-start.5) | async-done | bytes 786464 | tf_op jit(solution)/shard_map/gather_column/all_to_all | solution.py:14
  169.0 3.6 %all-to-all-start.6 = ((f32[16,96,128]{2,1,0:T(8,128)}), f32[16,96,128]{2,1,0:T(8,128)S(1)}, u32[]{:S(2)}, u32[]{:S(2)}) async-start(f32[16,96,128]{2,1,0:T(8,128)} %bitcast.89), calls=%async_computation.6 | async-start | bytes 1572864 | tf_op jit(solution)/shard_map/back_transposed/all_to_all | solution.py:14
  172.7 5.2 %direct.7 = (f32[4,96,128]{2,1,0:T(8,128)}, f32[4,96,128]{2,1,0:T(8,128)}) custom-call(s32[9]{0:T(128)} %get-tuple-element.69.where_ref, f32[8,2,96,1536]{3,2,1,0:T(8,128)} %bitcast.83, f32[1536,128]{1,0:T(8,128)} %bitcast.87), custom_call_target="tpu_custom_call" | custom-call | flops 905969664 | bytes 4718592 | tf_op jit(solution)/shard_map/direct/pallas_call | solution.py:106
  177.9 3.3 %collective-permute-start.18 = (f32[4,96,128]{2,1,0:T(8,128)}, f32[4,96,128]{2,1,0:T(8,128)S(1)}, u32[]{:S(2)}, u32[]{:S(2)}) collective-permute-start(f32[4,96,128]{2,1,0:T(8,128)} %get-tuple-element.52), channel_id=1, source_target_pairs={{0,1},{1,0},{2,3},{3,2},{4,5},{5,4},{6,7},{7,6},{8,9},{9,8},{10,11... | collective-permute-start | bytes 589832 | tf_op jit(solution)/shard_map/direct/ppermute | solution.py:178
  183.5 5.1 %direct.6 = (f32[4,96,128]{2,1,0:T(8,128)}, f32[4,96,128]{2,1,0:T(8,128)}) custom-call(s32[9]{0:T(128)} %get-tuple-element.70.where_ref, f32[8,2,96,1536]{3,2,1,0:T(8,128)} %bitcast.84, f32[1536,128]{1,0:T(8,128)} %bitcast.88), custom_call_target="tpu_custom_call" | custom-call | flops 905969664 | bytes 4718592 | tf_op jit(solution)/shard_map/direct/pallas_call | solution.py:106
  189.1 7.2 %collective-permute-done.19 = f32[4,96,128]{2,1,0:T(8,128)S(1)} collective-permute-done((f32[4,96,128]{2,1,0:T(8,128)}, f32[4,96,128]{2,1,0:T(8,128)S(1)}, u32[]{:S(2)}, u32[]{:S(2)}) %collective-permute-start.19) | collective-permute-done | bytes 196640 | tf_op jit(solution)/shard_map/direct/ppermute | solution.py:178
  199.2 3.8 %collective-permute-done.20 = f32[4,96,128]{2,1,0:T(8,128)S(1)} collective-permute-done((f32[4,96,128]{2,1,0:T(8,128)S(1)}, f32[4,96,128]{2,1,0:T(8,128)S(1)}, u32[]{:S(2)}, u32[]{:S(2)}) %collective-permute-start.20) | collective-permute-done | bytes 196640 | tf_op jit(solution)/shard_map/direct/ppermute | solution.py:178
  204.0 1.8 back_wide.3
  205.8 5.7 %all-to-all-start.7 = ((f32[16,104,128]{2,1,0:T(8,128)}), f32[16,104,128]{2,1,0:T(8,128)S(1)}, u32[]{:S(2)}, u32[]{:S(2)}) async-start(f32[16,104,128]{2,1,0:T(8,128)} %back_wide.3), calls=%async_computation.7 | async-start | bytes 1703936 | tf_op jit(solution)/shard_map/back_wide/all_to_all | solution.py:14
  211.4 5.3 %collective-permute-start.21 = (f32[96,128]{1,0:T(8,128)S(1)}, f32[96,128]{1,0:T(8,128)S(1)}, u32[]{:S(2)}, u32[]{:S(2)}) collective-permute-start(f32[96,128]{1,0:T(8,128)S(1)} %get-tuple-element.61), channel_id=1, source_target_pairs={{0,8},{1,9},{2,10},{3,11},{4,12},{5,13},{6,14},{7,15},{8,0},{9,1},... | collective-permute-start | bytes 147464 | tf_op jit(solution)/shard_map/back_direct/ppermute | solution.py:178
  218.0 6.3 %all-to-all-done.7 = f32[16,104,128]{2,1,0:T(8,128)S(1)} async-done(((f32[16,104,128]{2,1,0:T(8,128)}), f32[16,104,128]{2,1,0:T(8,128)S(1)}, u32[]{:S(2)}, u32[]{:S(2)}) %all-to-all-start.7) | async-done | bytes 852000 | tf_op jit(solution)/shard_map/back_wide/all_to_all | solution.py:14
  224.7 9.5 %all_to_all.55 = f32[16,16,128]{2,1,0:T(8,128)S(1)} all-to-all(f32[16,16,128]{2,1,0:T(8,128)S(1)} %pad_maximum_fusion.2), channel_id=1, replica_groups=mesh['wide'=16,'narrow'=16] {'wide'}, dimensions={0} | all-to-all | bytes 262144 | tf_op jit(solution)/shard_map/gram_sum_wide/all_to_all | solution.py:14
  234.9 18.6 %all_to_all.56 = f32[16,8,128]{2,1,0:T(8,128)S(1)} all-to-all(f32[16,8,128]{2,1,0:T(8,128)S(1)} %broadcast_in_dim.25), channel_id=1, replica_groups=mesh['wide'=16,'narrow'=16] {'narrow'}, dimensions={0} | all-to-all | bytes 131072 | tf_op jit(solution)/shard_map/gram_sum_narrow/all_to_all | solution.py:14
  254.1 5.2 %all-to-all-start.10 = ((f32[16,8,128]{2,1,0:T(8,128)}), f32[16,8,128]{2,1,0:T(8,128)S(1)}, u32[]{:S(2)}, u32[]{:S(2)}) async-start(f32[16,8,128]{2,1,0:T(8,128)} %broadcast_in_dim.26), calls=%async_computation.10 | async-start | bytes 131072 | tf_op jit(solution)/shard_map/gram_whole/all_to_all | solution.py:14
  259.4 3.8 %inverse_first.1.refs_1_ = f32[128,128]{1,0:T(8,128)} custom-call(f32[128,128]{1,0:T(8,128)} %get-tuple-element.67.refs_0_), custom_call_target="tpu_custom_call" | custom-call | flops 1073741824 | bytes 1048576 | tf_op jit(solution)/shard_map/inverse_first/pallas_call | solution.py:263
  264.9 4.5 %finish.1 = f32[96,128]{1,0:T(8,128)} custom-call(f32[128,128]{1,0:T(8,128)} %bitcast.93, f32[128,128]{1,0:T(8,128)} %inverse_first.1.refs_1_, f32[96,128]{1,0:T(8,128)} %copy-done.11), custom_call_target="tpu_custom_call" | custom-call | flops 1073741824 | bytes 1048576 | tf_op jit(solution)/shard_map/finish/pallas_call | solution.py:263
  (95 shorter events, 31.9 us)
Async XLA Ops:
  1.8 28.3 %all-to-all-start = ((f32[16,96,128]{2,1,0:T(8,128)}), f32[16,96,128]{2,1,0:T(8,128)S(1)}, u32[]{:S(2)}, u32[]{:S(2)}) async-start(f32[16,96,128]{2,1,0:T(8,128)} %broadcast_in_dim.19), calls=%async_computation | async-start | bytes 1572864 | tf_op jit(solution)/shard_map/gather_wide/all_to_all | solution.py:14
  7.6 10.0 %collective-permute-start = (f32[96,128]{1,0:T(8,128)}, f32[96,128]{1,0:T(8,128)S(1)}, u32[]{:S(2)}, u32[]{:S(2)}) collective-permute-start(f32[96,128]{1,0:T(8,128)} %param.7), channel_id=1, source_target_pairs={{0,8},{1,9},{2,10},{3,11},{4,12},{5,13},{6,14},{7,15},{8,0},{9,1},... | collective-permute-start | bytes 147464 | tf_op jit(solution)/shard_map/gather_row/ppermute | solution.py:178
  14.7 6.4 %collective-permute-start.2 = (f32[96,128]{1,0:T(8,128)}, f32[96,128]{1,0:T(8,128)S(1)}, u32[]{:S(2)}, u32[]{:S(2)}) collective-permute-start(f32[96,128]{1,0:T(8,128)} %param.7), channel_id=1, source_target_pairs={{0,12},{1,13},{2,14},{3,15},{4,8},{5,9},{6,10},{7,11},{8,4},{9,5},... | collective-permute-start | bytes 147464 | tf_op jit(solution)/shard_map/gather_row/ppermute | solution.py:178
  14.7 6.4 %collective-permute-start.1 = (f32[96,128]{1,0:T(8,128)}, f32[96,128]{1,0:T(8,128)S(1)}, u32[]{:S(2)}, u32[]{:S(2)}) collective-permute-start(f32[96,128]{1,0:T(8,128)} %param.7), channel_id=1, source_target_pairs={{0,4},{1,5},{2,6},{3,7},{4,0},{5,1},{6,2},{7,3},{8,12},{9,13},{10,... | collective-permute-start | bytes 147464 | tf_op jit(solution)/shard_map/gather_row/ppermute | solution.py:178
  22.0 22.1 %copy-start.10 = (f32[4,96,128]{2,1,0:T(8,128)}, f32[4,96,128]{2,1,0:T(8,128)S(1)}, u32[]{:S(2)}) copy-start(f32[4,96,128]{2,1,0:T(8,128)S(1)} %pad_maximum_fusion.first_ref) | copy-start | bytes 589828
  22.0 7.6 %collective-permute-start.4 = (f32[4,96,128]{2,1,0:T(8,128)S(1)}, f32[4,96,128]{2,1,0:T(8,128)S(1)}, u32[]{:S(2)}, u32[]{:S(2)}) collective-permute-start(f32[4,96,128]{2,1,0:T(8,128)S(1)} %pad_maximum_fusion.first_ref), channel_id=1, source_target_pairs={{0,1},{1,0},{2,3},{3,2},{4,5},{5,4},{6,7},{7,6},{8,9},{9,8},{10,11... | collective-permute-start | bytes 589832 | tf_op jit(solution)/shard_map/gather_row/ppermute | solution.py:178
  24.4 5.7 %collective-permute-start.3 = (f32[4,96,128]{2,1,0:T(8,128)S(1)}, f32[4,96,128]{2,1,0:T(8,128)S(1)}, u32[]{:S(2)}, u32[]{:S(2)}) collective-permute-start(f32[4,96,128]{2,1,0:T(8,128)S(1)} %pad_maximum_fusion.first_ref), channel_id=1, source_target_pairs={{0,2},{1,3},{2,0},{3,1},{4,6},{5,7},{6,4},{7,5},{8,10},{9,11},{10,... | collective-permute-start | bytes 589832 | tf_op jit(solution)/shard_map/gather_row/ppermute | solution.py:178
  29.6 20.2 %copy-start.12 = (f32[4,96,128]{2,1,0:T(8,128)}, f32[4,96,128]{2,1,0:T(8,128)S(1)}, u32[]{:S(2)}) copy-start(f32[4,96,128]{2,1,0:T(8,128)S(1)} %collective-permute-done.4.first_ref) | copy-start | bytes 589828
  30.1 14.0 %copy-start.13 = (f32[4,96,128]{2,1,0:T(8,128)}, f32[4,96,128]{2,1,0:T(8,128)S(1)}, u32[]{:S(2)}) copy-start(f32[4,96,128]{2,1,0:T(8,128)S(1)} %collective-permute-done.3.second_ref) | copy-start | bytes 589828
  30.1 0.7 copy-start
  32.3 29.2 %all-to-all-start.1 = ((f32[16,96,128]{2,1,0:T(8,128)}), f32[16,96,128]{2,1,0:T(8,128)S(1)}, u32[]{:S(2)}, u32[]{:S(2)}) async-start(f32[16,96,128]{2,1,0:T(8,128)} %gather_column.2), calls=%async_computation.1 | async-start | bytes 1572864 | tf_op jit(solution)/shard_map/gather_column/all_to_all | solution.py:14
  40.1 9.7 %collective-permute-start.5 = (f32[4,96,128]{2,1,0:T(8,128)S(1)}, f32[4,96,128]{2,1,0:T(8,128)S(1)}, u32[]{:S(2)}, u32[]{:S(2)}) collective-permute-start(f32[4,96,128]{2,1,0:T(8,128)S(1)} %collective-permute-done.3.second_ref), channel_id=1, source_target_pairs={{0,1},{1,0},{2,3},{3,2},{4,5},{5,4},{6,7},{7,6},{8,9},{9,8},{10,11... | collective-permute-start | bytes 589832 | tf_op jit(solution)/shard_map/gather_row/ppermute | solution.py:178
  49.8 0.7 copy-start.14
  61.5 5.2 %copy-start.2 = (f32[16,96,128]{2,1,0:T(8,128)}, f32[16,96,128]{2,1,0:T(8,128)S(1)}, u32[]{:S(2)}) copy-start(f32[16,96,128]{2,1,0:T(8,128)S(1)} %all-to-all-done.1) | copy-start | bytes 2359300
  61.5 31.6 %all-to-all-start.2 = ((f32[16,96,128]{2,1,0:T(8,128)}), f32[16,96,128]{2,1,0:T(8,128)S(1)}, u32[]{:S(2)}, u32[]{:S(2)}) async-start(f32[16,96,128]{2,1,0:T(8,128)} %bitcast.90), calls=%async_computation.2 | async-start | bytes 1572864 | tf_op jit(solution)/shard_map/back_transposed/all_to_all | solution.py:14
  66.8 26.4 %copy-start.1 = (s32[1,16]{1,0:T(1,128)S(1)}, s32[1,16]{1,0:T(1,128)}, u32[]{:S(2)}) copy-start(s32[1,16]{1,0:T(1,128)} %param.6) | copy-start | bytes 196
  72.0 13.5 %collective-permute-start.7 = (f32[4,96,128]{2,1,0:T(8,128)}, f32[4,96,128]{2,1,0:T(8,128)S(1)}, u32[]{:S(2)}, u32[]{:S(2)}) collective-permute-start(f32[4,96,128]{2,1,0:T(8,128)} %get-tuple-element.42), channel_id=1, source_target_pairs={{0,1},{1,0},{2,3},{3,2},{4,5},{5,4},{6,7},{7,6},{8,9},{9,8},{10,11... | collective-permute-start | bytes 589832 | tf_op jit(solution)/shard_map/direct/ppermute | solution.py:178
  75.4 13.0 %collective-permute-start.6 = (f32[4,96,128]{2,1,0:T(8,128)}, f32[4,96,128]{2,1,0:T(8,128)S(1)}, u32[]{:S(2)}, u32[]{:S(2)}) collective-permute-start(f32[4,96,128]{2,1,0:T(8,128)} %get-tuple-element.40), channel_id=1, source_target_pairs={{0,1},{1,0},{2,3},{3,2},{4,5},{5,4},{6,7},{7,6},{8,9},{9,8},{10,11... | collective-permute-start | bytes 589832 | tf_op jit(solution)/shard_map/direct/ppermute | solution.py:178
  86.4 5.8 %collective-permute-start.8 = (f32[4,96,128]{2,1,0:T(8,128)S(1)}, f32[4,96,128]{2,1,0:T(8,128)S(1)}, u32[]{:S(2)}, u32[]{:S(2)}) collective-permute-start(f32[4,96,128]{2,1,0:T(8,128)S(1)} %add.52), channel_id=1, source_target_pairs={{0,2},{1,3},{2,0},{3,1},{4,6},{5,7},{6,4},{7,5},{8,10},{9,11},{10,... | collective-permute-start | bytes 589832 | tf_op jit(solution)/shard_map/direct/ppermute | solution.py:178
  94.8 17.9 %all-to-all-start.3 = ((f32[16,96,128]{2,1,0:T(8,128)}), f32[16,96,128]{2,1,0:T(8,128)S(1)}, u32[]{:S(2)}, u32[]{:S(2)}) async-start(f32[16,96,128]{2,1,0:T(8,128)} %back_wide.2), calls=%async_computation.3 | async-start | bytes 1572864 | tf_op jit(solution)/shard_map/back_wide/all_to_all | solution.py:14
  100.5 12.2 %collective-permute-start.9 = (f32[96,128]{1,0:T(8,128)S(1)}, f32[96,128]{1,0:T(8,128)S(1)}, u32[]{:S(2)}, u32[]{:S(2)}) collective-permute-start(f32[96,128]{1,0:T(8,128)S(1)} %get-tuple-element.64), channel_id=1, source_target_pairs={{0,8},{1,9},{2,10},{3,11},{4,12},{5,13},{6,14},{7,15},{8,0},{9,1},... | collective-permute-start | bytes 147464 | tf_op jit(solution)/shard_map/back_direct/ppermute | solution.py:178
  106.2 6.5 %collective-permute-start.11 = (f32[96,128]{1,0:T(8,128)S(1)}, f32[96,128]{1,0:T(8,128)S(1)}, u32[]{:S(2)}, u32[]{:S(2)}) collective-permute-start(f32[96,128]{1,0:T(8,128)S(1)} %get-tuple-element.65), channel_id=1, source_target_pairs={{0,12},{1,13},{2,14},{3,15},{4,8},{5,9},{6,10},{7,11},{8,4},{9,5},... | collective-permute-start | bytes 147464 | tf_op jit(solution)/shard_map/back_direct/ppermute | solution.py:178
  106.5 6.2 %collective-permute-start.10 = (f32[96,128]{1,0:T(8,128)S(1)}, f32[96,128]{1,0:T(8,128)S(1)}, u32[]{:S(2)}, u32[]{:S(2)}) collective-permute-start(f32[96,128]{1,0:T(8,128)S(1)} %get-tuple-element.66), channel_id=1, source_target_pairs={{0,4},{1,5},{2,6},{3,7},{4,0},{5,1},{6,2},{7,3},{8,12},{9,13},{10,... | collective-permute-start | bytes 147464 | tf_op jit(solution)/shard_map/back_direct/ppermute | solution.py:178
  113.7 27.5 %all-to-all-start.4 = ((f32[16,96,128]{2,1,0:T(8,128)}), f32[16,96,128]{2,1,0:T(8,128)S(1)}, u32[]{:S(2)}, u32[]{:S(2)}) async-start(f32[16,96,128]{2,1,0:T(8,128)} %broadcast_in_dim.22), calls=%async_computation.4 | async-start | bytes 1572864 | tf_op jit(solution)/shard_map/gather_wide/all_to_all | solution.py:14
  119.3 6.5 %collective-permute-start.14 = (f32[96,128]{1,0:T(8,128)S(1)}, f32[96,128]{1,0:T(8,128)S(1)}, u32[]{:S(2)}, u32[]{:S(2)}) collective-permute-start(f32[96,128]{1,0:T(8,128)S(1)} %fusion.7), channel_id=1, source_target_pairs={{0,12},{1,13},{2,14},{3,15},{4,8},{5,9},{6,10},{7,11},{8,4},{9,5},... | collective-permute-start | bytes 147464 | tf_op jit(solution)/shard_map/gather_row/ppermute | solution.py:178
  123.1 5.2 %collective-permute-start.13 = (f32[96,128]{1,0:T(8,128)S(1)}, f32[96,128]{1,0:T(8,128)S(1)}, u32[]{:S(2)}, u32[]{:S(2)}) collective-permute-start(f32[96,128]{1,0:T(8,128)S(1)} %fusion.7), channel_id=1, source_target_pairs={{0,4},{1,5},{2,6},{3,7},{4,0},{5,1},{6,2},{7,3},{8,12},{9,13},{10,... | collective-permute-start | bytes 147464 | tf_op jit(solution)/shard_map/gather_row/ppermute | solution.py:178
  125.0 8.4 %collective-permute-start.12 = (f32[96,128]{1,0:T(8,128)S(1)}, f32[96,128]{1,0:T(8,128)S(1)}, u32[]{:S(2)}, u32[]{:S(2)}) collective-permute-start(f32[96,128]{1,0:T(8,128)S(1)} %fusion.7), channel_id=1, source_target_pairs={{0,8},{1,9},{2,10},{3,11},{4,12},{5,13},{6,14},{7,15},{8,0},{9,1},... | collective-permute-start | bytes 147464 | tf_op jit(solution)/shard_map/gather_row/ppermute | solution.py:178
  133.4 16.5 %copy-start.4 = (f32[4,96,128]{2,1,0:T(8,128)}, f32[4,96,128]{2,1,0:T(8,128)S(1)}, u32[]{:S(2)}) copy-start(f32[4,96,128]{2,1,0:T(8,128)S(1)} %pad_maximum_fusion.1.first_ref) | copy-start | bytes 589828
  133.4 7.3 %collective-permute-start.16 = (f32[4,96,128]{2,1,0:T(8,128)S(1)}, f32[4,96,128]{2,1,0:T(8,128)S(1)}, u32[]{:S(2)}, u32[]{:S(2)}) collective-permute-start(f32[4,96,128]{2,1,0:T(8,128)S(1)} %pad_maximum_fusion.1.first_ref), channel_id=1, source_target_pairs={{0,1},{1,0},{2,3},{3,2},{4,5},{5,4},{6,7},{7,6},{8,9},{9,8},{10,11... | collective-permute-start | bytes 589832 | tf_op jit(solution)/shard_map/gather_row/ppermute | solution.py:178
  135.4 5.8 %collective-permute-start.15 = (f32[4,96,128]{2,1,0:T(8,128)S(1)}, f32[4,96,128]{2,1,0:T(8,128)}, u32[]{:S(2)}, u32[]{:S(2)}) collective-permute-start(f32[4,96,128]{2,1,0:T(8,128)S(1)} %pad_maximum_fusion.1.first_ref), channel_id=1, source_target_pairs={{0,2},{1,3},{2,0},{3,1},{4,6},{5,7},{6,4},{7,5},{8,10},{9,11},{10,... | collective-permute-start | bytes 589832 | tf_op jit(solution)/shard_map/gather_row/ppermute | solution.py:178
  140.6 14.9 %copy-start.6 = (f32[4,96,128]{2,1,0:T(8,128)}, f32[4,96,128]{2,1,0:T(8,128)S(1)}, u32[]{:S(2)}) copy-start(f32[4,96,128]{2,1,0:T(8,128)S(1)} %collective-permute-done.16.first_ref) | copy-start | bytes 589828
  142.8 26.2 %all-to-all-start.5 = ((f32[16,96,128]{2,1,0:T(8,128)}), f32[16,96,128]{2,1,0:T(8,128)S(1)}, u32[]{:S(2)}, u32[]{:S(2)}) async-start(f32[16,96,128]{2,1,0:T(8,128)} %gather_column.3), calls=%async_computation.5 | async-start | bytes 1572864 | tf_op jit(solution)/shard_map/gather_column/all_to_all | solution.py:14
  146.4 9.1 %collective-permute-start.17 = (f32[4,96,128]{2,1,0:T(8,128)}, f32[4,96,128]{2,1,0:T(8,128)S(1)}, u32[]{:S(2)}, u32[]{:S(2)}) collective-permute-start(f32[4,96,128]{2,1,0:T(8,128)} %collective-permute-done.15.second_ref), channel_id=1, source_target_pairs={{0,1},{1,0},{2,3},{3,2},{4,5},{5,4},{6,7},{7,6},{8,9},{9,8},{10,11... | collective-permute-start | bytes 589832 | tf_op jit(solution)/shard_map/gather_row/ppermute | solution.py:178
  155.5 0.7 copy-start.8
  162.1 20.8 %copy-start.7 = (f32[4,96,128]{2,1,0:T(8,128)S(1)}, f32[4,96,128]{2,1,0:T(8,128)}, u32[]{:S(2)}) copy-start(f32[4,96,128]{2,1,0:T(8,128)} %copy-done.6) | copy-start | bytes 589828
  169.0 3.6 %copy-start.3 = (f32[16,96,128]{2,1,0:T(8,128)}, f32[16,96,128]{2,1,0:T(8,128)S(1)}, u32[]{:S(2)}) copy-start(f32[16,96,128]{2,1,0:T(8,128)S(1)} %all-to-all-done.5) | copy-start | bytes 2359300
  169.0 35.0 %all-to-all-start.6 = ((f32[16,96,128]{2,1,0:T(8,128)}), f32[16,96,128]{2,1,0:T(8,128)S(1)}, u32[]{:S(2)}, u32[]{:S(2)}) async-start(f32[16,96,128]{2,1,0:T(8,128)} %bitcast.89), calls=%async_computation.6 | async-start | bytes 1572864 | tf_op jit(solution)/shard_map/back_transposed/all_to_all | solution.py:14
  172.7 15.9 %copy-start.9 = (f32[4,96,128]{2,1,0:T(8,128)S(1)}, f32[4,96,128]{2,1,0:T(8,128)}, u32[]{:S(2)}) copy-start(f32[4,96,128]{2,1,0:T(8,128)} %copy-done.8) | copy-start | bytes 589828
  172.7 26.0 %copy-start.5 = (f32[4,96,128]{2,1,0:T(8,128)S(1)}, f32[4,96,128]{2,1,0:T(8,128)}, u32[]{:S(2)}) copy-start(f32[4,96,128]{2,1,0:T(8,128)} %copy-done.4) | copy-start | bytes 589828
  177.9 21.3 %collective-permute-start.18 = (f32[4,96,128]{2,1,0:T(8,128)}, f32[4,96,128]{2,1,0:T(8,128)S(1)}, u32[]{:S(2)}, u32[]{:S(2)}) collective-permute-start(f32[4,96,128]{2,1,0:T(8,128)} %get-tuple-element.52), channel_id=1, source_target_pairs={{0,1},{1,0},{2,3},{3,2},{4,5},{5,4},{6,7},{7,6},{8,9},{9,8},{10,11... | collective-permute-start | bytes 589832 | tf_op jit(solution)/shard_map/direct/ppermute | solution.py:178
  181.2 15.1 %collective-permute-start.19 = (f32[4,96,128]{2,1,0:T(8,128)}, f32[4,96,128]{2,1,0:T(8,128)S(1)}, u32[]{:S(2)}, u32[]{:S(2)}) collective-permute-start(f32[4,96,128]{2,1,0:T(8,128)} %get-tuple-element.54), channel_id=1, source_target_pairs={{0,1},{1,0},{2,3},{3,2},{4,5},{5,4},{6,7},{7,6},{8,9},{9,8},{10,11... | collective-permute-start | bytes 589832 | tf_op jit(solution)/shard_map/direct/ppermute | solution.py:178
  197.2 5.8 %collective-permute-start.20 = (f32[4,96,128]{2,1,0:T(8,128)S(1)}, f32[4,96,128]{2,1,0:T(8,128)S(1)}, u32[]{:S(2)}, u32[]{:S(2)}) collective-permute-start(f32[4,96,128]{2,1,0:T(8,128)S(1)} %add.59), channel_id=1, source_target_pairs={{0,2},{1,3},{2,0},{3,1},{4,6},{5,7},{6,4},{7,5},{8,10},{9,11},{10,... | collective-permute-start | bytes 589832 | tf_op jit(solution)/shard_map/direct/ppermute | solution.py:178
  205.8 18.5 %all-to-all-start.7 = ((f32[16,104,128]{2,1,0:T(8,128)}), f32[16,104,128]{2,1,0:T(8,128)S(1)}, u32[]{:S(2)}, u32[]{:S(2)}) async-start(f32[16,104,128]{2,1,0:T(8,128)} %back_wide.3), calls=%async_computation.7 | async-start | bytes 1703936 | tf_op jit(solution)/shard_map/back_wide/all_to_all | solution.py:14
  211.4 12.9 %collective-permute-start.21 = (f32[96,128]{1,0:T(8,128)S(1)}, f32[96,128]{1,0:T(8,128)S(1)}, u32[]{:S(2)}, u32[]{:S(2)}) collective-permute-start(f32[96,128]{1,0:T(8,128)S(1)} %get-tuple-element.61), channel_id=1, source_target_pairs={{0,8},{1,9},{2,10},{3,11},{4,12},{5,13},{6,14},{7,15},{8,0},{9,1},... | collective-permute-start | bytes 147464 | tf_op jit(solution)/shard_map/back_direct/ppermute | solution.py:178
  216.7 7.7 %collective-permute-start.23 = (f32[96,128]{1,0:T(8,128)S(1)}, f32[96,128]{1,0:T(8,128)S(1)}, u32[]{:S(2)}, u32[]{:S(2)}) collective-permute-start(f32[96,128]{1,0:T(8,128)S(1)} %get-tuple-element.62), channel_id=1, source_target_pairs={{0,12},{1,13},{2,14},{3,15},{4,8},{5,9},{6,10},{7,11},{8,4},{9,5},... | collective-permute-start | bytes 147464 | tf_op jit(solution)/shard_map/back_direct/ppermute | solution.py:178
  217.1 7.3 %collective-permute-start.22 = (f32[96,128]{1,0:T(8,128)S(1)}, f32[96,128]{1,0:T(8,128)S(1)}, u32[]{:S(2)}, u32[]{:S(2)}) collective-permute-start(f32[96,128]{1,0:T(8,128)S(1)} %get-tuple-element.63), channel_id=1, source_target_pairs={{0,4},{1,5},{2,6},{3,7},{4,0},{5,1},{6,2},{7,3},{8,12},{9,13},{10,... | collective-permute-start | bytes 147464 | tf_op jit(solution)/shard_map/back_direct/ppermute | solution.py:178
  224.4 39.9 %copy-start.11 = (f32[96,128]{1,0:T(8,128)}, f32[96,128]{1,0:T(8,128)S(1)}, u32[]{:S(2)}) copy-start(f32[96,128]{1,0:T(8,128)S(1)} %slice_add_fusion.refs_2_) | copy-start | bytes 147460
  254.1 10.2 %all-to-all-start.10 = ((f32[16,8,128]{2,1,0:T(8,128)}), f32[16,8,128]{2,1,0:T(8,128)S(1)}, u32[]{:S(2)}, u32[]{:S(2)}) async-start(f32[16,8,128]{2,1,0:T(8,128)} %broadcast_in_dim.26), calls=%async_computation.10 | async-start | bytes 131072 | tf_op jit(solution)/shard_map/gram_whole/all_to_all | solution.py:14
  (1 other events, 0.6 us)

commit v5 on v4

--- a/solution.py
+++ b/solution.py
@@ -72,13 +72,13 @@
     return pl.CostEstimate(flops=3 * tile.size * width, bytes_accessed=2 * tile.size, transcendentals=0)
 
 
-def direct_half(tile, column_block, half, places):
-    groups, _, rows, order = tile.shape
+def direct_quarters(tile, column_block, quarters, places):
+    each, _, _, rows, order = tile.shape
     width = column_block.shape[1]
-    steps = 2
-    each = groups // steps
-
-    def kernel(where_ref, tile_ref, column_ref, first_ref, second_ref, both):
+    steps = len(quarters)
+
+    def kernel(where_ref, tile_ref, column_ref, *rest):
+        out_refs, both = rest[:-1], rest[-1]
         step = pl.program_id(0)
 
         @pl.when(step == 0)
@@ -90,35 +90,35 @@
         high, low = high_low(tile_ref[...].reshape(each * rows, order))
         wide = product_of(high, both[...])
         total = wide[:, :width] + wide[:, width:] + product_of(low, both[:, :width])
-        for k in range(each):
-            place = where_ref[1 + step * each + k]
-            part = total[k * rows : (k + 1) * rows]
-
-            @pl.when(place < each)
+        for g, out_ref in enumerate(out_refs):
+
+            @pl.when(step == g)
             def _():
-                first_ref[place] = part
-
-            @pl.when(place >= each)
-            def _():
-                second_ref[place - each] = part
-
-    out = jax.ShapeDtypeStruct((each, rows, width), jnp.float32)
+                for k in range(each):
+                    out_ref[where_ref[2 * steps + k]] = total[k * rows : (k + 1) * rows]
+
     return pl.pallas_call(
         kernel,
-        out_shape=(out, out),
+        out_shape=[jax.ShapeDtypeStruct((each, rows, width), jnp.float32)] * steps,
         grid_spec=pltpu.PrefetchScalarGridSpec(
             num_scalar_prefetch=1,
             grid=(steps,),
             in_specs=[
-                pl.BlockSpec((each, 1, rows, order), lambda g, where: (g, where[0], 0, 0)),
+                pl.BlockSpec(
+                    (each, 1, 1, rows, order), lambda g, where: (0, where[2 * g], where[2 * g + 1], 0, 0)
+                ),
                 pl.BlockSpec((order, width), lambda g, where: (0, 0)),
             ],
-            out_specs=[pl.BlockSpec((each, rows, width), lambda g, where: (0, 0, 0))] * 2,
+            out_specs=[pl.BlockSpec((each, rows, width), lambda g, where: (0, 0, 0))] * steps,
             scratch_shapes=[pltpu.VMEM((order, 2 * width), jnp.bfloat16)],
         ),
         compiler_params=pltpu.CompilerParams(vmem_limit_bytes=60 << 20),
-        cost_estimate=kernel_cost(tile, width),
-    )(jnp.concatenate([half[None], places]), tile, column_block)
+        cost_estimate=pl.CostEstimate(
+            flops=3 * steps * each * rows * order * width,
+            bytes_accessed=4 * steps * each * rows * order,
+            transcendentals=0,
+        ),
+    )(jnp.concatenate([jnp.stack([bit for pair in quarters for bit in pair]), places]), tile, column_block)
 
 
 def transposed_half(tile, quarters, half, spots, partial=None):
@@ -180,10 +180,7 @@
 
 ENTRIES = (8, 4, 12)
 REVERSED = (0, 4, 2, 6, 1, 5, 3, 7)
-
-
-def reversed_bits(value):
-    return ((value & 1) << 2) | (value & 2) | (value >> 2)
+REVERSED_PAIR = (0, 2, 1, 3)
 
 
 def summed_part(kept):
@@ -201,7 +198,7 @@
     me = lax.axis_index(NARROW).astype(jnp.int32)
     near, far = me & 1, (me & 1) ^ 1
     table = jnp.array(REVERSED, jnp.int32)
-    spots, places = table ^ (me >> 1), table ^ reversed_bits(me >> 1)
+    spots = table ^ (me >> 1)
     tile = tile.reshape(groups, 2, rows, order)
     with jax.named_scope("gather_wide"):
         slices = to_everyone(vectors, WIDE)
@@ -220,15 +217,25 @@
     with jax.named_scope("back_transposed"):
         arrived = exchange(transposed.reshape(count, rows, width), NARROW)
     with jax.named_scope("direct"):
-        far_first, far_second = direct_half(tile, column_block, far, places)
-        got_second, got_first = swap(far_second, 1), swap(far_first, 1)
-        near_first, near_second = direct_half(tile, column_block, near, places)
+        quarters = tile.reshape(groups // 2, 2, 2, rows, order)
+        first, second = (me >> 1) & 1, ((me >> 1) & 1) ^ 1
+        high_bits = me >> 2
+        places = jnp.array(REVERSED_PAIR, jnp.int32) ^ ((high_bits & 1) << 1 | high_bits >> 1)
+        (far_second,) = direct_quarters(quarters, column_block, [(second, far)], places)
+        column_block, far_second = lax.optimization_barrier((column_block, far_second))
+        got_second = swap(far_second, 1)
+        far_first, near_second = direct_quarters(
+            quarters, column_block, [(first, far), (second, near)], places
+        )
+        column_block, far_first = lax.optimization_barrier((column_block, far_first))
+        got_first = swap(far_first, 1)
+        (near_first,) = direct_quarters(quarters, column_block, [(first, near)], places)
         kept = near_first + got_first + swap(near_second + got_second, 2)
         arrived, kept = lax.optimization_barrier((arrived, kept))
     gram = None
     if want_gram:
         with jax.named_scope("gram_block_row"):
-            block, _ = lax.optimization_barrier((near_rows + far_rows, far_first))
+            block, _ = lax.optimization_barrier((near_rows + far_rows, near_first))
             gram = sum(gram_of(quarter.reshape(-1, width)) for quarter in block)
     with jax.named_scope("back_direct"):
         direct_sum = summed_part(kept)

time: 273 us -> 269 us (0.985)
  waiting for transfers between devices: 66.1 us -> 54.8 us
  Pallas kernels: 58.8 us -> 64.7 us
    ppermute x24, waiting for transfers between devices: 41.3 us -> 30.1 us  [swap(): return lax.ppermute(value, NARROW, [(i, i ^ mask) for i in range(size)])]
    pallas_call x4 -> x6, Pallas kernels: 20.7 us -> 26.5 us  [direct_quarters(): pl.pallas_call(kernel, out_shape=[jax.ShapeDtypeStruct((each, rows, width...]
  transfers between devices with their start and end apart: 33 -> 33, of which waited for: 17 -> 17; matrix products, arithmetic and copies ran while one was open for 4% -> 3% of each run, Pallas kernels for 18% -> 20%
where the time goes in v5:
time: 269 us; the launch traced here: 265 us
  starting transfers between devices  101 us (38%)
  Pallas kernels  64.7 us (24%)
  waiting for transfers between devices  54.8 us (20%)
  blocking collectives  28.3 us (11%)
  local copies, waits for them, and re-layouts  6.86 us (3%)
  other arithmetic  6.5 us (2%)
    ppermute x24, starting transfers between devices, swap(): return lax.ppermute(value, NARROW, [(i, i ^ mask) for i in range(size)])  53.1 us
    all_to_all x9, starting transfers between devices, exchange(): return lax.all_to_all(parts, axis, 0, 0, tiled=True)  48.2 us
    ppermute x24, waiting for transfers between devices, swap(): return lax.ppermute(value, NARROW, [(i, i ^ mask) for i in range(size)])  30.1 us
    all_to_all x2, blocking collectives, exchange(): return lax.all_to_all(parts, axis, 0, 0, tiled=True)  28.3 us
    pallas_call x6, Pallas kernels, direct_quarters(): pl.pallas_call(kernel, out_shape=[jax.ShapeDtypeStruct((each, rows, width...  26.5 us
    all_to_all x9, waiting for transfers between devices, exchange(): return lax.all_to_all(parts, axis, 0, 0, tiled=True)  24.7 us
    pallas_call x4, Pallas kernels, transposed_half(): pl.pallas_call(kernel, out_shape=jax.ShapeDtypeStruct((width, order) if p...  23.3 us
    pallas_call x2, Pallas kernels, in_kernel(): pl.pallas_call(kernel, out_shape=jax.ShapeDtypeStruct(shape, jnp.float32)...  8.37 us
  transfers between devices with their start and end apart: 33, of which 17 were waited for; matrix products, arithmetic and copies ran while one was open for 3% of the time, Pallas kernels for 20%

profile of v5, /device:TPU:8, one launch (start us, length us, event | category | flops | bytes accessed | tf_op | source)
XLA Modules:
  0.0 264.9 jit_solution(12476693576855316430)
XLA Ops:
  0.0 1.8 broadcast_in_dim.19
  1.8 5.8 %all-to-all-start = ((f32[16,96,128]{2,1,0:T(8,128)}), f32[16,96,128]{2,1,0:T(8,128)S(1)}, u32[]{:S(2)}, u32[]{:S(2)}) async-start(f32[16,96,128]{2,1,0:T(8,128)} %broadcast_in_dim.19), calls=%async_computation | async-start | bytes 1572864 | tf_op jit(solution)/shard_map/gather_wide/all_to_all | solution.py:14
  7.6 7.2 %collective-permute-start = (f32[96,128]{1,0:T(8,128)}, f32[96,128]{1,0:T(8,128)S(1)}, u32[]{:S(2)}, u32[]{:S(2)}) collective-permute-start(f32[96,128]{1,0:T(8,128)} %param.9), channel_id=1, source_target_pairs={{0,8},{1,9},{2,10},{3,11},{4,12},{5,13},{6,14},{7,15},{8,0},{9,1},... | collective-permute-start | bytes 147464 | tf_op jit(solution)/shard_map/gather_row/ppermute | solution.py:178
  17.6 3.6 %collective-permute-done.2 = f32[96,128]{1,0:T(8,128)S(1)} collective-permute-done((f32[96,128]{1,0:T(8,128)}, f32[96,128]{1,0:T(8,128)S(1)}, u32[]{:S(2)}, u32[]{:S(2)}) %collective-permute-start.2) | collective-permute-done | bytes 49184 | tf_op jit(solution)/shard_map/gather_row/ppermute | solution.py:178
  22.0 2.4 collective-permute-start.4
  25.9 3.6 %collective-permute-done.4.first_ref = f32[4,96,128]{2,1,0:T(8,128)S(1)} collective-permute-done((f32[4,96,128]{2,1,0:T(8,128)S(1)}, f32[4,96,128]{2,1,0:T(8,128)S(1)}, u32[]{:S(2)}, u32[]{:S(2)}) %collective-permute-start.4) | collective-permute-done | bytes 196640 | tf_op jit(solution)/shard_map/gather_row/ppermute | solution.py:178
  32.3 7.1 %all-to-all-start.1 = ((f32[16,96,128]{2,1,0:T(8,128)}), f32[16,96,128]{2,1,0:T(8,128)S(1)}, u32[]{:S(2)}, u32[]{:S(2)}) async-start(f32[16,96,128]{2,1,0:T(8,128)} %gather_column.2), calls=%async_computation.1 | async-start | bytes 1572864 | tf_op jit(solution)/shard_map/gather_column/all_to_all | solution.py:14
  40.1 3.4 %collective-permute-start.5 = (f32[4,96,128]{2,1,0:T(8,128)S(1)}, f32[4,96,128]{2,1,0:T(8,128)S(1)}, u32[]{:S(2)}, u32[]{:S(2)}) collective-permute-start(f32[4,96,128]{2,1,0:T(8,128)S(1)} %collective-permute-done.3.second_ref), channel_id=1, source_target_pairs={{0,1},{1,0},{2,3},{3,2},{4,5},{5,4},{6,7},{7,6},{8,9},{9,8},{10,11... | collective-permute-start | bytes 589832 | tf_op jit(solution)/shard_map/gather_row/ppermute | solution.py:178
  44.2 5.8 %transposed.4.rest_0_ = f32[128,1536]{1,0:T(8,128)} custom-call(s32[9]{0:T(128)} %get-tuple-element.79.where_ref, f32[8,2,96,1536]{3,2,1,0:T(8,128)} %bitcast.80, f32[4,96,128]{2,1,0:T(8,128)} %copy-done.12, f32[4,96,128]{2,1,0:T(8,128)} %copy-done.16), custom_call_target="tpu_custom_call" | custom-call | flops 905969664 | bytes 4718592 | tf_op jit(solution)/shard_map/transposed/pallas_call | solution.py:154
  50.7 5.9 %transposed.5 = f32[1536,128]{1,0:T(8,128)} custom-call(s32[9]{0:T(128)} %get-tuple-element.80.where_ref, f32[8,2,96,1536]{3,2,1,0:T(8,128)} %bitcast.81, f32[4,96,128]{2,1,0:T(8,128)} %copy-done.15, f32[4,96,128]{2,1,0:T(8,128)} %copy-done.17, f32[128,1536]{1,0:T(8,128)} %transposed.4.rest_0_), custom_call_target="tpu_custom_call" | custom-call | flops 905969664 | bytes 4718592 | tf_op jit(solution)/shard_map/transposed/pallas_call | solution.py:154
  56.6 4.9 %all-to-all-done.1 = f32[16,96,128]{2,1,0:T(8,128)S(1)} async-done(((f32[16,96,128]{2,1,0:T(8,128)}), f32[16,96,128]{2,1,0:T(8,128)S(1)}, u32[]{:S(2)}, u32[]{:S(2)}) %all-to-all-start.1) | async-done | bytes 786464 | tf_op jit(solution)/shard_map/gather_column/all_to_all | solution.py:14
  61.5 4.6 %all-to-all-start.2 = ((f32[16,96,128]{2,1,0:T(8,128)}), f32[16,96,128]{2,1,0:T(8,128)S(1)}, u32[]{:S(2)}, u32[]{:S(2)}) async-start(f32[16,96,128]{2,1,0:T(8,128)} %bitcast.96), calls=%async_computation.2 | async-start | bytes 1572864 | tf_op jit(solution)/shard_map/back_transposed/all_to_all | solution.py:14
  66.8 4.0 %direct.6 = f32[4,96,128]{2,1,0:T(8,128)} custom-call(s32[6]{0:T(128)} %get-tuple-element.78.where_ref, f32[4,2,2,96,1536]{4,3,2,1,0:T(8,128)} %bitcast.82, f32[1536,128]{1,0:T(8,128)} %bitcast.90), custom_call_target="tpu_custom_call" | custom-call | flops 226492416 | bytes 2359296 | tf_op jit(solution)/shard_map/direct/pallas_call | solution.py:100
  70.8 3.4 %collective-permute-start.7 = (f32[4,96,128]{2,1,0:T(8,128)}, f32[4,96,128]{2,1,0:T(8,128)S(1)}, u32[]{:S(2)}, u32[]{:S(2)}) collective-permute-start(f32[4,96,128]{2,1,0:T(8,128)} %direct.6), channel_id=1, source_target_pairs={{0,1},{1,0},{2,3},{3,2},{4,5},{5,4},{6,7},{7,6},{8,9},{9,8},{10,11... | collective-permute-start | bytes 589832 | tf_op jit(solution)/shard_map/direct/ppermute | solution.py:178
  74.9 5.2 %direct.7 = (f32[4,96,128]{2,1,0:T(8,128)}, f32[4,96,128]{2,1,0:T(8,128)}) custom-call(s32[8]{0:T(128)} %concatenate.38.where_ref, f32[4,2,2,96,1536]{4,3,2,1,0:T(8,128)} %bitcast.83, f32[1536,128]{1,0:T(8,128)} %bitcast.91), custom_call_target="tpu_custom_call" | custom-call | flops 452984832 | bytes 4718592 | tf_op jit(solution)/shard_map/direct/pallas_call | solution.py:100
  80.2 3.2 %collective-permute-done.7 = f32[4,96,128]{2,1,0:T(8,128)S(1)} collective-permute-done((f32[4,96,128]{2,1,0:T(8,128)}, f32[4,96,128]{2,1,0:T(8,128)S(1)}, u32[]{:S(2)}, u32[]{:S(2)}) %collective-permute-start.7) | collective-permute-done | bytes 196640 | tf_op jit(solution)/shard_map/direct/ppermute | solution.py:178
  85.2 4.0 %direct.8 = f32[4,96,128]{2,1,0:T(8,128)} custom-call(s32[6]{0:T(128)} %get-tuple-element.77.where_ref, f32[4,2,2,96,1536]{4,3,2,1,0:T(8,128)} %bitcast.84, f32[1536,128]{1,0:T(8,128)} %bitcast.92), custom_call_target="tpu_custom_call" | custom-call | flops 226492416 | bytes 2359296 | tf_op jit(solution)/shard_map/direct/pallas_call | solution.py:100
  92.8 5.7 %all-to-all-start.3 = ((f32[16,96,128]{2,1,0:T(8,128)}), f32[16,96,128]{2,1,0:T(8,128)S(1)}, u32[]{:S(2)}, u32[]{:S(2)}) async-start(f32[16,96,128]{2,1,0:T(8,128)} %back_wide.2), calls=%async_computation.3 | async-start | bytes 1572864 | tf_op jit(solution)/shard_map/back_wide/all_to_all | solution.py:14
  98.5 5.7 %collective-permute-start.9 = (f32[96,128]{1,0:T(8,128)S(1)}, f32[96,128]{1,0:T(8,128)S(1)}, u32[]{:S(2)}, u32[]{:S(2)}) collective-permute-start(f32[96,128]{1,0:T(8,128)S(1)} %get-tuple-element.72), channel_id=1, source_target_pairs={{0,8},{1,9},{2,10},{3,11},{4,12},{5,13},{6,14},{7,15},{8,0},{9,1},... | collective-permute-start | bytes 147464 | tf_op jit(solution)/shard_map/back_direct/ppermute | solution.py:178
  105.2 5.5 %all-to-all-done.3 = f32[16,96,128]{2,1,0:T(8,128)S(1)} async-done(((f32[16,96,128]{2,1,0:T(8,128)}), f32[16,96,128]{2,1,0:T(8,128)S(1)}, u32[]{:S(2)}, u32[]{:S(2)}) %all-to-all-start.3) | async-done | bytes 786464 | tf_op jit(solution)/shard_map/back_wide/all_to_all | solution.py:14
  111.9 5.7 %all-to-all-start.4 = ((f32[16,96,128]{2,1,0:T(8,128)}), f32[16,96,128]{2,1,0:T(8,128)S(1)}, u32[]{:S(2)}, u32[]{:S(2)}) async-start(f32[16,96,128]{2,1,0:T(8,128)} %broadcast_in_dim.22), calls=%async_computation.4 | async-start | bytes 1572864 | tf_op jit(solution)/shard_map/gather_wide/all_to_all | solution.py:14
  117.6 3.4 %collective-permute-start.14 = (f32[96,128]{1,0:T(8,128)S(1)}, f32[96,128]{1,0:T(8,128)S(1)}, u32[]{:S(2)}, u32[]{:S(2)}) collective-permute-start(f32[96,128]{1,0:T(8,128)S(1)} %fusion.7), channel_id=1, source_target_pairs={{0,12},{1,13},{2,14},{3,15},{4,8},{5,9},{6,10},{7,11},{8,4},{9,5},... | collective-permute-start | bytes 147464 | tf_op jit(solution)/shard_map/gather_row/ppermute | solution.py:178
  121.0 1.9 collective-permute-start.13
  124.1 2.3 collective-permute-done.13
  126.5 4.8 %collective-permute-done.12 = f32[96,128]{1,0:T(8,128)S(1)} collective-permute-done((f32[96,128]{1,0:T(8,128)S(1)}, f32[96,128]{1,0:T(8,128)S(1)}, u32[]{:S(2)}, u32[]{:S(2)}) %collective-permute-start.12) | collective-permute-done | bytes 49184 | tf_op jit(solution)/shard_map/gather_row/ppermute | solution.py:178
  131.3 3.0 %collective-permute-start.16 = (f32[4,96,128]{2,1,0:T(8,128)S(1)}, f32[4,96,128]{2,1,0:T(8,128)S(1)}, u32[]{:S(2)}, u32[]{:S(2)}) collective-permute-start(f32[4,96,128]{2,1,0:T(8,128)S(1)} %pad_maximum_fusion.1.first_ref), channel_id=1, source_target_pairs={{0,1},{1,0},{2,3},{3,2},{4,5},{5,4},{6,7},{7,6},{8,9},{9,8},{10,11... | collective-permute-start | bytes 589832 | tf_op jit(solution)/shard_map/gather_row/ppermute | solution.py:178
  135.4 3.2 %collective-permute-done.16.first_ref = f32[4,96,128]{2,1,0:T(8,128)S(1)} collective-permute-done((f32[4,96,128]{2,1,0:T(8,128)S(1)}, f32[4,96,128]{2,1,0:T(8,128)S(1)}, u32[]{:S(2)}, u32[]{:S(2)}) %collective-permute-start.16) | collective-permute-done | bytes 196640 | tf_op jit(solution)/shard_map/gather_row/ppermute | solution.py:178
  141.6 4.7 %all-to-all-start.5 = ((f32[16,96,128]{2,1,0:T(8,128)}), f32[16,96,128]{2,1,0:T(8,128)S(1)}, u32[]{:S(2)}, u32[]{:S(2)}) async-start(f32[16,96,128]{2,1,0:T(8,128)} %gather_column.3), calls=%async_computation.5 | async-start | bytes 1572864 | tf_op jit(solution)/shard_map/gather_column/all_to_all | solution.py:14
  146.3 3.4 %collective-permute-start.17 = (f32[4,96,128]{2,1,0:T(8,128)S(1)}, f32[4,96,128]{2,1,0:T(8,128)S(1)}, u32[]{:S(2)}, u32[]{:S(2)}) collective-permute-start(f32[4,96,128]{2,1,0:T(8,128)S(1)} %collective-permute-done.15.second_ref), channel_id=1, source_target_pairs={{0,1},{1,0},{2,3},{3,2},{4,5},{5,4},{6,7},{7,6},{8,9},{9,8},{10,11... | collective-permute-start | bytes 589832 | tf_op jit(solution)/shard_map/gather_row/ppermute | solution.py:178
  149.7 5.7 %transposed.6.rest_0_ = f32[128,1536]{1,0:T(8,128)} custom-call(s32[9]{0:T(128)} %get-tuple-element.79.where_ref, f32[8,2,96,1536]{3,2,1,0:T(8,128)} %bitcast.85, f32[4,96,128]{2,1,0:T(8,128)} %copy-done.4, f32[4,96,128]{2,1,0:T(8,128)} %copy-done.8), custom_call_target="tpu_custom_call" | custom-call | flops 905969664 | bytes 4718592 | tf_op jit(solution)/shard_map/transposed/pallas_call | solution.py:154
  156.1 5.9 %transposed.7 = f32[1536,128]{1,0:T(8,128)} custom-call(s32[9]{0:T(128)} %get-tuple-element.80.where_ref, f32[8,2,96,1536]{3,2,1,0:T(8,128)} %bitcast.86, f32[4,96,128]{2,1,0:T(8,128)} %copy-done.6, f32[4,96,128]{2,1,0:T(8,128)} %copy-done.10, f32[128,1536]{1,0:T(8,128)} %transposed.6.rest_0_), custom_call_target="tpu_custom_call" | custom-call | flops 905969664 | bytes 4718592 | tf_op jit(solution)/shard_map/transposed/pallas_call | solution.py:154
  162.0 6.9 %all-to-all-done.5 = f32[16,96,128]{2,1,0:T(8,128)S(1)} async-done(((f32[16,96,128]{2,1,0:T(8,128)}), f32[16,96,128]{2,1,0:T(8,128)S(1)}, u32[]{:S(2)}, u32[]{:S(2)}) %all-to-all-start.5) | async-done | bytes 786464 | tf_op jit(solution)/shard_map/gather_column/all_to_all | solution.py:14
  168.9 3.6 %all-to-all-start.6 = ((f32[16,96,128]{2,1,0:T(8,128)}), f32[16,96,128]{2,1,0:T(8,128)S(1)}, u32[]{:S(2)}, u32[]{:S(2)}) async-start(f32[16,96,128]{2,1,0:T(8,128)} %bitcast.97), calls=%async_computation.6 | async-start | bytes 1572864 | tf_op jit(solution)/shard_map/back_transposed/all_to_all | solution.py:14
  172.6 4.0 %direct.9 = f32[4,96,128]{2,1,0:T(8,128)} custom-call(s32[6]{0:T(128)} %get-tuple-element.78.where_ref, f32[4,2,2,96,1536]{4,3,2,1,0:T(8,128)} %bitcast.87, f32[1536,128]{1,0:T(8,128)} %bitcast.93), custom_call_target="tpu_custom_call" | custom-call | flops 226492416 | bytes 2359296 | tf_op jit(solution)/shard_map/direct/pallas_call | solution.py:100
  176.6 3.4 %collective-permute-start.19 = (f32[4,96,128]{2,1,0:T(8,128)}, f32[4,96,128]{2,1,0:T(8,128)S(1)}, u32[]{:S(2)}, u32[]{:S(2)}) collective-permute-start(f32[4,96,128]{2,1,0:T(8,128)} %direct.9), channel_id=1, source_target_pairs={{0,1},{1,0},{2,3},{3,2},{4,5},{5,4},{6,7},{7,6},{8,9},{9,8},{10,11... | collective-permute-start | bytes 589832 | tf_op jit(solution)/shard_map/direct/ppermute | solution.py:178
  180.0 5.0 %direct.10 = (f32[4,96,128]{2,1,0:T(8,128)}, f32[4,96,128]{2,1,0:T(8,128)}) custom-call(s32[8]{0:T(128)} %concatenate.38.where_ref, f32[4,2,2,96,1536]{4,3,2,1,0:T(8,128)} %bitcast.88, f32[1536,128]{1,0:T(8,128)} %bitcast.94), custom_call_target="tpu_custom_call" | custom-call | flops 452984832 | bytes 4718592 | tf_op jit(solution)/shard_map/direct/pallas_call | solution.py:100
  185.0 4.2 %direct.11 = f32[4,96,128]{2,1,0:T(8,128)} custom-call(s32[6]{0:T(128)} %get-tuple-element.77.where_ref, f32[4,2,2,96,1536]{4,3,2,1,0:T(8,128)} %bitcast.89, f32[1536,128]{1,0:T(8,128)} %bitcast.95), custom_call_target="tpu_custom_call" | custom-call | flops 226492416 | bytes 2359296 | tf_op jit(solution)/shard_map/direct/pallas_call | solution.py:100
  191.1 1.8 collective-permute-start.20
  193.4 4.9 %collective-permute-done.18 = f32[4,96,128]{2,1,0:T(8,128)S(1)} collective-permute-done((f32[4,96,128]{2,1,0:T(8,128)S(1)}, f32[4,96,128]{2,1,0:T(8,128)S(1)}, u32[]{:S(2)}, u32[]{:S(2)}) %collective-permute-start.18) | collective-permute-done | bytes 196640 | tf_op jit(solution)/shard_map/direct/ppermute | solution.py:178
  199.2 1.8 back_wide.3
  201.0 5.7 %all-to-all-start.7 = ((f32[16,104,128]{2,1,0:T(8,128)}), f32[16,104,128]{2,1,0:T(8,128)S(1)}, u32[]{:S(2)}, u32[]{:S(2)}) async-start(f32[16,104,128]{2,1,0:T(8,128)} %back_wide.3), calls=%async_computation.7 | async-start | bytes 1703936 | tf_op jit(solution)/shard_map/back_wide/all_to_all | solution.py:14
  206.8 4.3 %collective-permute-start.21 = (f32[96,128]{1,0:T(8,128)S(1)}, f32[96,128]{1,0:T(8,128)S(1)}, u32[]{:S(2)}, u32[]{:S(2)}) collective-permute-start(f32[96,128]{1,0:T(8,128)S(1)} %get-tuple-element.69), channel_id=1, source_target_pairs={{0,8},{1,9},{2,10},{3,11},{4,12},{5,13},{6,14},{7,15},{8,0},{9,1},... | collective-permute-start | bytes 147464 | tf_op jit(solution)/shard_map/back_direct/ppermute | solution.py:178
  213.4 6.3 %all-to-all-done.7 = f32[16,104,128]{2,1,0:T(8,128)S(1)} async-done(((f32[16,104,128]{2,1,0:T(8,128)}), f32[16,104,128]{2,1,0:T(8,128)S(1)}, u32[]{:S(2)}, u32[]{:S(2)}) %all-to-all-start.7) | async-done | bytes 852000 | tf_op jit(solution)/shard_map/back_wide/all_to_all | solution.py:14
  220.1 9.4 %all_to_all.55 = f32[16,16,128]{2,1,0:T(8,128)S(1)} all-to-all(f32[16,16,128]{2,1,0:T(8,128)S(1)} %pad_maximum_fusion.2), channel_id=1, replica_groups=mesh['wide'=16,'narrow'=16] {'wide'}, dimensions={0} | all-to-all | bytes 262144 | tf_op jit(solution)/shard_map/gram_sum_wide/all_to_all | solution.py:14
  230.1 18.8 %all_to_all.56 = f32[16,8,128]{2,1,0:T(8,128)S(1)} all-to-all(f32[16,8,128]{2,1,0:T(8,128)S(1)} %broadcast_in_dim.49), channel_id=1, replica_groups=mesh['wide'=16,'narrow'=16] {'narrow'}, dimensions={0} | all-to-all | bytes 131072 | tf_op jit(solution)/shard_map/gram_sum_narrow/all_to_all | solution.py:14
  249.6 5.2 %all-to-all-start.10 = ((f32[16,8,128]{2,1,0:T(8,128)}), f32[16,8,128]{2,1,0:T(8,128)S(1)}, u32[]{:S(2)}, u32[]{:S(2)}) async-start(f32[16,8,128]{2,1,0:T(8,128)} %broadcast_in_dim.50), calls=%async_computation.10 | async-start | bytes 131072 | tf_op jit(solution)/shard_map/gram_whole/all_to_all | solution.py:14
  254.8 3.8 %inverse_first.1.refs_1_ = f32[128,128]{1,0:T(8,128)} custom-call(f32[128,128]{1,0:T(8,128)} %get-tuple-element.75.refs_0_), custom_call_target="tpu_custom_call" | custom-call | flops 1073741824 | bytes 1048576 | tf_op jit(solution)/shard_map/inverse_first/pallas_call | solution.py:270
  260.4 4.5 %finish.1 = f32[96,128]{1,0:T(8,128)} custom-call(f32[128,128]{1,0:T(8,128)} %bitcast.100, f32[128,128]{1,0:T(8,128)} %inverse_first.1.refs_1_, f32[96,128]{1,0:T(8,128)} %copy-done.13), custom_call_target="tpu_custom_call" | custom-call | flops 1073741824 | bytes 1048576 | tf_op jit(solution)/shard_map/finish/pallas_call | solution.py:270
  (109 shorter events, 33.8 us)
Async XLA Ops:
  1.8 28.3 %all-to-all-start = ((f32[16,96,128]{2,1,0:T(8,128)}), f32[16,96,128]{2,1,0:T(8,128)S(1)}, u32[]{:S(2)}, u32[]{:S(2)}) async-start(f32[16,96,128]{2,1,0:T(8,128)} %broadcast_in_dim.19), calls=%async_computation | async-start | bytes 1572864 | tf_op jit(solution)/shard_map/gather_wide/all_to_all | solution.py:14
  7.6 10.0 %collective-permute-start = (f32[96,128]{1,0:T(8,128)}, f32[96,128]{1,0:T(8,128)S(1)}, u32[]{:S(2)}, u32[]{:S(2)}) collective-permute-start(f32[96,128]{1,0:T(8,128)} %param.9), channel_id=1, source_target_pairs={{0,8},{1,9},{2,10},{3,11},{4,12},{5,13},{6,14},{7,15},{8,0},{9,1},... | collective-permute-start | bytes 147464 | tf_op jit(solution)/shard_map/gather_row/ppermute | solution.py:178
  14.8 6.4 %collective-permute-start.2 = (f32[96,128]{1,0:T(8,128)}, f32[96,128]{1,0:T(8,128)S(1)}, u32[]{:S(2)}, u32[]{:S(2)}) collective-permute-start(f32[96,128]{1,0:T(8,128)} %param.9), channel_id=1, source_target_pairs={{0,12},{1,13},{2,14},{3,15},{4,8},{5,9},{6,10},{7,11},{8,4},{9,5},... | collective-permute-start | bytes 147464 | tf_op jit(solution)/shard_map/gather_row/ppermute | solution.py:178
  14.8 6.4 %collective-permute-start.1 = (f32[96,128]{1,0:T(8,128)}, f32[96,128]{1,0:T(8,128)S(1)}, u32[]{:S(2)}, u32[]{:S(2)}) collective-permute-start(f32[96,128]{1,0:T(8,128)} %param.9), channel_id=1, source_target_pairs={{0,4},{1,5},{2,6},{3,7},{4,0},{5,1},{6,2},{7,3},{8,12},{9,13},{10,... | collective-permute-start | bytes 147464 | tf_op jit(solution)/shard_map/gather_row/ppermute | solution.py:178
  22.0 22.2 %copy-start.12 = (f32[4,96,128]{2,1,0:T(8,128)}, f32[4,96,128]{2,1,0:T(8,128)S(1)}, u32[]{:S(2)}) copy-start(f32[4,96,128]{2,1,0:T(8,128)S(1)} %pad_maximum_fusion.first_ref) | copy-start | bytes 589828
  22.0 7.6 %collective-permute-start.4 = (f32[4,96,128]{2,1,0:T(8,128)S(1)}, f32[4,96,128]{2,1,0:T(8,128)S(1)}, u32[]{:S(2)}, u32[]{:S(2)}) collective-permute-start(f32[4,96,128]{2,1,0:T(8,128)S(1)} %pad_maximum_fusion.first_ref), channel_id=1, source_target_pairs={{0,1},{1,0},{2,3},{3,2},{4,5},{5,4},{6,7},{7,6},{8,9},{9,8},{10,11... | collective-permute-start | bytes 589832 | tf_op jit(solution)/shard_map/gather_row/ppermute | solution.py:178
  24.4 5.7 %collective-permute-start.3 = (f32[4,96,128]{2,1,0:T(8,128)S(1)}, f32[4,96,128]{2,1,0:T(8,128)S(1)}, u32[]{:S(2)}, u32[]{:S(2)}) collective-permute-start(f32[4,96,128]{2,1,0:T(8,128)S(1)} %pad_maximum_fusion.first_ref), channel_id=1, source_target_pairs={{0,2},{1,3},{2,0},{3,1},{4,6},{5,7},{6,4},{7,5},{8,10},{9,11},{10,... | collective-permute-start | bytes 589832 | tf_op jit(solution)/shard_map/gather_row/ppermute | solution.py:178
  29.6 20.4 %copy-start.15 = (f32[4,96,128]{2,1,0:T(8,128)}, f32[4,96,128]{2,1,0:T(8,128)S(1)}, u32[]{:S(2)}) copy-start(f32[4,96,128]{2,1,0:T(8,128)S(1)} %collective-permute-done.4.first_ref) | copy-start | bytes 589828
  30.1 14.1 %copy-start.16 = (f32[4,96,128]{2,1,0:T(8,128)}, f32[4,96,128]{2,1,0:T(8,128)S(1)}, u32[]{:S(2)}) copy-start(f32[4,96,128]{2,1,0:T(8,128)S(1)} %collective-permute-done.3.second_ref) | copy-start | bytes 589828
  32.3 29.2 %all-to-all-start.1 = ((f32[16,96,128]{2,1,0:T(8,128)}), f32[16,96,128]{2,1,0:T(8,128)S(1)}, u32[]{:S(2)}, u32[]{:S(2)}) async-start(f32[16,96,128]{2,1,0:T(8,128)} %gather_column.2), calls=%async_computation.1 | async-start | bytes 1572864 | tf_op jit(solution)/shard_map/gather_column/all_to_all | solution.py:14
  40.1 9.9 %collective-permute-start.5 = (f32[4,96,128]{2,1,0:T(8,128)S(1)}, f32[4,96,128]{2,1,0:T(8,128)S(1)}, u32[]{:S(2)}, u32[]{:S(2)}) collective-permute-start(f32[4,96,128]{2,1,0:T(8,128)S(1)} %collective-permute-done.3.second_ref), channel_id=1, source_target_pairs={{0,1},{1,0},{2,3},{3,2},{4,5},{5,4},{6,7},{7,6},{8,9},{9,8},{10,11... | collective-permute-start | bytes 589832 | tf_op jit(solution)/shard_map/gather_row/ppermute | solution.py:178
  44.2 22.0 %copy-start.20 = (s32[4]{0:T(128)S(1)}, s32[4]{0:T(128)}, u32[]{:S(2)}) copy-start(s32[4]{0:T(128)} %constant.15.clone) | copy-start | bytes 52
  61.5 5.3 %copy-start.2 = (f32[16,96,128]{2,1,0:T(8,128)}, f32[16,96,128]{2,1,0:T(8,128)S(1)}, u32[]{:S(2)}) copy-start(f32[16,96,128]{2,1,0:T(8,128)S(1)} %all-to-all-done.1) | copy-start | bytes 2359300
  61.5 29.6 %all-to-all-start.2 = ((f32[16,96,128]{2,1,0:T(8,128)}), f32[16,96,128]{2,1,0:T(8,128)S(1)}, u32[]{:S(2)}, u32[]{:S(2)}) async-start(f32[16,96,128]{2,1,0:T(8,128)} %bitcast.96), calls=%async_computation.2 | async-start | bytes 1572864 | tf_op jit(solution)/shard_map/back_transposed/all_to_all | solution.py:14
  70.8 12.6 %collective-permute-start.7 = (f32[4,96,128]{2,1,0:T(8,128)}, f32[4,96,128]{2,1,0:T(8,128)S(1)}, u32[]{:S(2)}, u32[]{:S(2)}) collective-permute-start(f32[4,96,128]{2,1,0:T(8,128)} %direct.6), channel_id=1, source_target_pairs={{0,1},{1,0},{2,3},{3,2},{4,5},{5,4},{6,7},{7,6},{8,9},{9,8},{10,11... | collective-permute-start | bytes 589832 | tf_op jit(solution)/shard_map/direct/ppermute | solution.py:178
  74.9 16.2 %copy-start.1 = (s32[1,16]{1,0:T(1,128)S(1)}, s32[1,16]{1,0:T(1,128)}, u32[]{:S(2)}) copy-start(s32[1,16]{1,0:T(1,128)} %param.8) | copy-start | bytes 196
  80.1 9.1 %collective-permute-start.6 = (f32[4,96,128]{2,1,0:T(8,128)}, f32[4,96,128]{2,1,0:T(8,128)S(1)}, u32[]{:S(2)}, u32[]{:S(2)}) collective-permute-start(f32[4,96,128]{2,1,0:T(8,128)} %get-tuple-element.46), channel_id=1, source_target_pairs={{0,1},{1,0},{2,3},{3,2},{4,5},{5,4},{6,7},{7,6},{8,9},{9,8},{10,11... | collective-permute-start | bytes 589832 | tf_op jit(solution)/shard_map/direct/ppermute | solution.py:178
  84.4 5.8 %collective-permute-start.8 = (f32[4,96,128]{2,1,0:T(8,128)S(1)}, f32[4,96,128]{2,1,0:T(8,128)S(1)}, u32[]{:S(2)}, u32[]{:S(2)}) collective-permute-start(f32[4,96,128]{2,1,0:T(8,128)S(1)} %add.52), channel_id=1, source_target_pairs={{0,2},{1,3},{2,0},{3,1},{4,6},{5,7},{6,4},{7,5},{8,10},{9,11},{10,... | collective-permute-start | bytes 589832 | tf_op jit(solution)/shard_map/direct/ppermute | solution.py:178
  92.8 17.9 %all-to-all-start.3 = ((f32[16,96,128]{2,1,0:T(8,128)}), f32[16,96,128]{2,1,0:T(8,128)S(1)}, u32[]{:S(2)}, u32[]{:S(2)}) async-start(f32[16,96,128]{2,1,0:T(8,128)} %back_wide.2), calls=%async_computation.3 | async-start | bytes 1572864 | tf_op jit(solution)/shard_map/back_wide/all_to_all | solution.py:14
  98.5 12.2 %collective-permute-start.9 = (f32[96,128]{1,0:T(8,128)S(1)}, f32[96,128]{1,0:T(8,128)S(1)}, u32[]{:S(2)}, u32[]{:S(2)}) collective-permute-start(f32[96,128]{1,0:T(8,128)S(1)} %get-tuple-element.72), channel_id=1, source_target_pairs={{0,8},{1,9},{2,10},{3,11},{4,12},{5,13},{6,14},{7,15},{8,0},{9,1},... | collective-permute-start | bytes 147464 | tf_op jit(solution)/shard_map/back_direct/ppermute | solution.py:178
  104.2 6.7 %collective-permute-start.11 = (f32[96,128]{1,0:T(8,128)S(1)}, f32[96,128]{1,0:T(8,128)S(1)}, u32[]{:S(2)}, u32[]{:S(2)}) collective-permute-start(f32[96,128]{1,0:T(8,128)S(1)} %get-tuple-element.73), channel_id=1, source_target_pairs={{0,12},{1,13},{2,14},{3,15},{4,8},{5,9},{6,10},{7,11},{8,4},{9,5},... | collective-permute-start | bytes 147464 | tf_op jit(solution)/shard_map/back_direct/ppermute | solution.py:178
  104.8 6.1 %collective-permute-start.10 = (f32[96,128]{1,0:T(8,128)S(1)}, f32[96,128]{1,0:T(8,128)S(1)}, u32[]{:S(2)}, u32[]{:S(2)}) collective-permute-start(f32[96,128]{1,0:T(8,128)S(1)} %get-tuple-element.74), channel_id=1, source_target_pairs={{0,4},{1,5},{2,6},{3,7},{4,0},{5,1},{6,2},{7,3},{8,12},{9,13},{10,... | collective-permute-start | bytes 147464 | tf_op jit(solution)/shard_map/back_direct/ppermute | solution.py:178
  111.9 28.1 %all-to-all-start.4 = ((f32[16,96,128]{2,1,0:T(8,128)}), f32[16,96,128]{2,1,0:T(8,128)S(1)}, u32[]{:S(2)}, u32[]{:S(2)}) async-start(f32[16,96,128]{2,1,0:T(8,128)} %broadcast_in_dim.22), calls=%async_computation.4 | async-start | bytes 1572864 | tf_op jit(solution)/shard_map/gather_wide/all_to_all | solution.py:14
  117.6 6.5 %collective-permute-start.14 = (f32[96,128]{1,0:T(8,128)S(1)}, f32[96,128]{1,0:T(8,128)S(1)}, u32[]{:S(2)}, u32[]{:S(2)}) collective-permute-start(f32[96,128]{1,0:T(8,128)S(1)} %fusion.7), channel_id=1, source_target_pairs={{0,12},{1,13},{2,14},{3,15},{4,8},{5,9},{6,10},{7,11},{8,4},{9,5},... | collective-permute-start | bytes 147464 | tf_op jit(solution)/shard_map/gather_row/ppermute | solution.py:178
  121.0 5.5 %collective-permute-start.13 = (f32[96,128]{1,0:T(8,128)S(1)}, f32[96,128]{1,0:T(8,128)S(1)}, u32[]{:S(2)}, u32[]{:S(2)}) collective-permute-start(f32[96,128]{1,0:T(8,128)S(1)} %fusion.7), channel_id=1, source_target_pairs={{0,4},{1,5},{2,6},{3,7},{4,0},{5,1},{6,2},{7,3},{8,12},{9,13},{10,... | collective-permute-start | bytes 147464 | tf_op jit(solution)/shard_map/gather_row/ppermute | solution.py:178
  122.9 8.3 %collective-permute-start.12 = (f32[96,128]{1,0:T(8,128)S(1)}, f32[96,128]{1,0:T(8,128)S(1)}, u32[]{:S(2)}, u32[]{:S(2)}) collective-permute-start(f32[96,128]{1,0:T(8,128)S(1)} %fusion.7), channel_id=1, source_target_pairs={{0,8},{1,9},{2,10},{3,11},{4,12},{5,13},{6,14},{7,15},{8,0},{9,1},... | collective-permute-start | bytes 147464 | tf_op jit(solution)/shard_map/gather_row/ppermute | solution.py:178
  131.3 18.4 %copy-start.4 = (f32[4,96,128]{2,1,0:T(8,128)}, f32[4,96,128]{2,1,0:T(8,128)S(1)}, u32[]{:S(2)}) copy-start(f32[4,96,128]{2,1,0:T(8,128)S(1)} %pad_maximum_fusion.1.first_ref) | copy-start | bytes 589828
  131.3 7.3 %collective-permute-start.16 = (f32[4,96,128]{2,1,0:T(8,128)S(1)}, f32[4,96,128]{2,1,0:T(8,128)S(1)}, u32[]{:S(2)}, u32[]{:S(2)}) collective-permute-start(f32[4,96,128]{2,1,0:T(8,128)S(1)} %pad_maximum_fusion.1.first_ref), channel_id=1, source_target_pairs={{0,1},{1,0},{2,3},{3,2},{4,5},{5,4},{6,7},{7,6},{8,9},{9,8},{10,11... | collective-permute-start | bytes 589832 | tf_op jit(solution)/shard_map/gather_row/ppermute | solution.py:178
  134.3 5.7 %collective-permute-start.15 = (f32[4,96,128]{2,1,0:T(8,128)S(1)}, f32[4,96,128]{2,1,0:T(8,128)S(1)}, u32[]{:S(2)}, u32[]{:S(2)}) collective-permute-start(f32[4,96,128]{2,1,0:T(8,128)S(1)} %pad_maximum_fusion.1.first_ref), channel_id=1, source_target_pairs={{0,2},{1,3},{2,0},{3,1},{4,6},{5,7},{6,4},{7,5},{8,10},{9,11},{10,... | collective-permute-start | bytes 589832 | tf_op jit(solution)/shard_map/gather_row/ppermute | solution.py:178
  138.5 16.9 %copy-start.6 = (f32[4,96,128]{2,1,0:T(8,128)}, f32[4,96,128]{2,1,0:T(8,128)S(1)}, u32[]{:S(2)}) copy-start(f32[4,96,128]{2,1,0:T(8,128)S(1)} %collective-permute-done.16.first_ref) | copy-start | bytes 589828
  140.0 9.7 %copy-start.8 = (f32[4,96,128]{2,1,0:T(8,128)}, f32[4,96,128]{2,1,0:T(8,128)S(1)}, u32[]{:S(2)}) copy-start(f32[4,96,128]{2,1,0:T(8,128)S(1)} %collective-permute-done.15.second_ref) | copy-start | bytes 589828
  141.6 27.4 %all-to-all-start.5 = ((f32[16,96,128]{2,1,0:T(8,128)}), f32[16,96,128]{2,1,0:T(8,128)S(1)}, u32[]{:S(2)}, u32[]{:S(2)}) async-start(f32[16,96,128]{2,1,0:T(8,128)} %gather_column.3), calls=%async_computation.5 | async-start | bytes 1572864 | tf_op jit(solution)/shard_map/gather_column/all_to_all | solution.py:14
  146.3 9.1 %collective-permute-start.17 = (f32[4,96,128]{2,1,0:T(8,128)S(1)}, f32[4,96,128]{2,1,0:T(8,128)S(1)}, u32[]{:S(2)}, u32[]{:S(2)}) collective-permute-start(f32[4,96,128]{2,1,0:T(8,128)S(1)} %collective-permute-done.15.second_ref), channel_id=1, source_target_pairs={{0,1},{1,0},{2,3},{3,2},{4,5},{5,4},{6,7},{7,6},{8,9},{9,8},{10,11... | collective-permute-start | bytes 589832 | tf_op jit(solution)/shard_map/gather_row/ppermute | solution.py:178
  168.9 30.3 %all-to-all-start.6 = ((f32[16,96,128]{2,1,0:T(8,128)}), f32[16,96,128]{2,1,0:T(8,128)S(1)}, u32[]{:S(2)}, u32[]{:S(2)}) async-start(f32[16,96,128]{2,1,0:T(8,128)} %bitcast.97), calls=%async_computation.6 | async-start | bytes 1572864 | tf_op jit(solution)/shard_map/back_transposed/all_to_all | solution.py:14
  176.6 13.0 %copy-start.9 = (f32[4,96,128]{2,1,0:T(8,128)S(1)}, f32[4,96,128]{2,1,0:T(8,128)}, u32[]{:S(2)}) copy-start(f32[4,96,128]{2,1,0:T(8,128)} %copy-done.8) | copy-start | bytes 589828
  176.6 13.5 %copy-start.7 = (f32[4,96,128]{2,1,0:T(8,128)S(1)}, f32[4,96,128]{2,1,0:T(8,128)}, u32[]{:S(2)}) copy-start(f32[4,96,128]{2,1,0:T(8,128)} %copy-done.6) | copy-start | bytes 589828
  176.6 14.0 %copy-start.11 = (f32[4,96,128]{2,1,0:T(8,128)S(1)}, f32[4,96,128]{2,1,0:T(8,128)}, u32[]{:S(2)}) copy-start(f32[4,96,128]{2,1,0:T(8,128)} %copy-done.10) | copy-start | bytes 589828
  176.6 16.3 %copy-start.5 = (f32[4,96,128]{2,1,0:T(8,128)S(1)}, f32[4,96,128]{2,1,0:T(8,128)}, u32[]{:S(2)}) copy-start(f32[4,96,128]{2,1,0:T(8,128)} %copy-done.4) | copy-start | bytes 589828
  176.6 14.5 %collective-permute-start.19 = (f32[4,96,128]{2,1,0:T(8,128)}, f32[4,96,128]{2,1,0:T(8,128)S(1)}, u32[]{:S(2)}, u32[]{:S(2)}) collective-permute-start(f32[4,96,128]{2,1,0:T(8,128)} %direct.9), channel_id=1, source_target_pairs={{0,1},{1,0},{2,3},{3,2},{4,5},{5,4},{6,7},{7,6},{8,9},{9,8},{10,11... | collective-permute-start | bytes 589832 | tf_op jit(solution)/shard_map/direct/ppermute | solution.py:178
  185.0 6.0 %copy-start.14 = (f32[4,96,128]{2,1,0:T(8,128)S(1)}, f32[4,96,128]{2,1,0:T(8,128)}, u32[]{:S(2)}) copy-start(f32[4,96,128]{2,1,0:T(8,128)} %get-tuple-element.61) | copy-start | bytes 589828
  189.2 9.0 %collective-permute-start.18 = (f32[4,96,128]{2,1,0:T(8,128)S(1)}, f32[4,96,128]{2,1,0:T(8,128)S(1)}, u32[]{:S(2)}, u32[]{:S(2)}) collective-permute-start(f32[4,96,128]{2,1,0:T(8,128)S(1)} %copy-done.19), channel_id=1, source_target_pairs={{0,1},{1,0},{2,3},{3,2},{4,5},{5,4},{6,7},{7,6},{8,9},{9,8},{10,11... | collective-permute-start | bytes 589832 | tf_op jit(solution)/shard_map/direct/ppermute | solution.py:178
  191.1 7.1 %collective-permute-start.20 = (f32[4,96,128]{2,1,0:T(8,128)S(1)}, f32[4,96,128]{2,1,0:T(8,128)S(1)}, u32[]{:S(2)}, u32[]{:S(2)}) collective-permute-start(f32[4,96,128]{2,1,0:T(8,128)S(1)} %add.59), channel_id=1, source_target_pairs={{0,2},{1,3},{2,0},{3,1},{4,6},{5,7},{6,4},{7,5},{8,10},{9,11},{10,... | collective-permute-start | bytes 589832 | tf_op jit(solution)/shard_map/direct/ppermute | solution.py:178
  201.0 18.6 %all-to-all-start.7 = ((f32[16,104,128]{2,1,0:T(8,128)}), f32[16,104,128]{2,1,0:T(8,128)S(1)}, u32[]{:S(2)}, u32[]{:S(2)}) async-start(f32[16,104,128]{2,1,0:T(8,128)} %back_wide.3), calls=%async_computation.7 | async-start | bytes 1703936 | tf_op jit(solution)/shard_map/back_wide/all_to_all | solution.py:14
  206.8 12.9 %collective-permute-start.21 = (f32[96,128]{1,0:T(8,128)S(1)}, f32[96,128]{1,0:T(8,128)S(1)}, u32[]{:S(2)}, u32[]{:S(2)}) collective-permute-start(f32[96,128]{1,0:T(8,128)S(1)} %get-tuple-element.69), channel_id=1, source_target_pairs={{0,8},{1,9},{2,10},{3,11},{4,12},{5,13},{6,14},{7,15},{8,0},{9,1},... | collective-permute-start | bytes 147464 | tf_op jit(solution)/shard_map/back_direct/ppermute | solution.py:178
  211.1 8.6 %collective-permute-start.23 = (f32[96,128]{1,0:T(8,128)S(1)}, f32[96,128]{1,0:T(8,128)S(1)}, u32[]{:S(2)}, u32[]{:S(2)}) collective-permute-start(f32[96,128]{1,0:T(8,128)S(1)} %get-tuple-element.70), channel_id=1, source_target_pairs={{0,12},{1,13},{2,14},{3,15},{4,8},{5,9},{6,10},{7,11},{8,4},{9,5},... | collective-permute-start | bytes 147464 | tf_op jit(solution)/shard_map/back_direct/ppermute | solution.py:178
  212.3 7.4 %collective-permute-start.22 = (f32[96,128]{1,0:T(8,128)S(1)}, f32[96,128]{1,0:T(8,128)S(1)}, u32[]{:S(2)}, u32[]{:S(2)}) collective-permute-start(f32[96,128]{1,0:T(8,128)S(1)} %get-tuple-element.71), channel_id=1, source_target_pairs={{0,4},{1,5},{2,6},{3,7},{4,0},{5,1},{6,2},{7,3},{8,12},{9,13},{10,... | collective-permute-start | bytes 147464 | tf_op jit(solution)/shard_map/back_direct/ppermute | solution.py:178
  219.7 40.0 %copy-start.13 = (f32[96,128]{1,0:T(8,128)}, f32[96,128]{1,0:T(8,128)S(1)}, u32[]{:S(2)}) copy-start(f32[96,128]{1,0:T(8,128)S(1)} %slice_add_fusion.refs_2_) | copy-start | bytes 147460
  249.6 10.2 %all-to-all-start.10 = ((f32[16,8,128]{2,1,0:T(8,128)}), f32[16,8,128]{2,1,0:T(8,128)S(1)}, u32[]{:S(2)}, u32[]{:S(2)}) async-start(f32[16,8,128]{2,1,0:T(8,128)} %broadcast_in_dim.50), calls=%async_computation.10 | async-start | bytes 131072 | tf_op jit(solution)/shard_map/gram_whole/all_to_all | solution.py:14
  (6 other events, 10.5 us)

commit v6 on v5

--- a/solution.py
+++ b/solution.py
@@ -3,10 +3,12 @@
 from jax import lax
 from jax.experimental import pallas as pl
 from jax.experimental.pallas import tpu as pltpu
+from jax.sharding import Mesh
 from jax.sharding import PartitionSpec as P
 
 NS_STEPS = 5
-WIDE, NARROW = "wide", "narrow"
+CHIP, CORE, NARROW = "chip", "core", "narrow"
+WIDE = (CHIP, CORE)
 HIGHEST = lax.Precision.HIGHEST
 
 
@@ -18,30 +20,14 @@
     return exchange(jnp.broadcast_to(value[None], (lax.axis_size(axis), *value.shape)), axis)
 
 
-def move_blocks(blocks, columns, scatter, extra=None):
-    count, rows, width = blocks.shape
-    arrays = [blocks] if extra is None else [blocks, extra]
-    more = 0 if extra is None else extra.shape[0] // count
-
-    def kernel(columns_ref, blocks_ref, *rest):
-        moved_ref, done = rest[-2:]
-        copies = []
-        for i in range(count):
-            column = columns_ref[i]
-            source, target = (i, column) if scatter else (column, i)
-            copies.append(
-                pltpu.make_async_copy(
-                    blocks_ref.at[source], moved_ref.at[target, pl.ds(0, rows)], done.at[i]
-                )
-            )
-            if more:
-                copies.append(
-                    pltpu.make_async_copy(
-                        rest[0].at[pl.ds(i * more, more)],
-                        moved_ref.at[i, pl.ds(rows, more)],
-                        done.at[count + i],
-                    )
-                )
+def picked_blocks(blocks, columns):
+    count = blocks.shape[0]
+
+    def kernel(columns_ref, blocks_ref, picked_ref, done):
+        copies = [
+            pltpu.make_async_copy(blocks_ref.at[columns_ref[i]], picked_ref.at[i], done.at[i])
+            for i in range(count)
+        ]
         for copy in copies:
             copy.start()
         for copy in copies:
@@ -49,14 +35,53 @@
 
     return pl.pallas_call(
         kernel,
-        out_shape=jax.ShapeDtypeStruct((count, rows + more, width), blocks.dtype),
+        out_shape=jax.ShapeDtypeStruct(blocks.shape, blocks.dtype),
+        in_specs=[pl.BlockSpec(memory_space=pltpu.SMEM), pl.BlockSpec(memory_space=pl.ANY)],
+        out_specs=pl.BlockSpec(memory_space=pl.ANY),
+        scratch_shapes=[pltpu.SemaphoreType.DMA((count,))],
+        compiler_params=pltpu.CompilerParams(vmem_limit_bytes=1 << 20),
+        cost_estimate=pl.CostEstimate(flops=0, bytes_accessed=8 * blocks.size, transcendentals=0),
+    )(columns, blocks)
+
+
+def placed_by_core(blocks, columns, core, extra=None):
+    count, rows, width = blocks.shape
+    arrays = [blocks] if extra is None else [blocks, extra]
+    more = 0 if extra is None else extra.shape[0] // count
+
+    def kernel(where_ref, blocks_ref, *rest):
+        kept_ref, sent_ref, done = rest[-3:]
+        core = where_ref[count]
+
+        def place(source, device, span, semaphore):
+            kept, sent = (
+                pltpu.make_async_copy(source, ref.at[device // 2, span], semaphore)
+                for ref in (kept_ref, sent_ref)
+            )
+            pl.when(device % 2 == core)(kept.start)
+            pl.when(device % 2 != core)(sent.start)
+            return kept
+
+        copies = []
+        for i in range(count):
+            copies.append(place(blocks_ref.at[i], where_ref[i], pl.ds(0, rows), done.at[i]))
+            if more:
+                part = rest[0].at[pl.ds(i * more, more)]
+                copies.append(place(part, jnp.int32(i), pl.ds(rows, more), done.at[count + i]))
+        for copy in copies:
+            copy.wait()
+
+    out = jax.ShapeDtypeStruct((count // 2, rows + more, width), blocks.dtype)
+    return pl.pallas_call(
+        kernel,
+        out_shape=[out, out],
         in_specs=[pl.BlockSpec(memory_space=pltpu.SMEM)]
         + [pl.BlockSpec(memory_space=pl.ANY)] * len(arrays),
-        out_specs=pl.BlockSpec(memory_space=pl.ANY),
+        out_specs=[pl.BlockSpec(memory_space=pl.ANY)] * 2,
         scratch_shapes=[pltpu.SemaphoreType.DMA((len(arrays) * count,))],
         compiler_params=pltpu.CompilerParams(vmem_limit_bytes=1 << 20),
         cost_estimate=pl.CostEstimate(flops=0, bytes_accessed=8 * blocks.size, transcendentals=0),
-    )(columns, *arrays)
+    )(jnp.concatenate([columns, core[None]]), *arrays)
 
 
 def high_low(value):
@@ -208,7 +233,7 @@
         slices, near_rows, far_rows = lax.optimization_barrier((slices, near_rows, far_rows))
         far_rows.append(swap(near_rows[1], 1))
     with jax.named_scope("gather_column"):
-        picked = move_blocks(slices, columns, scatter=False)
+        picked = picked_blocks(slices, columns)
         column_block = exchange(picked, NARROW).reshape(order, width)
     with jax.named_scope("transposed"):
         partial = transposed_half(tile, near_rows, near, spots)
@@ -240,8 +265,10 @@
     with jax.named_scope("back_direct"):
         direct_sum = summed_part(kept)
     with jax.named_scope("back_wide"):
-        placed = move_blocks(arrived, columns, scatter=True, extra=gram)
-        sums = exchange(placed, WIDE).sum(axis=0)
+        core = lax.axis_index(CORE).astype(jnp.int32)
+        kept, sent = placed_by_core(arrived, columns, core, extra=gram)
+        kept = kept + lax.ppermute(sent, CORE, [(0, 1), (1, 0)])
+        sums = exchange(kept, CHIP).sum(axis=0)
     return direct_sum + sums[:rows], sums[rows:]
 
 
@@ -307,10 +334,12 @@
 
 
 def solution(mesh):
+    wide, narrow = mesh.devices.shape
+    finer = Mesh(mesh.devices.reshape(wide // 2, 2, narrow), (CHIP, CORE, NARROW))
     return jax.shard_map(
         on_device,
-        mesh=mesh,
-        in_specs=(P(WIDE, NARROW), P(WIDE, None), P((WIDE, NARROW), None)),
-        out_specs=P((WIDE, NARROW), None),
+        mesh=finer,
+        in_specs=(P(WIDE, NARROW), P(WIDE, None), P((CHIP, CORE, NARROW), None)),
+        out_specs=P((CHIP, CORE, NARROW), None),
         check_vma=False,
     )

time: 269 us -> 271 us (level)
    all_to_all x9, waiting for transfers between devices: 24.7 us -> 14.4 us  [exchange(): return lax.all_to_all(parts, axis, 0, 0, tiled=True)]
    ppermute x24, waiting for transfers between devices: 30.1 us -> 36 us  [swap(): return lax.ppermute(value, NARROW, [(i, i ^ mask) for i in range(size)])]
    ppermute x0 -> x2, waiting for transfers between devices: none -> 3.47 us  [apply_hamiltonian(): kept = kept + lax.ppermute(sent, CORE, [(0, 1), (1, 0)])]
  transfers between devices with their start and end apart: 33 -> 35, of which waited for: 17 -> 23; matrix products, arithmetic and copies ran while one was open for 3% -> 3% of each run, Pallas kernels for 20% -> 20%
where the time goes in v6:
time: 271 us; the launch traced here: 268 us
  starting transfers between devices  103 us (38%)
  Pallas kernels  65.6 us (24%)
  waiting for transfers between devices  53.9 us (20%)
  blocking collectives  27.7 us (10%)
  other arithmetic  8.14 us (3%)
  local copies, waits for them, and re-layouts  6.82 us (3%)
    ppermute x24, starting transfers between devices, swap(): return lax.ppermute(value, NARROW, [(i, i ^ mask) for i in range(size)])  53.9 us
    all_to_all x9, starting transfers between devices, exchange(): return lax.all_to_all(parts, axis, 0, 0, tiled=True)  48.9 us
    ppermute x24, waiting for transfers between devices, swap(): return lax.ppermute(value, NARROW, [(i, i ^ mask) for i in range(size)])  36 us
    all_to_all x2, blocking collectives, exchange(): return lax.all_to_all(parts, axis, 0, 0, tiled=True)  27.7 us
    pallas_call x6, Pallas kernels, direct_quarters(): pl.pallas_call(kernel, out_shape=[jax.ShapeDtypeStruct((each, rows, width...  26.4 us
    pallas_call x4, Pallas kernels, transposed_half(): pl.pallas_call(kernel, out_shape=jax.ShapeDtypeStruct((width, order) if p...  23.4 us
    all_to_all x9, waiting for transfers between devices, exchange(): return lax.all_to_all(parts, axis, 0, 0, tiled=True)  14.4 us
    pallas_call x2, Pallas kernels, in_kernel(): pl.pallas_call(kernel, out_shape=jax.ShapeDtypeStruct(shape, jnp.float32)...  8.35 us
  transfers between devices with their start and end apart: 35, of which 23 were waited for; matrix products, arithmetic and copies ran while one was open for 3% of the time, Pallas kernels for 20%

profile of v6, /device:TPU:8, one launch (start us, length us, event | category | flops | bytes accessed | tf_op | source)
XLA Modules:
  0.0 267.8 jit_solution(5342969488526953907)
XLA Ops:
  1.8 5.8 %all-to-all-start = ((f32[16,96,128]{2,1,0:T(8,128)}), f32[16,96,128]{2,1,0:T(8,128)S(1)}, u32[]{:S(2)}, u32[]{:S(2)}) async-start(f32[16,96,128]{2,1,0:T(8,128)} %broadcast_in_dim.21), calls=%async_computation | async-start | bytes 1572864 | tf_op jit(solution)/shard_map/gather_wide/all_to_all | solution.py:16
  7.6 7.2 %collective-permute-start = (f32[96,128]{1,0:T(8,128)}, f32[96,128]{1,0:T(8,128)S(1)}, u32[]{:S(2)}, u32[]{:S(2)}) collective-permute-start(f32[96,128]{1,0:T(8,128)} %param.9), channel_id=1, source_target_pairs={{0,8},{1,9},{2,10},{3,11},{4,12},{5,13},{6,14},{7,15},{8,0},{9,1},... | collective-permute-start | bytes 147464 | tf_op jit(solution)/shard_map/gather_row/ppermute | solution.py:203
  17.6 3.6 %collective-permute-done.2 = f32[96,128]{1,0:T(8,128)S(1)} collective-permute-done((f32[96,128]{1,0:T(8,128)}, f32[96,128]{1,0:T(8,128)S(1)}, u32[]{:S(2)}, u32[]{:S(2)}) %collective-permute-start.2) | collective-permute-done | bytes 49184 | tf_op jit(solution)/shard_map/gather_row/ppermute | solution.py:203
  22.0 2.4 collective-permute-start.4
  25.9 3.6 %collective-permute-done.4.first_ref = f32[4,96,128]{2,1,0:T(8,128)S(1)} collective-permute-done((f32[4,96,128]{2,1,0:T(8,128)S(1)}, f32[4,96,128]{2,1,0:T(8,128)S(1)}, u32[]{:S(2)}, u32[]{:S(2)}) %collective-permute-start.4) | collective-permute-done | bytes 196640 | tf_op jit(solution)/shard_map/gather_row/ppermute | solution.py:203
  32.4 7.1 %all-to-all-start.1 = ((f32[16,96,128]{2,1,0:T(8,128)}), f32[16,96,128]{2,1,0:T(8,128)S(1)}, u32[]{:S(2)}, u32[]{:S(2)}) async-start(f32[16,96,128]{2,1,0:T(8,128)} %gather_column.2), calls=%async_computation.1 | async-start | bytes 1572864 | tf_op jit(solution)/shard_map/gather_column/all_to_all | solution.py:16
  40.1 3.4 %collective-permute-start.5 = (f32[4,96,128]{2,1,0:T(8,128)S(1)}, f32[4,96,128]{2,1,0:T(8,128)S(1)}, u32[]{:S(2)}, u32[]{:S(2)}) collective-permute-start(f32[4,96,128]{2,1,0:T(8,128)S(1)} %collective-permute-done.3.second_ref), channel_id=1, source_target_pairs={{0,1},{1,0},{2,3},{3,2},{4,5},{5,4},{6,7},{7,6},{8,9},{9,8},{10,11... | collective-permute-start | bytes 589832 | tf_op jit(solution)/shard_map/gather_row/ppermute | solution.py:203
  44.1 5.8 %transposed.4.rest_0_ = f32[128,1536]{1,0:T(8,128)} custom-call(s32[9]{0:T(128)} %get-tuple-element.87.where_ref, f32[8,2,96,1536]{3,2,1,0:T(8,128)} %bitcast.80, f32[4,96,128]{2,1,0:T(8,128)} %copy-done.12, f32[4,96,128]{2,1,0:T(8,128)} %copy-done.16), custom_call_target="tpu_custom_call" | custom-call | flops 905969664 | bytes 4718592 | tf_op jit(solution)/shard_map/transposed/pallas_call | solution.py:179
  50.6 5.9 %transposed.5 = f32[1536,128]{1,0:T(8,128)} custom-call(s32[9]{0:T(128)} %get-tuple-element.88.where_ref, f32[8,2,96,1536]{3,2,1,0:T(8,128)} %bitcast.81, f32[4,96,128]{2,1,0:T(8,128)} %copy-done.15, f32[4,96,128]{2,1,0:T(8,128)} %copy-done.17, f32[128,1536]{1,0:T(8,128)} %transposed.4.rest_0_), custom_call_target="tpu_custom_call" | custom-call | flops 905969664 | bytes 4718592 | tf_op jit(solution)/shard_map/transposed/pallas_call | solution.py:179
  56.6 5.0 %all-to-all-done.1 = f32[16,96,128]{2,1,0:T(8,128)S(1)} async-done(((f32[16,96,128]{2,1,0:T(8,128)}), f32[16,96,128]{2,1,0:T(8,128)S(1)}, u32[]{:S(2)}, u32[]{:S(2)}) %all-to-all-start.1) | async-done | bytes 786464 | tf_op jit(solution)/shard_map/gather_column/all_to_all | solution.py:16
  61.6 4.6 %all-to-all-start.2 = ((f32[16,96,128]{2,1,0:T(8,128)}), f32[16,96,128]{2,1,0:T(8,128)S(1)}, u32[]{:S(2)}, u32[]{:S(2)}) async-start(f32[16,96,128]{2,1,0:T(8,128)} %bitcast.96), calls=%async_computation.2 | async-start | bytes 1572864 | tf_op jit(solution)/shard_map/back_transposed/all_to_all | solution.py:16
  66.8 4.1 %direct.6 = f32[4,96,128]{2,1,0:T(8,128)} custom-call(s32[6]{0:T(128)} %get-tuple-element.86.where_ref, f32[4,2,2,96,1536]{4,3,2,1,0:T(8,128)} %bitcast.82, f32[1536,128]{1,0:T(8,128)} %bitcast.90), custom_call_target="tpu_custom_call" | custom-call | flops 226492416 | bytes 2359296 | tf_op jit(solution)/shard_map/direct/pallas_call | solution.py:125
  71.0 3.4 %collective-permute-start.7 = (f32[4,96,128]{2,1,0:T(8,128)}, f32[4,96,128]{2,1,0:T(8,128)S(1)}, u32[]{:S(2)}, u32[]{:S(2)}) collective-permute-start(f32[4,96,128]{2,1,0:T(8,128)} %direct.6), channel_id=1, source_target_pairs={{0,1},{1,0},{2,3},{3,2},{4,5},{5,4},{6,7},{7,6},{8,9},{9,8},{10,11... | collective-permute-start | bytes 589832 | tf_op jit(solution)/shard_map/direct/ppermute | solution.py:203
  75.0 5.0 %direct.7 = (f32[4,96,128]{2,1,0:T(8,128)}, f32[4,96,128]{2,1,0:T(8,128)}) custom-call(s32[8]{0:T(128)} %concatenate.42.where_ref, f32[4,2,2,96,1536]{4,3,2,1,0:T(8,128)} %bitcast.83, f32[1536,128]{1,0:T(8,128)} %bitcast.91), custom_call_target="tpu_custom_call" | custom-call | flops 452984832 | bytes 4718592 | tf_op jit(solution)/shard_map/direct/pallas_call | solution.py:125
  80.2 3.3 %collective-permute-done.7 = f32[4,96,128]{2,1,0:T(8,128)S(1)} collective-permute-done((f32[4,96,128]{2,1,0:T(8,128)}, f32[4,96,128]{2,1,0:T(8,128)S(1)}, u32[]{:S(2)}, u32[]{:S(2)}) %collective-permute-start.7) | collective-permute-done | bytes 196640 | tf_op jit(solution)/shard_map/direct/ppermute | solution.py:203
  85.5 4.0 %direct.8 = f32[4,96,128]{2,1,0:T(8,128)} custom-call(s32[6]{0:T(128)} %get-tuple-element.85.where_ref, f32[4,2,2,96,1536]{4,3,2,1,0:T(8,128)} %bitcast.84, f32[1536,128]{1,0:T(8,128)} %bitcast.92), custom_call_target="tpu_custom_call" | custom-call | flops 226492416 | bytes 2359296 | tf_op jit(solution)/shard_map/direct/pallas_call | solution.py:125
  91.2 2.0 back_wide.2
  95.8 5.7 %all-to-all-start.3 = ((f32[8,96,128]{2,1,0:T(8,128)}), f32[8,96,128]{2,1,0:T(8,128)S(1)}, u32[]{:S(2)}, u32[]{:S(2)}) async-start(f32[8,96,128]{2,1,0:T(8,128)} %add.63), calls=%async_computation.3 | async-start | bytes 786432 | tf_op jit(solution)/shard_map/back_wide/all_to_all | solution.py:16
  101.5 5.9 %collective-permute-start.9 = (f32[96,128]{1,0:T(8,128)S(1)}, f32[96,128]{1,0:T(8,128)S(1)}, u32[]{:S(2)}, u32[]{:S(2)}) collective-permute-start(f32[96,128]{1,0:T(8,128)S(1)} %get-tuple-element.80), channel_id=1, source_target_pairs={{0,8},{1,9},{2,10},{3,11},{4,12},{5,13},{6,14},{7,15},{8,0},{9,1},... | collective-permute-start | bytes 147464 | tf_op jit(solution)/shard_map/back_direct/ppermute | solution.py:203
  110.4 3.5 %collective-permute-done.11 = f32[96,128]{1,0:T(8,128)S(1)} collective-permute-done((f32[96,128]{1,0:T(8,128)S(1)}, f32[96,128]{1,0:T(8,128)S(1)}, u32[]{:S(2)}, u32[]{:S(2)}) %collective-permute-start.11) | collective-permute-done | bytes 49184 | tf_op jit(solution)/shard_map/back_direct/ppermute | solution.py:203
  114.9 5.7 %all-to-all-start.4 = ((f32[16,96,128]{2,1,0:T(8,128)}), f32[16,96,128]{2,1,0:T(8,128)S(1)}, u32[]{:S(2)}, u32[]{:S(2)}) async-start(f32[16,96,128]{2,1,0:T(8,128)} %broadcast_in_dim.25), calls=%async_computation.4 | async-start | bytes 1572864 | tf_op jit(solution)/shard_map/gather_wide/all_to_all | solution.py:16
  120.7 2.7 %collective-permute-start.15 = (f32[96,128]{1,0:T(8,128)S(1)}, f32[96,128]{1,0:T(8,128)S(1)}, u32[]{:S(2)}, u32[]{:S(2)}) collective-permute-start(f32[96,128]{1,0:T(8,128)S(1)} %fusion.7), channel_id=1, source_target_pairs={{0,12},{1,13},{2,14},{3,15},{4,8},{5,9},{6,10},{7,11},{8,4},{9,5},... | collective-permute-start | bytes 147464 | tf_op jit(solution)/shard_map/gather_row/ppermute | solution.py:203
  124.8 2.3 collective-permute-start.13
  128.8 4.0 %collective-permute-done.13 = f32[96,128]{1,0:T(8,128)S(1)} collective-permute-done((f32[96,128]{1,0:T(8,128)S(1)}, f32[96,128]{1,0:T(8,128)S(1)}, u32[]{:S(2)}, u32[]{:S(2)}) %collective-permute-start.13) | collective-permute-done | bytes 49184 | tf_op jit(solution)/shard_map/gather_row/ppermute | solution.py:203
  132.8 3.8 %collective-permute-start.17 = (f32[4,96,128]{2,1,0:T(8,128)S(1)}, f32[4,96,128]{2,1,0:T(8,128)S(1)}, u32[]{:S(2)}, u32[]{:S(2)}) collective-permute-start(f32[4,96,128]{2,1,0:T(8,128)S(1)} %pad_maximum_fusion.1.first_ref), channel_id=1, source_target_pairs={{0,1},{1,0},{2,3},{3,2},{4,5},{5,4},{6,7},{7,6},{8,9},{9,8},{10,11... | collective-permute-start | bytes 589832 | tf_op jit(solution)/shard_map/gather_row/ppermute | solution.py:203
  137.1 3.2 %collective-permute-done.17.first_ref = f32[4,96,128]{2,1,0:T(8,128)S(1)} collective-permute-done((f32[4,96,128]{2,1,0:T(8,128)S(1)}, f32[4,96,128]{2,1,0:T(8,128)S(1)}, u32[]{:S(2)}, u32[]{:S(2)}) %collective-permute-start.17) | collective-permute-done | bytes 196640 | tf_op jit(solution)/shard_map/gather_row/ppermute | solution.py:203
  140.3 2.0 collective-permute-done.16.second_ref
  143.9 5.1 %all-to-all-start.5 = ((f32[16,96,128]{2,1,0:T(8,128)}), f32[16,96,128]{2,1,0:T(8,128)S(1)}, u32[]{:S(2)}, u32[]{:S(2)}) async-start(f32[16,96,128]{2,1,0:T(8,128)} %gather_column.3), calls=%async_computation.5 | async-start | bytes 1572864 | tf_op jit(solution)/shard_map/gather_column/all_to_all | solution.py:16
  149.0 3.4 %collective-permute-start.18 = (f32[4,96,128]{2,1,0:T(8,128)S(1)}, f32[4,96,128]{2,1,0:T(8,128)S(1)}, u32[]{:S(2)}, u32[]{:S(2)}) collective-permute-start(f32[4,96,128]{2,1,0:T(8,128)S(1)} %collective-permute-done.16.second_ref), channel_id=1, source_target_pairs={{0,1},{1,0},{2,3},{3,2},{4,5},{5,4},{6,7},{7,6},{8,9},{9,8},{10,11... | collective-permute-start | bytes 589832 | tf_op jit(solution)/shard_map/gather_row/ppermute | solution.py:203
  152.4 5.7 %transposed.6.rest_0_ = f32[128,1536]{1,0:T(8,128)} custom-call(s32[9]{0:T(128)} %get-tuple-element.87.where_ref, f32[8,2,96,1536]{3,2,1,0:T(8,128)} %bitcast.85, f32[4,96,128]{2,1,0:T(8,128)} %copy-done.4, f32[4,96,128]{2,1,0:T(8,128)} %copy-done.8), custom_call_target="tpu_custom_call" | custom-call | flops 905969664 | bytes 4718592 | tf_op jit(solution)/shard_map/transposed/pallas_call | solution.py:179
  158.8 5.9 %transposed.7 = f32[1536,128]{1,0:T(8,128)} custom-call(s32[9]{0:T(128)} %get-tuple-element.88.where_ref, f32[8,2,96,1536]{3,2,1,0:T(8,128)} %bitcast.86, f32[4,96,128]{2,1,0:T(8,128)} %copy-done.6, f32[4,96,128]{2,1,0:T(8,128)} %copy-done.10, f32[128,1536]{1,0:T(8,128)} %transposed.6.rest_0_), custom_call_target="tpu_custom_call" | custom-call | flops 905969664 | bytes 4718592 | tf_op jit(solution)/shard_map/transposed/pallas_call | solution.py:179
  164.7 5.7 %all-to-all-done.5 = f32[16,96,128]{2,1,0:T(8,128)S(1)} async-done(((f32[16,96,128]{2,1,0:T(8,128)}), f32[16,96,128]{2,1,0:T(8,128)S(1)}, u32[]{:S(2)}, u32[]{:S(2)}) %all-to-all-start.5) | async-done | bytes 786464 | tf_op jit(solution)/shard_map/gather_column/all_to_all | solution.py:16
  170.4 4.0 %all-to-all-start.6 = ((f32[16,96,128]{2,1,0:T(8,128)}), f32[16,96,128]{2,1,0:T(8,128)S(1)}, u32[]{:S(2)}, u32[]{:S(2)}) async-start(f32[16,96,128]{2,1,0:T(8,128)} %bitcast.97), calls=%async_computation.6 | async-start | bytes 1572864 | tf_op jit(solution)/shard_map/back_transposed/all_to_all | solution.py:16
  174.5 4.0 %direct.9 = f32[4,96,128]{2,1,0:T(8,128)} custom-call(s32[6]{0:T(128)} %get-tuple-element.86.where_ref, f32[4,2,2,96,1536]{4,3,2,1,0:T(8,128)} %bitcast.87, f32[1536,128]{1,0:T(8,128)} %bitcast.93), custom_call_target="tpu_custom_call" | custom-call | flops 226492416 | bytes 2359296 | tf_op jit(solution)/shard_map/direct/pallas_call | solution.py:125
  178.5 3.5 %collective-permute-start.20 = (f32[4,96,128]{2,1,0:T(8,128)}, f32[4,96,128]{2,1,0:T(8,128)S(1)}, u32[]{:S(2)}, u32[]{:S(2)}) collective-permute-start(f32[4,96,128]{2,1,0:T(8,128)} %direct.9), channel_id=1, source_target_pairs={{0,1},{1,0},{2,3},{3,2},{4,5},{5,4},{6,7},{7,6},{8,9},{9,8},{10,11... | collective-permute-start | bytes 589832 | tf_op jit(solution)/shard_map/direct/ppermute | solution.py:203
  182.0 5.0 %direct.10 = (f32[4,96,128]{2,1,0:T(8,128)}, f32[4,96,128]{2,1,0:T(8,128)}) custom-call(s32[8]{0:T(128)} %concatenate.42.where_ref, f32[4,2,2,96,1536]{4,3,2,1,0:T(8,128)} %bitcast.88, f32[1536,128]{1,0:T(8,128)} %bitcast.94), custom_call_target="tpu_custom_call" | custom-call | flops 452984832 | bytes 4718592 | tf_op jit(solution)/shard_map/direct/pallas_call | solution.py:125
  187.1 4.2 %direct.11 = f32[4,96,128]{2,1,0:T(8,128)} custom-call(s32[6]{0:T(128)} %get-tuple-element.85.where_ref, f32[4,2,2,96,1536]{4,3,2,1,0:T(8,128)} %bitcast.89, f32[1536,128]{1,0:T(8,128)} %bitcast.95), custom_call_target="tpu_custom_call" | custom-call | flops 226492416 | bytes 2359296 | tf_op jit(solution)/shard_map/direct/pallas_call | solution.py:125
  193.0 2.1 collective-permute-start.21
  195.6 3.1 %collective-permute-done.19 = f32[4,96,128]{2,1,0:T(8,128)S(1)} collective-permute-done((f32[4,96,128]{2,1,0:T(8,128)S(1)}, f32[4,96,128]{2,1,0:T(8,128)S(1)}, u32[]{:S(2)}, u32[]{:S(2)}) %collective-permute-start.19) | collective-permute-done | bytes 196640 | tf_op jit(solution)/shard_map/direct/ppermute | solution.py:203
  200.0 2.3 back_wide.3
  205.0 5.7 %all-to-all-start.7 = ((f32[8,104,128]{2,1,0:T(8,128)}), f32[8,104,128]{2,1,0:T(8,128)S(1)}, u32[]{:S(2)}, u32[]{:S(2)}) async-start(f32[8,104,128]{2,1,0:T(8,128)} %add.74), calls=%async_computation.7 | async-start | bytes 851968 | tf_op jit(solution)/shard_map/back_wide/all_to_all | solution.py:16
  210.7 5.8 %collective-permute-start.22 = (f32[96,128]{1,0:T(8,128)S(1)}, f32[96,128]{1,0:T(8,128)S(1)}, u32[]{:S(2)}, u32[]{:S(2)}) collective-permute-start(f32[96,128]{1,0:T(8,128)S(1)} %get-tuple-element.77), channel_id=1, source_target_pairs={{0,8},{1,9},{2,10},{3,11},{4,12},{5,13},{6,14},{7,15},{8,0},{9,1},... | collective-permute-start | bytes 147464 | tf_op jit(solution)/shard_map/back_direct/ppermute | solution.py:203
  219.4 3.7 %collective-permute-done.24 = f32[96,128]{1,0:T(8,128)S(1)} collective-permute-done((f32[96,128]{1,0:T(8,128)S(1)}, f32[96,128]{1,0:T(8,128)S(1)}, u32[]{:S(2)}, u32[]{:S(2)}) %collective-permute-start.24) | collective-permute-done | bytes 49184 | tf_op jit(solution)/shard_map/back_direct/ppermute | solution.py:203
  223.5 10.7 %all_to_all.55 = f32[16,16,128]{2,1,0:T(8,128)S(1)} all-to-all(f32[16,16,128]{2,1,0:T(8,128)S(1)} %pad_maximum_fusion.2), channel_id=1, replica_groups=mesh['chip'=8,'core'=2,'narrow'=16] {'chip','core'}, dimensions={0} | all-to-all | bytes 262144 | tf_op jit(solution)/shard_map/gram_sum_wide/all_to_all | solution.py:16
  234.9 17.0 %all_to_all.56 = f32[16,8,128]{2,1,0:T(8,128)S(1)} all-to-all(f32[16,8,128]{2,1,0:T(8,128)S(1)} %broadcast_in_dim.54), channel_id=1, replica_groups=mesh['chip'=8,'core'=2,'narrow'=16] {'narrow'}, dimensions={0} | all-to-all | bytes 131072 | tf_op jit(solution)/shard_map/gram_sum_narrow/all_to_all | solution.py:16
  252.5 5.2 %all-to-all-start.10 = ((f32[16,8,128]{2,1,0:T(8,128)}), f32[16,8,128]{2,1,0:T(8,128)S(1)}, u32[]{:S(2)}, u32[]{:S(2)}) async-start(f32[16,8,128]{2,1,0:T(8,128)} %broadcast_in_dim.55), calls=%async_computation.10 | async-start | bytes 131072 | tf_op jit(solution)/shard_map/gram_whole/all_to_all | solution.py:16
  257.7 3.8 %inverse_first.1.refs_1_ = f32[128,128]{1,0:T(8,128)} custom-call(f32[128,128]{1,0:T(8,128)} %get-tuple-element.83.refs_0_), custom_call_target="tpu_custom_call" | custom-call | flops 1073741824 | bytes 1048576 | tf_op jit(solution)/shard_map/inverse_first/pallas_call | solution.py:297
  263.3 4.5 %finish.1 = f32[96,128]{1,0:T(8,128)} custom-call(f32[128,128]{1,0:T(8,128)} %bitcast.100, f32[128,128]{1,0:T(8,128)} %inverse_first.1.refs_1_, f32[96,128]{1,0:T(8,128)} %copy-done.13), custom_call_target="tpu_custom_call" | custom-call | flops 1073741824 | bytes 1048576 | tf_op jit(solution)/shard_map/finish/pallas_call | solution.py:297
  (116 shorter events, 41.6 us)
Async XLA Ops:
  1.8 28.3 %all-to-all-start = ((f32[16,96,128]{2,1,0:T(8,128)}), f32[16,96,128]{2,1,0:T(8,128)S(1)}, u32[]{:S(2)}, u32[]{:S(2)}) async-start(f32[16,96,128]{2,1,0:T(8,128)} %broadcast_in_dim.21), calls=%async_computation | async-start | bytes 1572864 | tf_op jit(solution)/shard_map/gather_wide/all_to_all | solution.py:16
  7.6 10.0 %collective-permute-start = (f32[96,128]{1,0:T(8,128)}, f32[96,128]{1,0:T(8,128)S(1)}, u32[]{:S(2)}, u32[]{:S(2)}) collective-permute-start(f32[96,128]{1,0:T(8,128)} %param.9), channel_id=1, source_target_pairs={{0,8},{1,9},{2,10},{3,11},{4,12},{5,13},{6,14},{7,15},{8,0},{9,1},... | collective-permute-start | bytes 147464 | tf_op jit(solution)/shard_map/gather_row/ppermute | solution.py:203
  14.8 6.4 %collective-permute-start.2 = (f32[96,128]{1,0:T(8,128)}, f32[96,128]{1,0:T(8,128)S(1)}, u32[]{:S(2)}, u32[]{:S(2)}) collective-permute-start(f32[96,128]{1,0:T(8,128)} %param.9), channel_id=1, source_target_pairs={{0,12},{1,13},{2,14},{3,15},{4,8},{5,9},{6,10},{7,11},{8,4},{9,5},... | collective-permute-start | bytes 147464 | tf_op jit(solution)/shard_map/gather_row/ppermute | solution.py:203
  14.8 6.4 %collective-permute-start.1 = (f32[96,128]{1,0:T(8,128)}, f32[96,128]{1,0:T(8,128)S(1)}, u32[]{:S(2)}, u32[]{:S(2)}) collective-permute-start(f32[96,128]{1,0:T(8,128)} %param.9), channel_id=1, source_target_pairs={{0,4},{1,5},{2,6},{3,7},{4,0},{5,1},{6,2},{7,3},{8,12},{9,13},{10,... | collective-permute-start | bytes 147464 | tf_op jit(solution)/shard_map/gather_row/ppermute | solution.py:203
  22.0 22.1 %copy-start.12 = (f32[4,96,128]{2,1,0:T(8,128)}, f32[4,96,128]{2,1,0:T(8,128)S(1)}, u32[]{:S(2)}) copy-start(f32[4,96,128]{2,1,0:T(8,128)S(1)} %pad_maximum_fusion.first_ref) | copy-start | bytes 589828
  22.0 7.6 %collective-permute-start.4 = (f32[4,96,128]{2,1,0:T(8,128)S(1)}, f32[4,96,128]{2,1,0:T(8,128)S(1)}, u32[]{:S(2)}, u32[]{:S(2)}) collective-permute-start(f32[4,96,128]{2,1,0:T(8,128)S(1)} %pad_maximum_fusion.first_ref), channel_id=1, source_target_pairs={{0,1},{1,0},{2,3},{3,2},{4,5},{5,4},{6,7},{7,6},{8,9},{9,8},{10,11... | collective-permute-start | bytes 589832 | tf_op jit(solution)/shard_map/gather_row/ppermute | solution.py:203
  24.4 5.7 %collective-permute-start.3 = (f32[4,96,128]{2,1,0:T(8,128)S(1)}, f32[4,96,128]{2,1,0:T(8,128)S(1)}, u32[]{:S(2)}, u32[]{:S(2)}) collective-permute-start(f32[4,96,128]{2,1,0:T(8,128)S(1)} %pad_maximum_fusion.first_ref), channel_id=1, source_target_pairs={{0,2},{1,3},{2,0},{3,1},{4,6},{5,7},{6,4},{7,5},{8,10},{9,11},{10,... | collective-permute-start | bytes 589832 | tf_op jit(solution)/shard_map/gather_row/ppermute | solution.py:203
  29.6 20.4 %copy-start.15 = (f32[4,96,128]{2,1,0:T(8,128)}, f32[4,96,128]{2,1,0:T(8,128)S(1)}, u32[]{:S(2)}) copy-start(f32[4,96,128]{2,1,0:T(8,128)S(1)} %collective-permute-done.4.first_ref) | copy-start | bytes 589828
  30.1 14.0 %copy-start.16 = (f32[4,96,128]{2,1,0:T(8,128)}, f32[4,96,128]{2,1,0:T(8,128)S(1)}, u32[]{:S(2)}) copy-start(f32[4,96,128]{2,1,0:T(8,128)S(1)} %collective-permute-done.3.second_ref) | copy-start | bytes 589828
  32.4 29.2 %all-to-all-start.1 = ((f32[16,96,128]{2,1,0:T(8,128)}), f32[16,96,128]{2,1,0:T(8,128)S(1)}, u32[]{:S(2)}, u32[]{:S(2)}) async-start(f32[16,96,128]{2,1,0:T(8,128)} %gather_column.2), calls=%async_computation.1 | async-start | bytes 1572864 | tf_op jit(solution)/shard_map/gather_column/all_to_all | solution.py:16
  40.1 9.9 %collective-permute-start.5 = (f32[4,96,128]{2,1,0:T(8,128)S(1)}, f32[4,96,128]{2,1,0:T(8,128)S(1)}, u32[]{:S(2)}, u32[]{:S(2)}) collective-permute-start(f32[4,96,128]{2,1,0:T(8,128)S(1)} %collective-permute-done.3.second_ref), channel_id=1, source_target_pairs={{0,1},{1,0},{2,3},{3,2},{4,5},{5,4},{6,7},{7,6},{8,9},{9,8},{10,11... | collective-permute-start | bytes 589832 | tf_op jit(solution)/shard_map/gather_row/ppermute | solution.py:203
  44.1 22.0 %copy-start.20 = (s32[4]{0:T(128)S(1)}, s32[4]{0:T(128)}, u32[]{:S(2)}) copy-start(s32[4]{0:T(128)} %constant.20.clone) | copy-start | bytes 52
  61.6 29.6 %all-to-all-start.2 = ((f32[16,96,128]{2,1,0:T(8,128)}), f32[16,96,128]{2,1,0:T(8,128)S(1)}, u32[]{:S(2)}, u32[]{:S(2)}) async-start(f32[16,96,128]{2,1,0:T(8,128)} %bitcast.96), calls=%async_computation.2 | async-start | bytes 1572864 | tf_op jit(solution)/shard_map/back_transposed/all_to_all | solution.py:16
  66.8 18.6 %copy-start.1 = (s32[1,16]{1,0:T(1,128)S(1)}, s32[1,16]{1,0:T(1,128)}, u32[]{:S(2)}) copy-start(s32[1,16]{1,0:T(1,128)} %param.8) | copy-start | bytes 196
  71.0 12.5 %collective-permute-start.7 = (f32[4,96,128]{2,1,0:T(8,128)}, f32[4,96,128]{2,1,0:T(8,128)S(1)}, u32[]{:S(2)}, u32[]{:S(2)}) collective-permute-start(f32[4,96,128]{2,1,0:T(8,128)} %direct.6), channel_id=1, source_target_pairs={{0,1},{1,0},{2,3},{3,2},{4,5},{5,4},{6,7},{7,6},{8,9},{9,8},{10,11... | collective-permute-start | bytes 589832 | tf_op jit(solution)/shard_map/direct/ppermute | solution.py:203
  80.1 9.5 %collective-permute-start.6 = (f32[4,96,128]{2,1,0:T(8,128)}, f32[4,96,128]{2,1,0:T(8,128)S(1)}, u32[]{:S(2)}, u32[]{:S(2)}) collective-permute-start(f32[4,96,128]{2,1,0:T(8,128)} %get-tuple-element.50), channel_id=1, source_target_pairs={{0,1},{1,0},{2,3},{3,2},{4,5},{5,4},{6,7},{7,6},{8,9},{9,8},{10,11... | collective-permute-start | bytes 589832 | tf_op jit(solution)/shard_map/direct/ppermute | solution.py:203
  84.5 5.8 %collective-permute-start.8 = (f32[4,96,128]{2,1,0:T(8,128)S(1)}, f32[4,96,128]{2,1,0:T(8,128)S(1)}, u32[]{:S(2)}, u32[]{:S(2)}) collective-permute-start(f32[4,96,128]{2,1,0:T(8,128)S(1)} %add.58), channel_id=1, source_target_pairs={{0,2},{1,3},{2,0},{3,1},{4,6},{5,7},{6,4},{7,5},{8,10},{9,11},{10,... | collective-permute-start | bytes 589832 | tf_op jit(solution)/shard_map/direct/ppermute | solution.py:203
  93.2 1.8 collective-permute-start.12
  95.8 13.5 %all-to-all-start.3 = ((f32[8,96,128]{2,1,0:T(8,128)}), f32[8,96,128]{2,1,0:T(8,128)S(1)}, u32[]{:S(2)}, u32[]{:S(2)}) async-start(f32[8,96,128]{2,1,0:T(8,128)} %add.63), calls=%async_computation.3 | async-start | bytes 786432 | tf_op jit(solution)/shard_map/back_wide/all_to_all | solution.py:16
  101.5 8.9 %collective-permute-start.9 = (f32[96,128]{1,0:T(8,128)S(1)}, f32[96,128]{1,0:T(8,128)S(1)}, u32[]{:S(2)}, u32[]{:S(2)}) collective-permute-start(f32[96,128]{1,0:T(8,128)S(1)} %get-tuple-element.80), channel_id=1, source_target_pairs={{0,8},{1,9},{2,10},{3,11},{4,12},{5,13},{6,14},{7,15},{8,0},{9,1},... | collective-permute-start | bytes 147464 | tf_op jit(solution)/shard_map/back_direct/ppermute | solution.py:203
  107.5 6.4 %collective-permute-start.11 = (f32[96,128]{1,0:T(8,128)S(1)}, f32[96,128]{1,0:T(8,128)S(1)}, u32[]{:S(2)}, u32[]{:S(2)}) collective-permute-start(f32[96,128]{1,0:T(8,128)S(1)} %get-tuple-element.81), channel_id=1, source_target_pairs={{0,12},{1,13},{2,14},{3,15},{4,8},{5,9},{6,10},{7,11},{8,4},{9,5},... | collective-permute-start | bytes 147464 | tf_op jit(solution)/shard_map/back_direct/ppermute | solution.py:203
  108.0 5.9 %collective-permute-start.10 = (f32[96,128]{1,0:T(8,128)S(1)}, f32[96,128]{1,0:T(8,128)S(1)}, u32[]{:S(2)}, u32[]{:S(2)}) collective-permute-start(f32[96,128]{1,0:T(8,128)S(1)} %get-tuple-element.82), channel_id=1, source_target_pairs={{0,4},{1,5},{2,6},{3,7},{4,0},{5,1},{6,2},{7,3},{8,12},{9,13},{10,... | collective-permute-start | bytes 147464 | tf_op jit(solution)/shard_map/back_direct/ppermute | solution.py:203
  114.9 27.3 %all-to-all-start.4 = ((f32[16,96,128]{2,1,0:T(8,128)}), f32[16,96,128]{2,1,0:T(8,128)S(1)}, u32[]{:S(2)}, u32[]{:S(2)}) async-start(f32[16,96,128]{2,1,0:T(8,128)} %broadcast_in_dim.25), calls=%async_computation.4 | async-start | bytes 1572864 | tf_op jit(solution)/shard_map/gather_wide/all_to_all | solution.py:16
  120.7 6.5 %collective-permute-start.15 = (f32[96,128]{1,0:T(8,128)S(1)}, f32[96,128]{1,0:T(8,128)S(1)}, u32[]{:S(2)}, u32[]{:S(2)}) collective-permute-start(f32[96,128]{1,0:T(8,128)S(1)} %fusion.7), channel_id=1, source_target_pairs={{0,12},{1,13},{2,14},{3,15},{4,8},{5,9},{6,10},{7,11},{8,4},{9,5},... | collective-permute-start | bytes 147464 | tf_op jit(solution)/shard_map/gather_row/ppermute | solution.py:203
  123.4 5.4 %collective-permute-start.14 = (f32[96,128]{1,0:T(8,128)S(1)}, f32[96,128]{1,0:T(8,128)S(1)}, u32[]{:S(2)}, u32[]{:S(2)}) collective-permute-start(f32[96,128]{1,0:T(8,128)S(1)} %fusion.7), channel_id=1, source_target_pairs={{0,4},{1,5},{2,6},{3,7},{4,0},{5,1},{6,2},{7,3},{8,12},{9,13},{10,... | collective-permute-start | bytes 147464 | tf_op jit(solution)/shard_map/gather_row/ppermute | solution.py:203
  124.8 8.0 %collective-permute-start.13 = (f32[96,128]{1,0:T(8,128)S(1)}, f32[96,128]{1,0:T(8,128)S(1)}, u32[]{:S(2)}, u32[]{:S(2)}) collective-permute-start(f32[96,128]{1,0:T(8,128)S(1)} %fusion.7), channel_id=1, source_target_pairs={{0,8},{1,9},{2,10},{3,11},{4,12},{5,13},{6,14},{7,15},{8,0},{9,1},... | collective-permute-start | bytes 147464 | tf_op jit(solution)/shard_map/gather_row/ppermute | solution.py:203
  132.8 19.6 %copy-start.4 = (f32[4,96,128]{2,1,0:T(8,128)}, f32[4,96,128]{2,1,0:T(8,128)S(1)}, u32[]{:S(2)}) copy-start(f32[4,96,128]{2,1,0:T(8,128)S(1)} %pad_maximum_fusion.1.first_ref) | copy-start | bytes 589828
  132.8 7.4 %collective-permute-start.17 = (f32[4,96,128]{2,1,0:T(8,128)S(1)}, f32[4,96,128]{2,1,0:T(8,128)S(1)}, u32[]{:S(2)}, u32[]{:S(2)}) collective-permute-start(f32[4,96,128]{2,1,0:T(8,128)S(1)} %pad_maximum_fusion.1.first_ref), channel_id=1, source_target_pairs={{0,1},{1,0},{2,3},{3,2},{4,5},{5,4},{6,7},{7,6},{8,9},{9,8},{10,11... | collective-permute-start | bytes 589832 | tf_op jit(solution)/shard_map/gather_row/ppermute | solution.py:203
  136.6 5.7 %collective-permute-start.16 = (f32[4,96,128]{2,1,0:T(8,128)S(1)}, f32[4,96,128]{2,1,0:T(8,128)S(1)}, u32[]{:S(2)}, u32[]{:S(2)}) collective-permute-start(f32[4,96,128]{2,1,0:T(8,128)S(1)} %pad_maximum_fusion.1.first_ref), channel_id=1, source_target_pairs={{0,2},{1,3},{2,0},{3,1},{4,6},{5,7},{6,4},{7,5},{8,10},{9,11},{10,... | collective-permute-start | bytes 589832 | tf_op jit(solution)/shard_map/gather_row/ppermute | solution.py:203
  140.3 17.8 %copy-start.6 = (f32[4,96,128]{2,1,0:T(8,128)}, f32[4,96,128]{2,1,0:T(8,128)S(1)}, u32[]{:S(2)}) copy-start(f32[4,96,128]{2,1,0:T(8,128)S(1)} %collective-permute-done.17.first_ref) | copy-start | bytes 589828
  142.3 10.1 %copy-start.8 = (f32[4,96,128]{2,1,0:T(8,128)}, f32[4,96,128]{2,1,0:T(8,128)S(1)}, u32[]{:S(2)}) copy-start(f32[4,96,128]{2,1,0:T(8,128)S(1)} %collective-permute-done.16.second_ref) | copy-start | bytes 589828
  143.9 26.5 %all-to-all-start.5 = ((f32[16,96,128]{2,1,0:T(8,128)}), f32[16,96,128]{2,1,0:T(8,128)S(1)}, u32[]{:S(2)}, u32[]{:S(2)}) async-start(f32[16,96,128]{2,1,0:T(8,128)} %gather_column.3), calls=%async_computation.5 | async-start | bytes 1572864 | tf_op jit(solution)/shard_map/gather_column/all_to_all | solution.py:16
  149.0 9.1 %collective-permute-start.18 = (f32[4,96,128]{2,1,0:T(8,128)S(1)}, f32[4,96,128]{2,1,0:T(8,128)S(1)}, u32[]{:S(2)}, u32[]{:S(2)}) collective-permute-start(f32[4,96,128]{2,1,0:T(8,128)S(1)} %collective-permute-done.16.second_ref), channel_id=1, source_target_pairs={{0,1},{1,0},{2,3},{3,2},{4,5},{5,4},{6,7},{7,6},{8,9},{9,8},{10,11... | collective-permute-start | bytes 589832 | tf_op jit(solution)/shard_map/gather_row/ppermute | solution.py:203
  170.4 29.6 %all-to-all-start.6 = ((f32[16,96,128]{2,1,0:T(8,128)}), f32[16,96,128]{2,1,0:T(8,128)S(1)}, u32[]{:S(2)}, u32[]{:S(2)}) async-start(f32[16,96,128]{2,1,0:T(8,128)} %bitcast.97), calls=%async_computation.6 | async-start | bytes 1572864 | tf_op jit(solution)/shard_map/back_transposed/all_to_all | solution.py:16
  178.5 13.0 %copy-start.9 = (f32[4,96,128]{2,1,0:T(8,128)S(1)}, f32[4,96,128]{2,1,0:T(8,128)}, u32[]{:S(2)}) copy-start(f32[4,96,128]{2,1,0:T(8,128)} %copy-done.8) | copy-start | bytes 589828
  178.5 13.5 %copy-start.7 = (f32[4,96,128]{2,1,0:T(8,128)S(1)}, f32[4,96,128]{2,1,0:T(8,128)}, u32[]{:S(2)}) copy-start(f32[4,96,128]{2,1,0:T(8,128)} %copy-done.6) | copy-start | bytes 589828
  178.5 14.0 %copy-start.11 = (f32[4,96,128]{2,1,0:T(8,128)S(1)}, f32[4,96,128]{2,1,0:T(8,128)}, u32[]{:S(2)}) copy-start(f32[4,96,128]{2,1,0:T(8,128)} %copy-done.10) | copy-start | bytes 589828
  178.5 16.6 %copy-start.5 = (f32[4,96,128]{2,1,0:T(8,128)S(1)}, f32[4,96,128]{2,1,0:T(8,128)}, u32[]{:S(2)}) copy-start(f32[4,96,128]{2,1,0:T(8,128)} %copy-done.4) | copy-start | bytes 589828
  178.5 14.5 %collective-permute-start.20 = (f32[4,96,128]{2,1,0:T(8,128)}, f32[4,96,128]{2,1,0:T(8,128)S(1)}, u32[]{:S(2)}, u32[]{:S(2)}) collective-permute-start(f32[4,96,128]{2,1,0:T(8,128)} %direct.9), channel_id=1, source_target_pairs={{0,1},{1,0},{2,3},{3,2},{4,5},{5,4},{6,7},{7,6},{8,9},{9,8},{10,11... | collective-permute-start | bytes 589832 | tf_op jit(solution)/shard_map/direct/ppermute | solution.py:203
  191.2 7.5 %collective-permute-start.19 = (f32[4,96,128]{2,1,0:T(8,128)S(1)}, f32[4,96,128]{2,1,0:T(8,128)S(1)}, u32[]{:S(2)}, u32[]{:S(2)}) collective-permute-start(f32[4,96,128]{2,1,0:T(8,128)S(1)} %copy-done.19), channel_id=1, source_target_pairs={{0,1},{1,0},{2,3},{3,2},{4,5},{5,4},{6,7},{7,6},{8,9},{9,8},{10,11... | collective-permute-start | bytes 589832 | tf_op jit(solution)/shard_map/direct/ppermute | solution.py:203
  193.0 6.0 %collective-permute-start.21 = (f32[4,96,128]{2,1,0:T(8,128)S(1)}, f32[4,96,128]{2,1,0:T(8,128)S(1)}, u32[]{:S(2)}, u32[]{:S(2)}) collective-permute-start(f32[4,96,128]{2,1,0:T(8,128)S(1)} %add.66), channel_id=1, source_target_pairs={{0,2},{1,3},{2,0},{3,1},{4,6},{5,7},{6,4},{7,5},{8,10},{9,11},{10,... | collective-permute-start | bytes 589832 | tf_op jit(solution)/shard_map/direct/ppermute | solution.py:203
  202.3 1.9 collective-permute-start.25
  205.0 14.0 %all-to-all-start.7 = ((f32[8,104,128]{2,1,0:T(8,128)}), f32[8,104,128]{2,1,0:T(8,128)S(1)}, u32[]{:S(2)}, u32[]{:S(2)}) async-start(f32[8,104,128]{2,1,0:T(8,128)} %add.74), calls=%async_computation.7 | async-start | bytes 851968 | tf_op jit(solution)/shard_map/back_wide/all_to_all | solution.py:16
  210.7 8.7 %collective-permute-start.22 = (f32[96,128]{1,0:T(8,128)S(1)}, f32[96,128]{1,0:T(8,128)S(1)}, u32[]{:S(2)}, u32[]{:S(2)}) collective-permute-start(f32[96,128]{1,0:T(8,128)S(1)} %get-tuple-element.77), channel_id=1, source_target_pairs={{0,8},{1,9},{2,10},{3,11},{4,12},{5,13},{6,14},{7,15},{8,0},{9,1},... | collective-permute-start | bytes 147464 | tf_op jit(solution)/shard_map/back_direct/ppermute | solution.py:203
  216.5 6.6 %collective-permute-start.24 = (f32[96,128]{1,0:T(8,128)S(1)}, f32[96,128]{1,0:T(8,128)S(1)}, u32[]{:S(2)}, u32[]{:S(2)}) collective-permute-start(f32[96,128]{1,0:T(8,128)S(1)} %get-tuple-element.78), channel_id=1, source_target_pairs={{0,12},{1,13},{2,14},{3,15},{4,8},{5,9},{6,10},{7,11},{8,4},{9,5},... | collective-permute-start | bytes 147464 | tf_op jit(solution)/shard_map/back_direct/ppermute | solution.py:203
  217.1 6.1 %collective-permute-start.23 = (f32[96,128]{1,0:T(8,128)S(1)}, f32[96,128]{1,0:T(8,128)S(1)}, u32[]{:S(2)}, u32[]{:S(2)}) collective-permute-start(f32[96,128]{1,0:T(8,128)S(1)} %get-tuple-element.79), channel_id=1, source_target_pairs={{0,4},{1,5},{2,6},{3,7},{4,0},{5,1},{6,2},{7,3},{8,12},{9,13},{10,... | collective-permute-start | bytes 147464 | tf_op jit(solution)/shard_map/back_direct/ppermute | solution.py:203
  223.2 39.5 %copy-start.13 = (f32[96,128]{1,0:T(8,128)}, f32[96,128]{1,0:T(8,128)S(1)}, u32[]{:S(2)}) copy-start(f32[96,128]{1,0:T(8,128)S(1)} %slice_add_fusion.refs_2_) | copy-start | bytes 147460
  252.5 10.2 %all-to-all-start.10 = ((f32[16,8,128]{2,1,0:T(8,128)}), f32[16,8,128]{2,1,0:T(8,128)S(1)}, u32[]{:S(2)}, u32[]{:S(2)}) async-start(f32[16,8,128]{2,1,0:T(8,128)} %broadcast_in_dim.55), calls=%async_computation.10 | async-start | bytes 131072 | tf_op jit(solution)/shard_map/gram_whole/all_to_all | solution.py:16
  (8 other events, 22.1 us)

commit v7 on v5

--- a/solution.py
+++ b/solution.py
@@ -72,10 +72,16 @@
     return pl.CostEstimate(flops=3 * tile.size * width, bytes_accessed=2 * tile.size, transcendentals=0)
 
 
-def direct_quarters(tile, column_block, quarters, places):
+def direct_quarters(tile, column_block, quarters, where):
     each, _, _, rows, order = tile.shape
     width = column_block.shape[1]
     steps = len(quarters)
+
+    def second_of(g):
+        return quarters[0][0] + g * (quarters[-1][0] - quarters[0][0])
+
+    def far_of(g):
+        return quarters[0][1] + g * (quarters[-1][1] - quarters[0][1])
 
     def kernel(where_ref, tile_ref, column_ref, *rest):
         out_refs, both = rest[:-1], rest[-1]
@@ -95,7 +101,7 @@
             @pl.when(step == g)
             def _():
                 for k in range(each):
-                    out_ref[where_ref[2 * steps + k]] = total[k * rows : (k + 1) * rows]
+                    out_ref[where_ref[PLACES + k]] = total[k * rows : (k + 1) * rows]
 
     return pl.pallas_call(
         kernel,
@@ -105,23 +111,24 @@
             grid=(steps,),
             in_specs=[
                 pl.BlockSpec(
-                    (each, 1, 1, rows, order), lambda g, where: (0, where[2 * g], where[2 * g + 1], 0, 0)
+                    (each, 1, 1, rows, order),
+                    lambda g, where: (0, where[HALVES + 2] ^ second_of(g), where[HALVES] ^ far_of(g), 0, 0),
                 ),
                 pl.BlockSpec((order, width), lambda g, where: (0, 0)),
             ],
             out_specs=[pl.BlockSpec((each, rows, width), lambda g, where: (0, 0, 0))] * steps,
             scratch_shapes=[pltpu.VMEM((order, 2 * width), jnp.bfloat16)],
         ),
-        compiler_params=pltpu.CompilerParams(vmem_limit_bytes=60 << 20),
+        compiler_params=pltpu.CompilerParams(vmem_limit_bytes=50 << 20),
         cost_estimate=pl.CostEstimate(
             flops=3 * steps * each * rows * order * width,
             bytes_accessed=4 * steps * each * rows * order,
             transcendentals=0,
         ),
-    )(jnp.concatenate([jnp.stack([bit for pair in quarters for bit in pair]), places]), tile, column_block)
-
-
-def transposed_half(tile, quarters, half, spots, partial=None):
+    )(where, tile, column_block)
+
+
+def transposed_half(tile, quarters, half, where, partial=None):
     groups, _, rows, order = tile.shape
     width = quarters[0].shape[2]
     depth = groups * rows
@@ -135,7 +142,7 @@
         @pl.when(pl.program_id(0) == 0)
         def _():
             for k in range(groups):
-                spot = pl.multiple_of(where_ref[1 + k] * rows, rows)
+                spot = pl.multiple_of(where_ref[SPOTS + k] * rows, rows)
                 part = first_ref[k] if k < each else second_ref[k - each]
                 gathered[pl.ds(spot, rows)] = part
             high, low = high_low(gathered[...].T)
@@ -158,7 +165,7 @@
             num_scalar_prefetch=1,
             grid=(steps,),
             in_specs=[
-                pl.BlockSpec((groups, 1, rows, chunk), lambda g, where: (0, where[0], 0, g)),
+                pl.BlockSpec((groups, 1, rows, chunk), lambda g, where: (0, where[HALVES + half], 0, g)),
             ]
             + [pl.BlockSpec((each, rows, width), lambda g, where: (0, 0, 0))] * 2
             + ([] if partial is None else [flat]),
@@ -168,9 +175,9 @@
                 pltpu.VMEM((2 * width, depth), jnp.bfloat16),
             ],
         ),
-        compiler_params=pltpu.CompilerParams(vmem_limit_bytes=60 << 20),
+        compiler_params=pltpu.CompilerParams(vmem_limit_bytes=50 << 20),
         cost_estimate=kernel_cost(tile, width),
-    )(jnp.concatenate([half[None], spots]), tile, *quarters, *([] if partial is None else [partial]))
+    )(where, tile, *quarters, *([] if partial is None else [partial]))
 
 
 def swap(value, mask):
@@ -181,6 +188,19 @@
 ENTRIES = (8, 4, 12)
 REVERSED = (0, 4, 2, 6, 1, 5, 3, 7)
 REVERSED_PAIR = (0, 2, 1, 3)
+
+HALVES, SPOTS, PLACES = 0, 3, 11
+
+
+def kernel_indices(me):
+    high_bits = me >> 2
+    return jnp.concatenate(
+        [
+            jnp.stack([me & 1, (me & 1) ^ 1, (me >> 1) & 1]),
+            jnp.array(REVERSED, jnp.int32) ^ (me >> 1),
+            jnp.array(REVERSED_PAIR, jnp.int32) ^ ((high_bits & 1) << 1 | high_bits >> 1),
+        ]
+    )
 
 
 def summed_part(kept):
@@ -190,15 +210,11 @@
     return total
 
 
-def apply_hamiltonian(tile, columns, vectors, want_gram):
+def apply_hamiltonian(tile, columns, where, vectors, want_gram):
     rows, width = vectors.shape
     count = lax.axis_size(NARROW)
     order = count * rows
     groups = count // 2
-    me = lax.axis_index(NARROW).astype(jnp.int32)
-    near, far = me & 1, (me & 1) ^ 1
-    table = jnp.array(REVERSED, jnp.int32)
-    spots = table ^ (me >> 1)
     tile = tile.reshape(groups, 2, rows, order)
     with jax.named_scope("gather_wide"):
         slices = to_everyone(vectors, WIDE)
@@ -211,25 +227,22 @@
         picked = move_blocks(slices, columns, scatter=False)
         column_block = exchange(picked, NARROW).reshape(order, width)
     with jax.named_scope("transposed"):
-        partial = transposed_half(tile, near_rows, near, spots)
-        transposed = transposed_half(tile, far_rows, far, spots, partial)
+        partial = transposed_half(tile, near_rows, 0, where)
+        transposed = transposed_half(tile, far_rows, 1, where, partial)
         transposed, column_block = lax.optimization_barrier((transposed, column_block))
     with jax.named_scope("back_transposed"):
         arrived = exchange(transposed.reshape(count, rows, width), NARROW)
     with jax.named_scope("direct"):
         quarters = tile.reshape(groups // 2, 2, 2, rows, order)
-        first, second = (me >> 1) & 1, ((me >> 1) & 1) ^ 1
-        high_bits = me >> 2
-        places = jnp.array(REVERSED_PAIR, jnp.int32) ^ ((high_bits & 1) << 1 | high_bits >> 1)
-        (far_second,) = direct_quarters(quarters, column_block, [(second, far)], places)
+        (far_second,) = direct_quarters(quarters, column_block, [(1, 1)], where)
         column_block, far_second = lax.optimization_barrier((column_block, far_second))
         got_second = swap(far_second, 1)
         far_first, near_second = direct_quarters(
-            quarters, column_block, [(first, far), (second, near)], places
+            quarters, column_block, [(0, 1), (1, 0)], where
         )
         column_block, far_first = lax.optimization_barrier((column_block, far_first))
         got_first = swap(far_first, 1)
-        (near_first,) = direct_quarters(quarters, column_block, [(first, near)], places)
+        (near_first,) = direct_quarters(quarters, column_block, [(0, 0)], where)
         kept = near_first + got_first + swap(near_second + got_second, 2)
         arrived, kept = lax.optimization_barrier((arrived, kept))
     gram = None
@@ -255,21 +268,25 @@
     identity = (row == lax.broadcasted_iota(jnp.int32, (width, width), 1)).astype(jnp.float32)
     scale = jnp.sqrt(jnp.sum(gram * gram, keepdims=True) + 1e-06)
     current = gram / scale
-    inverse = identity
+    inverse = None
     for repeat in range(NS_STEPS):
-        middle = 1.5 * identity - 0.5 * exact(inverse, current)
-        current = exact(current, middle)
-        inverse = exact(middle, inverse)
+        middle = 1.5 * identity - 0.5 * (current if repeat == 0 else exact(inverse, current))
+        if repeat + 1 < NS_STEPS:
+            current = exact(current, middle)
+        inverse = middle if repeat == 0 else exact(middle, inverse)
     return inverse * jnp.sqrt(total_rows / scale)
 
 
-def in_kernel(function, shape, *arrays):
+def in_kernel(function, shapes, *arrays):
     def kernel(*refs):
-        refs[-1][...] = function(*(ref[...] for ref in refs[:-1]))
+        results = function(*(ref[...] for ref in refs[: len(arrays)]))
+        for ref, result in zip(refs[len(arrays) :], results):
+            ref[...] = result
 
     return pl.pallas_call(
         kernel,
-        out_shape=jax.ShapeDtypeStruct(shape, jnp.float32),
+        out_shape=[jax.ShapeDtypeStruct(shape, jnp.float32) for shape in shapes],
+        compiler_params=pltpu.CompilerParams(vmem_limit_bytes=8 << 20),
         cost_estimate=pl.CostEstimate(flops=1 << 30, bytes_accessed=1 << 20, transcendentals=0),
     )(*arrays)
 
@@ -281,8 +298,9 @@
 def on_device(tile, row_columns, start_vectors):
     total_rows = float(lax.axis_size(WIDE) * lax.axis_size(NARROW) * start_vectors.shape[0])
     columns = row_columns[0]
-    first, _ = apply_hamiltonian(tile, columns, start_vectors, want_gram=False)
-    second, gram_rows = apply_hamiltonian(tile, columns, first, want_gram=True)
+    where = kernel_indices(lax.axis_index(NARROW).astype(jnp.int32))
+    first, _ = apply_hamiltonian(tile, columns, where, start_vectors, want_gram=False)
+    second, gram_rows = apply_hamiltonian(tile, columns, where, first, want_gram=True)
     width = second.shape[1]
     wide = lax.axis_size(WIDE)
     with jax.named_scope("gram_sum_wide"):
@@ -293,17 +311,20 @@
         gram_first = got[:, width // wide :].reshape(width, width)
     with jax.named_scope("gram_sum_narrow"):
         gram_second = to_everyone(gram_second, NARROW).sum(axis=0)
+    def begin(gram, value):
+        root = inverse_root(gram, total_rows)
+        return root, exact(value, root)
+
+    def finish(gram, root, value):
+        gram = exact(root.T, exact(gram, root))
+        return (exact(value, inverse_root(gram, total_rows)),)
+
     with jax.named_scope("inverse_first"):
-        root_first = in_kernel(lambda gram: inverse_root(gram, total_rows), (width, width), gram_first)
+        root_first, second = in_kernel(begin, [(width, width), second.shape], gram_first, second)
     with jax.named_scope("gram_whole"):
         gram_second = to_everyone(gram_second, WIDE).reshape(width, width)
-
-    def finish(gram, root, value):
-        gram = exact(root.T, exact(gram, root))
-        return exact(exact(value, root), inverse_root(gram, total_rows))
-
     with jax.named_scope("finish"):
-        return in_kernel(finish, second.shape, gram_second, root_first, second)
+        return in_kernel(finish, [second.shape], gram_second, root_first, second)[0]
 
 
 def solution(mesh):

time: 269 us -> 260 us (0.967)
  Pallas kernels: 64.7 us -> 52.8 us
  waiting for transfers between devices: 54.8 us -> 63.3 us
  other arithmetic: 6.5 us -> 2.46 us
  starting transfers between devices: 101 us -> 104 us
  local copies, waits for them, and re-layouts: 6.86 us -> 4.14 us
    all_to_all x9, waiting for transfers between devices: 24.7 us -> 32.4 us  [exchange(): return lax.all_to_all(parts, axis, 0, 0, tiled=True)]
    pallas_call x6, Pallas kernels: 26.5 us -> 20.1 us  [direct_quarters(): pl.pallas_call(kernel, out_shape=[jax.ShapeDtypeStruct((each, rows, width...]
    ppermute x24, starting transfers between devices: 53.1 us -> 57.4 us  [swap(): return lax.ppermute(value, NARROW, [(i, i ^ mask) for i in range(size)])]
    pallas_call x4, Pallas kernels: 23.3 us -> 20.4 us  [transposed_half(): pl.pallas_call(kernel, out_shape=jax.ShapeDtypeStruct((width, order) if p...]
    add x4, other arithmetic: 2.92 us -> 0.13 us  [apply_hamiltonian(): kept = near_first + got_first + swap(near_second + got_second, 2)]
  transfers between devices with their start and end apart: 33 -> 33, of which waited for: 17 -> 20; matrix products, arithmetic and copies ran while one was open for 3% -> 2% of each run, Pallas kernels for 20% -> 17%
where the time goes in v7:
time: 260 us; the launch traced here: 256 us
  starting transfers between devices  104 us (40%)
  waiting for transfers between devices  63.3 us (24%)
  Pallas kernels  52.8 us (20%)
  blocking collectives  26.9 us (10%)
  local copies, waits for them, and re-layouts  4.14 us (2%)
    ppermute x24, starting transfers between devices, swap(): return lax.ppermute(value, NARROW, [(i, i ^ mask) for i in range(size)])  57.4 us
    all_to_all x9, starting transfers between devices, exchange(): return lax.all_to_all(parts, axis, 0, 0, tiled=True)  46.6 us
    all_to_all x9, waiting for transfers between devices, exchange(): return lax.all_to_all(parts, axis, 0, 0, tiled=True)  32.4 us
    ppermute x24, waiting for transfers between devices, swap(): return lax.ppermute(value, NARROW, [(i, i ^ mask) for i in range(size)])  30.9 us
    all_to_all x2, blocking collectives, exchange(): return lax.all_to_all(parts, axis, 0, 0, tiled=True)  26.9 us
    pallas_call x4, Pallas kernels, transposed_half(): pl.pallas_call(kernel, out_shape=jax.ShapeDtypeStruct((width, order) if p...  20.4 us
    pallas_call x6, Pallas kernels, direct_quarters(): pl.pallas_call(kernel, out_shape=[jax.ShapeDtypeStruct((each, rows, width...  20.1 us
    pallas_call x4, Pallas kernels, move_blocks(): pl.pallas_call(kernel, out_shape=jax.ShapeDtypeStruct((count, rows + more...  6.51 us
  transfers between devices with their start and end apart: 33, of which 20 were waited for; matrix products, arithmetic and copies ran while one was open for 2% of the time, Pallas kernels for 17%

profile of v7, /device:TPU:8, one launch (start us, length us, event | category | flops | bytes accessed | tf_op | source)
XLA Modules:
  0.0 256.2 jit_solution(14091573637693547414)
XLA Ops:
  1.8 5.8 %all-to-all-start = ((f32[16,96,128]{2,1,0:T(8,128)}), f32[16,96,128]{2,1,0:T(8,128)S(1)}, u32[]{:S(2)}, u32[]{:S(2)}) async-start(f32[16,96,128]{2,1,0:T(8,128)} %broadcast_in_dim.14), calls=%async_computation | async-start | bytes 1572864 | tf_op jit(solution)/shard_map/gather_wide/all_to_all | solution.py:14
  7.5 7.2 %collective-permute-start = (f32[96,128]{1,0:T(8,128)}, f32[96,128]{1,0:T(8,128)S(1)}, u32[]{:S(2)}, u32[]{:S(2)}) collective-permute-start(f32[96,128]{1,0:T(8,128)} %param.7), channel_id=1, source_target_pairs={{0,8},{1,9},{2,10},{3,11},{4,12},{5,13},{6,14},{7,15},{8,0},{9,1},... | collective-permute-start | bytes 147464 | tf_op jit(solution)/shard_map/gather_row/ppermute | solution.py:185
  17.5 3.6 %collective-permute-done.2 = f32[96,128]{1,0:T(8,128)S(1)} collective-permute-done((f32[96,128]{1,0:T(8,128)}, f32[96,128]{1,0:T(8,128)S(1)}, u32[]{:S(2)}, u32[]{:S(2)}) %collective-permute-start.2) | collective-permute-done | bytes 49184 | tf_op jit(solution)/shard_map/gather_row/ppermute | solution.py:185
  22.0 2.4 collective-permute-start.4
  25.9 3.6 %collective-permute-done.4.first_ref = f32[4,96,128]{2,1,0:T(8,128)S(1)} collective-permute-done((f32[4,96,128]{2,1,0:T(8,128)S(1)}, f32[4,96,128]{2,1,0:T(8,128)S(1)}, u32[]{:S(2)}, u32[]{:S(2)}) %collective-permute-start.4) | collective-permute-done | bytes 196640 | tf_op jit(solution)/shard_map/gather_row/ppermute | solution.py:185
  32.3 7.0 %all-to-all-start.1 = ((f32[16,96,128]{2,1,0:T(8,128)}), f32[16,96,128]{2,1,0:T(8,128)S(1)}, u32[]{:S(2)}, u32[]{:S(2)}) async-start(f32[16,96,128]{2,1,0:T(8,128)} %gather_column.2), calls=%async_computation.1 | async-start | bytes 1572864 | tf_op jit(solution)/shard_map/gather_column/all_to_all | solution.py:14
  40.0 3.4 %collective-permute-start.5 = (f32[4,96,128]{2,1,0:T(8,128)S(1)}, f32[4,96,128]{2,1,0:T(8,128)S(1)}, u32[]{:S(2)}, u32[]{:S(2)}) collective-permute-start(f32[4,96,128]{2,1,0:T(8,128)S(1)} %collective-permute-done.3.second_ref), channel_id=1, source_target_pairs={{0,1},{1,0},{2,3},{3,2},{4,5},{5,4},{6,7},{7,6},{8,9},{9,8},{10,11... | collective-permute-start | bytes 589832 | tf_op jit(solution)/shard_map/gather_row/ppermute | solution.py:185
  44.2 4.6 %transposed.4.rest_0_ = f32[128,1536]{1,0:T(8,128)S(1)} custom-call(s32[15]{0:T(128)S(1)} %concatenate.6.where_ref, f32[8,2,96,1536]{3,2,1,0:T(8,128)} %bitcast.86, f32[4,96,128]{2,1,0:T(8,128)S(1)} %pad_maximum_fusion.first_ref, f32[4,96,128]{2,1,0:T(8,128)S(1)} %collective-permute-done.3.second_ref), custom_call_target="tpu_custom_call" | custom-call | flops 905969664 | bytes 4718592 | tf_op jit(solution)/shard_map/transposed/pallas_call | solution.py:161
  48.8 5.6 %transposed.5 = f32[1536,128]{1,0:T(8,128)} custom-call(s32[15]{0:T(128)S(1)} %concatenate.6.where_ref, f32[8,2,96,1536]{3,2,1,0:T(8,128)} %bitcast.87, f32[4,96,128]{2,1,0:T(8,128)S(1)} %collective-permute-done.4.first_ref, f32[4,96,128]{2,1,0:T(8,128)S(1)} %collective-permute-done.5.second_ref, f32[128,1536]{1,0:T(8,128)S(1)} %transposed.4.rest_0_), custom_call_target="tpu_custom_call" | custom-call | flops 905969664 | bytes 4718592 | tf_op jit(solution)/shard_map/transposed/pallas_call | solution.py:161
  54.4 7.1 %all-to-all-done.1 = f32[16,96,128]{2,1,0:T(8,128)S(1)} async-done(((f32[16,96,128]{2,1,0:T(8,128)}), f32[16,96,128]{2,1,0:T(8,128)S(1)}, u32[]{:S(2)}, u32[]{:S(2)}) %all-to-all-start.1) | async-done | bytes 786464 | tf_op jit(solution)/shard_map/gather_column/all_to_all | solution.py:14
  61.5 3.6 %all-to-all-start.2 = ((f32[16,96,128]{2,1,0:T(8,128)}), f32[16,96,128]{2,1,0:T(8,128)S(1)}, u32[]{:S(2)}, u32[]{:S(2)}) async-start(f32[16,96,128]{2,1,0:T(8,128)} %bitcast.10), calls=%async_computation.2 | async-start | bytes 1572864 | tf_op jit(solution)/shard_map/back_transposed/all_to_all | solution.py:14
  65.1 3.0 %direct.6 = f32[4,96,128]{2,1,0:T(8,128)S(1)} custom-call(s32[15]{0:T(128)S(1)} %concatenate.6.where_ref, f32[4,2,2,96,1536]{4,3,2,1,0:T(8,128)} %bitcast.88, f32[1536,128]{1,0:T(8,128)S(1)} %bitcast.75), custom_call_target="tpu_custom_call" | custom-call | flops 226492416 | bytes 2359296 | tf_op jit(solution)/shard_map/direct/pallas_call | solution.py:106
  68.1 3.4 %collective-permute-start.7 = (f32[4,96,128]{2,1,0:T(8,128)S(1)}, f32[4,96,128]{2,1,0:T(8,128)S(1)}, u32[]{:S(2)}, u32[]{:S(2)}) collective-permute-start(f32[4,96,128]{2,1,0:T(8,128)S(1)} %direct.6), channel_id=1, source_target_pairs={{0,1},{1,0},{2,3},{3,2},{4,5},{5,4},{6,7},{7,6},{8,9},{9,8},{10,11... | collective-permute-start | bytes 589832 | tf_op jit(solution)/shard_map/direct/ppermute | solution.py:185
  71.6 4.0 %direct.7 = (f32[4,96,128]{2,1,0:T(8,128)S(1)}, f32[4,96,128]{2,1,0:T(8,128)S(1)}) custom-call(s32[15]{0:T(128)S(1)} %concatenate.6.where_ref, f32[4,2,2,96,1536]{4,3,2,1,0:T(8,128)} %bitcast.89, f32[1536,128]{1,0:T(8,128)S(1)} %bitcast.76), custom_call_target="tpu_custom_call" | custom-call | flops 452984832 | bytes 4718592 | tf_op jit(solution)/shard_map/direct/pallas_call | solution.py:106
  75.8 2.9 %collective-permute-done.7 = f32[4,96,128]{2,1,0:T(8,128)S(1)} collective-permute-done((f32[4,96,128]{2,1,0:T(8,128)S(1)}, f32[4,96,128]{2,1,0:T(8,128)S(1)}, u32[]{:S(2)}, u32[]{:S(2)}) %collective-permute-start.7) | collective-permute-done | bytes 196640 | tf_op jit(solution)/shard_map/direct/ppermute | solution.py:185
  78.8 4.2 %collective-permute-start.8 = (f32[4,96,128]{2,1,0:T(8,128)S(1)}, f32[4,96,128]{2,1,0:T(8,128)S(1)}, u32[]{:S(2)}, u32[]{:S(2)}) collective-permute-start(f32[4,96,128]{2,1,0:T(8,128)S(1)} %add.52), channel_id=1, source_target_pairs={{0,2},{1,3},{2,0},{3,1},{4,6},{5,7},{6,4},{7,5},{8,10},{9,11},{10,... | collective-permute-start | bytes 589832 | tf_op jit(solution)/shard_map/direct/ppermute | solution.py:185
  82.9 3.0 %direct.8 = f32[4,96,128]{2,1,0:T(8,128)S(1)} custom-call(s32[15]{0:T(128)S(1)} %concatenate.6.where_ref, f32[4,2,2,96,1536]{4,3,2,1,0:T(8,128)} %bitcast.90, f32[1536,128]{1,0:T(8,128)S(1)} %bitcast.77), custom_call_target="tpu_custom_call" | custom-call | flops 226492416 | bytes 2359296 | tf_op jit(solution)/shard_map/direct/pallas_call | solution.py:106
  86.6 2.6 %all-to-all-done.2.blocks_ref = f32[16,96,128]{2,1,0:T(8,128)S(1)} async-done(((f32[16,96,128]{2,1,0:T(8,128)}), f32[16,96,128]{2,1,0:T(8,128)S(1)}, u32[]{:S(2)}, u32[]{:S(2)}) %all-to-all-start.2) | async-done | bytes 786464 | tf_op jit(solution)/shard_map/back_transposed/all_to_all | solution.py:14
  90.8 5.7 %all-to-all-start.3 = ((f32[16,96,128]{2,1,0:T(8,128)}), f32[16,96,128]{2,1,0:T(8,128)S(1)}, u32[]{:S(2)}, u32[]{:S(2)}) async-start(f32[16,96,128]{2,1,0:T(8,128)} %back_wide.2), calls=%async_computation.3 | async-start | bytes 1572864 | tf_op jit(solution)/shard_map/back_wide/all_to_all | solution.py:14
  96.6 4.1 %collective-permute-start.9 = (f32[96,128]{1,0:T(8,128)S(1)}, f32[96,128]{1,0:T(8,128)S(1)}, u32[]{:S(2)}, u32[]{:S(2)}) collective-permute-start(f32[96,128]{1,0:T(8,128)S(1)} %get-tuple-element.76), channel_id=1, source_target_pairs={{0,8},{1,9},{2,10},{3,11},{4,12},{5,13},{6,14},{7,15},{8,0},{9,1},... | collective-permute-start | bytes 147464 | tf_op jit(solution)/shard_map/back_direct/ppermute | solution.py:185
  100.7 2.4 collective-permute-start.10
  103.1 5.6 %all-to-all-done.3 = f32[16,96,128]{2,1,0:T(8,128)S(1)} async-done(((f32[16,96,128]{2,1,0:T(8,128)}), f32[16,96,128]{2,1,0:T(8,128)S(1)}, u32[]{:S(2)}, u32[]{:S(2)}) %all-to-all-start.3) | async-done | bytes 786464 | tf_op jit(solution)/shard_map/back_wide/all_to_all | solution.py:14
  109.8 5.2 %all-to-all-start.4 = ((f32[16,96,128]{2,1,0:T(8,128)}), f32[16,96,128]{2,1,0:T(8,128)S(1)}, u32[]{:S(2)}, u32[]{:S(2)}) async-start(f32[16,96,128]{2,1,0:T(8,128)} %broadcast_in_dim.16), calls=%async_computation.4 | async-start | bytes 1572864 | tf_op jit(solution)/shard_map/gather_wide/all_to_all | solution.py:14
  115.0 2.4 collective-permute-start.14
  117.3 2.3 collective-permute-start.13
  122.3 5.3 %collective-permute-done.12 = f32[96,128]{1,0:T(8,128)S(1)} collective-permute-done((f32[96,128]{1,0:T(8,128)S(1)}, f32[96,128]{1,0:T(8,128)S(1)}, u32[]{:S(2)}, u32[]{:S(2)}) %collective-permute-start.12) | collective-permute-done | bytes 49184 | tf_op jit(solution)/shard_map/gather_row/ppermute | solution.py:185
  127.7 4.4 %collective-permute-start.16 = (f32[4,96,128]{2,1,0:T(8,128)S(1)}, f32[4,96,128]{2,1,0:T(8,128)S(1)}, u32[]{:S(2)}, u32[]{:S(2)}) collective-permute-start(f32[4,96,128]{2,1,0:T(8,128)S(1)} %pad_maximum_fusion.1.first_ref), channel_id=1, source_target_pairs={{0,1},{1,0},{2,3},{3,2},{4,5},{5,4},{6,7},{7,6},{8,9},{9,8},{10,11... | collective-permute-start | bytes 589832 | tf_op jit(solution)/shard_map/gather_row/ppermute | solution.py:185
  132.4 3.6 %collective-permute-done.16.first_ref = f32[4,96,128]{2,1,0:T(8,128)S(1)} collective-permute-done((f32[4,96,128]{2,1,0:T(8,128)S(1)}, f32[4,96,128]{2,1,0:T(8,128)S(1)}, u32[]{:S(2)}, u32[]{:S(2)}) %collective-permute-start.16) | collective-permute-done | bytes 196640 | tf_op jit(solution)/shard_map/gather_row/ppermute | solution.py:185
  139.4 3.6 %all-to-all-start.5 = ((f32[16,96,128]{2,1,0:T(8,128)}), f32[16,96,128]{2,1,0:T(8,128)S(1)}, u32[]{:S(2)}, u32[]{:S(2)}) async-start(f32[16,96,128]{2,1,0:T(8,128)} %gather_column.3), calls=%async_computation.5 | async-start | bytes 1572864 | tf_op jit(solution)/shard_map/gather_column/all_to_all | solution.py:14
  143.0 3.4 %collective-permute-start.17 = (f32[4,96,128]{2,1,0:T(8,128)S(1)}, f32[4,96,128]{2,1,0:T(8,128)S(1)}, u32[]{:S(2)}, u32[]{:S(2)}) collective-permute-start(f32[4,96,128]{2,1,0:T(8,128)S(1)} %collective-permute-done.15.second_ref), channel_id=1, source_target_pairs={{0,1},{1,0},{2,3},{3,2},{4,5},{5,4},{6,7},{7,6},{8,9},{9,8},{10,11... | collective-permute-start | bytes 589832 | tf_op jit(solution)/shard_map/gather_row/ppermute | solution.py:185
  146.4 4.6 %transposed.6.rest_0_ = f32[128,1536]{1,0:T(8,128)S(1)} custom-call(s32[15]{0:T(128)S(1)} %concatenate.6.where_ref, f32[8,2,96,1536]{3,2,1,0:T(8,128)} %bitcast.91, f32[4,96,128]{2,1,0:T(8,128)S(1)} %pad_maximum_fusion.1.first_ref, f32[4,96,128]{2,1,0:T(8,128)S(1)} %collective-permute-done.15.second_ref), custom_call_target="tpu_custom_call" | custom-call | flops 905969664 | bytes 4718592 | tf_op jit(solution)/shard_map/transposed/pallas_call | solution.py:161
  151.3 5.6 %transposed.7 = f32[1536,128]{1,0:T(8,128)} custom-call(s32[15]{0:T(128)S(1)} %concatenate.6.where_ref, f32[8,2,96,1536]{3,2,1,0:T(8,128)} %bitcast.92, f32[4,96,128]{2,1,0:T(8,128)S(1)} %collective-permute-done.16.first_ref, f32[4,96,128]{2,1,0:T(8,128)S(1)} %collective-permute-done.17.second_ref, f32[128,1536]{1,0:T(8,128)S(1)} %transposed.6.rest_0_), custom_call_target="tpu_custom_call" | custom-call | flops 905969664 | bytes 4718592 | tf_op jit(solution)/shard_map/transposed/pallas_call | solution.py:161
  156.9 8.5 %all-to-all-done.5 = f32[16,96,128]{2,1,0:T(8,128)S(1)} async-done(((f32[16,96,128]{2,1,0:T(8,128)}), f32[16,96,128]{2,1,0:T(8,128)S(1)}, u32[]{:S(2)}, u32[]{:S(2)}) %all-to-all-start.5) | async-done | bytes 786464 | tf_op jit(solution)/shard_map/gather_column/all_to_all | solution.py:14
  165.4 3.6 %all-to-all-start.6 = ((f32[16,96,128]{2,1,0:T(8,128)}), f32[16,96,128]{2,1,0:T(8,128)S(1)}, u32[]{:S(2)}, u32[]{:S(2)}) async-start(f32[16,96,128]{2,1,0:T(8,128)} %bitcast.21), calls=%async_computation.6 | async-start | bytes 1572864 | tf_op jit(solution)/shard_map/back_transposed/all_to_all | solution.py:14
  169.0 3.0 %direct.9 = f32[4,96,128]{2,1,0:T(8,128)S(1)} custom-call(s32[15]{0:T(128)S(1)} %concatenate.6.where_ref, f32[4,2,2,96,1536]{4,3,2,1,0:T(8,128)} %bitcast.93, f32[1536,128]{1,0:T(8,128)S(1)} %bitcast.78), custom_call_target="tpu_custom_call" | custom-call | flops 226492416 | bytes 2359296 | tf_op jit(solution)/shard_map/direct/pallas_call | solution.py:106
  172.1 3.4 %collective-permute-start.19 = (f32[4,96,128]{2,1,0:T(8,128)S(1)}, f32[4,96,128]{2,1,0:T(8,128)S(1)}, u32[]{:S(2)}, u32[]{:S(2)}) collective-permute-start(f32[4,96,128]{2,1,0:T(8,128)S(1)} %direct.9), channel_id=1, source_target_pairs={{0,1},{1,0},{2,3},{3,2},{4,5},{5,4},{6,7},{7,6},{8,9},{9,8},{10,11... | collective-permute-start | bytes 589832 | tf_op jit(solution)/shard_map/direct/ppermute | solution.py:185
  175.5 4.0 %direct.10 = (f32[4,96,128]{2,1,0:T(8,128)S(1)}, f32[4,96,128]{2,1,0:T(8,128)S(1)}) custom-call(s32[15]{0:T(128)S(1)} %concatenate.6.where_ref, f32[4,2,2,96,1536]{4,3,2,1,0:T(8,128)} %bitcast.94, f32[1536,128]{1,0:T(8,128)S(1)} %bitcast.79), custom_call_target="tpu_custom_call" | custom-call | flops 452984832 | bytes 4718592 | tf_op jit(solution)/shard_map/direct/pallas_call | solution.py:106
  179.5 3.0 %direct.11 = f32[4,96,128]{2,1,0:T(8,128)S(1)} custom-call(s32[15]{0:T(128)S(1)} %concatenate.6.where_ref, f32[4,2,2,96,1536]{4,3,2,1,0:T(8,128)} %bitcast.95, f32[1536,128]{1,0:T(8,128)S(1)} %bitcast.80), custom_call_target="tpu_custom_call" | custom-call | flops 226492416 | bytes 2359296 | tf_op jit(solution)/shard_map/direct/pallas_call | solution.py:106
  186.7 6.4 %collective-permute-done.18 = f32[4,96,128]{2,1,0:T(8,128)S(1)} collective-permute-done((f32[4,96,128]{2,1,0:T(8,128)S(1)}, f32[4,96,128]{2,1,0:T(8,128)S(1)}, u32[]{:S(2)}, u32[]{:S(2)}) %collective-permute-start.18) | collective-permute-done | bytes 196640 | tf_op jit(solution)/shard_map/direct/ppermute | solution.py:185
  195.0 6.7 %all-to-all-start.7 = ((f32[16,104,128]{2,1,0:T(8,128)}), f32[16,104,128]{2,1,0:T(8,128)S(1)}, u32[]{:S(2)}, u32[]{:S(2)}) async-start(f32[16,104,128]{2,1,0:T(8,128)} %back_wide.3), calls=%async_computation.7 | async-start | bytes 1703936 | tf_op jit(solution)/shard_map/back_wide/all_to_all | solution.py:14
  201.8 4.5 %collective-permute-start.21 = (f32[96,128]{1,0:T(8,128)S(1)}, f32[96,128]{1,0:T(8,128)S(1)}, u32[]{:S(2)}, u32[]{:S(2)}) collective-permute-start(f32[96,128]{1,0:T(8,128)S(1)} %get-tuple-element.73), channel_id=1, source_target_pairs={{0,8},{1,9},{2,10},{3,11},{4,12},{5,13},{6,14},{7,15},{8,0},{9,1},... | collective-permute-start | bytes 147464 | tf_op jit(solution)/shard_map/back_direct/ppermute | solution.py:185
  208.6 6.1 %all-to-all-done.7 = f32[16,104,128]{2,1,0:T(8,128)S(1)} async-done(((f32[16,104,128]{2,1,0:T(8,128)}), f32[16,104,128]{2,1,0:T(8,128)S(1)}, u32[]{:S(2)}, u32[]{:S(2)}) %all-to-all-start.7) | async-done | bytes 852000 | tf_op jit(solution)/shard_map/back_wide/all_to_all | solution.py:14
  215.1 9.4 %all_to_all.55 = f32[16,16,128]{2,1,0:T(8,128)S(1)} all-to-all(f32[16,16,128]{2,1,0:T(8,128)S(1)} %pad_maximum_fusion.2), channel_id=1, replica_groups=mesh['wide'=16,'narrow'=16] {'wide'}, dimensions={0} | all-to-all | bytes 262144 | tf_op jit(solution)/shard_map/gram_sum_wide/all_to_all | solution.py:14
  224.5 17.5 %all_to_all.56 = f32[16,8,128]{2,1,0:T(8,128)S(1)} all-to-all(f32[16,8,128]{2,1,0:T(8,128)S(1)} %broadcast_in_dim.19), channel_id=1, replica_groups=mesh['wide'=16,'narrow'=16] {'narrow'}, dimensions={0} | all-to-all | bytes 131072 | tf_op jit(solution)/shard_map/gram_sum_narrow/all_to_all | solution.py:14
  242.7 5.2 %all-to-all-start.10 = ((f32[16,8,128]{2,1,0:T(8,128)}), f32[16,8,128]{2,1,0:T(8,128)S(1)}, u32[]{:S(2)}, u32[]{:S(2)}) async-start(f32[16,8,128]{2,1,0:T(8,128)} %broadcast_in_dim.40), calls=%async_computation.10 | async-start | bytes 131072 | tf_op jit(solution)/shard_map/gram_whole/all_to_all | solution.py:14
  247.9 2.3 inverse_first.1
  250.3 2.6 %all-to-all-done.10 = f32[16,8,128]{2,1,0:T(8,128)S(1)} async-done(((f32[16,8,128]{2,1,0:T(8,128)}), f32[16,8,128]{2,1,0:T(8,128)S(1)}, u32[]{:S(2)}, u32[]{:S(2)}) %all-to-all-start.10) | async-done | bytes 65568 | tf_op jit(solution)/shard_map/gram_whole/all_to_all | solution.py:14
  252.8 3.4 %finish.1 = f32[96,128]{1,0:T(8,128)} custom-call(f32[128,128]{1,0:T(8,128)S(1)} %bitcast.81, f32[128,128]{1,0:T(8,128)S(1)} %get-tuple-element.71.refs_1_, f32[96,128]{1,0:T(8,128)S(1)} %get-tuple-element.72.refs_2_), custom_call_target="tpu_custom_call" | custom-call | flops 1073741824 | bytes 1048576 | tf_op jit(solution)/shard_map/finish/pallas_call | solution.py:286
  (69 shorter events, 30.7 us)
Async XLA Ops:
  1.8 28.3 %all-to-all-start = ((f32[16,96,128]{2,1,0:T(8,128)}), f32[16,96,128]{2,1,0:T(8,128)S(1)}, u32[]{:S(2)}, u32[]{:S(2)}) async-start(f32[16,96,128]{2,1,0:T(8,128)} %broadcast_in_dim.14), calls=%async_computation | async-start | bytes 1572864 | tf_op jit(solution)/shard_map/gather_wide/all_to_all | solution.py:14
  7.5 10.0 %collective-permute-start = (f32[96,128]{1,0:T(8,128)}, f32[96,128]{1,0:T(8,128)S(1)}, u32[]{:S(2)}, u32[]{:S(2)}) collective-permute-start(f32[96,128]{1,0:T(8,128)} %param.7), channel_id=1, source_target_pairs={{0,8},{1,9},{2,10},{3,11},{4,12},{5,13},{6,14},{7,15},{8,0},{9,1},... | collective-permute-start | bytes 147464 | tf_op jit(solution)/shard_map/gather_row/ppermute | solution.py:185
  14.7 6.4 %collective-permute-start.2 = (f32[96,128]{1,0:T(8,128)}, f32[96,128]{1,0:T(8,128)S(1)}, u32[]{:S(2)}, u32[]{:S(2)}) collective-permute-start(f32[96,128]{1,0:T(8,128)} %param.7), channel_id=1, source_target_pairs={{0,12},{1,13},{2,14},{3,15},{4,8},{5,9},{6,10},{7,11},{8,4},{9,5},... | collective-permute-start | bytes 147464 | tf_op jit(solution)/shard_map/gather_row/ppermute | solution.py:185
  14.7 6.4 %collective-permute-start.1 = (f32[96,128]{1,0:T(8,128)}, f32[96,128]{1,0:T(8,128)S(1)}, u32[]{:S(2)}, u32[]{:S(2)}) collective-permute-start(f32[96,128]{1,0:T(8,128)} %param.7), channel_id=1, source_target_pairs={{0,4},{1,5},{2,6},{3,7},{4,0},{5,1},{6,2},{7,3},{8,12},{9,13},{10,... | collective-permute-start | bytes 147464 | tf_op jit(solution)/shard_map/gather_row/ppermute | solution.py:185
  22.0 7.6 %collective-permute-start.4 = (f32[4,96,128]{2,1,0:T(8,128)S(1)}, f32[4,96,128]{2,1,0:T(8,128)S(1)}, u32[]{:S(2)}, u32[]{:S(2)}) collective-permute-start(f32[4,96,128]{2,1,0:T(8,128)S(1)} %pad_maximum_fusion.first_ref), channel_id=1, source_target_pairs={{0,1},{1,0},{2,3},{3,2},{4,5},{5,4},{6,7},{7,6},{8,9},{9,8},{10,11... | collective-permute-start | bytes 589832 | tf_op jit(solution)/shard_map/gather_row/ppermute | solution.py:185
  24.3 5.7 %collective-permute-start.3 = (f32[4,96,128]{2,1,0:T(8,128)S(1)}, f32[4,96,128]{2,1,0:T(8,128)S(1)}, u32[]{:S(2)}, u32[]{:S(2)}) collective-permute-start(f32[4,96,128]{2,1,0:T(8,128)S(1)} %pad_maximum_fusion.first_ref), channel_id=1, source_target_pairs={{0,2},{1,3},{2,0},{3,1},{4,6},{5,7},{6,4},{7,5},{8,10},{9,11},{10,... | collective-permute-start | bytes 589832 | tf_op jit(solution)/shard_map/gather_row/ppermute | solution.py:185
  30.1 0.7 copy-start
  32.3 29.2 %all-to-all-start.1 = ((f32[16,96,128]{2,1,0:T(8,128)}), f32[16,96,128]{2,1,0:T(8,128)S(1)}, u32[]{:S(2)}, u32[]{:S(2)}) async-start(f32[16,96,128]{2,1,0:T(8,128)} %gather_column.2), calls=%async_computation.1 | async-start | bytes 1572864 | tf_op jit(solution)/shard_map/gather_column/all_to_all | solution.py:14
  40.0 8.8 %collective-permute-start.5 = (f32[4,96,128]{2,1,0:T(8,128)S(1)}, f32[4,96,128]{2,1,0:T(8,128)S(1)}, u32[]{:S(2)}, u32[]{:S(2)}) collective-permute-start(f32[4,96,128]{2,1,0:T(8,128)S(1)} %collective-permute-done.3.second_ref), channel_id=1, source_target_pairs={{0,1},{1,0},{2,3},{3,2},{4,5},{5,4},{6,7},{7,6},{8,9},{9,8},{10,11... | collective-permute-start | bytes 589832 | tf_op jit(solution)/shard_map/gather_row/ppermute | solution.py:185
  61.5 27.7 %all-to-all-start.2 = ((f32[16,96,128]{2,1,0:T(8,128)}), f32[16,96,128]{2,1,0:T(8,128)S(1)}, u32[]{:S(2)}, u32[]{:S(2)}) async-start(f32[16,96,128]{2,1,0:T(8,128)} %bitcast.10), calls=%async_computation.2 | async-start | bytes 1572864 | tf_op jit(solution)/shard_map/back_transposed/all_to_all | solution.py:14
  68.1 21.1 %copy-start.1 = (s32[1,16]{1,0:T(1,128)S(1)}, s32[1,16]{1,0:T(1,128)}, u32[]{:S(2)}) copy-start(s32[1,16]{1,0:T(1,128)} %param.6) | copy-start | bytes 196
  68.1 10.6 %collective-permute-start.7 = (f32[4,96,128]{2,1,0:T(8,128)S(1)}, f32[4,96,128]{2,1,0:T(8,128)S(1)}, u32[]{:S(2)}, u32[]{:S(2)}) collective-permute-start(f32[4,96,128]{2,1,0:T(8,128)S(1)} %direct.6), channel_id=1, source_target_pairs={{0,1},{1,0},{2,3},{3,2},{4,5},{5,4},{6,7},{7,6},{8,9},{9,8},{10,11... | collective-permute-start | bytes 589832 | tf_op jit(solution)/shard_map/direct/ppermute | solution.py:185
  75.6 10.8 %collective-permute-start.6 = (f32[4,96,128]{2,1,0:T(8,128)S(1)}, f32[4,96,128]{2,1,0:T(8,128)S(1)}, u32[]{:S(2)}, u32[]{:S(2)}) collective-permute-start(f32[4,96,128]{2,1,0:T(8,128)S(1)} %get-tuple-element.48), channel_id=1, source_target_pairs={{0,1},{1,0},{2,3},{3,2},{4,5},{5,4},{6,7},{7,6},{8,9},{9,8},{10,11... | collective-permute-start | bytes 589832 | tf_op jit(solution)/shard_map/direct/ppermute | solution.py:185
  78.8 7.8 %collective-permute-start.8 = (f32[4,96,128]{2,1,0:T(8,128)S(1)}, f32[4,96,128]{2,1,0:T(8,128)S(1)}, u32[]{:S(2)}, u32[]{:S(2)}) collective-permute-start(f32[4,96,128]{2,1,0:T(8,128)S(1)} %add.52), channel_id=1, source_target_pairs={{0,2},{1,3},{2,0},{3,1},{4,6},{5,7},{6,4},{7,5},{8,10},{9,11},{10,... | collective-permute-start | bytes 589832 | tf_op jit(solution)/shard_map/direct/ppermute | solution.py:185
  90.8 17.9 %all-to-all-start.3 = ((f32[16,96,128]{2,1,0:T(8,128)}), f32[16,96,128]{2,1,0:T(8,128)S(1)}, u32[]{:S(2)}, u32[]{:S(2)}) async-start(f32[16,96,128]{2,1,0:T(8,128)} %back_wide.2), calls=%async_computation.3 | async-start | bytes 1572864 | tf_op jit(solution)/shard_map/back_wide/all_to_all | solution.py:14
  96.6 12.2 %collective-permute-start.9 = (f32[96,128]{1,0:T(8,128)S(1)}, f32[96,128]{1,0:T(8,128)S(1)}, u32[]{:S(2)}, u32[]{:S(2)}) collective-permute-start(f32[96,128]{1,0:T(8,128)S(1)} %get-tuple-element.76), channel_id=1, source_target_pairs={{0,8},{1,9},{2,10},{3,11},{4,12},{5,13},{6,14},{7,15},{8,0},{9,1},... | collective-permute-start | bytes 147464 | tf_op jit(solution)/shard_map/back_direct/ppermute | solution.py:185
  100.7 8.1 %collective-permute-start.11 = (f32[96,128]{1,0:T(8,128)S(1)}, f32[96,128]{1,0:T(8,128)S(1)}, u32[]{:S(2)}, u32[]{:S(2)}) collective-permute-start(f32[96,128]{1,0:T(8,128)S(1)} %get-tuple-element.77), channel_id=1, source_target_pairs={{0,12},{1,13},{2,14},{3,15},{4,8},{5,9},{6,10},{7,11},{8,4},{9,5},... | collective-permute-start | bytes 147464 | tf_op jit(solution)/shard_map/back_direct/ppermute | solution.py:185
  100.7 8.1 %collective-permute-start.10 = (f32[96,128]{1,0:T(8,128)S(1)}, f32[96,128]{1,0:T(8,128)S(1)}, u32[]{:S(2)}, u32[]{:S(2)}) collective-permute-start(f32[96,128]{1,0:T(8,128)S(1)} %get-tuple-element.78), channel_id=1, source_target_pairs={{0,4},{1,5},{2,6},{3,7},{4,0},{5,1},{6,2},{7,3},{8,12},{9,13},{10,... | collective-permute-start | bytes 147464 | tf_op jit(solution)/shard_map/back_direct/ppermute | solution.py:185
  109.8 28.0 %all-to-all-start.4 = ((f32[16,96,128]{2,1,0:T(8,128)}), f32[16,96,128]{2,1,0:T(8,128)S(1)}, u32[]{:S(2)}, u32[]{:S(2)}) async-start(f32[16,96,128]{2,1,0:T(8,128)} %broadcast_in_dim.16), calls=%async_computation.4 | async-start | bytes 1572864 | tf_op jit(solution)/shard_map/gather_wide/all_to_all | solution.py:14
  115.0 7.0 %collective-permute-start.14 = (f32[96,128]{1,0:T(8,128)S(1)}, f32[96,128]{1,0:T(8,128)S(1)}, u32[]{:S(2)}, u32[]{:S(2)}) collective-permute-start(f32[96,128]{1,0:T(8,128)S(1)} %fusion.7), channel_id=1, source_target_pairs={{0,12},{1,13},{2,14},{3,15},{4,8},{5,9},{6,10},{7,11},{8,4},{9,5},... | collective-permute-start | bytes 147464 | tf_op jit(solution)/shard_map/gather_row/ppermute | solution.py:185
  117.3 5.0 %collective-permute-start.13 = (f32[96,128]{1,0:T(8,128)S(1)}, f32[96,128]{1,0:T(8,128)S(1)}, u32[]{:S(2)}, u32[]{:S(2)}) collective-permute-start(f32[96,128]{1,0:T(8,128)S(1)} %fusion.7), channel_id=1, source_target_pairs={{0,4},{1,5},{2,6},{3,7},{4,0},{5,1},{6,2},{7,3},{8,12},{9,13},{10,... | collective-permute-start | bytes 147464 | tf_op jit(solution)/shard_map/gather_row/ppermute | solution.py:185
  119.6 8.1 %collective-permute-start.12 = (f32[96,128]{1,0:T(8,128)S(1)}, f32[96,128]{1,0:T(8,128)S(1)}, u32[]{:S(2)}, u32[]{:S(2)}) collective-permute-start(f32[96,128]{1,0:T(8,128)S(1)} %fusion.7), channel_id=1, source_target_pairs={{0,8},{1,9},{2,10},{3,11},{4,12},{5,13},{6,14},{7,15},{8,0},{9,1},... | collective-permute-start | bytes 147464 | tf_op jit(solution)/shard_map/gather_row/ppermute | solution.py:185
  127.7 8.3 %collective-permute-start.16 = (f32[4,96,128]{2,1,0:T(8,128)S(1)}, f32[4,96,128]{2,1,0:T(8,128)S(1)}, u32[]{:S(2)}, u32[]{:S(2)}) collective-permute-start(f32[4,96,128]{2,1,0:T(8,128)S(1)} %pad_maximum_fusion.1.first_ref), channel_id=1, source_target_pairs={{0,1},{1,0},{2,3},{3,2},{4,5},{5,4},{6,7},{7,6},{8,9},{9,8},{10,11... | collective-permute-start | bytes 589832 | tf_op jit(solution)/shard_map/gather_row/ppermute | solution.py:185
  132.1 5.7 %collective-permute-start.15 = (f32[4,96,128]{2,1,0:T(8,128)S(1)}, f32[4,96,128]{2,1,0:T(8,128)S(1)}, u32[]{:S(2)}, u32[]{:S(2)}) collective-permute-start(f32[4,96,128]{2,1,0:T(8,128)S(1)} %pad_maximum_fusion.1.first_ref), channel_id=1, source_target_pairs={{0,2},{1,3},{2,0},{3,1},{4,6},{5,7},{6,4},{7,5},{8,10},{9,11},{10,... | collective-permute-start | bytes 589832 | tf_op jit(solution)/shard_map/gather_row/ppermute | solution.py:185
  139.4 26.0 %all-to-all-start.5 = ((f32[16,96,128]{2,1,0:T(8,128)}), f32[16,96,128]{2,1,0:T(8,128)S(1)}, u32[]{:S(2)}, u32[]{:S(2)}) async-start(f32[16,96,128]{2,1,0:T(8,128)} %gather_column.3), calls=%async_computation.5 | async-start | bytes 1572864 | tf_op jit(solution)/shard_map/gather_column/all_to_all | solution.py:14
  143.0 8.3 %collective-permute-start.17 = (f32[4,96,128]{2,1,0:T(8,128)S(1)}, f32[4,96,128]{2,1,0:T(8,128)S(1)}, u32[]{:S(2)}, u32[]{:S(2)}) collective-permute-start(f32[4,96,128]{2,1,0:T(8,128)S(1)} %collective-permute-done.15.second_ref), channel_id=1, source_target_pairs={{0,1},{1,0},{2,3},{3,2},{4,5},{5,4},{6,7},{7,6},{8,9},{9,8},{10,11... | collective-permute-start | bytes 589832 | tf_op jit(solution)/shard_map/gather_row/ppermute | solution.py:185
  165.4 27.8 %all-to-all-start.6 = ((f32[16,96,128]{2,1,0:T(8,128)}), f32[16,96,128]{2,1,0:T(8,128)S(1)}, u32[]{:S(2)}, u32[]{:S(2)}) async-start(f32[16,96,128]{2,1,0:T(8,128)} %bitcast.21), calls=%async_computation.6 | async-start | bytes 1572864 | tf_op jit(solution)/shard_map/back_transposed/all_to_all | solution.py:14
  172.1 12.2 %collective-permute-start.19 = (f32[4,96,128]{2,1,0:T(8,128)S(1)}, f32[4,96,128]{2,1,0:T(8,128)S(1)}, u32[]{:S(2)}, u32[]{:S(2)}) collective-permute-start(f32[4,96,128]{2,1,0:T(8,128)S(1)} %direct.9), channel_id=1, source_target_pairs={{0,1},{1,0},{2,3},{3,2},{4,5},{5,4},{6,7},{7,6},{8,9},{9,8},{10,11... | collective-permute-start | bytes 589832 | tf_op jit(solution)/shard_map/direct/ppermute | solution.py:185
  182.5 10.7 %collective-permute-start.18 = (f32[4,96,128]{2,1,0:T(8,128)S(1)}, f32[4,96,128]{2,1,0:T(8,128)S(1)}, u32[]{:S(2)}, u32[]{:S(2)}) collective-permute-start(f32[4,96,128]{2,1,0:T(8,128)S(1)} %get-tuple-element.62), channel_id=1, source_target_pairs={{0,1},{1,0},{2,3},{3,2},{4,5},{5,4},{6,7},{7,6},{8,9},{9,8},{10,11... | collective-permute-start | bytes 589832 | tf_op jit(solution)/shard_map/direct/ppermute | solution.py:185
  184.3 8.8 %collective-permute-start.20 = (f32[4,96,128]{2,1,0:T(8,128)S(1)}, f32[4,96,128]{2,1,0:T(8,128)S(1)}, u32[]{:S(2)}, u32[]{:S(2)}) collective-permute-start(f32[4,96,128]{2,1,0:T(8,128)S(1)} %add.59), channel_id=1, source_target_pairs={{0,2},{1,3},{2,0},{3,1},{4,6},{5,7},{6,4},{7,5},{8,10},{9,11},{10,... | collective-permute-start | bytes 589832 | tf_op jit(solution)/shard_map/direct/ppermute | solution.py:185
  195.0 19.6 %all-to-all-start.7 = ((f32[16,104,128]{2,1,0:T(8,128)}), f32[16,104,128]{2,1,0:T(8,128)S(1)}, u32[]{:S(2)}, u32[]{:S(2)}) async-start(f32[16,104,128]{2,1,0:T(8,128)} %back_wide.3), calls=%async_computation.7 | async-start | bytes 1703936 | tf_op jit(solution)/shard_map/back_wide/all_to_all | solution.py:14
  201.8 13.0 %collective-permute-start.21 = (f32[96,128]{1,0:T(8,128)S(1)}, f32[96,128]{1,0:T(8,128)S(1)}, u32[]{:S(2)}, u32[]{:S(2)}) collective-permute-start(f32[96,128]{1,0:T(8,128)S(1)} %get-tuple-element.73), channel_id=1, source_target_pairs={{0,8},{1,9},{2,10},{3,11},{4,12},{5,13},{6,14},{7,15},{8,0},{9,1},... | collective-permute-start | bytes 147464 | tf_op jit(solution)/shard_map/back_direct/ppermute | solution.py:185
  206.2 8.5 %collective-permute-start.23 = (f32[96,128]{1,0:T(8,128)S(1)}, f32[96,128]{1,0:T(8,128)S(1)}, u32[]{:S(2)}, u32[]{:S(2)}) collective-permute-start(f32[96,128]{1,0:T(8,128)S(1)} %get-tuple-element.74), channel_id=1, source_target_pairs={{0,12},{1,13},{2,14},{3,15},{4,8},{5,9},{6,10},{7,11},{8,4},{9,5},... | collective-permute-start | bytes 147464 | tf_op jit(solution)/shard_map/back_direct/ppermute | solution.py:185
  207.3 7.4 %collective-permute-start.22 = (f32[96,128]{1,0:T(8,128)S(1)}, f32[96,128]{1,0:T(8,128)S(1)}, u32[]{:S(2)}, u32[]{:S(2)}) collective-permute-start(f32[96,128]{1,0:T(8,128)S(1)} %get-tuple-element.75), channel_id=1, source_target_pairs={{0,4},{1,5},{2,6},{3,7},{4,0},{5,1},{6,2},{7,3},{8,12},{9,13},{10,... | collective-permute-start | bytes 147464 | tf_op jit(solution)/shard_map/back_direct/ppermute | solution.py:185
  242.7 10.1 %all-to-all-start.10 = ((f32[16,8,128]{2,1,0:T(8,128)}), f32[16,8,128]{2,1,0:T(8,128)S(1)}, u32[]{:S(2)}, u32[]{:S(2)}) async-start(f32[16,8,128]{2,1,0:T(8,128)} %broadcast_in_dim.40), calls=%async_computation.10 | async-start | bytes 131072 | tf_op jit(solution)/shard_map/gram_whole/all_to_all | solution.py:14

commit v8 on v7

--- a/solution.py
+++ b/solution.py
@@ -27,7 +27,7 @@
         moved_ref, done = rest[-2:]
         copies = []
         for i in range(count):
-            column = columns_ref[i]
+            column = columns_ref[0, i]
             source, target = (i, column) if scatter else (column, i)
             copies.append(
                 pltpu.make_async_copy(
@@ -248,7 +248,7 @@
     gram = None
     if want_gram:
         with jax.named_scope("gram_block_row"):
-            block, _ = lax.optimization_barrier((near_rows + far_rows, near_first))
+            block, _ = lax.optimization_barrier((near_rows + far_rows, got_second))
             gram = sum(gram_of(quarter.reshape(-1, width)) for quarter in block)
     with jax.named_scope("back_direct"):
         direct_sum = summed_part(kept)
@@ -297,7 +297,7 @@
 
 def on_device(tile, row_columns, start_vectors):
     total_rows = float(lax.axis_size(WIDE) * lax.axis_size(NARROW) * start_vectors.shape[0])
-    columns = row_columns[0]
+    columns = row_columns
     where = kernel_indices(lax.axis_index(NARROW).astype(jnp.int32))
     first, _ = apply_hamiltonian(tile, columns, where, start_vectors, want_gram=False)
     second, gram_rows = apply_hamiltonian(tile, columns, where, first, want_gram=True)

time: 260 us -> 261 us (level)
    all_to_all x9, waiting for transfers between devices: 32.4 us -> 35 us  [exchange(): return lax.all_to_all(parts, axis, 0, 0, tiled=True)]
  transfers between devices with their start and end apart: 33 -> 33, of which waited for: 20 -> 22; matrix products, arithmetic and copies ran while one was open for 2% -> 2% of each run, Pallas kernels for 17% -> 17%
where the time goes in v8:
time: 261 us; the launch traced here: 257 us
  starting transfers between devices  104 us (40%)
  waiting for transfers between devices  63.5 us (24%)
  Pallas kernels  52.8 us (20%)
  blocking collectives  28 us (11%)
  local copies, waits for them, and re-layouts  4.14 us (2%)
    ppermute x24, starting transfers between devices, swap(): return lax.ppermute(value, NARROW, [(i, i ^ mask) for i in range(size)])  57.6 us
    all_to_all x9, starting transfers between devices, exchange(): return lax.all_to_all(parts, axis, 0, 0, tiled=True)  46.2 us
    all_to_all x9, waiting for transfers between devices, exchange(): return lax.all_to_all(parts, axis, 0, 0, tiled=True)  35 us
    ppermute x24, waiting for transfers between devices, swap(): return lax.ppermute(value, NARROW, [(i, i ^ mask) for i in range(size)])  28.5 us
    all_to_all x2, blocking collectives, exchange(): return lax.all_to_all(parts, axis, 0, 0, tiled=True)  28 us
    pallas_call x4, Pallas kernels, transposed_half(): pl.pallas_call(kernel, out_shape=jax.ShapeDtypeStruct((width, order) if p...  20.4 us
    pallas_call x6, Pallas kernels, direct_quarters(): pl.pallas_call(kernel, out_shape=[jax.ShapeDtypeStruct((each, rows, width...  20.1 us
    pallas_call x4, Pallas kernels, move_blocks(): pl.pallas_call(kernel, out_shape=jax.ShapeDtypeStruct((count, rows + more...  6.51 us
  transfers between devices with their start and end apart: 33, of which 22 were waited for; matrix products, arithmetic and copies ran while one was open for 2% of the time, Pallas kernels for 17%

profile of v8, /device:TPU:8, one launch (start us, length us, event | category | flops | bytes accessed | tf_op | source)
XLA Modules:
  0.0 257.3 jit_solution(16600312635437194701)
XLA Ops:
  1.8 5.8 %all-to-all-start = ((f32[16,96,128]{2,1,0:T(8,128)}), f32[16,96,128]{2,1,0:T(8,128)S(1)}, u32[]{:S(2)}, u32[]{:S(2)}) async-start(f32[16,96,128]{2,1,0:T(8,128)} %broadcast_in_dim.14), calls=%async_computation | async-start | bytes 1572864 | tf_op jit(solution)/shard_map/gather_wide/all_to_all | solution.py:14
  7.5 7.2 %collective-permute-start = (f32[96,128]{1,0:T(8,128)}, f32[96,128]{1,0:T(8,128)S(1)}, u32[]{:S(2)}, u32[]{:S(2)}) collective-permute-start(f32[96,128]{1,0:T(8,128)} %param.7), channel_id=1, source_target_pairs={{0,8},{1,9},{2,10},{3,11},{4,12},{5,13},{6,14},{7,15},{8,0},{9,1},... | collective-permute-start | bytes 147464 | tf_op jit(solution)/shard_map/gather_row/ppermute | solution.py:185
  17.5 3.6 %collective-permute-done.2 = f32[96,128]{1,0:T(8,128)S(1)} collective-permute-done((f32[96,128]{1,0:T(8,128)}, f32[96,128]{1,0:T(8,128)S(1)}, u32[]{:S(2)}, u32[]{:S(2)}) %collective-permute-start.2) | collective-permute-done | bytes 49184 | tf_op jit(solution)/shard_map/gather_row/ppermute | solution.py:185
  22.0 2.4 collective-permute-start.4
  25.9 3.6 %collective-permute-done.4.first_ref = f32[4,96,128]{2,1,0:T(8,128)S(1)} collective-permute-done((f32[4,96,128]{2,1,0:T(8,128)S(1)}, f32[4,96,128]{2,1,0:T(8,128)S(1)}, u32[]{:S(2)}, u32[]{:S(2)}) %collective-permute-start.4) | collective-permute-done | bytes 196640 | tf_op jit(solution)/shard_map/gather_row/ppermute | solution.py:185
  32.3 7.0 %all-to-all-start.1 = ((f32[16,96,128]{2,1,0:T(8,128)}), f32[16,96,128]{2,1,0:T(8,128)S(1)}, u32[]{:S(2)}, u32[]{:S(2)}) async-start(f32[16,96,128]{2,1,0:T(8,128)} %gather_column.2), calls=%async_computation.1 | async-start | bytes 1572864 | tf_op jit(solution)/shard_map/gather_column/all_to_all | solution.py:14
  40.0 3.4 %collective-permute-start.5 = (f32[4,96,128]{2,1,0:T(8,128)S(1)}, f32[4,96,128]{2,1,0:T(8,128)S(1)}, u32[]{:S(2)}, u32[]{:S(2)}) collective-permute-start(f32[4,96,128]{2,1,0:T(8,128)S(1)} %collective-permute-done.3.second_ref), channel_id=1, source_target_pairs={{0,1},{1,0},{2,3},{3,2},{4,5},{5,4},{6,7},{7,6},{8,9},{9,8},{10,11... | collective-permute-start | bytes 589832 | tf_op jit(solution)/shard_map/gather_row/ppermute | solution.py:185
  44.2 4.6 %transposed.4.rest_0_ = f32[128,1536]{1,0:T(8,128)S(1)} custom-call(s32[15]{0:T(128)S(1)} %concatenate.6.where_ref, f32[8,2,96,1536]{3,2,1,0:T(8,128)} %bitcast.81, f32[4,96,128]{2,1,0:T(8,128)S(1)} %pad_maximum_fusion.first_ref, f32[4,96,128]{2,1,0:T(8,128)S(1)} %collective-permute-done.3.second_ref), custom_call_target="tpu_custom_call" | custom-call | flops 905969664 | bytes 4718592 | tf_op jit(solution)/shard_map/transposed/pallas_call | solution.py:161
  48.8 5.6 %transposed.5 = f32[1536,128]{1,0:T(8,128)} custom-call(s32[15]{0:T(128)S(1)} %concatenate.6.where_ref, f32[8,2,96,1536]{3,2,1,0:T(8,128)} %bitcast.82, f32[4,96,128]{2,1,0:T(8,128)S(1)} %collective-permute-done.4.first_ref, f32[4,96,128]{2,1,0:T(8,128)S(1)} %collective-permute-done.5.second_ref, f32[128,1536]{1,0:T(8,128)S(1)} %transposed.4.rest_0_), custom_call_target="tpu_custom_call" | custom-call | flops 905969664 | bytes 4718592 | tf_op jit(solution)/shard_map/transposed/pallas_call | solution.py:161
  54.4 7.1 %all-to-all-done.1 = f32[16,96,128]{2,1,0:T(8,128)S(1)} async-done(((f32[16,96,128]{2,1,0:T(8,128)}), f32[16,96,128]{2,1,0:T(8,128)S(1)}, u32[]{:S(2)}, u32[]{:S(2)}) %all-to-all-start.1) | async-done | bytes 786464 | tf_op jit(solution)/shard_map/gather_column/all_to_all | solution.py:14
  61.5 3.6 %all-to-all-start.2 = ((f32[16,96,128]{2,1,0:T(8,128)}), f32[16,96,128]{2,1,0:T(8,128)S(1)}, u32[]{:S(2)}, u32[]{:S(2)}) async-start(f32[16,96,128]{2,1,0:T(8,128)} %bitcast.9), calls=%async_computation.2 | async-start | bytes 1572864 | tf_op jit(solution)/shard_map/back_transposed/all_to_all | solution.py:14
  65.1 3.0 %direct.6 = f32[4,96,128]{2,1,0:T(8,128)S(1)} custom-call(s32[15]{0:T(128)S(1)} %concatenate.6.where_ref, f32[4,2,2,96,1536]{4,3,2,1,0:T(8,128)} %bitcast.83, f32[1536,128]{1,0:T(8,128)S(1)} %bitcast.74), custom_call_target="tpu_custom_call" | custom-call | flops 226492416 | bytes 2359296 | tf_op jit(solution)/shard_map/direct/pallas_call | solution.py:106
  68.1 3.4 %collective-permute-start.7 = (f32[4,96,128]{2,1,0:T(8,128)S(1)}, f32[4,96,128]{2,1,0:T(8,128)S(1)}, u32[]{:S(2)}, u32[]{:S(2)}) collective-permute-start(f32[4,96,128]{2,1,0:T(8,128)S(1)} %direct.6), channel_id=1, source_target_pairs={{0,1},{1,0},{2,3},{3,2},{4,5},{5,4},{6,7},{7,6},{8,9},{9,8},{10,11... | collective-permute-start | bytes 589832 | tf_op jit(solution)/shard_map/direct/ppermute | solution.py:185
  71.6 4.0 %direct.7 = (f32[4,96,128]{2,1,0:T(8,128)S(1)}, f32[4,96,128]{2,1,0:T(8,128)S(1)}) custom-call(s32[15]{0:T(128)S(1)} %concatenate.6.where_ref, f32[4,2,2,96,1536]{4,3,2,1,0:T(8,128)} %bitcast.84, f32[1536,128]{1,0:T(8,128)S(1)} %bitcast.75), custom_call_target="tpu_custom_call" | custom-call | flops 452984832 | bytes 4718592 | tf_op jit(solution)/shard_map/direct/pallas_call | solution.py:106
  75.8 2.9 %collective-permute-done.7 = f32[4,96,128]{2,1,0:T(8,128)S(1)} collective-permute-done((f32[4,96,128]{2,1,0:T(8,128)S(1)}, f32[4,96,128]{2,1,0:T(8,128)S(1)}, u32[]{:S(2)}, u32[]{:S(2)}) %collective-permute-start.7) | collective-permute-done | bytes 196640 | tf_op jit(solution)/shard_map/direct/ppermute | solution.py:185
  78.8 4.2 %collective-permute-start.8 = (f32[4,96,128]{2,1,0:T(8,128)S(1)}, f32[4,96,128]{2,1,0:T(8,128)S(1)}, u32[]{:S(2)}, u32[]{:S(2)}) collective-permute-start(f32[4,96,128]{2,1,0:T(8,128)S(1)} %add.52), channel_id=1, source_target_pairs={{0,2},{1,3},{2,0},{3,1},{4,6},{5,7},{6,4},{7,5},{8,10},{9,11},{10,... | collective-permute-start | bytes 589832 | tf_op jit(solution)/shard_map/direct/ppermute | solution.py:185
  82.9 3.0 %direct.8 = f32[4,96,128]{2,1,0:T(8,128)S(1)} custom-call(s32[15]{0:T(128)S(1)} %concatenate.6.where_ref, f32[4,2,2,96,1536]{4,3,2,1,0:T(8,128)} %bitcast.85, f32[1536,128]{1,0:T(8,128)S(1)} %bitcast.76), custom_call_target="tpu_custom_call" | custom-call | flops 226492416 | bytes 2359296 | tf_op jit(solution)/shard_map/direct/pallas_call | solution.py:106
  86.6 2.6 %all-to-all-done.2.blocks_ref = f32[16,96,128]{2,1,0:T(8,128)S(1)} async-done(((f32[16,96,128]{2,1,0:T(8,128)}), f32[16,96,128]{2,1,0:T(8,128)S(1)}, u32[]{:S(2)}, u32[]{:S(2)}) %all-to-all-start.2) | async-done | bytes 786464 | tf_op jit(solution)/shard_map/back_transposed/all_to_all | solution.py:14
  90.8 5.7 %all-to-all-start.3 = ((f32[16,96,128]{2,1,0:T(8,128)}), f32[16,96,128]{2,1,0:T(8,128)S(1)}, u32[]{:S(2)}, u32[]{:S(2)}) async-start(f32[16,96,128]{2,1,0:T(8,128)} %back_wide.2), calls=%async_computation.3 | async-start | bytes 1572864 | tf_op jit(solution)/shard_map/back_wide/all_to_all | solution.py:14
  96.6 4.1 %collective-permute-start.9 = (f32[96,128]{1,0:T(8,128)S(1)}, f32[96,128]{1,0:T(8,128)S(1)}, u32[]{:S(2)}, u32[]{:S(2)}) collective-permute-start(f32[96,128]{1,0:T(8,128)S(1)} %get-tuple-element.76), channel_id=1, source_target_pairs={{0,8},{1,9},{2,10},{3,11},{4,12},{5,13},{6,14},{7,15},{8,0},{9,1},... | collective-permute-start | bytes 147464 | tf_op jit(solution)/shard_map/back_direct/ppermute | solution.py:185
  100.7 2.4 collective-permute-start.10
  103.1 5.6 %all-to-all-done.3 = f32[16,96,128]{2,1,0:T(8,128)S(1)} async-done(((f32[16,96,128]{2,1,0:T(8,128)}), f32[16,96,128]{2,1,0:T(8,128)S(1)}, u32[]{:S(2)}, u32[]{:S(2)}) %all-to-all-start.3) | async-done | bytes 786464 | tf_op jit(solution)/shard_map/back_wide/all_to_all | solution.py:14
  109.8 5.2 %all-to-all-start.4 = ((f32[16,96,128]{2,1,0:T(8,128)}), f32[16,96,128]{2,1,0:T(8,128)S(1)}, u32[]{:S(2)}, u32[]{:S(2)}) async-start(f32[16,96,128]{2,1,0:T(8,128)} %broadcast_in_dim.16), calls=%async_computation.4 | async-start | bytes 1572864 | tf_op jit(solution)/shard_map/gather_wide/all_to_all | solution.py:14
  115.0 2.4 collective-permute-start.14
  122.3 5.3 %collective-permute-done.12 = f32[96,128]{1,0:T(8,128)S(1)} collective-permute-done((f32[96,128]{1,0:T(8,128)S(1)}, f32[96,128]{1,0:T(8,128)S(1)}, u32[]{:S(2)}, u32[]{:S(2)}) %collective-permute-start.12) | collective-permute-done | bytes 49184 | tf_op jit(solution)/shard_map/gather_row/ppermute | solution.py:185
  127.7 4.4 %collective-permute-start.16 = (f32[4,96,128]{2,1,0:T(8,128)S(1)}, f32[4,96,128]{2,1,0:T(8,128)S(1)}, u32[]{:S(2)}, u32[]{:S(2)}) collective-permute-start(f32[4,96,128]{2,1,0:T(8,128)S(1)} %pad_maximum_fusion.1.first_ref), channel_id=1, source_target_pairs={{0,1},{1,0},{2,3},{3,2},{4,5},{5,4},{6,7},{7,6},{8,9},{9,8},{10,11... | collective-permute-start | bytes 589832 | tf_op jit(solution)/shard_map/gather_row/ppermute | solution.py:185
  132.4 3.6 %collective-permute-done.16.first_ref = f32[4,96,128]{2,1,0:T(8,128)S(1)} collective-permute-done((f32[4,96,128]{2,1,0:T(8,128)S(1)}, f32[4,96,128]{2,1,0:T(8,128)S(1)}, u32[]{:S(2)}, u32[]{:S(2)}) %collective-permute-start.16) | collective-permute-done | bytes 196640 | tf_op jit(solution)/shard_map/gather_row/ppermute | solution.py:185
  139.4 3.6 %all-to-all-start.5 = ((f32[16,96,128]{2,1,0:T(8,128)}), f32[16,96,128]{2,1,0:T(8,128)S(1)}, u32[]{:S(2)}, u32[]{:S(2)}) async-start(f32[16,96,128]{2,1,0:T(8,128)} %gather_column.3), calls=%async_computation.5 | async-start | bytes 1572864 | tf_op jit(solution)/shard_map/gather_column/all_to_all | solution.py:14
  143.0 3.4 %collective-permute-start.17 = (f32[4,96,128]{2,1,0:T(8,128)S(1)}, f32[4,96,128]{2,1,0:T(8,128)S(1)}, u32[]{:S(2)}, u32[]{:S(2)}) collective-permute-start(f32[4,96,128]{2,1,0:T(8,128)S(1)} %collective-permute-done.15.second_ref), channel_id=1, source_target_pairs={{0,1},{1,0},{2,3},{3,2},{4,5},{5,4},{6,7},{7,6},{8,9},{9,8},{10,11... | collective-permute-start | bytes 589832 | tf_op jit(solution)/shard_map/gather_row/ppermute | solution.py:185
  146.4 4.6 %transposed.6.rest_0_ = f32[128,1536]{1,0:T(8,128)S(1)} custom-call(s32[15]{0:T(128)S(1)} %concatenate.6.where_ref, f32[8,2,96,1536]{3,2,1,0:T(8,128)} %bitcast.86, f32[4,96,128]{2,1,0:T(8,128)S(1)} %pad_maximum_fusion.1.first_ref, f32[4,96,128]{2,1,0:T(8,128)S(1)} %collective-permute-done.15.second_ref), custom_call_target="tpu_custom_call" | custom-call | flops 905969664 | bytes 4718592 | tf_op jit(solution)/shard_map/transposed/pallas_call | solution.py:161
  151.3 5.6 %transposed.7 = f32[1536,128]{1,0:T(8,128)} custom-call(s32[15]{0:T(128)S(1)} %concatenate.6.where_ref, f32[8,2,96,1536]{3,2,1,0:T(8,128)} %bitcast.87, f32[4,96,128]{2,1,0:T(8,128)S(1)} %collective-permute-done.16.first_ref, f32[4,96,128]{2,1,0:T(8,128)S(1)} %collective-permute-done.17.second_ref, f32[128,1536]{1,0:T(8,128)S(1)} %transposed.6.rest_0_), custom_call_target="tpu_custom_call" | custom-call | flops 905969664 | bytes 4718592 | tf_op jit(solution)/shard_map/transposed/pallas_call | solution.py:161
  156.9 8.5 %all-to-all-done.5 = f32[16,96,128]{2,1,0:T(8,128)S(1)} async-done(((f32[16,96,128]{2,1,0:T(8,128)}), f32[16,96,128]{2,1,0:T(8,128)S(1)}, u32[]{:S(2)}, u32[]{:S(2)}) %all-to-all-start.5) | async-done | bytes 786464 | tf_op jit(solution)/shard_map/gather_column/all_to_all | solution.py:14
  165.4 3.6 %all-to-all-start.6 = ((f32[16,96,128]{2,1,0:T(8,128)}), f32[16,96,128]{2,1,0:T(8,128)S(1)}, u32[]{:S(2)}, u32[]{:S(2)}) async-start(f32[16,96,128]{2,1,0:T(8,128)} %bitcast.20), calls=%async_computation.6 | async-start | bytes 1572864 | tf_op jit(solution)/shard_map/back_transposed/all_to_all | solution.py:14
  169.0 3.0 %direct.9 = f32[4,96,128]{2,1,0:T(8,128)S(1)} custom-call(s32[15]{0:T(128)S(1)} %concatenate.6.where_ref, f32[4,2,2,96,1536]{4,3,2,1,0:T(8,128)} %bitcast.88, f32[1536,128]{1,0:T(8,128)S(1)} %bitcast.77), custom_call_target="tpu_custom_call" | custom-call | flops 226492416 | bytes 2359296 | tf_op jit(solution)/shard_map/direct/pallas_call | solution.py:106
  172.1 3.4 %collective-permute-start.19 = (f32[4,96,128]{2,1,0:T(8,128)S(1)}, f32[4,96,128]{2,1,0:T(8,128)S(1)}, u32[]{:S(2)}, u32[]{:S(2)}) collective-permute-start(f32[4,96,128]{2,1,0:T(8,128)S(1)} %direct.9), channel_id=1, source_target_pairs={{0,1},{1,0},{2,3},{3,2},{4,5},{5,4},{6,7},{7,6},{8,9},{9,8},{10,11... | collective-permute-start | bytes 589832 | tf_op jit(solution)/shard_map/direct/ppermute | solution.py:185
  175.5 4.0 %direct.10 = (f32[4,96,128]{2,1,0:T(8,128)S(1)}, f32[4,96,128]{2,1,0:T(8,128)S(1)}) custom-call(s32[15]{0:T(128)S(1)} %concatenate.6.where_ref, f32[4,2,2,96,1536]{4,3,2,1,0:T(8,128)} %bitcast.89, f32[1536,128]{1,0:T(8,128)S(1)} %bitcast.78), custom_call_target="tpu_custom_call" | custom-call | flops 452984832 | bytes 4718592 | tf_op jit(solution)/shard_map/direct/pallas_call | solution.py:106
  179.8 3.0 %direct.11 = f32[4,96,128]{2,1,0:T(8,128)S(1)} custom-call(s32[15]{0:T(128)S(1)} %concatenate.6.where_ref, f32[4,2,2,96,1536]{4,3,2,1,0:T(8,128)} %bitcast.90, f32[1536,128]{1,0:T(8,128)S(1)} %bitcast.79), custom_call_target="tpu_custom_call" | custom-call | flops 226492416 | bytes 2359296 | tf_op jit(solution)/shard_map/direct/pallas_call | solution.py:106
  186.9 3.8 %collective-permute-done.18 = f32[4,96,128]{2,1,0:T(8,128)S(1)} collective-permute-done((f32[4,96,128]{2,1,0:T(8,128)S(1)}, f32[4,96,128]{2,1,0:T(8,128)S(1)}, u32[]{:S(2)}, u32[]{:S(2)}) %collective-permute-start.18) | collective-permute-done | bytes 196640 | tf_op jit(solution)/shard_map/direct/ppermute | solution.py:185
  191.0 2.6 %all-to-all-done.6.blocks_ref = f32[16,96,128]{2,1,0:T(8,128)S(1)} async-done(((f32[16,96,128]{2,1,0:T(8,128)}), f32[16,96,128]{2,1,0:T(8,128)S(1)}, u32[]{:S(2)}, u32[]{:S(2)}) %all-to-all-start.6) | async-done | bytes 786464 | tf_op jit(solution)/shard_map/back_transposed/all_to_all | solution.py:14
  195.4 6.4 %all-to-all-start.7 = ((f32[16,104,128]{2,1,0:T(8,128)}), f32[16,104,128]{2,1,0:T(8,128)S(1)}, u32[]{:S(2)}, u32[]{:S(2)}) async-start(f32[16,104,128]{2,1,0:T(8,128)} %back_wide.3), calls=%async_computation.7 | async-start | bytes 1703936 | tf_op jit(solution)/shard_map/back_wide/all_to_all | solution.py:14
  201.8 4.0 %collective-permute-start.21 = (f32[96,128]{1,0:T(8,128)S(1)}, f32[96,128]{1,0:T(8,128)S(1)}, u32[]{:S(2)}, u32[]{:S(2)}) collective-permute-start(f32[96,128]{1,0:T(8,128)S(1)} %get-tuple-element.73), channel_id=1, source_target_pairs={{0,8},{1,9},{2,10},{3,11},{4,12},{5,13},{6,14},{7,15},{8,0},{9,1},... | collective-permute-start | bytes 147464 | tf_op jit(solution)/shard_map/back_direct/ppermute | solution.py:185
  206.1 2.5 collective-permute-start.22
  208.6 6.1 %all-to-all-done.7 = f32[16,104,128]{2,1,0:T(8,128)S(1)} async-done(((f32[16,104,128]{2,1,0:T(8,128)}), f32[16,104,128]{2,1,0:T(8,128)S(1)}, u32[]{:S(2)}, u32[]{:S(2)}) %all-to-all-start.7) | async-done | bytes 852000 | tf_op jit(solution)/shard_map/back_wide/all_to_all | solution.py:14
  215.1 9.4 %all_to_all.55 = f32[16,16,128]{2,1,0:T(8,128)S(1)} all-to-all(f32[16,16,128]{2,1,0:T(8,128)S(1)} %pad_maximum_fusion.2), channel_id=1, replica_groups=mesh['wide'=16,'narrow'=16] {'wide'}, dimensions={0} | all-to-all | bytes 262144 | tf_op jit(solution)/shard_map/gram_sum_wide/all_to_all | solution.py:14
  224.5 18.6 %all_to_all.56 = f32[16,8,128]{2,1,0:T(8,128)S(1)} all-to-all(f32[16,8,128]{2,1,0:T(8,128)S(1)} %broadcast_in_dim.19), channel_id=1, replica_groups=mesh['wide'=16,'narrow'=16] {'narrow'}, dimensions={0} | all-to-all | bytes 131072 | tf_op jit(solution)/shard_map/gram_sum_narrow/all_to_all | solution.py:14
  243.8 5.2 %all-to-all-start.10 = ((f32[16,8,128]{2,1,0:T(8,128)}), f32[16,8,128]{2,1,0:T(8,128)S(1)}, u32[]{:S(2)}, u32[]{:S(2)}) async-start(f32[16,8,128]{2,1,0:T(8,128)} %broadcast_in_dim.40), calls=%async_computation.10 | async-start | bytes 131072 | tf_op jit(solution)/shard_map/gram_whole/all_to_all | solution.py:14
  251.3 2.6 %all-to-all-done.10 = f32[16,8,128]{2,1,0:T(8,128)S(1)} async-done(((f32[16,8,128]{2,1,0:T(8,128)}), f32[16,8,128]{2,1,0:T(8,128)S(1)}, u32[]{:S(2)}, u32[]{:S(2)}) %all-to-all-start.10) | async-done | bytes 65568 | tf_op jit(solution)/shard_map/gram_whole/all_to_all | solution.py:14
  253.9 3.4 %finish.1 = f32[96,128]{1,0:T(8,128)} custom-call(f32[128,128]{1,0:T(8,128)S(1)} %bitcast.80, f32[128,128]{1,0:T(8,128)S(1)} %get-tuple-element.71.refs_1_, f32[96,128]{1,0:T(8,128)S(1)} %get-tuple-element.72.refs_2_), custom_call_target="tpu_custom_call" | custom-call | flops 1073741824 | bytes 1048576 | tf_op jit(solution)/shard_map/finish/pallas_call | solution.py:286
  (69 shorter events, 33.7 us)
Async XLA Ops:
  1.8 28.3 %all-to-all-start = ((f32[16,96,128]{2,1,0:T(8,128)}), f32[16,96,128]{2,1,0:T(8,128)S(1)}, u32[]{:S(2)}, u32[]{:S(2)}) async-start(f32[16,96,128]{2,1,0:T(8,128)} %broadcast_in_dim.14), calls=%async_computation | async-start | bytes 1572864 | tf_op jit(solution)/shard_map/gather_wide/all_to_all | solution.py:14
  7.5 10.0 %collective-permute-start = (f32[96,128]{1,0:T(8,128)}, f32[96,128]{1,0:T(8,128)S(1)}, u32[]{:S(2)}, u32[]{:S(2)}) collective-permute-start(f32[96,128]{1,0:T(8,128)} %param.7), channel_id=1, source_target_pairs={{0,8},{1,9},{2,10},{3,11},{4,12},{5,13},{6,14},{7,15},{8,0},{9,1},... | collective-permute-start | bytes 147464 | tf_op jit(solution)/shard_map/gather_row/ppermute | solution.py:185
  14.7 6.4 %collective-permute-start.2 = (f32[96,128]{1,0:T(8,128)}, f32[96,128]{1,0:T(8,128)S(1)}, u32[]{:S(2)}, u32[]{:S(2)}) collective-permute-start(f32[96,128]{1,0:T(8,128)} %param.7), channel_id=1, source_target_pairs={{0,12},{1,13},{2,14},{3,15},{4,8},{5,9},{6,10},{7,11},{8,4},{9,5},... | collective-permute-start | bytes 147464 | tf_op jit(solution)/shard_map/gather_row/ppermute | solution.py:185
  14.7 6.4 %collective-permute-start.1 = (f32[96,128]{1,0:T(8,128)}, f32[96,128]{1,0:T(8,128)S(1)}, u32[]{:S(2)}, u32[]{:S(2)}) collective-permute-start(f32[96,128]{1,0:T(8,128)} %param.7), channel_id=1, source_target_pairs={{0,4},{1,5},{2,6},{3,7},{4,0},{5,1},{6,2},{7,3},{8,12},{9,13},{10,... | collective-permute-start | bytes 147464 | tf_op jit(solution)/shard_map/gather_row/ppermute | solution.py:185
  22.0 7.6 %collective-permute-start.4 = (f32[4,96,128]{2,1,0:T(8,128)S(1)}, f32[4,96,128]{2,1,0:T(8,128)S(1)}, u32[]{:S(2)}, u32[]{:S(2)}) collective-permute-start(f32[4,96,128]{2,1,0:T(8,128)S(1)} %pad_maximum_fusion.first_ref), channel_id=1, source_target_pairs={{0,1},{1,0},{2,3},{3,2},{4,5},{5,4},{6,7},{7,6},{8,9},{9,8},{10,11... | collective-permute-start | bytes 589832 | tf_op jit(solution)/shard_map/gather_row/ppermute | solution.py:185
  24.3 5.7 %collective-permute-start.3 = (f32[4,96,128]{2,1,0:T(8,128)S(1)}, f32[4,96,128]{2,1,0:T(8,128)S(1)}, u32[]{:S(2)}, u32[]{:S(2)}) collective-permute-start(f32[4,96,128]{2,1,0:T(8,128)S(1)} %pad_maximum_fusion.first_ref), channel_id=1, source_target_pairs={{0,2},{1,3},{2,0},{3,1},{4,6},{5,7},{6,4},{7,5},{8,10},{9,11},{10,... | collective-permute-start | bytes 589832 | tf_op jit(solution)/shard_map/gather_row/ppermute | solution.py:185
  30.1 0.7 copy-start
  32.3 29.2 %all-to-all-start.1 = ((f32[16,96,128]{2,1,0:T(8,128)}), f32[16,96,128]{2,1,0:T(8,128)S(1)}, u32[]{:S(2)}, u32[]{:S(2)}) async-start(f32[16,96,128]{2,1,0:T(8,128)} %gather_column.2), calls=%async_computation.1 | async-start | bytes 1572864 | tf_op jit(solution)/shard_map/gather_column/all_to_all | solution.py:14
  40.0 8.8 %collective-permute-start.5 = (f32[4,96,128]{2,1,0:T(8,128)S(1)}, f32[4,96,128]{2,1,0:T(8,128)S(1)}, u32[]{:S(2)}, u32[]{:S(2)}) collective-permute-start(f32[4,96,128]{2,1,0:T(8,128)S(1)} %collective-permute-done.3.second_ref), channel_id=1, source_target_pairs={{0,1},{1,0},{2,3},{3,2},{4,5},{5,4},{6,7},{7,6},{8,9},{9,8},{10,11... | collective-permute-start | bytes 589832 | tf_op jit(solution)/shard_map/gather_row/ppermute | solution.py:185
  61.5 27.7 %all-to-all-start.2 = ((f32[16,96,128]{2,1,0:T(8,128)}), f32[16,96,128]{2,1,0:T(8,128)S(1)}, u32[]{:S(2)}, u32[]{:S(2)}) async-start(f32[16,96,128]{2,1,0:T(8,128)} %bitcast.9), calls=%async_computation.2 | async-start | bytes 1572864 | tf_op jit(solution)/shard_map/back_transposed/all_to_all | solution.py:14
  68.1 21.1 %copy-start.1 = (s32[1,16]{1,0:T(1,128)S(1)}, s32[1,16]{1,0:T(1,128)}, u32[]{:S(2)}) copy-start(s32[1,16]{1,0:T(1,128)} %columns_ref.7) | copy-start | bytes 196
  68.1 10.6 %collective-permute-start.7 = (f32[4,96,128]{2,1,0:T(8,128)S(1)}, f32[4,96,128]{2,1,0:T(8,128)S(1)}, u32[]{:S(2)}, u32[]{:S(2)}) collective-permute-start(f32[4,96,128]{2,1,0:T(8,128)S(1)} %direct.6), channel_id=1, source_target_pairs={{0,1},{1,0},{2,3},{3,2},{4,5},{5,4},{6,7},{7,6},{8,9},{9,8},{10,11... | collective-permute-start | bytes 589832 | tf_op jit(solution)/shard_map/direct/ppermute | solution.py:185
  75.6 10.8 %collective-permute-start.6 = (f32[4,96,128]{2,1,0:T(8,128)S(1)}, f32[4,96,128]{2,1,0:T(8,128)S(1)}, u32[]{:S(2)}, u32[]{:S(2)}) collective-permute-start(f32[4,96,128]{2,1,0:T(8,128)S(1)} %get-tuple-element.48), channel_id=1, source_target_pairs={{0,1},{1,0},{2,3},{3,2},{4,5},{5,4},{6,7},{7,6},{8,9},{9,8},{10,11... | collective-permute-start | bytes 589832 | tf_op jit(solution)/shard_map/direct/ppermute | solution.py:185
  78.8 7.8 %collective-permute-start.8 = (f32[4,96,128]{2,1,0:T(8,128)S(1)}, f32[4,96,128]{2,1,0:T(8,128)S(1)}, u32[]{:S(2)}, u32[]{:S(2)}) collective-permute-start(f32[4,96,128]{2,1,0:T(8,128)S(1)} %add.52), channel_id=1, source_target_pairs={{0,2},{1,3},{2,0},{3,1},{4,6},{5,7},{6,4},{7,5},{8,10},{9,11},{10,... | collective-permute-start | bytes 589832 | tf_op jit(solution)/shard_map/direct/ppermute | solution.py:185
  90.8 17.9 %all-to-all-start.3 = ((f32[16,96,128]{2,1,0:T(8,128)}), f32[16,96,128]{2,1,0:T(8,128)S(1)}, u32[]{:S(2)}, u32[]{:S(2)}) async-start(f32[16,96,128]{2,1,0:T(8,128)} %back_wide.2), calls=%async_computation.3 | async-start | bytes 1572864 | tf_op jit(solution)/shard_map/back_wide/all_to_all | solution.py:14
  96.6 12.2 %collective-permute-start.9 = (f32[96,128]{1,0:T(8,128)S(1)}, f32[96,128]{1,0:T(8,128)S(1)}, u32[]{:S(2)}, u32[]{:S(2)}) collective-permute-start(f32[96,128]{1,0:T(8,128)S(1)} %get-tuple-element.76), channel_id=1, source_target_pairs={{0,8},{1,9},{2,10},{3,11},{4,12},{5,13},{6,14},{7,15},{8,0},{9,1},... | collective-permute-start | bytes 147464 | tf_op jit(solution)/shard_map/back_direct/ppermute | solution.py:185
  100.7 8.1 %collective-permute-start.11 = (f32[96,128]{1,0:T(8,128)S(1)}, f32[96,128]{1,0:T(8,128)S(1)}, u32[]{:S(2)}, u32[]{:S(2)}) collective-permute-start(f32[96,128]{1,0:T(8,128)S(1)} %get-tuple-element.77), channel_id=1, source_target_pairs={{0,12},{1,13},{2,14},{3,15},{4,8},{5,9},{6,10},{7,11},{8,4},{9,5},... | collective-permute-start | bytes 147464 | tf_op jit(solution)/shard_map/back_direct/ppermute | solution.py:185
  100.7 8.1 %collective-permute-start.10 = (f32[96,128]{1,0:T(8,128)S(1)}, f32[96,128]{1,0:T(8,128)S(1)}, u32[]{:S(2)}, u32[]{:S(2)}) collective-permute-start(f32[96,128]{1,0:T(8,128)S(1)} %get-tuple-element.78), channel_id=1, source_target_pairs={{0,4},{1,5},{2,6},{3,7},{4,0},{5,1},{6,2},{7,3},{8,12},{9,13},{10,... | collective-permute-start | bytes 147464 | tf_op jit(solution)/shard_map/back_direct/ppermute | solution.py:185
  109.8 28.0 %all-to-all-start.4 = ((f32[16,96,128]{2,1,0:T(8,128)}), f32[16,96,128]{2,1,0:T(8,128)S(1)}, u32[]{:S(2)}, u32[]{:S(2)}) async-start(f32[16,96,128]{2,1,0:T(8,128)} %broadcast_in_dim.16), calls=%async_computation.4 | async-start | bytes 1572864 | tf_op jit(solution)/shard_map/gather_wide/all_to_all | solution.py:14
  115.0 7.0 %collective-permute-start.14 = (f32[96,128]{1,0:T(8,128)S(1)}, f32[96,128]{1,0:T(8,128)S(1)}, u32[]{:S(2)}, u32[]{:S(2)}) collective-permute-start(f32[96,128]{1,0:T(8,128)S(1)} %fusion.7), channel_id=1, source_target_pairs={{0,12},{1,13},{2,14},{3,15},{4,8},{5,9},{6,10},{7,11},{8,4},{9,5},... | collective-permute-start | bytes 147464 | tf_op jit(solution)/shard_map/gather_row/ppermute | solution.py:185
  117.3 5.0 %collective-permute-start.13 = (f32[96,128]{1,0:T(8,128)S(1)}, f32[96,128]{1,0:T(8,128)S(1)}, u32[]{:S(2)}, u32[]{:S(2)}) collective-permute-start(f32[96,128]{1,0:T(8,128)S(1)} %fusion.7), channel_id=1, source_target_pairs={{0,4},{1,5},{2,6},{3,7},{4,0},{5,1},{6,2},{7,3},{8,12},{9,13},{10,... | collective-permute-start | bytes 147464 | tf_op jit(solution)/shard_map/gather_row/ppermute | solution.py:185
  119.6 8.1 %collective-permute-start.12 = (f32[96,128]{1,0:T(8,128)S(1)}, f32[96,128]{1,0:T(8,128)S(1)}, u32[]{:S(2)}, u32[]{:S(2)}) collective-permute-start(f32[96,128]{1,0:T(8,128)S(1)} %fusion.7), channel_id=1, source_target_pairs={{0,8},{1,9},{2,10},{3,11},{4,12},{5,13},{6,14},{7,15},{8,0},{9,1},... | collective-permute-start | bytes 147464 | tf_op jit(solution)/shard_map/gather_row/ppermute | solution.py:185
  127.7 8.3 %collective-permute-start.16 = (f32[4,96,128]{2,1,0:T(8,128)S(1)}, f32[4,96,128]{2,1,0:T(8,128)S(1)}, u32[]{:S(2)}, u32[]{:S(2)}) collective-permute-start(f32[4,96,128]{2,1,0:T(8,128)S(1)} %pad_maximum_fusion.1.first_ref), channel_id=1, source_target_pairs={{0,1},{1,0},{2,3},{3,2},{4,5},{5,4},{6,7},{7,6},{8,9},{9,8},{10,11... | collective-permute-start | bytes 589832 | tf_op jit(solution)/shard_map/gather_row/ppermute | solution.py:185
  132.1 5.7 %collective-permute-start.15 = (f32[4,96,128]{2,1,0:T(8,128)S(1)}, f32[4,96,128]{2,1,0:T(8,128)S(1)}, u32[]{:S(2)}, u32[]{:S(2)}) collective-permute-start(f32[4,96,128]{2,1,0:T(8,128)S(1)} %pad_maximum_fusion.1.first_ref), channel_id=1, source_target_pairs={{0,2},{1,3},{2,0},{3,1},{4,6},{5,7},{6,4},{7,5},{8,10},{9,11},{10,... | collective-permute-start | bytes 589832 | tf_op jit(solution)/shard_map/gather_row/ppermute | solution.py:185
  139.4 26.0 %all-to-all-start.5 = ((f32[16,96,128]{2,1,0:T(8,128)}), f32[16,96,128]{2,1,0:T(8,128)S(1)}, u32[]{:S(2)}, u32[]{:S(2)}) async-start(f32[16,96,128]{2,1,0:T(8,128)} %gather_column.3), calls=%async_computation.5 | async-start | bytes 1572864 | tf_op jit(solution)/shard_map/gather_column/all_to_all | solution.py:14
  143.0 8.3 %collective-permute-start.17 = (f32[4,96,128]{2,1,0:T(8,128)S(1)}, f32[4,96,128]{2,1,0:T(8,128)S(1)}, u32[]{:S(2)}, u32[]{:S(2)}) collective-permute-start(f32[4,96,128]{2,1,0:T(8,128)S(1)} %collective-permute-done.15.second_ref), channel_id=1, source_target_pairs={{0,1},{1,0},{2,3},{3,2},{4,5},{5,4},{6,7},{7,6},{8,9},{9,8},{10,11... | collective-permute-start | bytes 589832 | tf_op jit(solution)/shard_map/gather_row/ppermute | solution.py:185
  165.4 28.2 %all-to-all-start.6 = ((f32[16,96,128]{2,1,0:T(8,128)}), f32[16,96,128]{2,1,0:T(8,128)S(1)}, u32[]{:S(2)}, u32[]{:S(2)}) async-start(f32[16,96,128]{2,1,0:T(8,128)} %bitcast.20), calls=%async_computation.6 | async-start | bytes 1572864 | tf_op jit(solution)/shard_map/back_transposed/all_to_all | solution.py:14
  172.1 10.8 %collective-permute-start.19 = (f32[4,96,128]{2,1,0:T(8,128)S(1)}, f32[4,96,128]{2,1,0:T(8,128)S(1)}, u32[]{:S(2)}, u32[]{:S(2)}) collective-permute-start(f32[4,96,128]{2,1,0:T(8,128)S(1)} %direct.9), channel_id=1, source_target_pairs={{0,1},{1,0},{2,3},{3,2},{4,5},{5,4},{6,7},{7,6},{8,9},{9,8},{10,11... | collective-permute-start | bytes 589832 | tf_op jit(solution)/shard_map/direct/ppermute | solution.py:185
  179.5 11.2 %collective-permute-start.18 = (f32[4,96,128]{2,1,0:T(8,128)S(1)}, f32[4,96,128]{2,1,0:T(8,128)S(1)}, u32[]{:S(2)}, u32[]{:S(2)}) collective-permute-start(f32[4,96,128]{2,1,0:T(8,128)S(1)} %get-tuple-element.62), channel_id=1, source_target_pairs={{0,1},{1,0},{2,3},{3,2},{4,5},{5,4},{6,7},{7,6},{8,9},{9,8},{10,11... | collective-permute-start | bytes 589832 | tf_op jit(solution)/shard_map/direct/ppermute | solution.py:185
  182.9 8.1 %collective-permute-start.20 = (f32[4,96,128]{2,1,0:T(8,128)S(1)}, f32[4,96,128]{2,1,0:T(8,128)S(1)}, u32[]{:S(2)}, u32[]{:S(2)}) collective-permute-start(f32[4,96,128]{2,1,0:T(8,128)S(1)} %add.59), channel_id=1, source_target_pairs={{0,2},{1,3},{2,0},{3,1},{4,6},{5,7},{6,4},{7,5},{8,10},{9,11},{10,... | collective-permute-start | bytes 589832 | tf_op jit(solution)/shard_map/direct/ppermute | solution.py:185
  195.4 19.3 %all-to-all-start.7 = ((f32[16,104,128]{2,1,0:T(8,128)}), f32[16,104,128]{2,1,0:T(8,128)S(1)}, u32[]{:S(2)}, u32[]{:S(2)}) async-start(f32[16,104,128]{2,1,0:T(8,128)} %back_wide.3), calls=%async_computation.7 | async-start | bytes 1703936 | tf_op jit(solution)/shard_map/back_wide/all_to_all | solution.py:14
  201.8 13.0 %collective-permute-start.21 = (f32[96,128]{1,0:T(8,128)S(1)}, f32[96,128]{1,0:T(8,128)S(1)}, u32[]{:S(2)}, u32[]{:S(2)}) collective-permute-start(f32[96,128]{1,0:T(8,128)S(1)} %get-tuple-element.73), channel_id=1, source_target_pairs={{0,8},{1,9},{2,10},{3,11},{4,12},{5,13},{6,14},{7,15},{8,0},{9,1},... | collective-permute-start | bytes 147464 | tf_op jit(solution)/shard_map/back_direct/ppermute | solution.py:185
  205.8 8.9 %collective-permute-start.23 = (f32[96,128]{1,0:T(8,128)S(1)}, f32[96,128]{1,0:T(8,128)S(1)}, u32[]{:S(2)}, u32[]{:S(2)}) collective-permute-start(f32[96,128]{1,0:T(8,128)S(1)} %get-tuple-element.74), channel_id=1, source_target_pairs={{0,12},{1,13},{2,14},{3,15},{4,8},{5,9},{6,10},{7,11},{8,4},{9,5},... | collective-permute-start | bytes 147464 | tf_op jit(solution)/shard_map/back_direct/ppermute | solution.py:185
  206.1 8.7 %collective-permute-start.22 = (f32[96,128]{1,0:T(8,128)S(1)}, f32[96,128]{1,0:T(8,128)S(1)}, u32[]{:S(2)}, u32[]{:S(2)}) collective-permute-start(f32[96,128]{1,0:T(8,128)S(1)} %get-tuple-element.75), channel_id=1, source_target_pairs={{0,4},{1,5},{2,6},{3,7},{4,0},{5,1},{6,2},{7,3},{8,12},{9,13},{10,... | collective-permute-start | bytes 147464 | tf_op jit(solution)/shard_map/back_direct/ppermute | solution.py:185
  243.8 10.1 %all-to-all-start.10 = ((f32[16,8,128]{2,1,0:T(8,128)}), f32[16,8,128]{2,1,0:T(8,128)S(1)}, u32[]{:S(2)}, u32[]{:S(2)}) async-start(f32[16,8,128]{2,1,0:T(8,128)} %broadcast_in_dim.40), calls=%async_computation.10 | async-start | bytes 131072 | tf_op jit(solution)/shard_map/gram_whole/all_to_all | solution.py:14

commit v9 on v8

--- a/solution.py
+++ b/solution.py
@@ -234,15 +234,14 @@
         arrived = exchange(transposed.reshape(count, rows, width), NARROW)
     with jax.named_scope("direct"):
         quarters = tile.reshape(groups // 2, 2, 2, rows, order)
-        (far_second,) = direct_quarters(quarters, column_block, [(1, 1)], where)
-        column_block, far_second = lax.optimization_barrier((column_block, far_second))
-        got_second = swap(far_second, 1)
-        far_first, near_second = direct_quarters(
-            quarters, column_block, [(0, 1), (1, 0)], where
+        far_second, far_first = direct_quarters(quarters, column_block, [(1, 1), (0, 1)], where)
+        column_block, far_second, far_first = lax.optimization_barrier(
+            (column_block, far_second, far_first)
         )
-        column_block, far_first = lax.optimization_barrier((column_block, far_first))
-        got_first = swap(far_first, 1)
-        (near_first,) = direct_quarters(quarters, column_block, [(0, 0)], where)
+        got_second, got_first = swap(far_second, 1), swap(far_first, 1)
+        near_second, near_first = direct_quarters(
+            quarters, column_block, [(1, 0), (0, 0)], where
+        )
         kept = near_first + got_first + swap(near_second + got_second, 2)
         arrived, kept = lax.optimization_barrier((arrived, kept))
     gram = None

time: 261 us -> 264 us (1.011)
  waiting for transfers between devices: 63.5 us -> 71.6 us
  Pallas kernels: 52.8 us -> 48.7 us
  starting transfers between devices: 104 us -> 101 us
    ppermute x24, waiting for transfers between devices: 28.5 us -> 42 us  [swap(): return lax.ppermute(value, NARROW, [(i, i ^ mask) for i in range(size)])]
    all_to_all x9, waiting for transfers between devices: 35 us -> 29.6 us  [exchange(): return lax.all_to_all(parts, axis, 0, 0, tiled=True)]
    pallas_call x6 -> x4, Pallas kernels: 20.1 us -> 16 us  [direct_quarters(): pl.pallas_call(kernel, out_shape=[jax.ShapeDtypeStruct((each, rows, width...]
    ppermute x24, starting transfers between devices: 57.6 us -> 54.3 us  [swap(): return lax.ppermute(value, NARROW, [(i, i ^ mask) for i in range(size)])]
  transfers between devices with their start and end apart: 33 -> 33, of which waited for: 22 -> 23; matrix products, arithmetic and copies ran while one was open for 2% -> 2% of each run, Pallas kernels for 17% -> 15%
where the time goes in v9:
time: 264 us; the launch traced here: 260 us
  starting transfers between devices  101 us (38%)
  waiting for transfers between devices  71.6 us (27%)
  Pallas kernels  48.7 us (18%)
  blocking collectives  30.2 us (11%)
  local copies, waits for them, and re-layouts  4.13 us (2%)
    ppermute x24, starting transfers between devices, swap(): return lax.ppermute(value, NARROW, [(i, i ^ mask) for i in range(size)])  54.3 us
    all_to_all x9, starting transfers between devices, exchange(): return lax.all_to_all(parts, axis, 0, 0, tiled=True)  46.6 us
    ppermute x24, waiting for transfers between devices, swap(): return lax.ppermute(value, NARROW, [(i, i ^ mask) for i in range(size)])  42 us
    all_to_all x2, blocking collectives, exchange(): return lax.all_to_all(parts, axis, 0, 0, tiled=True)  30.2 us
    all_to_all x9, waiting for transfers between devices, exchange(): return lax.all_to_all(parts, axis, 0, 0, tiled=True)  29.6 us
    pallas_call x4, Pallas kernels, transposed_half(): pl.pallas_call(kernel, out_shape=jax.ShapeDtypeStruct((width, order) if p...  20.5 us
    pallas_call x4, Pallas kernels, direct_quarters(): pl.pallas_call(kernel, out_shape=[jax.ShapeDtypeStruct((each, rows, width...  16 us
    pallas_call x4, Pallas kernels, move_blocks(): pl.pallas_call(kernel, out_shape=jax.ShapeDtypeStruct((count, rows + more...  6.52 us
  transfers between devices with their start and end apart: 33, of which 23 were waited for; matrix products, arithmetic and copies ran while one was open for 2% of the time, Pallas kernels for 15%

profile of v9, /device:TPU:8, one launch (start us, length us, event | category | flops | bytes accessed | tf_op | source)
XLA Modules:
  0.0 260.5 jit_solution(10236901526018048011)
XLA Ops:
  1.8 5.8 %all-to-all-start = ((f32[16,96,128]{2,1,0:T(8,128)}), f32[16,96,128]{2,1,0:T(8,128)S(1)}, u32[]{:S(2)}, u32[]{:S(2)}) async-start(f32[16,96,128]{2,1,0:T(8,128)} %broadcast_in_dim.14), calls=%async_computation | async-start | bytes 1572864 | tf_op jit(solution)/shard_map/gather_wide/all_to_all | solution.py:14
  7.5 7.2 %collective-permute-start = (f32[96,128]{1,0:T(8,128)}, f32[96,128]{1,0:T(8,128)S(1)}, u32[]{:S(2)}, u32[]{:S(2)}) collective-permute-start(f32[96,128]{1,0:T(8,128)} %param.7), channel_id=1, source_target_pairs={{0,8},{1,9},{2,10},{3,11},{4,12},{5,13},{6,14},{7,15},{8,0},{9,1},... | collective-permute-start | bytes 147464 | tf_op jit(solution)/shard_map/gather_row/ppermute | solution.py:185
  17.5 3.6 %collective-permute-done.2 = f32[96,128]{1,0:T(8,128)S(1)} collective-permute-done((f32[96,128]{1,0:T(8,128)}, f32[96,128]{1,0:T(8,128)S(1)}, u32[]{:S(2)}, u32[]{:S(2)}) %collective-permute-start.2) | collective-permute-done | bytes 49184 | tf_op jit(solution)/shard_map/gather_row/ppermute | solution.py:185
  22.0 2.4 collective-permute-start.4
  25.9 3.6 %collective-permute-done.4.first_ref = f32[4,96,128]{2,1,0:T(8,128)S(1)} collective-permute-done((f32[4,96,128]{2,1,0:T(8,128)S(1)}, f32[4,96,128]{2,1,0:T(8,128)S(1)}, u32[]{:S(2)}, u32[]{:S(2)}) %collective-permute-start.4) | collective-permute-done | bytes 196640 | tf_op jit(solution)/shard_map/gather_row/ppermute | solution.py:185
  32.3 7.0 %all-to-all-start.1 = ((f32[16,96,128]{2,1,0:T(8,128)}), f32[16,96,128]{2,1,0:T(8,128)S(1)}, u32[]{:S(2)}, u32[]{:S(2)}) async-start(f32[16,96,128]{2,1,0:T(8,128)} %gather_column.2), calls=%async_computation.1 | async-start | bytes 1572864 | tf_op jit(solution)/shard_map/gather_column/all_to_all | solution.py:14
  40.0 3.4 %collective-permute-start.5 = (f32[4,96,128]{2,1,0:T(8,128)S(1)}, f32[4,96,128]{2,1,0:T(8,128)S(1)}, u32[]{:S(2)}, u32[]{:S(2)}) collective-permute-start(f32[4,96,128]{2,1,0:T(8,128)S(1)} %collective-permute-done.3.second_ref), channel_id=1, source_target_pairs={{0,1},{1,0},{2,3},{3,2},{4,5},{5,4},{6,7},{7,6},{8,9},{9,8},{10,11... | collective-permute-start | bytes 589832 | tf_op jit(solution)/shard_map/gather_row/ppermute | solution.py:185
  44.2 4.6 %transposed.4.rest_0_ = f32[128,1536]{1,0:T(8,128)S(1)} custom-call(s32[15]{0:T(128)S(1)} %concatenate.6.where_ref, f32[8,2,96,1536]{3,2,1,0:T(8,128)} %bitcast.79, f32[4,96,128]{2,1,0:T(8,128)S(1)} %pad_maximum_fusion.first_ref, f32[4,96,128]{2,1,0:T(8,128)S(1)} %collective-permute-done.3.second_ref), custom_call_target="tpu_custom_call" | custom-call | flops 905969664 | bytes 4718592 | tf_op jit(solution)/shard_map/transposed/pallas_call | solution.py:161
  48.8 5.6 %transposed.5 = f32[1536,128]{1,0:T(8,128)} custom-call(s32[15]{0:T(128)S(1)} %concatenate.6.where_ref, f32[8,2,96,1536]{3,2,1,0:T(8,128)} %bitcast.80, f32[4,96,128]{2,1,0:T(8,128)S(1)} %collective-permute-done.4.first_ref, f32[4,96,128]{2,1,0:T(8,128)S(1)} %collective-permute-done.5.second_ref, f32[128,1536]{1,0:T(8,128)S(1)} %transposed.4.rest_0_), custom_call_target="tpu_custom_call" | custom-call | flops 905969664 | bytes 4718592 | tf_op jit(solution)/shard_map/transposed/pallas_call | solution.py:161
  54.4 7.0 %all-to-all-done.1 = f32[16,96,128]{2,1,0:T(8,128)S(1)} async-done(((f32[16,96,128]{2,1,0:T(8,128)}), f32[16,96,128]{2,1,0:T(8,128)S(1)}, u32[]{:S(2)}, u32[]{:S(2)}) %all-to-all-start.1) | async-done | bytes 786464 | tf_op jit(solution)/shard_map/gather_column/all_to_all | solution.py:14
  61.5 3.6 %all-to-all-start.2 = ((f32[16,96,128]{2,1,0:T(8,128)}), f32[16,96,128]{2,1,0:T(8,128)S(1)}, u32[]{:S(2)}, u32[]{:S(2)}) async-start(f32[16,96,128]{2,1,0:T(8,128)} %bitcast.9), calls=%async_computation.2 | async-start | bytes 1572864 | tf_op jit(solution)/shard_map/back_transposed/all_to_all | solution.py:14
  65.1 4.0 %direct.4 = (f32[4,96,128]{2,1,0:T(8,128)S(1)}, f32[4,96,128]{2,1,0:T(8,128)S(1)}) custom-call(s32[15]{0:T(128)S(1)} %concatenate.6.where_ref, f32[4,2,2,96,1536]{4,3,2,1,0:T(8,128)} %bitcast.81, f32[1536,128]{1,0:T(8,128)S(1)} %bitcast.74), custom_call_target="tpu_custom_call" | custom-call | flops 452984832 | bytes 4718592 | tf_op jit(solution)/shard_map/direct/pallas_call | solution.py:106
  69.1 3.4 %collective-permute-start.7 = (f32[4,96,128]{2,1,0:T(8,128)S(1)}, f32[4,96,128]{2,1,0:T(8,128)S(1)}, u32[]{:S(2)}, u32[]{:S(2)}) collective-permute-start(f32[4,96,128]{2,1,0:T(8,128)S(1)} %get-tuple-element.53), channel_id=1, source_target_pairs={{0,1},{1,0},{2,3},{3,2},{4,5},{5,4},{6,7},{7,6},{8,9},{9,8},{10,11... | collective-permute-start | bytes 589832 | tf_op jit(solution)/shard_map/direct/ppermute | solution.py:185
  72.7 4.0 %direct.5 = (f32[4,96,128]{2,1,0:T(8,128)S(1)}, f32[4,96,128]{2,1,0:T(8,128)S(1)}) custom-call(s32[15]{0:T(128)S(1)} %concatenate.6.where_ref, f32[4,2,2,96,1536]{4,3,2,1,0:T(8,128)} %bitcast.82, f32[1536,128]{1,0:T(8,128)S(1)} %bitcast.75), custom_call_target="tpu_custom_call" | custom-call | flops 452984832 | bytes 4718592 | tf_op jit(solution)/shard_map/direct/pallas_call | solution.py:106
  76.7 5.8 %collective-permute-done.7 = f32[4,96,128]{2,1,0:T(8,128)S(1)} collective-permute-done((f32[4,96,128]{2,1,0:T(8,128)S(1)}, f32[4,96,128]{2,1,0:T(8,128)S(1)}, u32[]{:S(2)}, u32[]{:S(2)}) %collective-permute-start.7) | collective-permute-done | bytes 196640 | tf_op jit(solution)/shard_map/direct/ppermute | solution.py:185
  82.6 2.0 collective-permute-start.8
  84.5 1.8 collective-permute-done.6
  86.3 2.0 collective-permute-done.8
  90.6 5.7 %all-to-all-start.3 = ((f32[16,96,128]{2,1,0:T(8,128)}), f32[16,96,128]{2,1,0:T(8,128)S(1)}, u32[]{:S(2)}, u32[]{:S(2)}) async-start(f32[16,96,128]{2,1,0:T(8,128)} %back_wide.2), calls=%async_computation.3 | async-start | bytes 1572864 | tf_op jit(solution)/shard_map/back_wide/all_to_all | solution.py:14
  96.4 7.0 %collective-permute-start.9 = (f32[96,128]{1,0:T(8,128)S(1)}, f32[96,128]{1,0:T(8,128)S(1)}, u32[]{:S(2)}, u32[]{:S(2)}) collective-permute-start(f32[96,128]{1,0:T(8,128)S(1)} %get-tuple-element.80), channel_id=1, source_target_pairs={{0,8},{1,9},{2,10},{3,11},{4,12},{5,13},{6,14},{7,15},{8,0},{9,1},... | collective-permute-start | bytes 147464 | tf_op jit(solution)/shard_map/back_direct/ppermute | solution.py:185
  104.0 4.5 %all-to-all-done.3 = f32[16,96,128]{2,1,0:T(8,128)S(1)} async-done(((f32[16,96,128]{2,1,0:T(8,128)}), f32[16,96,128]{2,1,0:T(8,128)S(1)}, u32[]{:S(2)}, u32[]{:S(2)}) %all-to-all-start.3) | async-done | bytes 786464 | tf_op jit(solution)/shard_map/back_wide/all_to_all | solution.py:14
  111.0 5.7 %all-to-all-start.4 = ((f32[16,96,128]{2,1,0:T(8,128)}), f32[16,96,128]{2,1,0:T(8,128)S(1)}, u32[]{:S(2)}, u32[]{:S(2)}) async-start(f32[16,96,128]{2,1,0:T(8,128)} %broadcast_in_dim.16), calls=%async_computation.4 | async-start | bytes 1572864 | tf_op jit(solution)/shard_map/gather_wide/all_to_all | solution.py:14
  116.7 2.5 collective-permute-start.14
  119.2 2.9 %collective-permute-start.13 = (f32[96,128]{1,0:T(8,128)S(1)}, f32[96,128]{1,0:T(8,128)S(1)}, u32[]{:S(2)}, u32[]{:S(2)}) collective-permute-start(f32[96,128]{1,0:T(8,128)S(1)} %fusion.7), channel_id=1, source_target_pairs={{0,4},{1,5},{2,6},{3,7},{4,0},{5,1},{6,2},{7,3},{8,12},{9,13},{10,... | collective-permute-start | bytes 147464 | tf_op jit(solution)/shard_map/gather_row/ppermute | solution.py:185
  124.3 6.1 %collective-permute-done.12 = f32[96,128]{1,0:T(8,128)S(1)} collective-permute-done((f32[96,128]{1,0:T(8,128)S(1)}, f32[96,128]{1,0:T(8,128)S(1)}, u32[]{:S(2)}, u32[]{:S(2)}) %collective-permute-start.12) | collective-permute-done | bytes 49184 | tf_op jit(solution)/shard_map/gather_row/ppermute | solution.py:185
  130.4 2.0 collective-permute-start.16
  133.1 4.6 %collective-permute-done.16.first_ref = f32[4,96,128]{2,1,0:T(8,128)S(1)} collective-permute-done((f32[4,96,128]{2,1,0:T(8,128)S(1)}, f32[4,96,128]{2,1,0:T(8,128)S(1)}, u32[]{:S(2)}, u32[]{:S(2)}) %collective-permute-start.16) | collective-permute-done | bytes 196640 | tf_op jit(solution)/shard_map/gather_row/ppermute | solution.py:185
  139.7 4.1 %all-to-all-start.5 = ((f32[16,96,128]{2,1,0:T(8,128)}), f32[16,96,128]{2,1,0:T(8,128)S(1)}, u32[]{:S(2)}, u32[]{:S(2)}) async-start(f32[16,96,128]{2,1,0:T(8,128)} %gather_column.3), calls=%async_computation.5 | async-start | bytes 1572864 | tf_op jit(solution)/shard_map/gather_column/all_to_all | solution.py:14
  143.8 3.4 %collective-permute-start.17 = (f32[4,96,128]{2,1,0:T(8,128)S(1)}, f32[4,96,128]{2,1,0:T(8,128)S(1)}, u32[]{:S(2)}, u32[]{:S(2)}) collective-permute-start(f32[4,96,128]{2,1,0:T(8,128)S(1)} %collective-permute-done.15.second_ref), channel_id=1, source_target_pairs={{0,1},{1,0},{2,3},{3,2},{4,5},{5,4},{6,7},{7,6},{8,9},{9,8},{10,11... | collective-permute-start | bytes 589832 | tf_op jit(solution)/shard_map/gather_row/ppermute | solution.py:185
  147.3 4.6 %transposed.6.rest_0_ = f32[128,1536]{1,0:T(8,128)S(1)} custom-call(s32[15]{0:T(128)S(1)} %concatenate.6.where_ref, f32[8,2,96,1536]{3,2,1,0:T(8,128)} %bitcast.83, f32[4,96,128]{2,1,0:T(8,128)S(1)} %pad_maximum_fusion.1.first_ref, f32[4,96,128]{2,1,0:T(8,128)S(1)} %collective-permute-done.15.second_ref), custom_call_target="tpu_custom_call" | custom-call | flops 905969664 | bytes 4718592 | tf_op jit(solution)/shard_map/transposed/pallas_call | solution.py:161
  152.2 5.6 %transposed.7 = f32[1536,128]{1,0:T(8,128)} custom-call(s32[15]{0:T(128)S(1)} %concatenate.6.where_ref, f32[8,2,96,1536]{3,2,1,0:T(8,128)} %bitcast.84, f32[4,96,128]{2,1,0:T(8,128)S(1)} %collective-permute-done.16.first_ref, f32[4,96,128]{2,1,0:T(8,128)S(1)} %collective-permute-done.17.second_ref, f32[128,1536]{1,0:T(8,128)S(1)} %transposed.6.rest_0_), custom_call_target="tpu_custom_call" | custom-call | flops 905969664 | bytes 4718592 | tf_op jit(solution)/shard_map/transposed/pallas_call | solution.py:161
  157.8 8.9 %all-to-all-done.5 = f32[16,96,128]{2,1,0:T(8,128)S(1)} async-done(((f32[16,96,128]{2,1,0:T(8,128)}), f32[16,96,128]{2,1,0:T(8,128)S(1)}, u32[]{:S(2)}, u32[]{:S(2)}) %all-to-all-start.5) | async-done | bytes 786464 | tf_op jit(solution)/shard_map/gather_column/all_to_all | solution.py:14
  166.7 3.6 %all-to-all-start.6 = ((f32[16,96,128]{2,1,0:T(8,128)}), f32[16,96,128]{2,1,0:T(8,128)S(1)}, u32[]{:S(2)}, u32[]{:S(2)}) async-start(f32[16,96,128]{2,1,0:T(8,128)} %bitcast.20), calls=%async_computation.6 | async-start | bytes 1572864 | tf_op jit(solution)/shard_map/back_transposed/all_to_all | solution.py:14
  170.3 4.0 %direct.6 = (f32[4,96,128]{2,1,0:T(8,128)S(1)}, f32[4,96,128]{2,1,0:T(8,128)S(1)}) custom-call(s32[15]{0:T(128)S(1)} %concatenate.6.where_ref, f32[4,2,2,96,1536]{4,3,2,1,0:T(8,128)} %bitcast.85, f32[1536,128]{1,0:T(8,128)S(1)} %bitcast.76), custom_call_target="tpu_custom_call" | custom-call | flops 452984832 | bytes 4718592 | tf_op jit(solution)/shard_map/direct/pallas_call | solution.py:106
  174.3 3.4 %collective-permute-start.19 = (f32[4,96,128]{2,1,0:T(8,128)S(1)}, f32[4,96,128]{2,1,0:T(8,128)S(1)}, u32[]{:S(2)}, u32[]{:S(2)}) collective-permute-start(f32[4,96,128]{2,1,0:T(8,128)S(1)} %get-tuple-element.68), channel_id=1, source_target_pairs={{0,1},{1,0},{2,3},{3,2},{4,5},{5,4},{6,7},{7,6},{8,9},{9,8},{10,11... | collective-permute-start | bytes 589832 | tf_op jit(solution)/shard_map/direct/ppermute | solution.py:185
  177.9 4.0 %direct.7 = (f32[4,96,128]{2,1,0:T(8,128)S(1)}, f32[4,96,128]{2,1,0:T(8,128)S(1)}) custom-call(s32[15]{0:T(128)S(1)} %concatenate.6.where_ref, f32[4,2,2,96,1536]{4,3,2,1,0:T(8,128)} %bitcast.86, f32[1536,128]{1,0:T(8,128)S(1)} %bitcast.77), custom_call_target="tpu_custom_call" | custom-call | flops 452984832 | bytes 4718592 | tf_op jit(solution)/shard_map/direct/pallas_call | solution.py:106
  181.9 7.3 %collective-permute-done.19 = f32[4,96,128]{2,1,0:T(8,128)S(1)} collective-permute-done((f32[4,96,128]{2,1,0:T(8,128)S(1)}, f32[4,96,128]{2,1,0:T(8,128)S(1)}, u32[]{:S(2)}, u32[]{:S(2)}) %collective-permute-start.19) | collective-permute-done | bytes 196640 | tf_op jit(solution)/shard_map/direct/ppermute | solution.py:185
  192.8 2.1 collective-permute-done.20
  195.2 1.8 back_wide.3
  197.0 5.8 %all-to-all-start.7 = ((f32[16,104,128]{2,1,0:T(8,128)}), f32[16,104,128]{2,1,0:T(8,128)S(1)}, u32[]{:S(2)}, u32[]{:S(2)}) async-start(f32[16,104,128]{2,1,0:T(8,128)} %back_wide.3), calls=%async_computation.7 | async-start | bytes 1703936 | tf_op jit(solution)/shard_map/back_wide/all_to_all | solution.py:14
  202.8 6.5 %collective-permute-start.21 = (f32[96,128]{1,0:T(8,128)S(1)}, f32[96,128]{1,0:T(8,128)S(1)}, u32[]{:S(2)}, u32[]{:S(2)}) collective-permute-start(f32[96,128]{1,0:T(8,128)S(1)} %get-tuple-element.77), channel_id=1, source_target_pairs={{0,8},{1,9},{2,10},{3,11},{4,12},{5,13},{6,14},{7,15},{8,0},{9,1},... | collective-permute-start | bytes 147464 | tf_op jit(solution)/shard_map/back_direct/ppermute | solution.py:185
  210.0 5.7 %all-to-all-done.7 = f32[16,104,128]{2,1,0:T(8,128)S(1)} async-done(((f32[16,104,128]{2,1,0:T(8,128)}), f32[16,104,128]{2,1,0:T(8,128)S(1)}, u32[]{:S(2)}, u32[]{:S(2)}) %all-to-all-start.7) | async-done | bytes 852000 | tf_op jit(solution)/shard_map/back_wide/all_to_all | solution.py:14
  216.1 10.5 %all_to_all.55 = f32[16,16,128]{2,1,0:T(8,128)S(1)} all-to-all(f32[16,16,128]{2,1,0:T(8,128)S(1)} %pad_maximum_fusion.2), channel_id=1, replica_groups=mesh['wide'=16,'narrow'=16] {'wide'}, dimensions={0} | all-to-all | bytes 262144 | tf_op jit(solution)/shard_map/gram_sum_wide/all_to_all | solution.py:14
  226.6 19.7 %all_to_all.56 = f32[16,8,128]{2,1,0:T(8,128)S(1)} all-to-all(f32[16,8,128]{2,1,0:T(8,128)S(1)} %broadcast_in_dim.19), channel_id=1, replica_groups=mesh['wide'=16,'narrow'=16] {'narrow'}, dimensions={0} | all-to-all | bytes 131072 | tf_op jit(solution)/shard_map/gram_sum_narrow/all_to_all | solution.py:14
  246.9 5.2 %all-to-all-start.10 = ((f32[16,8,128]{2,1,0:T(8,128)}), f32[16,8,128]{2,1,0:T(8,128)S(1)}, u32[]{:S(2)}, u32[]{:S(2)}) async-start(f32[16,8,128]{2,1,0:T(8,128)} %broadcast_in_dim.40), calls=%async_computation.10 | async-start | bytes 131072 | tf_op jit(solution)/shard_map/gram_whole/all_to_all | solution.py:14
  252.2 2.3 inverse_first.1
  254.5 2.6 all-to-all-done.10
  257.1 3.4 %finish.1 = f32[96,128]{1,0:T(8,128)} custom-call(f32[128,128]{1,0:T(8,128)S(1)} %bitcast.78, f32[128,128]{1,0:T(8,128)S(1)} %get-tuple-element.75.refs_1_, f32[96,128]{1,0:T(8,128)S(1)} %get-tuple-element.76.refs_2_), custom_call_target="tpu_custom_call" | custom-call | flops 1073741824 | bytes 1048576 | tf_op jit(solution)/shard_map/finish/pallas_call | solution.py:285
  (67 shorter events, 27.7 us)
Async XLA Ops:
  1.8 28.3 %all-to-all-start = ((f32[16,96,128]{2,1,0:T(8,128)}), f32[16,96,128]{2,1,0:T(8,128)S(1)}, u32[]{:S(2)}, u32[]{:S(2)}) async-start(f32[16,96,128]{2,1,0:T(8,128)} %broadcast_in_dim.14), calls=%async_computation | async-start | bytes 1572864 | tf_op jit(solution)/shard_map/gather_wide/all_to_all | solution.py:14
  7.5 10.0 %collective-permute-start = (f32[96,128]{1,0:T(8,128)}, f32[96,128]{1,0:T(8,128)S(1)}, u32[]{:S(2)}, u32[]{:S(2)}) collective-permute-start(f32[96,128]{1,0:T(8,128)} %param.7), channel_id=1, source_target_pairs={{0,8},{1,9},{2,10},{3,11},{4,12},{5,13},{6,14},{7,15},{8,0},{9,1},... | collective-permute-start | bytes 147464 | tf_op jit(solution)/shard_map/gather_row/ppermute | solution.py:185
  14.7 6.4 %collective-permute-start.2 = (f32[96,128]{1,0:T(8,128)}, f32[96,128]{1,0:T(8,128)S(1)}, u32[]{:S(2)}, u32[]{:S(2)}) collective-permute-start(f32[96,128]{1,0:T(8,128)} %param.7), channel_id=1, source_target_pairs={{0,12},{1,13},{2,14},{3,15},{4,8},{5,9},{6,10},{7,11},{8,4},{9,5},... | collective-permute-start | bytes 147464 | tf_op jit(solution)/shard_map/gather_row/ppermute | solution.py:185
  14.7 6.4 %collective-permute-start.1 = (f32[96,128]{1,0:T(8,128)}, f32[96,128]{1,0:T(8,128)S(1)}, u32[]{:S(2)}, u32[]{:S(2)}) collective-permute-start(f32[96,128]{1,0:T(8,128)} %param.7), channel_id=1, source_target_pairs={{0,4},{1,5},{2,6},{3,7},{4,0},{5,1},{6,2},{7,3},{8,12},{9,13},{10,... | collective-permute-start | bytes 147464 | tf_op jit(solution)/shard_map/gather_row/ppermute | solution.py:185
  22.0 7.6 %collective-permute-start.4 = (f32[4,96,128]{2,1,0:T(8,128)S(1)}, f32[4,96,128]{2,1,0:T(8,128)S(1)}, u32[]{:S(2)}, u32[]{:S(2)}) collective-permute-start(f32[4,96,128]{2,1,0:T(8,128)S(1)} %pad_maximum_fusion.first_ref), channel_id=1, source_target_pairs={{0,1},{1,0},{2,3},{3,2},{4,5},{5,4},{6,7},{7,6},{8,9},{9,8},{10,11... | collective-permute-start | bytes 589832 | tf_op jit(solution)/shard_map/gather_row/ppermute | solution.py:185
  24.3 5.7 %collective-permute-start.3 = (f32[4,96,128]{2,1,0:T(8,128)S(1)}, f32[4,96,128]{2,1,0:T(8,128)S(1)}, u32[]{:S(2)}, u32[]{:S(2)}) collective-permute-start(f32[4,96,128]{2,1,0:T(8,128)S(1)} %pad_maximum_fusion.first_ref), channel_id=1, source_target_pairs={{0,2},{1,3},{2,0},{3,1},{4,6},{5,7},{6,4},{7,5},{8,10},{9,11},{10,... | collective-permute-start | bytes 589832 | tf_op jit(solution)/shard_map/gather_row/ppermute | solution.py:185
  30.1 0.7 copy-start
  32.3 29.2 %all-to-all-start.1 = ((f32[16,96,128]{2,1,0:T(8,128)}), f32[16,96,128]{2,1,0:T(8,128)S(1)}, u32[]{:S(2)}, u32[]{:S(2)}) async-start(f32[16,96,128]{2,1,0:T(8,128)} %gather_column.2), calls=%async_computation.1 | async-start | bytes 1572864 | tf_op jit(solution)/shard_map/gather_column/all_to_all | solution.py:14
  40.0 8.8 %collective-permute-start.5 = (f32[4,96,128]{2,1,0:T(8,128)S(1)}, f32[4,96,128]{2,1,0:T(8,128)S(1)}, u32[]{:S(2)}, u32[]{:S(2)}) collective-permute-start(f32[4,96,128]{2,1,0:T(8,128)S(1)} %collective-permute-done.3.second_ref), channel_id=1, source_target_pairs={{0,1},{1,0},{2,3},{3,2},{4,5},{5,4},{6,7},{7,6},{8,9},{9,8},{10,11... | collective-permute-start | bytes 589832 | tf_op jit(solution)/shard_map/gather_row/ppermute | solution.py:185
  61.5 27.6 %all-to-all-start.2 = ((f32[16,96,128]{2,1,0:T(8,128)}), f32[16,96,128]{2,1,0:T(8,128)S(1)}, u32[]{:S(2)}, u32[]{:S(2)}) async-start(f32[16,96,128]{2,1,0:T(8,128)} %bitcast.9), calls=%async_computation.2 | async-start | bytes 1572864 | tf_op jit(solution)/shard_map/back_transposed/all_to_all | solution.py:14
  65.1 24.0 %copy-start.1 = (s32[1,16]{1,0:T(1,128)S(1)}, s32[1,16]{1,0:T(1,128)}, u32[]{:S(2)}) copy-start(s32[1,16]{1,0:T(1,128)} %columns_ref.7) | copy-start | bytes 196
  69.1 13.4 %collective-permute-start.7 = (f32[4,96,128]{2,1,0:T(8,128)S(1)}, f32[4,96,128]{2,1,0:T(8,128)S(1)}, u32[]{:S(2)}, u32[]{:S(2)}) collective-permute-start(f32[4,96,128]{2,1,0:T(8,128)S(1)} %get-tuple-element.53), channel_id=1, source_target_pairs={{0,1},{1,0},{2,3},{3,2},{4,5},{5,4},{6,7},{7,6},{8,9},{9,8},{10,11... | collective-permute-start | bytes 589832 | tf_op jit(solution)/shard_map/direct/ppermute | solution.py:185
  72.5 13.8 %collective-permute-start.6 = (f32[4,96,128]{2,1,0:T(8,128)S(1)}, f32[4,96,128]{2,1,0:T(8,128)S(1)}, u32[]{:S(2)}, u32[]{:S(2)}) collective-permute-start(f32[4,96,128]{2,1,0:T(8,128)S(1)} %get-tuple-element.51), channel_id=1, source_target_pairs={{0,1},{1,0},{2,3},{3,2},{4,5},{5,4},{6,7},{7,6},{8,9},{9,8},{10,11... | collective-permute-start | bytes 589832 | tf_op jit(solution)/shard_map/direct/ppermute | solution.py:185
  82.6 5.8 %collective-permute-start.8 = (f32[4,96,128]{2,1,0:T(8,128)S(1)}, f32[4,96,128]{2,1,0:T(8,128)S(1)}, u32[]{:S(2)}, u32[]{:S(2)}) collective-permute-start(f32[4,96,128]{2,1,0:T(8,128)S(1)} %add.52), channel_id=1, source_target_pairs={{0,2},{1,3},{2,0},{3,1},{4,6},{5,7},{6,4},{7,5},{8,10},{9,11},{10,... | collective-permute-start | bytes 589832 | tf_op jit(solution)/shard_map/direct/ppermute | solution.py:185
  90.6 17.9 %all-to-all-start.3 = ((f32[16,96,128]{2,1,0:T(8,128)}), f32[16,96,128]{2,1,0:T(8,128)S(1)}, u32[]{:S(2)}, u32[]{:S(2)}) async-start(f32[16,96,128]{2,1,0:T(8,128)} %back_wide.2), calls=%async_computation.3 | async-start | bytes 1572864 | tf_op jit(solution)/shard_map/back_wide/all_to_all | solution.py:14
  96.4 12.2 %collective-permute-start.9 = (f32[96,128]{1,0:T(8,128)S(1)}, f32[96,128]{1,0:T(8,128)S(1)}, u32[]{:S(2)}, u32[]{:S(2)}) collective-permute-start(f32[96,128]{1,0:T(8,128)S(1)} %get-tuple-element.80), channel_id=1, source_target_pairs={{0,8},{1,9},{2,10},{3,11},{4,12},{5,13},{6,14},{7,15},{8,0},{9,1},... | collective-permute-start | bytes 147464 | tf_op jit(solution)/shard_map/back_direct/ppermute | solution.py:185
  103.4 6.7 %collective-permute-start.11 = (f32[96,128]{1,0:T(8,128)S(1)}, f32[96,128]{1,0:T(8,128)S(1)}, u32[]{:S(2)}, u32[]{:S(2)}) collective-permute-start(f32[96,128]{1,0:T(8,128)S(1)} %get-tuple-element.81), channel_id=1, source_target_pairs={{0,12},{1,13},{2,14},{3,15},{4,8},{5,9},{6,10},{7,11},{8,4},{9,5},... | collective-permute-start | bytes 147464 | tf_op jit(solution)/shard_map/back_direct/ppermute | solution.py:185
  103.4 6.7 %collective-permute-start.10 = (f32[96,128]{1,0:T(8,128)S(1)}, f32[96,128]{1,0:T(8,128)S(1)}, u32[]{:S(2)}, u32[]{:S(2)}) collective-permute-start(f32[96,128]{1,0:T(8,128)S(1)} %get-tuple-element.82), channel_id=1, source_target_pairs={{0,4},{1,5},{2,6},{3,7},{4,0},{5,1},{6,2},{7,3},{8,12},{9,13},{10,... | collective-permute-start | bytes 147464 | tf_op jit(solution)/shard_map/back_direct/ppermute | solution.py:185
  111.0 27.1 %all-to-all-start.4 = ((f32[16,96,128]{2,1,0:T(8,128)}), f32[16,96,128]{2,1,0:T(8,128)S(1)}, u32[]{:S(2)}, u32[]{:S(2)}) async-start(f32[16,96,128]{2,1,0:T(8,128)} %broadcast_in_dim.16), calls=%async_computation.4 | async-start | bytes 1572864 | tf_op jit(solution)/shard_map/gather_wide/all_to_all | solution.py:14
  116.7 6.7 %collective-permute-start.14 = (f32[96,128]{1,0:T(8,128)S(1)}, f32[96,128]{1,0:T(8,128)S(1)}, u32[]{:S(2)}, u32[]{:S(2)}) collective-permute-start(f32[96,128]{1,0:T(8,128)S(1)} %fusion.7), channel_id=1, source_target_pairs={{0,12},{1,13},{2,14},{3,15},{4,8},{5,9},{6,10},{7,11},{8,4},{9,5},... | collective-permute-start | bytes 147464 | tf_op jit(solution)/shard_map/gather_row/ppermute | solution.py:185
  119.2 5.1 %collective-permute-start.13 = (f32[96,128]{1,0:T(8,128)S(1)}, f32[96,128]{1,0:T(8,128)S(1)}, u32[]{:S(2)}, u32[]{:S(2)}) collective-permute-start(f32[96,128]{1,0:T(8,128)S(1)} %fusion.7), channel_id=1, source_target_pairs={{0,4},{1,5},{2,6},{3,7},{4,0},{5,1},{6,2},{7,3},{8,12},{9,13},{10,... | collective-permute-start | bytes 147464 | tf_op jit(solution)/shard_map/gather_row/ppermute | solution.py:185
  122.1 8.3 %collective-permute-start.12 = (f32[96,128]{1,0:T(8,128)S(1)}, f32[96,128]{1,0:T(8,128)S(1)}, u32[]{:S(2)}, u32[]{:S(2)}) collective-permute-start(f32[96,128]{1,0:T(8,128)S(1)} %fusion.7), channel_id=1, source_target_pairs={{0,8},{1,9},{2,10},{3,11},{4,12},{5,13},{6,14},{7,15},{8,0},{9,1},... | collective-permute-start | bytes 147464 | tf_op jit(solution)/shard_map/gather_row/ppermute | solution.py:185
  130.4 7.3 %collective-permute-start.16 = (f32[4,96,128]{2,1,0:T(8,128)S(1)}, f32[4,96,128]{2,1,0:T(8,128)S(1)}, u32[]{:S(2)}, u32[]{:S(2)}) collective-permute-start(f32[4,96,128]{2,1,0:T(8,128)S(1)} %pad_maximum_fusion.1.first_ref), channel_id=1, source_target_pairs={{0,1},{1,0},{2,3},{3,2},{4,5},{5,4},{6,7},{7,6},{8,9},{9,8},{10,11... | collective-permute-start | bytes 589832 | tf_op jit(solution)/shard_map/gather_row/ppermute | solution.py:185
  132.5 5.7 %collective-permute-start.15 = (f32[4,96,128]{2,1,0:T(8,128)S(1)}, f32[4,96,128]{2,1,0:T(8,128)S(1)}, u32[]{:S(2)}, u32[]{:S(2)}) collective-permute-start(f32[4,96,128]{2,1,0:T(8,128)S(1)} %pad_maximum_fusion.1.first_ref), channel_id=1, source_target_pairs={{0,2},{1,3},{2,0},{3,1},{4,6},{5,7},{6,4},{7,5},{8,10},{9,11},{10,... | collective-permute-start | bytes 589832 | tf_op jit(solution)/shard_map/gather_row/ppermute | solution.py:185
  139.7 27.0 %all-to-all-start.5 = ((f32[16,96,128]{2,1,0:T(8,128)}), f32[16,96,128]{2,1,0:T(8,128)S(1)}, u32[]{:S(2)}, u32[]{:S(2)}) async-start(f32[16,96,128]{2,1,0:T(8,128)} %gather_column.3), calls=%async_computation.5 | async-start | bytes 1572864 | tf_op jit(solution)/shard_map/gather_column/all_to_all | solution.py:14
  143.8 8.4 %collective-permute-start.17 = (f32[4,96,128]{2,1,0:T(8,128)S(1)}, f32[4,96,128]{2,1,0:T(8,128)S(1)}, u32[]{:S(2)}, u32[]{:S(2)}) collective-permute-start(f32[4,96,128]{2,1,0:T(8,128)S(1)} %collective-permute-done.15.second_ref), channel_id=1, source_target_pairs={{0,1},{1,0},{2,3},{3,2},{4,5},{5,4},{6,7},{7,6},{8,9},{9,8},{10,11... | collective-permute-start | bytes 589832 | tf_op jit(solution)/shard_map/gather_row/ppermute | solution.py:185
  166.7 28.5 %all-to-all-start.6 = ((f32[16,96,128]{2,1,0:T(8,128)}), f32[16,96,128]{2,1,0:T(8,128)S(1)}, u32[]{:S(2)}, u32[]{:S(2)}) async-start(f32[16,96,128]{2,1,0:T(8,128)} %bitcast.20), calls=%async_computation.6 | async-start | bytes 1572864 | tf_op jit(solution)/shard_map/back_transposed/all_to_all | solution.py:14
  174.3 14.9 %collective-permute-start.19 = (f32[4,96,128]{2,1,0:T(8,128)S(1)}, f32[4,96,128]{2,1,0:T(8,128)S(1)}, u32[]{:S(2)}, u32[]{:S(2)}) collective-permute-start(f32[4,96,128]{2,1,0:T(8,128)S(1)} %get-tuple-element.68), channel_id=1, source_target_pairs={{0,1},{1,0},{2,3},{3,2},{4,5},{5,4},{6,7},{7,6},{8,9},{9,8},{10,11... | collective-permute-start | bytes 589832 | tf_op jit(solution)/shard_map/direct/ppermute | solution.py:185
  177.7 15.1 %collective-permute-start.18 = (f32[4,96,128]{2,1,0:T(8,128)S(1)}, f32[4,96,128]{2,1,0:T(8,128)S(1)}, u32[]{:S(2)}, u32[]{:S(2)}) collective-permute-start(f32[4,96,128]{2,1,0:T(8,128)S(1)} %get-tuple-element.66), channel_id=1, source_target_pairs={{0,1},{1,0},{2,3},{3,2},{4,5},{5,4},{6,7},{7,6},{8,9},{9,8},{10,11... | collective-permute-start | bytes 589832 | tf_op jit(solution)/shard_map/direct/ppermute | solution.py:185
  189.2 5.8 %collective-permute-start.20 = (f32[4,96,128]{2,1,0:T(8,128)S(1)}, f32[4,96,128]{2,1,0:T(8,128)S(1)}, u32[]{:S(2)}, u32[]{:S(2)}) collective-permute-start(f32[4,96,128]{2,1,0:T(8,128)S(1)} %add.59), channel_id=1, source_target_pairs={{0,2},{1,3},{2,0},{3,1},{4,6},{5,7},{6,4},{7,5},{8,10},{9,11},{10,... | collective-permute-start | bytes 589832 | tf_op jit(solution)/shard_map/direct/ppermute | solution.py:185
  197.0 18.6 %all-to-all-start.7 = ((f32[16,104,128]{2,1,0:T(8,128)}), f32[16,104,128]{2,1,0:T(8,128)S(1)}, u32[]{:S(2)}, u32[]{:S(2)}) async-start(f32[16,104,128]{2,1,0:T(8,128)} %back_wide.3), calls=%async_computation.7 | async-start | bytes 1703936 | tf_op jit(solution)/shard_map/back_wide/all_to_all | solution.py:14
  202.8 12.9 %collective-permute-start.21 = (f32[96,128]{1,0:T(8,128)S(1)}, f32[96,128]{1,0:T(8,128)S(1)}, u32[]{:S(2)}, u32[]{:S(2)}) collective-permute-start(f32[96,128]{1,0:T(8,128)S(1)} %get-tuple-element.77), channel_id=1, source_target_pairs={{0,8},{1,9},{2,10},{3,11},{4,12},{5,13},{6,14},{7,15},{8,0},{9,1},... | collective-permute-start | bytes 147464 | tf_op jit(solution)/shard_map/back_direct/ppermute | solution.py:185
  209.3 6.4 %collective-permute-start.23 = (f32[96,128]{1,0:T(8,128)S(1)}, f32[96,128]{1,0:T(8,128)S(1)}, u32[]{:S(2)}, u32[]{:S(2)}) collective-permute-start(f32[96,128]{1,0:T(8,128)S(1)} %get-tuple-element.78), channel_id=1, source_target_pairs={{0,12},{1,13},{2,14},{3,15},{4,8},{5,9},{6,10},{7,11},{8,4},{9,5},... | collective-permute-start | bytes 147464 | tf_op jit(solution)/shard_map/back_direct/ppermute | solution.py:185
  209.3 6.4 %collective-permute-start.22 = (f32[96,128]{1,0:T(8,128)S(1)}, f32[96,128]{1,0:T(8,128)S(1)}, u32[]{:S(2)}, u32[]{:S(2)}) collective-permute-start(f32[96,128]{1,0:T(8,128)S(1)} %get-tuple-element.79), channel_id=1, source_target_pairs={{0,4},{1,5},{2,6},{3,7},{4,0},{5,1},{6,2},{7,3},{8,12},{9,13},{10,... | collective-permute-start | bytes 147464 | tf_op jit(solution)/shard_map/back_direct/ppermute | solution.py:185
  246.9 10.2 %all-to-all-start.10 = ((f32[16,8,128]{2,1,0:T(8,128)}), f32[16,8,128]{2,1,0:T(8,128)S(1)}, u32[]{:S(2)}, u32[]{:S(2)}) async-start(f32[16,8,128]{2,1,0:T(8,128)} %broadcast_in_dim.40), calls=%async_computation.10 | async-start | bytes 131072 | tf_op jit(solution)/shard_map/gram_whole/all_to_all | solution.py:14
